TPU v7x, 32 devices: a whole 2x2x4 slice. The times are simulated.
32 devices in a mesh: dp: 32 (over z, y, x, core).
Axes of the slice: x: 2, y: 2, z: 4, core: 2. Of those that a mesh axis runs over, the one named last changes fastest.
Arguments:
- tokens: bfloat16 [32768, 512], P('dp'), may hold values from -6 to 6
- cotangent: bfloat16 [32768, 512], P('dp'), may hold values from -6 to 6
- patches: bfloat16 [256, 256, 1664], P('dp'), may hold values from -6 to 6
- lengths: int32 [256], P('dp'), may hold values from 8 to 128
- group_member: int32 [32], replicated, may hold values from 0 to 1, as said below
- mix: float32 [2], replicated, may hold values from 0.3 to 3
- gain_one: float32 [512], replicated, may hold values from 0.5 to 1.5
- w_query: bfloat16 [512, 384], replicated, may hold values from -0.25 to 0.25
- w_key: bfloat16 [512, 384], replicated, may hold values from -0.25 to 0.25
- w_value: bfloat16 [512, 384], replicated, may hold values from -0.25 to 0.25
- w_out: bfloat16 [384, 512], replicated, may hold values from -1.25 to 1.25
- gain_two: float32 [512], replicated, may hold values from 0.5 to 1.5
- w_patch: bfloat16 [1664, 512], replicated, may hold values from -0.15625 to 0.15625
- bias_patch: float32 [512], replicated, may hold values from -3 to 3
- w_cross_query: bfloat16 [512, 384], replicated, may hold values from -0.25 to 0.25
- w_cross_key: bfloat16 [512, 384], replicated, may hold values from -0.25 to 0.25
- w_cross_value: bfloat16 [512, 384], replicated, may hold values from -0.25 to 0.25
- w_cross_out: bfloat16 [384, 512], replicated, may hold values from -2.5 to 2.5
- gain_three: float32 [512], replicated, may hold values from 0.5 to 1.5
- w_gate: bfloat16 [512, 1024], replicated, may hold values from -0.25 to 0.25
- w_up: bfloat16 [512, 1024], replicated, may hold values from -0.25 to 0.25
- w_down: bfloat16 [1024, 512], replicated, may hold values from -0.1875 to 0.1875
Outputs:
- mixed_out: bfloat16 [32768, 512], P('dp')
- grad_tokens: float32 [32768, 512], P('dp')
- grad_patches: float32 [256, 256, 1664], P('dp')
- grad_gain_one: float32 [512], replicated
- grad_w_query: float32 [512, 384], replicated
- grad_w_key: float32 [512, 384], replicated
- grad_w_value: float32 [512, 384], replicated
- grad_w_out: float32 [384, 512], replicated
- grad_gain_two: float32 [512], replicated
- grad_w_patch: float32 [1664, 512], replicated
- grad_bias_patch: float32 [512], replicated
- grad_w_cross_query: float32 [512, 384], replicated
- grad_w_cross_key: float32 [512, 384], replicated
- grad_w_cross_value: float32 [512, 384], replicated
- grad_w_cross_out: float32 [384, 512], replicated
- grad_gain_three: float32 [512], replicated
- grad_w_gate: float32 [512, 1024], replicated
- grad_w_up: float32 [512, 1024], replicated
- grad_w_down: float32 [1024, 512], replicated
Inputs may be any that keep to these rules, and one draw needn't show every extreme that they name: `group_member`: between 4 and 16 devices, anywhere on the axis, hold 1 and form the robot trajectory group; the others form the web question answering group.
All inputs are finite; a program needn't handle non-finite values.
Results may differ from a plain program's by a relative error of at most 0.02.
The roundings to bfloat16 on the way count: a program that leaves them out, or rounds other values in their place, can miss the bound.
Values sent between devices are 32-bit elements; how exact they have to be, the bound alone decides.
No kernel may reach another device: no remote copies, remote signals or barrier semaphores. Data moves between devices by JAX's collectives and lax.ppermute only.
A program may use at most 192 MiB of HBM per device.

v0:
```python
import functools

import jax
import jax.numpy as jnp
from jax import lax
from jax.experimental import pallas as pl
from jax.experimental.pallas import tpu as pltpu
from jax.sharding import PartitionSpec as P

HEADS = 6
HEAD_DIM = 64
PAIRS = HEADS // 2
PAIR = 2 * HEAD_DIM
INNER = HEADS * HEAD_DIM
BLOCKS = 32
HALF = 16
EPSILON = 1e-06
F32 = jnp.float32
BF16 = jnp.bfloat16
VMEM = pltpu.VMEM
SMEM = pltpu.SMEM


def dot_plain(left_op, right_op):
    return jnp.dot(left_op, right_op, preferred_element_type=F32)


def dot_rows(left_op, right_op):
    return lax.dot_general(left_op, right_op, (((0,), (0,)), ((), ())), preferred_element_type=F32)


def dot_back(left_op, right_op):
    return lax.dot_general(left_op, right_op, (((1,), (1,)), ((), ())), preferred_element_type=F32)


def inverse_rms(values):
    return lax.rsqrt(jnp.mean(values * values, axis=-1, keepdims=True) + EPSILON)


def norm_backward(values, gain, grad):
    inverse = inverse_rms(values)
    unit = values * inverse
    scaled = grad * gain
    along = jnp.mean(scaled * unit, axis=-1, keepdims=True)
    return inverse * (scaled - unit * along), jnp.sum(grad * unit, axis=0, keepdims=True)


def lane_masks():
    lane = lax.broadcasted_iota(jnp.int32, (1, PAIR), 1)
    first = jnp.where(lane < HEAD_DIM, 1.0, 0.0)
    return first.astype(BF16), (1.0 - first).astype(BF16)


def stack_heads(values):
    first, second = lane_masks()
    return jnp.concatenate([values * first, values * second], axis=0)


def fold_heads(values):
    half = values.shape[0] // 2
    lane = lax.broadcasted_iota(jnp.int32, (half, PAIR), 1)
    return jnp.where(lane < HEAD_DIM, values[:half], values[half:])


def pair_forward(queries, key_rows, value_rows, allowed):
    keys = key_rows.shape[0]
    scores = dot_back(stack_heads(key_rows), queries).reshape(2, keys, queries.shape[0])
    if allowed is not None:
        scores = jnp.where(allowed, scores, -1000000000.0)
    expo = jnp.exp(scores - jnp.max(scores, axis=1, keepdims=True))
    chances = expo * (1.0 / jnp.sum(expo, axis=1, keepdims=True))
    chances = chances.reshape(2 * keys, queries.shape[0]).astype(BF16)
    return chances, dot_rows(chances, stack_heads(value_rows)).astype(BF16)


def pair_backward(queries, key_rows, value_rows, chances, grad_mixed):
    keys, count = key_rows.shape[0], queries.shape[0]
    wide = chances.astype(F32)
    grad_chances = dot_back(stack_heads(value_rows), grad_mixed)
    product = wide * grad_chances
    inner = jnp.sum(product.reshape(2, keys, count), axis=1, keepdims=True)
    spread = (wide.reshape(2, keys, count) * inner).reshape(2 * keys, count)
    grad_scores = (product - spread).astype(BF16)
    grad_values = fold_heads(dot_plain(chances, grad_mixed))
    grad_keys = fold_heads(dot_plain(grad_scores, queries))
    grad_queries = dot_rows(grad_scores, stack_heads(key_rows)) * 0.125
    return grad_queries.astype(BF16), grad_keys.astype(BF16), grad_values.astype(BF16)


def pair_lanes(index, offset=0):
    return pl.ds(offset + index * PAIR, PAIR)


def features_kernel(patch_ref, weight_ref, bias_ref, wk_ref, wv_ref, feat_ref, kv_ref, joined):
    @pl.when(pl.program_id(0) == 0)
    def join():
        joined[:, :INNER] = wk_ref[...]
        joined[:, INNER:] = wv_ref[...]

    feat = (dot_plain(patch_ref[...], weight_ref[...]) + bias_ref[...]).astype(BF16)
    feat_ref[...] = feat
    kv_ref[...] = dot_plain(feat, joined[...]).astype(BF16)


def self_forward_kernel(
    len_ref, tok_ref, g1_ref, wq_ref, wk_ref, wv_ref, wo_ref, g2_ref, wcq_ref,
    h1_ref, qkv_ref, pt_ref, o_ref, x1_ref, h2_ref, cq_ref, joined, wcq,
):
    step = pl.program_id(0)

    @pl.when(step == 0)
    def join():
        joined[:, :INNER] = wq_ref[...] * 0.125
        joined[:, INNER : 2 * INNER] = wk_ref[...]
        joined[:, 2 * INNER :] = wv_ref[...]
        wcq[...] = wcq_ref[...] * 0.125

    seqs, _, _, maxlen = pt_ref.shape
    x = tok_ref[...].astype(F32)
    h1 = (x * inverse_rms(x) * g1_ref[...]).astype(BF16)
    h1_ref[...] = h1
    qkv_ref[...] = dot_plain(h1, joined[...]).astype(BF16)
    key_at = lax.broadcasted_iota(jnp.int32, (1, maxlen, maxlen), 1)
    query_at = lax.broadcasted_iota(jnp.int32, (1, maxlen, maxlen), 2)
    for s in range(seqs):
        rows = pl.ds(s * maxlen, maxlen)
        allowed = (key_at <= query_at) & (key_at < len_ref[step * seqs + s])
        for p in range(PAIRS):
            pt_ref[s, p], o_ref[rows, pair_lanes(p)] = pair_forward(
                qkv_ref[rows, pair_lanes(p)],
                qkv_ref[rows, pair_lanes(p, INNER)],
                qkv_ref[rows, pair_lanes(p, 2 * INNER)],
                allowed,
            )
    x1 = x + dot_plain(o_ref[...], wo_ref[...])
    x1_ref[...] = x1
    h2 = (x1 * inverse_rms(x1) * g2_ref[...]).astype(BF16)
    h2_ref[...] = h2
    cq_ref[...] = dot_plain(h2, wcq[...]).astype(BF16)


def cross_forward_kernel(cq_ref, kv_ref, x1_ref, wco_ref, pt_ref, oc_ref, x2_ref):
    seqs, _, both, maxlen = pt_ref.shape
    patches = both // 2
    for s in range(seqs):
        rows, wide = pl.ds(s * maxlen, maxlen), pl.ds(s * patches, patches)
        for p in range(PAIRS):
            pt_ref[s, p], oc_ref[rows, pair_lanes(p)] = pair_forward(
                cq_ref[rows, pair_lanes(p)],
                kv_ref[wide, pair_lanes(p)],
                kv_ref[wide, pair_lanes(p, INNER)],
                None,
            )
    x2_ref[...] = x1_ref[...] + dot_plain(oc_ref[...], wco_ref[...])


def add_to(ref, first, value):
    @pl.when(first)
    def fresh():
        ref[...] = value

    @pl.when(jnp.logical_not(first))
    def more():
        ref[...] += value


def feed_forward_kernel(
    len_ref, code_ref, x2_ref, cot_ref, g3_ref, wg_ref, wu_ref, wd_ref,
    out_ref, dx2_ref, gain_ref, keep_ref, send_ref,
    hid, dgate, dup, acc_down, acc_gate, acc_up, *, maxlen,
):
    step, steps = pl.program_id(0), pl.num_programs(0)
    x2 = x2_ref[...]
    h3 = (x2 * inverse_rms(x2) * g3_ref[...]).astype(BF16)
    rows = x2.shape[0]
    seqs = rows // maxlen
    at = lax.broadcasted_iota(jnp.int32, (maxlen, 1), 0)
    keep = jnp.concatenate(
        [jnp.where(at < len_ref[step * seqs + s], 1.0, 0.0) for s in range(seqs)], axis=0
    )
    e = cot_ref[...].astype(F32) * keep
    de = e.astype(BF16)
    wide = wg_ref.shape[1]
    chunk = 256
    for c in range(wide // chunk):
        cols = pl.ds(c * chunk, chunk)
        gate = dot_plain(h3, wg_ref[:, cols])
        up = dot_plain(h3, wu_ref[:, cols])
        grad = dot_back(de, wd_ref[cols, :])
        square = gate * gate
        tanh = jnp.tanh(gate * (0.7978845608028654 + (0.7978845608028654 * 0.044715) * square))
        half = 0.5 * (1.0 + tanh)
        gelu = gate * half
        slope = half + (0.5 * gate) * (1.0 - tanh * tanh) * (
            0.7978845608028654 + (3.0 * 0.7978845608028654 * 0.044715) * square
        )
        hid[:, cols] = (gelu * up).astype(BF16)
        dgate[:, cols] = (grad * up * slope).astype(BF16)
        dup[:, cols] = (grad * gelu).astype(BF16)
    out_ref[...] = (x2 + dot_plain(hid[...], wd_ref[...])).astype(BF16)
    dh3 = dot_back(dgate[...], wg_ref[...]) + dot_back(dup[...], wu_ref[...])
    dx, gain = norm_backward(x2, g3_ref[...], dh3)
    dx2_ref[...] = e + dx
    add_to(gain_ref, step == 0, gain)
    add_to(acc_down, step == 0, dot_rows(hid[...], de))
    add_to(acc_gate, step == 0, dot_rows(h3, dgate[...]))
    add_to(acc_up, step == 0, dot_rows(h3, dup[...]))

    @pl.when(step == steps - 1)
    def finish():
        items = [(acc_down, acc_down.shape, 0), (acc_gate, acc_gate.shape, 0), (acc_up, acc_up.shape, 0)]
        pack(items, code_ref, keep_ref, send_ref)


def cross_backward_kernel(
    code_ref, dx2_ref, oc_ref, cq_ref, pt_ref, kv_ref, h2_ref, feat_ref, x1_ref, g2_ref,
    wco_ref, wcq_ref, wck_ref, wcv_ref,
    dfeat_ref, dx1_ref, gain_ref, bias_ref, keep_ref, send_ref,
    joined, dcq, dkv, acc_out, acc_query, acc_kv,
):
    step, steps = pl.program_id(0), pl.num_programs(0)

    @pl.when(step == 0)
    def join():
        joined[:, :INNER] = wck_ref[...]
        joined[:, INNER:] = wcv_ref[...]

    seqs, _, both, maxlen = pt_ref.shape
    patches = both // 2
    dx2 = dx2_ref[...]
    dc = dx2.astype(BF16)
    doc = dot_back(dc, wco_ref[...]).astype(BF16)
    for s in range(seqs):
        rows, wide = pl.ds(s * maxlen, maxlen), pl.ds(s * patches, patches)
        for p in range(PAIRS):
            dcq[rows, pair_lanes(p)], dkv[wide, pair_lanes(p)], dkv[wide, pair_lanes(p, INNER)] = (
                pair_backward(
                    cq_ref[rows, pair_lanes(p)],
                    kv_ref[wide, pair_lanes(p)],
                    kv_ref[wide, pair_lanes(p, INNER)],
                    pt_ref[s, p],
                    doc[s * maxlen : (s + 1) * maxlen, p * PAIR : (p + 1) * PAIR],
                )
            )
    dh2 = dot_back(dcq[...], wcq_ref[...])
    dfeat = dot_back(dkv[...], joined[...]).astype(BF16)
    dfeat_ref[...] = dfeat
    dx, gain = norm_backward(x1_ref[...], g2_ref[...], dh2)
    dx1_ref[...] = dx2 + dx
    add_to(gain_ref, step == 0, gain)
    add_to(bias_ref, step == 0, jnp.sum(dfeat.astype(F32), axis=0, keepdims=True))
    add_to(acc_out, step == 0, dot_rows(oc_ref[...], dc))
    add_to(acc_query, step == 0, dot_rows(h2_ref[...], dcq[...]))
    add_to(acc_kv, step == 0, dot_rows(feat_ref[...], dkv[...]))

    @pl.when(step == steps - 1)
    def finish():
        small = acc_query.shape
        items = [(acc_out, acc_out.shape, 0), (acc_query, small, 0), (acc_kv, small, 0), (acc_kv, small, INNER)]
        pack(items, code_ref, keep_ref, send_ref)


def patch_weight_kernel(code_ref, patch_ref, dfeat_ref, keep_ref, send_ref, acc, turned):
    step, steps = pl.program_id(0), pl.num_programs(0)
    add_to(acc, step == 0, dot_rows(dfeat_ref[...], patch_ref[...]))

    @pl.when(step == steps - 1)
    def finish():
        turned[...] = acc[...].T
        pack([(turned, turned.shape, 0)], code_ref, keep_ref, send_ref)


def patch_input_kernel(weight_ref, dfeat_ref, w_ref, out_ref):
    out_ref[...] = dot_back(dfeat_ref[...], w_ref[...]) * weight_ref[0]


def self_backward_kernel(
    code_ref, weight_ref, dx1_ref, o_ref, qkv_ref, pt_ref, h1_ref, tok_ref, g1_ref,
    wo_ref, wq_ref, wk_ref, wv_ref, gain_two_ref, gain_three_ref, bias_ref,
    dtok_ref, keep_ref, send_ref,
    joined, dqkv, acc_out, acc_qkv, gain, gain_block,
):
    step, steps = pl.program_id(0), pl.num_programs(0)

    @pl.when(step == 0)
    def join():
        joined[:, :INNER] = wq_ref[...]
        joined[:, INNER : 2 * INNER] = wk_ref[...]
        joined[:, 2 * INNER :] = wv_ref[...]

    seqs, _, _, maxlen = pt_ref.shape
    dx1 = dx1_ref[...]
    da = dx1.astype(BF16)
    do = dot_back(da, wo_ref[...]).astype(BF16)
    for s in range(seqs):
        rows = pl.ds(s * maxlen, maxlen)
        for p in range(PAIRS):
            lanes = [pair_lanes(p, k * INNER) for k in range(3)]
            dqkv[rows, lanes[0]], dqkv[rows, lanes[1]], dqkv[rows, lanes[2]] = pair_backward(
                qkv_ref[rows, lanes[0]],
                qkv_ref[rows, lanes[1]],
                qkv_ref[rows, lanes[2]],
                pt_ref[s, p],
                do[s * maxlen : (s + 1) * maxlen, p * PAIR : (p + 1) * PAIR],
            )
    dh1 = dot_back(dqkv[...], joined[...])
    dx, grad_gain = norm_backward(tok_ref[...].astype(F32), g1_ref[...], dh1)
    dtok_ref[...] = (dx1 + dx) * weight_ref[0]
    add_to(gain, step == 0, grad_gain)
    add_to(acc_out, step == 0, dot_rows(o_ref[...], da))
    add_to(acc_qkv, step == 0, dot_rows(h1_ref[...], dqkv[...]))

    @pl.when(step == steps - 1)
    def finish():
        gain_block[...] = jnp.zeros_like(gain_block)
        for k, ref in enumerate((gain, gain_two_ref, gain_three_ref, bias_ref)):
            for t in range(4):
                gain_block[pl.ds((4 * k + t) * 8, 1), :] = ref[:, pl.ds(t * 128, 128)]
        small = (acc_qkv.shape[0], INNER)
        items = [(acc_out, acc_out.shape, 0)]
        items += [(acc_qkv, small, k * INNER) for k in range(3)]
        items += [(gain_block, gain_block.shape, 0)]
        pack(items, code_ref, keep_ref, send_ref)


def flips(count, first, second):
    return [(i, i ^ (first if i % 2 == 0 else second)) for i in range(count)]


def code_pair(me):
    core, ex, why = me & 1, (me >> 1) & 1, (me >> 2) & 1
    low = (me >> 3) & 3
    low = ((low & 1) << 1) | (low >> 1)
    first = jnp.where(core == 0, ex, why)
    second = jnp.where(core == 0, why, ex)
    own = core * 16 + first * 8 + second * 4 + low
    other = (1 - core) * 16 + second * 8 + first * 4 + low
    return own, other


def exchange(values, first, second=None):
    count = lax.axis_size("dp")
    return lax.ppermute(values, "dp", flips(count, first, first if second is None else second))


def block_rows(shape):
    return shape[0] * shape[1] // (BLOCKS * 128)


def block_parts(shape, index, offset):
    rows, lanes = shape
    tiles = lanes // 128
    if BLOCKS % tiles:
        height = rows // BLOCKS
        return [
            (pl.ds(pl.multiple_of(index * height, 8), height), pl.ds(offset + t * 128, 128))
            for t in range(tiles)
        ]
    height = rows * tiles // BLOCKS
    row, lane = index // tiles, index % tiles
    return [
        (
            pl.ds(pl.multiple_of(row * height, 8), height),
            pl.ds(pl.multiple_of(offset + lane * 128, 128), 128),
        )
    ]


def pack(items, code_ref, keep_ref, send_ref):
    def step(p, carry):
        for code, out_ref in ((code_ref[0], keep_ref), (code_ref[1], send_ref)):
            start = 0
            for ref, shape, offset in items:
                for rows, lanes in block_parts(shape, p ^ code, offset):
                    out_ref[p, pl.ds(start, rows.size), :] = ref[rows, lanes]
                    start += rows.size
        return carry

    lax.fori_loop(0, HALF, step, 0)


def unpack_kernel(shapes, with_gains, code_ref, *refs):
    ins, outs = refs[:4], refs[4:]
    for k, piece in enumerate(ins):

        def step(p, carry, piece=piece, k=k):
            index = (p + 8 * (k % 2)) ^ code_ref[k // 2]
            start = 0
            for shape, out_ref in zip(shapes, outs):
                for rows, lanes in block_parts(shape, index, 0):
                    out_ref[rows, lanes] = piece[p, pl.ds(start, rows.size), :]
                    start += rows.size
            return carry

        lax.fori_loop(0, 8, step, 0)
    if with_gains:
        count = len(shapes)
        block = outs[count - 1]
        for k, out_ref in enumerate(outs[count:]):
            for t in range(4):
                out_ref[:, pl.ds(t * 128, 128)] = block[pl.ds((4 * k + t) * 8, 1), :]


def vmem(count):
    return [pl.BlockSpec(memory_space=VMEM)] * count


def unpack(pieces, shapes, codes, with_gains=False):
    outs = [jax.ShapeDtypeStruct(s, F32) for s in shapes]
    if with_gains:
        outs += [jax.ShapeDtypeStruct((1, 512), F32)] * 4
    return pl.pallas_call(
        functools.partial(unpack_kernel, shapes, with_gains),
        out_shape=outs,
        in_specs=[pl.BlockSpec(memory_space=SMEM)] + vmem(4),
        out_specs=vmem(len(outs)),
        compiler_params=pltpu.CompilerParams(vmem_limit_bytes=40 * 2**20),
        name="unpack",
    )(codes, *pieces)


def sum_blocks(packed, own, other):
    keep, send = packed
    got = exchange(send, 1)
    keep, got = keep * own, got * other
    for first, second in ((2, 4), (4, 2), (8, 8), (16, 16)):
        half = keep.shape[0] // 2
        send, keep = keep[half:] + got[half:], keep[:half] + got[:half]
        got = exchange(send, first, second)
    keep = keep + got
    extra = BLOCKS
    while extra < lax.axis_size("dp"):
        keep = keep + exchange(keep, extra)
        extra *= 2
    return keep


def spread_blocks(held):
    held = jnp.concatenate([held, exchange(held, 16)])
    held = jnp.concatenate([held, exchange(held, 8)])
    held = jnp.concatenate([held, exchange(held, 4, 2)])
    near = exchange(held, 1)
    rest = exchange(held, 2, 4)
    far = exchange(rest, 1)
    return held, rest, near, far


def by_step(array_shape, steps):
    block = (array_shape[0] // steps,) + tuple(array_shape[1:])
    return pl.BlockSpec(block, lambda i: (i,) + (0,) * (len(block) - 1))


def whole(array_shape):
    return pl.BlockSpec(tuple(array_shape), lambda i: (0,) * len(array_shape))


SCALARS = pl.BlockSpec(memory_space=SMEM)


def run(kernel, name, steps, scalars, stepped, fixed, order, outs, scratch, cost):
    lists = {"s": iter(scalars), "r": iter(stepped), "f": iter(fixed)}
    operands = [next(lists[c]) for c in order]
    in_specs = [
        SCALARS if c == "s" else by_step(v.shape, steps) if c == "r" else whole(v.shape)
        for c, v in zip(order, operands)
    ]
    return pl.pallas_call(
        kernel,
        grid=(steps,),
        out_shape=[jax.ShapeDtypeStruct(s, d) for s, d, _ in outs],
        in_specs=in_specs,
        out_specs=[by_step(s, steps) if moves else whole(s) for s, _, moves in outs],
        scratch_shapes=[VMEM(s, d) for s, d in scratch],
        compiler_params=pltpu.CompilerParams(vmem_limit_bytes=56 * 2**20),
        cost_estimate=pl.CostEstimate(flops=int(cost * 1e9), bytes_accessed=2**20, transcendentals=0),
        name=name,
    )(*operands)


def local(
    tokens,
    cotangent,
    patches,
    lengths,
    group_member,
    mix,
    gain_one,
    w_query,
    w_key,
    w_value,
    w_out,
    gain_two,
    w_patch,
    bias_patch,
    w_cross_query,
    w_cross_key,
    w_cross_value,
    w_cross_out,
    gain_three,
    w_gate,
    w_up,
    w_down,
):
    seqs = lengths.shape[0]
    rows, width = tokens.shape
    maxlen = rows // seqs
    images, patch_dim = patches.shape[1], patches.shape[2]
    image_rows = seqs * images
    wide = w_gate.shape[1]
    steps = seqs // 2
    part = rows // steps
    flat = patches.reshape(image_rows, patch_dim)
    gain_one, gain_two, gain_three, bias_patch = (
        g.reshape(1, width) for g in (gain_one, gain_two, gain_three, bias_patch)
    )

    me = lax.axis_index("dp")
    codes = jnp.stack(code_pair(me))
    members = lax.dynamic_slice_in_dim(group_member, me & ~1, 2)
    in_first = lax.dynamic_index_in_dim(members, me & 1, keepdims=False) == 1
    other_first = lax.dynamic_index_in_dim(members, 1 - (me & 1), keepdims=False) == 1
    own_count = jnp.sum(lengths).astype(F32)
    counts = own_count * jnp.where(in_first, jnp.array([1.0, 0.0], F32), jnp.array([0.0, 1.0], F32))
    bit = 1
    while bit < lax.axis_size("dp"):
        counts = counts + exchange(counts, bit)
        bit *= 2
    group_weights = mix * jnp.sum(counts) / counts
    weight_own = jnp.where(in_first, group_weights[0], group_weights[1])
    weight_other = jnp.where(other_first, group_weights[0], group_weights[1])
    weight_ref = weight_own[None]

    feat, cross_kv = run(
        features_kernel, "features", steps, [], [flat],
        [w_patch, bias_patch, w_cross_key, w_cross_value], "rffff",
        [((image_rows, width), BF16, True), ((image_rows, 2 * INNER), BF16, True)],
        [((width, 2 * INNER), BF16)], 5.1,
    )
    h1, qkv, chances, mixed, x1, h2, cross_q = run(
        self_forward_kernel, "self_forward", steps, [lengths], [tokens],
        [gain_one, w_query, w_key, w_value, w_out, gain_two, w_cross_query], "srfffffff",
        [
            ((rows, width), BF16, True),
            ((rows, 3 * INNER), BF16, True),
            ((seqs, PAIRS, 2 * maxlen, maxlen), BF16, True),
            ((rows, INNER), BF16, True),
            ((rows, width), F32, True),
            ((rows, width), BF16, True),
            ((rows, INNER), BF16, True),
        ],
        [((width, 3 * INNER), BF16), ((width, INNER), BF16)], 6.0,
    )
    cross_chances, cross_mixed, x2 = run(
        cross_forward_kernel, "cross_forward", steps, [], [cross_q, cross_kv, x1], [w_cross_out], "rrrf",
        [
            ((seqs, PAIRS, 2 * images, maxlen), BF16, True),
            ((rows, INNER), BF16, True),
            ((rows, width), F32, True),
        ],
        [], 6.0,
    )
    late_shapes = [w_down.shape, w_gate.shape, w_up.shape]
    late_rows = sum(block_rows(s) for s in late_shapes)
    result, dx2, gain3, *late = run(
        functools.partial(feed_forward_kernel, maxlen=maxlen), "feed_forward", steps,
        [lengths, codes], [x2, cotangent], [gain_three, w_gate, w_up, w_down], "ssrrffff",
        [
            ((rows, width), BF16, True),
            ((rows, width), F32, True),
            ((1, width), F32, False),
            ((HALF, late_rows, 128), F32, False),
            ((HALF, late_rows, 128), F32, False),
        ],
        [
            ((part, wide), BF16),
            ((part, wide), BF16),
            ((part, wide), BF16),
            (w_down.shape, F32),
            (w_gate.shape, F32),
            (w_up.shape, F32),
        ],
        14.0,
    )
    cross_shapes = [w_cross_out.shape, w_cross_query.shape, w_cross_key.shape, w_cross_value.shape]
    cross_rows = sum(block_rows(s) for s in cross_shapes)
    dfeat, dx1, gain2, dbias, *cross = run(
        cross_backward_kernel, "cross_backward", steps, [codes],
        [dx2, cross_mixed, cross_q, cross_chances, cross_kv, h2, feat, x1],
        [gain_two, w_cross_out, w_cross_query, w_cross_key, w_cross_value], "srrrrrrrrfffff",
        [
            ((image_rows, width), BF16, True),
            ((rows, width), F32, True),
            ((1, width), F32, False),
            ((1, width), F32, False),
            ((HALF, cross_rows, 128), F32, False),
            ((HALF, cross_rows, 128), F32, False),
        ],
        [
            ((width, 2 * INNER), BF16),
            ((part, INNER), BF16),
            ((image_rows // steps, 2 * INNER), BF16),
            (w_cross_out.shape, F32),
            (w_cross_query.shape, F32),
            ((width, 2 * INNER), F32),
        ],
        10.0,
    )
    patch_shapes = [w_patch.shape]
    patch_rows = block_rows(w_patch.shape)
    patch = run(
        patch_weight_kernel, "patch_weight", steps, [codes], [flat, dfeat], [], "srr",
        [((HALF, patch_rows, 128), F32, False), ((HALF, patch_rows, 128), F32, False)],
        [((width, patch_dim), F32), ((patch_dim, width), F32)], 5.0,
    )
    own_shapes = [w_out.shape, w_query.shape, w_key.shape, w_value.shape, (BLOCKS * 8, 128)]
    own_rows = sum(block_rows(s) for s in own_shapes)
    grad_tokens, *own = run(
        self_backward_kernel, "self_backward", steps, [codes, weight_ref],
        [dx1, mixed, qkv, chances, h1, tokens],
        [gain_one, w_out, w_query, w_key, w_value, gain2, gain3, dbias], "ssrrrrrrffffffff",
        [
            ((rows, width), F32, True),
            ((HALF, own_rows, 128), F32, False),
            ((HALF, own_rows, 128), F32, False),
        ],
        [
            ((width, 3 * INNER), BF16),
            ((part, 3 * INNER), BF16),
            (w_out.shape, F32),
            ((width, 3 * INNER), F32),
            ((1, width), F32),
            ((BLOCKS * 8, 128), F32),
        ],
        8.0,
    )
    (grad_patches,) = run(
        patch_input_kernel, "patch_input", 2 * steps, [weight_ref], [dfeat], [w_patch], "srf",
        [((image_rows, patch_dim), F32, True)], [], 4.0,
    )

    pieces = [spread_blocks(sum_blocks(v, weight_own, weight_other)) for v in (late, cross, patch, own)]
    late = unpack(pieces[0], late_shapes, codes)
    cross = unpack(pieces[1], cross_shapes, codes)
    patch = unpack(pieces[2], patch_shapes, codes)
    own = unpack(pieces[3], own_shapes, codes, True)
    gains = [g.reshape(width) for g in own[5:]]
    return (
        result,
        grad_tokens,
        grad_patches.reshape(seqs, images, patch_dim),
        gains[0],
        own[1],
        own[2],
        own[3],
        own[0],
        gains[1],
        patch[0],
        gains[3],
        cross[1],
        cross[2],
        cross[3],
        cross[0],
        gains[2],
        late[1],
        late[2],
        late[0],
    )


def solution(mesh):
    split = P("dp", None)
    images = P("dp", None, None)
    return jax.shard_map(
        local,
        mesh=mesh,
        in_specs=(split, split, images, P("dp")) + (P(),) * 18,
        out_specs=(split, split, images) + (P(),) * 16,
        check_vma=False,
    )
```

profile of v0, /device:TPU:0, one launch (start us, length us, event | category | flops | bytes accessed | tf_op | source)
XLA Modules:
  0.0 358.0 jit_solution(5223245238042875019)
XLA Ops:
  0.7 1.3 reduce_sum.18
  2.6 1.3 fusion.6
  6.3 9.8 %features.1 = (bf16[2048,512]{1,0:T(8,128)(2,1)}, bf16[2048,768]{1,0:T(8,128)(2,1)}) custom-call(bf16[2048,1664]{1,0:T(8,128)(2,1)} %bitcast.18, bf16[1664,512]{1,0:T(8,128)(2,1)} %w_ref.1, f32[1,512]{1,0:T(1,128)} %bitcast.20, bf16[512,384]{1,0:T(8,128)(2,1)} %wck_ref.1, bf16[512,384]{1,0:T(8,128)(2,1)} %wcv_ref.1), custom_call_target="tpu_custom_call" | custom-call | flops 5100000256 | bytes 1048576 | tf_op jit(solution)/shard_map/features/pallas_call | solution.py:467
  16.2 9.4 %self_forward.1 = (bf16[1024,512]{1,0:T(8,128)(2,1)}, bf16[1024,1152]{1,0:T(8,128)(2,1)}, bf16[8,3,256,128]{3,2,1,0:T(8,128)(2,1)}, bf16[1024,384]{1,0:T(8,128)(...) custom-call(s32[8]{0:T(128)} %len_ref.3, bf16[1024,512]{1,0:T(8,128)(2,1)} %tok_ref.3, ...), custom_call_target="tpu_custom_call" | custom-call | flops 6000000000 | bytes 1048576 | tf_op jit(solution)/shard_map/self_forward/pallas_call | solution.py:467
  25.5 8.1 %cross_forward.1 = (bf16[8,3,512,128]{3,2,1,0:T(8,128)(2,1)}, bf16[1024,384]{1,0:T(8,128)(2,1)}, f32[1024,512]{1,0:T(8,128)}) custom-call(bf16[1024,384]{1,0:T(8,128)(2,1)} %get-tuple-element.62.cq_ref, bf16[2048,768]{1,0:T(8,128)(2,1)} %get-tuple-element.63.kv_ref, f32[1024,512]{1,0:T(8,128)} %get-tuple-element.64.x1_ref, bf16[384,512]{1,0:T(8,128)(2,1)} %wco_ref.3), custom_call_target="tpu_custom_call" | custom-call | flops 6000000000 | bytes 1048576 | tf_op jit(solution)/shard_map/cross_forward/pallas_call | solution.py:467
  33.7 23.4 %feed_forward.1 = (bf16[1024,512]{1,0:T(8,128)(2,1)}, f32[1024,512]{1,0:T(8,128)}, f32[1,512]{1,0:T(1,128)}, f32[16,384,128]{2,1,0:T(8,128)}, f32[16,384,128]{2,1,0:T(8,128)}) custom-call(s32[8]{0:T(128)} %len_ref.3, s32[2]{0:T(128)} %pad_add_fusion.code_ref, f32[1024,512]{1,0:T(8,128)} %get-tuple-element.65.x2_ref, bf16[1024,512]{1,0:T(8,128)(2,1)} %cot_ref.1, ...), custom_call_target="tpu_custom_call" | custom-call | flops 14000000000 | bytes 1048576 | tf_op jit(solution)/shard_map/feed_forward/pallas_call | solution.py:467
  57.1 24.0 %cross_backward.1 = (bf16[2048,512]{1,0:T(8,128)(2,1)}, f32[1024,512]{1,0:T(8,128)}, f32[1,512]{1,0:T(1,128)}, f32[1,512]{1,0:T(1,128)}, f32[16,192,128]{2,1,0:T(8,128)}, /*index=5*/f32[16,192,128]{2,1,0:T(8,128)}) custom-call(s32[2]{0:T(128)} %pad_add_fusion.code_ref, f32[1024,512]{1,0:T(8,128)} %get-tuple-element.67.dx2_ref, ...), custom_call_target="tpu_custom_call" | custom-call | flops 10000000000 | bytes 1048576 | tf_op jit(solution)/shard_map/cross_backward/pallas_call | solution.py:467
  81.7 10.9 %patch_weight.1 = (f32[16,208,128]{2,1,0:T(8,128)}, f32[16,208,128]{2,1,0:T(8,128)}) custom-call(s32[2]{0:T(128)} %pad_add_fusion.code_ref, bf16[2048,1664]{1,0:T(8,128)(2,1)} %bitcast.19, bf16[2048,512]{1,0:T(8,128)(2,1)} %get-tuple-element.81.dfeat_ref), custom_call_target="tpu_custom_call" | custom-call | flops 5000000000 | bytes 1048576 | tf_op jit(solution)/shard_map/patch_weight/pallas_call | solution.py:467
  93.4 3.0 collective-permute-start.1
  96.4 1.5 collective-permute-done.1
  97.9 2.0 collective-permute-start.2
  100.0 1.5 collective-permute-done.2
  101.5 1.5 collective-permute-start.3
  103.0 2.0 collective-permute-done.3
  105.0 2.7 collective-permute-start.4
  107.7 1.8 collective-permute-done.4
  112.6 18.3 %self_backward.1 = (f32[1024,512]{1,0:T(8,128)}, f32[16,200,128]{2,1,0:T(8,128)}, f32[16,200,128]{2,1,0:T(8,128)}) custom-call(s32[2]{0:T(128)} %pad_add_fusion.code_ref, f32[1]{0:T(128)} %bitcast.10.weight_ref, f32[1024,512]{1,0:T(8,128)} %get-tuple-element.72.dx1_ref, bf16[1024,384]{1,0:T(8,128)(2,1)} %get-tuple-element.73.o_ref, ...), custom_call_target="tpu_custom_call" | custom-call | flops 8000000000 | bytes 1048576 | tf_op jit(solution)/shard_map/self_backward/pallas_call | solution.py:467
  131.1 1.3 copy-done.10
  133.8 2.3 broadcast_multiply_fusion.1
  136.3 2.2 broadcast_multiply_fusion
  138.9 2.1 collective-permute-start.39
  141.0 1.5 broadcast_multiply_fusion.6
  142.8 1.5 broadcast_multiply_fusion.4
  144.6 2.1 collective-permute-start.6
  146.6 1.6 broadcast_multiply_fusion.2
  148.5 10.8 %collective-permute-done.39 = f32[8,384,128]{2,1,0:T(8,128)S(1)} collective-permute-done((f32[8,384,128]{2,1,0:T(8,128)S(1)}, f32[8,384,128]{2,1,0:T(8,128)S(1)}, u32[]{:S(2)}, u32[]{:S(2)}) %collective-permute-start.39) | collective-permute-done | bytes 1572896 | tf_op jit(solution)/shard_map/ppermute | solution.py:343
  159.6 2.1 collective-permute-start.40
  161.7 11.7 %collective-permute-done.28 = f32[8,192,128]{2,1,0:T(8,128)S(1)} collective-permute-done((f32[8,192,128]{2,1,0:T(8,128)S(1)}, f32[8,192,128]{2,1,0:T(8,128)S(1)}, u32[]{:S(2)}, u32[]{:S(2)}) %collective-permute-start.28) | collective-permute-done | bytes 786464 | tf_op jit(solution)/shard_map/ppermute | solution.py:343
  173.5 2.4 collective-permute-start.29
  175.9 13.4 %collective-permute-done.6 = f32[8,200,128]{2,1,0:T(8,128)S(1)} collective-permute-done((f32[8,200,128]{2,1,0:T(8,128)S(1)}, f32[8,200,128]{2,1,0:T(8,128)S(1)}, u32[]{:S(2)}, u32[]{:S(2)}) %collective-permute-start.6) | collective-permute-done | bytes 819232 | tf_op jit(solution)/shard_map/ppermute | solution.py:343
  189.3 2.1 collective-permute-start.7
  191.4 11.3 %collective-permute-done.17 = f32[8,208,128]{2,1,0:T(8,128)S(1)} collective-permute-done((f32[8,208,128]{2,1,0:T(8,128)S(1)}, f32[8,208,128]{2,1,0:T(8,128)S(1)}, u32[]{:S(2)}, u32[]{:S(2)}) %collective-permute-start.17) | collective-permute-done | bytes 852000 | tf_op jit(solution)/shard_map/ppermute | solution.py:343
  202.9 2.1 collective-permute-start.18
  208.4 8.8 %collective-permute-done.41 = f32[2,384,128]{2,1,0:T(8,128)S(1)} collective-permute-done((f32[2,384,128]{2,1,0:T(8,128)S(1)}, f32[2,384,128]{2,1,0:T(8,128)S(1)}, u32[]{:S(2)}, u32[]{:S(2)}) %collective-permute-start.41) | collective-permute-done | bytes 393248 | tf_op jit(solution)/shard_map/ppermute | solution.py:343
  217.2 2.0 collective-permute-start.42
  219.3 7.4 %collective-permute-done.30 = f32[2,192,128]{2,1,0:T(8,128)S(1)} collective-permute-done((f32[2,192,128]{2,1,0:T(8,128)S(1)}, f32[2,192,128]{2,1,0:T(8,128)S(1)}, u32[]{:S(2)}, u32[]{:S(2)}) %collective-permute-start.30) | collective-permute-done | bytes 196640 | tf_op jit(solution)/shard_map/ppermute | solution.py:343
  226.8 1.2 collective-permute-done.42
  228.0 3.5 collective-permute-start.43
  231.5 5.2 %collective-permute-start.19 = (f32[2,208,128]{2,1,0:T(8,128)S(1)}, f32[2,208,128]{2,1,0:T(8,128)S(1)}, u32[]{:S(2)}, u32[]{:S(2)}) collective-permute-start(f32[2,208,128]{2,1,0:T(8,128)S(1)} %get-tuple-element.126), channel_id=1, source_target_pairs={{0,8},{1,9},{2,10},{3,11},{4,12},{5,13},{6,14},{7,15},{8,0},{9,1},... | collective-permute-start | bytes 638984 | tf_op jit(solution)/shard_map/ppermute | solution.py:343
  236.7 5.3 %collective-permute-done.43 = f32[1,384,128]{2,1,0:T(8,128)S(1)} collective-permute-done((f32[1,384,128]{2,1,0:T(8,128)S(1)}, f32[1,384,128]{2,1,0:T(8,128)S(1)}, u32[]{:S(2)}, u32[]{:S(2)}) %collective-permute-start.43) | collective-permute-done | bytes 196640 | tf_op jit(solution)/shard_map/ppermute | solution.py:343
  242.2 2.5 collective-permute-start.32
  245.2 11.1 %collective-permute-done.44 = f32[2,384,128]{2,1,0:T(8,128)S(1)} collective-permute-done((f32[2,384,128]{2,1,0:T(8,128)S(1)}, f32[2,384,128]{2,1,0:T(8,128)S(1)}, u32[]{:S(2)}, u32[]{:S(2)}) %collective-permute-start.44) | collective-permute-done | bytes 393248 | tf_op jit(solution)/shard_map/ppermute | solution.py:343
  256.4 3.5 collective-permute-start.45
  260.1 1.8 collective-permute-start.10
  261.9 1.3 collective-permute-start.20
  263.1 2.6 collective-permute-done.10
  265.8 3.1 collective-permute-start.11
  268.9 1.9 collective-permute-done.33
  271.2 1.9 collective-permute-done.11
  273.1 3.6 %collective-permute-start.12 = (f32[4,200,128]{2,1,0:T(8,128)S(1)}, f32[4,200,128]{2,1,0:T(8,128)S(1)}, u32[]{:S(2)}, u32[]{:S(2)}) collective-permute-start(f32[4,200,128]{2,1,0:T(8,128)S(1)} %pad_maximum_fusion.6), channel_id=1, source_target_pairs={{0,4},{1,3},{2,6},{3,1},{4,0},{5,7},{6,2},{7,5},{8,12},{9,11},{10,... | collective-permute-start | bytes 1228808 | tf_op jit(solution)/shard_map/ppermute | solution.py:343
  276.9 6.4 %collective-permute-done.21 = f32[1,208,128]{2,1,0:T(8,128)S(1)} collective-permute-done((f32[1,208,128]{2,1,0:T(8,128)S(1)}, f32[1,208,128]{2,1,0:T(8,128)S(1)}, u32[]{:S(2)}, u32[]{:S(2)}) %collective-permute-start.21) | collective-permute-done | bytes 106528 | tf_op jit(solution)/shard_map/ppermute | solution.py:343
  283.9 7.9 %collective-permute-done.12 = f32[4,200,128]{2,1,0:T(8,128)S(1)} collective-permute-done((f32[4,200,128]{2,1,0:T(8,128)S(1)}, f32[4,200,128]{2,1,0:T(8,128)S(1)}, u32[]{:S(2)}, u32[]{:S(2)}) %collective-permute-start.12) | collective-permute-done | bytes 409632 | tf_op jit(solution)/shard_map/ppermute | solution.py:343
  292.1 12.7 %collective-permute-done.23 = f32[4,208,128]{2,1,0:T(8,128)S(1)} collective-permute-done((f32[4,208,128]{2,1,0:T(8,128)S(1)}, f32[4,208,128]{2,1,0:T(8,128)S(1)}, u32[]{:S(2)}, u32[]{:S(2)}) %collective-permute-start.23) | collective-permute-done | bytes 426016 | tf_op jit(solution)/shard_map/ppermute | solution.py:343
  305.8 2.0 collective-permute-start.13
  307.9 1.9 collective-permute-start.37
  312.1 14.3 %collective-permute-done.13.refs_1_ = f32[8,200,128]{2,1,0:T(8,128)} collective-permute-done((f32[8,200,128]{2,1,0:T(8,128)S(1)}, f32[8,200,128]{2,1,0:T(8,128)}, u32[]{:S(2)}, u32[]{:S(2)}) %collective-permute-start.13) | collective-permute-done | bytes 819232 | tf_op jit(solution)/shard_map/ppermute | solution.py:343
  329.0 10.1 %patch_input.1 = f32[2048,1664]{1,0:T(8,128)} custom-call(f32[1]{0:T(128)} %bitcast.10.weight_ref, bf16[2048,512]{1,0:T(8,128)(2,1)} %get-tuple-element.81.dfeat_ref, bf16[1664,512]{1,0:T(8,128)(2,1)} %w_ref.1), custom_call_target="tpu_custom_call" | custom-call | flops 4000000000 | bytes 1048576 | tf_op jit(solution)/shard_map/patch_input/pallas_call | solution.py:467
  339.1 1.1 copy-done.3
  340.3 1.1 copy-done.5
  341.4 1.1 copy-done.7
  342.5 2.8 unpack.6
  345.3 3.7 %unpack.4 = (f32[384,512]{1,0:T(8,128)}, f32[512,384]{1,0:T(8,128)}, f32[512,384]{1,0:T(8,128)}, f32[512,384]{1,0:T(8,128)}, f32[256,128]{1,0:T(8,128)}, /*index...) custom-call(s32[2]{0:T(128)S(1)} %copy-done.8, ...), custom_call_target="tpu_custom_call" | custom-call | tf_op jit(solution)/shard_map/unpack/pallas_call | solution.py:412
  349.0 3.8 %unpack.5 = f32[1664,512]{1,0:T(8,128)} custom-call(s32[2]{0:T(128)S(1)} %copy-done.8, f32[8,208,128]{2,1,0:T(8,128)S(1)} %pad_maximum_fusion.1.refs_0_, f32[8,208,128]{2,1,0:T(8,128)S(1)} %collective-permute-done.24.refs_1_, f32[8,208,128]{2,1,0:T(8,128)} %collective-permute-done.25.refs_2_, f32[8,208,128]{2,1,0:T(8,128)} %collective-permute-done.26.refs_3_), custom_call_target="tpu_custom_call" | custom-call | tf_op jit(solution)/shard_map/unpack/pallas_call | solution.py:412
  352.8 5.1 %unpack.7 = (f32[1024,512]{1,0:T(8,128)}, f32[512,1024]{1,0:T(8,128)}, f32[512,1024]{1,0:T(8,128)}) custom-call(s32[2]{0:T(128)S(1)} %copy-done.8, f32[8,384,128]{2,1,0:T(8,128)S(1)} %pad_maximum_fusion.refs_0_, f32[8,384,128]{2,1,0:T(8,128)S(1)} %collective-permute-done.46.refs_1_, f32[8,384,128]{2,1,0:T(8,128)S(1)} %collective-permute-done.47.refs_2_, ...), custom_call_target="tpu_custom_call" | custom-call | tf_op jit(solution)/shard_map/unpack/pallas_call | solution.py:412
  (125 shorter events, 18.5 us)
Async XLA Ops:
  5.3 88.1 %collective-permute-start = (f32[2]{0:T(128)S(1)}, f32[2]{0:T(128)S(1)}, u32[]{:S(2)}, u32[]{:S(2)}) collective-permute-start(f32[2]{0:T(128)S(1)} %fusion.4), channel_id=1, source_target_pairs={{0,1},{1,0},{2,3},{3,2},{4,5},{5,4},{6,7},{7,6},{8,9},{9,8},{10,11... | collective-permute-start | bytes 32 | tf_op jit(solution)/shard_map/ppermute | solution.py:343
  81.2 59.8 %collective-permute-start.27 = (f32[16,192,128]{2,1,0:T(8,128)}, f32[16,192,128]{2,1,0:T(8,128)}, u32[]{:S(2)}, u32[]{:S(2)}) collective-permute-start(f32[16,192,128]{2,1,0:T(8,128)} %get-tuple-element.94), channel_id=1, source_target_pairs={{0,1},{1,0},{2,3},{3,2},{4,5},{5,4},{6,7},{7,6},{8,9},{9,8},{10,11... | collective-permute-start | bytes 4718600 | tf_op jit(solution)/shard_map/ppermute | solution.py:343
  81.3 55.1 %collective-permute-start.38 = (f32[16,384,128]{2,1,0:T(8,128)}, f32[16,384,128]{2,1,0:T(8,128)}, u32[]{:S(2)}, u32[]{:S(2)}) collective-permute-start(f32[16,384,128]{2,1,0:T(8,128)} %get-tuple-element.101), channel_id=1, source_target_pairs={{0,1},{1,0},{2,3},{3,2},{4,5},{5,4},{6,7},{7,6},{8,9},{9,8},{10,11... | collective-permute-start | bytes 9437192 | tf_op jit(solution)/shard_map/ppermute | solution.py:343
  81.7 11.7 %copy-start.12 = (f32[2]{0:T(128)S(1)}, f32[2]{0:T(128)}, u32[]{:S(2)}) copy-start(f32[2]{0:T(128)} %constant.47.clone) | copy-start | bytes 28
  81.7 28.3 %copy-start.13 = (f32[2]{0:T(128)S(1)}, f32[2]{0:T(128)}, u32[]{:S(2)}) copy-start(f32[2]{0:T(128)} %param.29) | copy-start | bytes 28
  92.6 54.0 %collective-permute-start.16 = (f32[16,208,128]{2,1,0:T(8,128)}, f32[16,208,128]{2,1,0:T(8,128)}, u32[]{:S(2)}, u32[]{:S(2)}) collective-permute-start(f32[16,208,128]{2,1,0:T(8,128)} %get-tuple-element.91), channel_id=1, source_target_pairs={{0,1},{1,0},{2,3},{3,2},{4,5},{5,4},{6,7},{7,6},{8,9},{9,8},{10,11... | collective-permute-start | bytes 5111816 | tf_op jit(solution)/shard_map/ppermute | solution.py:343
  93.4 4.5 %collective-permute-start.1 = (f32[2]{0:T(128)S(1)}, f32[2]{0:T(128)S(1)}, u32[]{:S(2)}, u32[]{:S(2)}) collective-permute-start(f32[2]{0:T(128)S(1)} %fusion.8), channel_id=1, source_target_pairs={{0,2},{1,3},{2,0},{3,1},{4,6},{5,7},{6,4},{7,5},{8,10},{9,11},{10,... | collective-permute-start | bytes 32 | tf_op jit(solution)/shard_map/ppermute | solution.py:343
  97.9 3.6 collective-permute-start.2
  101.5 3.5 collective-permute-start.3
  105.0 4.4 %collective-permute-start.4 = (f32[2]{0:T(128)S(1)}, f32[2]{0:T(128)S(1)}, u32[]{:S(2)}, u32[]{:S(2)}) collective-permute-start(f32[2]{0:T(128)S(1)} %add.165), channel_id=1, source_target_pairs={{0,16},{1,17},{2,18},{3,19},{4,20},{5,21},{6,22},{7,23},{8,24},{9,... | collective-permute-start | bytes 32 | tf_op jit(solution)/shard_map/ppermute | solution.py:343
  112.6 18.4 %copy-start.9 = (f32[16,208,128]{2,1,0:T(8,128)S(1)}, f32[16,208,128]{2,1,0:T(8,128)}, u32[]{:S(2)}) copy-start(f32[16,208,128]{2,1,0:T(8,128)} %get-tuple-element.90) | copy-start | bytes 5111812
  130.9 11.9 %collective-permute-start.5 = (f32[16,200,128]{2,1,0:T(8,128)}, f32[16,200,128]{2,1,0:T(8,128)}, u32[]{:S(2)}, u32[]{:S(2)}) collective-permute-start(f32[16,200,128]{2,1,0:T(8,128)} %get-tuple-element.83), channel_id=1, source_target_pairs={{0,1},{1,0},{2,3},{3,2},{4,5},{5,4},{6,7},{7,6},{8,9},{9,8},{10,11... | collective-permute-start | bytes 4915208 | tf_op jit(solution)/shard_map/ppermute | solution.py:343
  131.0 1.4 copy-start.10
  133.8 2.4 copy-start.11
  138.9 20.5 %collective-permute-start.39 = (f32[8,384,128]{2,1,0:T(8,128)S(1)}, f32[8,384,128]{2,1,0:T(8,128)S(1)}, u32[]{:S(2)}, u32[]{:S(2)}) collective-permute-start(f32[8,384,128]{2,1,0:T(8,128)S(1)} %get-tuple-element.108), channel_id=1, source_target_pairs={{0,2},{1,5},{2,0},{3,7},{4,6},{5,1},{6,4},{7,3},{8,10},{9,13},{10,... | collective-permute-start | bytes 4718600 | tf_op jit(solution)/shard_map/ppermute | solution.py:343
  142.7 30.7 %collective-permute-start.28 = (f32[8,192,128]{2,1,0:T(8,128)S(1)}, f32[8,192,128]{2,1,0:T(8,128)S(1)}, u32[]{:S(2)}, u32[]{:S(2)}) collective-permute-start(f32[8,192,128]{2,1,0:T(8,128)S(1)} %get-tuple-element.116), channel_id=1, source_target_pairs={{0,2},{1,5},{2,0},{3,7},{4,6},{5,1},{6,4},{7,3},{8,10},{9,13},{10,... | collective-permute-start | bytes 2359304 | tf_op jit(solution)/shard_map/ppermute | solution.py:343
  144.6 44.6 %collective-permute-start.6 = (f32[8,200,128]{2,1,0:T(8,128)S(1)}, f32[8,200,128]{2,1,0:T(8,128)S(1)}, u32[]{:S(2)}, u32[]{:S(2)}) collective-permute-start(f32[8,200,128]{2,1,0:T(8,128)S(1)} %get-tuple-element.112), channel_id=1, source_target_pairs={{0,2},{1,5},{2,0},{3,7},{4,6},{5,1},{6,4},{7,3},{8,10},{9,13},{10,... | collective-permute-start | bytes 2457608 | tf_op jit(solution)/shard_map/ppermute | solution.py:343
  148.4 54.3 %collective-permute-start.17 = (f32[8,208,128]{2,1,0:T(8,128)S(1)}, f32[8,208,128]{2,1,0:T(8,128)S(1)}, u32[]{:S(2)}, u32[]{:S(2)}) collective-permute-start(f32[8,208,128]{2,1,0:T(8,128)S(1)} %get-tuple-element.110), channel_id=1, source_target_pairs={{0,2},{1,5},{2,0},{3,7},{4,6},{5,1},{6,4},{7,3},{8,10},{9,13},{10,... | collective-permute-start | bytes 2555912 | tf_op jit(solution)/shard_map/ppermute | solution.py:343
  159.6 45.4 %collective-permute-start.40 = (f32[4,384,128]{2,1,0:T(8,128)S(1)}, f32[4,384,128]{2,1,0:T(8,128)S(1)}, u32[]{:S(2)}, u32[]{:S(2)}) collective-permute-start(f32[4,384,128]{2,1,0:T(8,128)S(1)} %get-tuple-element.114), channel_id=1, source_target_pairs={{0,4},{1,3},{2,6},{3,1},{4,0},{5,7},{6,2},{7,5},{8,12},{9,11},{10,... | collective-permute-start | bytes 2359304 | tf_op jit(solution)/shard_map/ppermute | solution.py:343
  173.5 32.7 %collective-permute-start.29 = (f32[4,192,128]{2,1,0:T(8,128)S(1)}, f32[4,192,128]{2,1,0:T(8,128)S(1)}, u32[]{:S(2)}, u32[]{:S(2)}) collective-permute-start(f32[4,192,128]{2,1,0:T(8,128)S(1)} %get-tuple-element.124), channel_id=1, source_target_pairs={{0,4},{1,3},{2,6},{3,1},{4,0},{5,7},{6,2},{7,5},{8,12},{9,11},{10,... | collective-permute-start | bytes 1179656 | tf_op jit(solution)/shard_map/ppermute | solution.py:343
  189.3 18.0 %collective-permute-start.7 = (f32[4,200,128]{2,1,0:T(8,128)S(1)}, f32[4,200,128]{2,1,0:T(8,128)S(1)}, u32[]{:S(2)}, u32[]{:S(2)}) collective-permute-start(f32[4,200,128]{2,1,0:T(8,128)S(1)} %get-tuple-element.120), channel_id=1, source_target_pairs={{0,4},{1,3},{2,6},{3,1},{4,0},{5,7},{6,2},{7,5},{8,12},{9,11},{10,... | collective-permute-start | bytes 1228808 | tf_op jit(solution)/shard_map/ppermute | solution.py:343
  202.9 28.6 %collective-permute-start.18 = (f32[4,208,128]{2,1,0:T(8,128)S(1)}, f32[4,208,128]{2,1,0:T(8,128)S(1)}, u32[]{:S(2)}, u32[]{:S(2)}) collective-permute-start(f32[4,208,128]{2,1,0:T(8,128)S(1)} %get-tuple-element.118), channel_id=1, source_target_pairs={{0,4},{1,3},{2,6},{3,1},{4,0},{5,7},{6,2},{7,5},{8,12},{9,11},{10,... | collective-permute-start | bytes 1277960 | tf_op jit(solution)/shard_map/ppermute | solution.py:343
  205.1 12.1 %collective-permute-start.41 = (f32[2,384,128]{2,1,0:T(8,128)S(1)}, f32[2,384,128]{2,1,0:T(8,128)S(1)}, u32[]{:S(2)}, u32[]{:S(2)}) collective-permute-start(f32[2,384,128]{2,1,0:T(8,128)S(1)} %get-tuple-element.122), channel_id=1, source_target_pairs={{0,8},{1,9},{2,10},{3,11},{4,12},{5,13},{6,14},{7,15},{8,0},{9,1},... | collective-permute-start | bytes 1179656 | tf_op jit(solution)/shard_map/ppermute | solution.py:343
  206.2 20.5 %collective-permute-start.30 = (f32[2,192,128]{2,1,0:T(8,128)S(1)}, f32[2,192,128]{2,1,0:T(8,128)S(1)}, u32[]{:S(2)}, u32[]{:S(2)}) collective-permute-start(f32[2,192,128]{2,1,0:T(8,128)S(1)} %get-tuple-element.130), channel_id=1, source_target_pairs={{0,8},{1,9},{2,10},{3,11},{4,12},{5,13},{6,14},{7,15},{8,0},{9,1},... | collective-permute-start | bytes 589832 | tf_op jit(solution)/shard_map/ppermute | solution.py:343
  207.4 37.3 %collective-permute-start.8 = (f32[2,200,128]{2,1,0:T(8,128)S(1)}, f32[2,200,128]{2,1,0:T(8,128)S(1)}, u32[]{:S(2)}, u32[]{:S(2)}) collective-permute-start(f32[2,200,128]{2,1,0:T(8,128)S(1)} %get-tuple-element.128), channel_id=1, source_target_pairs={{0,8},{1,9},{2,10},{3,11},{4,12},{5,13},{6,14},{7,15},{8,0},{9,1},... | collective-permute-start | bytes 614408 | tf_op jit(solution)/shard_map/ppermute | solution.py:343
  217.2 10.7 %collective-permute-start.42 = (f32[1,384,128]{2,1,0:T(8,128)S(1)}, f32[1,384,128]{2,1,0:T(8,128)S(1)}, u32[]{:S(2)}, u32[]{:S(2)}) collective-permute-start(f32[1,384,128]{2,1,0:T(8,128)S(1)} %slice_add_fusion.22), channel_id=1, source_target_pairs={{0,16},{1,17},{2,18},{3,19},{4,20},{5,21},{6,22},{7,23},{8,24},{9,... | collective-permute-start | bytes 589832 | tf_op jit(solution)/shard_map/ppermute | solution.py:343
  226.7 15.4 %collective-permute-start.31 = (f32[1,192,128]{2,1,0:T(8,128)S(1)}, f32[1,192,128]{2,1,0:T(8,128)S(1)}, u32[]{:S(2)}, u32[]{:S(2)}) collective-permute-start(f32[1,192,128]{2,1,0:T(8,128)S(1)} %slice_add_fusion.30), channel_id=1, source_target_pairs={{0,16},{1,17},{2,18},{3,19},{4,20},{5,21},{6,22},{7,23},{8,24},{9,... | collective-permute-start | bytes 294920 | tf_op jit(solution)/shard_map/ppermute | solution.py:343
  228.0 14.0 %collective-permute-start.43 = (f32[1,384,128]{2,1,0:T(8,128)S(1)}, f32[1,384,128]{2,1,0:T(8,128)S(1)}, u32[]{:S(2)}, u32[]{:S(2)}) collective-permute-start(f32[1,384,128]{2,1,0:T(8,128)S(1)} %fusion), channel_id=1, source_target_pairs={{0,16},{1,17},{2,18},{3,19},{4,20},{5,21},{6,22},{7,23},{8,24},{9,... | collective-permute-start | bytes 589832 | tf_op jit(solution)/shard_map/ppermute | solution.py:343
  231.5 30.3 %collective-permute-start.19 = (f32[2,208,128]{2,1,0:T(8,128)S(1)}, f32[2,208,128]{2,1,0:T(8,128)S(1)}, u32[]{:S(2)}, u32[]{:S(2)}) collective-permute-start(f32[2,208,128]{2,1,0:T(8,128)S(1)} %get-tuple-element.126), channel_id=1, source_target_pairs={{0,8},{1,9},{2,10},{3,11},{4,12},{5,13},{6,14},{7,15},{8,0},{9,1},... | collective-permute-start | bytes 638984 | tf_op jit(solution)/shard_map/ppermute | solution.py:343
  242.1 14.3 %collective-permute-start.44 = (f32[2,384,128]{2,1,0:T(8,128)S(1)}, f32[2,384,128]{2,1,0:T(8,128)S(1)}, u32[]{:S(2)}, u32[]{:S(2)}) collective-permute-start(f32[2,384,128]{2,1,0:T(8,128)S(1)} %pad_maximum_fusion.8), channel_id=1, source_target_pairs={{0,8},{1,9},{2,10},{3,11},{4,12},{5,13},{6,14},{7,15},{8,0},{9,1},... | collective-permute-start | bytes 1179656 | tf_op jit(solution)/shard_map/ppermute | solution.py:343
  242.2 17.8 %collective-permute-start.32 = (f32[1,192,128]{2,1,0:T(8,128)S(1)}, f32[1,192,128]{2,1,0:T(8,128)S(1)}, u32[]{:S(2)}, u32[]{:S(2)}) collective-permute-start(f32[1,192,128]{2,1,0:T(8,128)S(1)} %fusion.3), channel_id=1, source_target_pairs={{0,16},{1,17},{2,18},{3,19},{4,20},{5,21},{6,22},{7,23},{8,24},{9,... | collective-permute-start | bytes 294920 | tf_op jit(solution)/shard_map/ppermute | solution.py:343
  244.7 15.3 %collective-permute-start.9 = (f32[1,200,128]{2,1,0:T(8,128)S(1)}, f32[1,200,128]{2,1,0:T(8,128)S(1)}, u32[]{:S(2)}, u32[]{:S(2)}) collective-permute-start(f32[1,200,128]{2,1,0:T(8,128)S(1)} %slice_add_fusion.28), channel_id=1, source_target_pairs={{0,16},{1,17},{2,18},{3,19},{4,20},{5,21},{6,22},{7,23},{8,24},{9,... | collective-permute-start | bytes 307208 | tf_op jit(solution)/shard_map/ppermute | solution.py:343
  256.4 14.6 %collective-permute-start.45 = (f32[4,384,128]{2,1,0:T(8,128)S(1)}, f32[4,384,128]{2,1,0:T(8,128)S(1)}, u32[]{:S(2)}, u32[]{:S(2)}) collective-permute-start(f32[4,384,128]{2,1,0:T(8,128)S(1)} %pad_maximum_fusion.4), channel_id=1, source_target_pairs={{0,4},{1,3},{2,6},{3,1},{4,0},{5,7},{6,2},{7,5},{8,12},{9,11},{10,... | collective-permute-start | bytes 2359304 | tf_op jit(solution)/shard_map/ppermute | solution.py:343
  260.0 10.8 %collective-permute-start.33 = (f32[2,192,128]{2,1,0:T(8,128)S(1)}, f32[2,192,128]{2,1,0:T(8,128)S(1)}, u32[]{:S(2)}, u32[]{:S(2)}) collective-permute-start(f32[2,192,128]{2,1,0:T(8,128)S(1)} %pad_maximum_fusion.11), channel_id=1, source_target_pairs={{0,8},{1,9},{2,10},{3,11},{4,12},{5,13},{6,14},{7,15},{8,0},{9,1},... | collective-permute-start | bytes 589832 | tf_op jit(solution)/shard_map/ppermute | solution.py:343
  260.1 5.7 %collective-permute-start.10 = (f32[1,200,128]{2,1,0:T(8,128)S(1)}, f32[1,200,128]{2,1,0:T(8,128)S(1)}, u32[]{:S(2)}, u32[]{:S(2)}) collective-permute-start(f32[1,200,128]{2,1,0:T(8,128)S(1)} %fusion.2), channel_id=1, source_target_pairs={{0,16},{1,17},{2,18},{3,19},{4,20},{5,21},{6,22},{7,23},{8,24},{9,... | collective-permute-start | bytes 307208 | tf_op jit(solution)/shard_map/ppermute | solution.py:343
  261.9 14.8 %collective-permute-start.20 = (f32[1,208,128]{2,1,0:T(8,128)S(1)}, f32[1,208,128]{2,1,0:T(8,128)S(1)}, u32[]{:S(2)}, u32[]{:S(2)}) collective-permute-start(f32[1,208,128]{2,1,0:T(8,128)S(1)} %slice_add_fusion.26), channel_id=1, source_target_pairs={{0,16},{1,17},{2,18},{3,19},{4,20},{5,21},{6,22},{7,23},{8,24},{9,... | collective-permute-start | bytes 319496 | tf_op jit(solution)/shard_map/ppermute | solution.py:343
  265.8 7.3 %collective-permute-start.11 = (f32[2,200,128]{2,1,0:T(8,128)S(1)}, f32[2,200,128]{2,1,0:T(8,128)S(1)}, u32[]{:S(2)}, u32[]{:S(2)}) collective-permute-start(f32[2,200,128]{2,1,0:T(8,128)S(1)} %pad_maximum_fusion.10), channel_id=1, source_target_pairs={{0,8},{1,9},{2,10},{3,11},{4,12},{5,13},{6,14},{7,15},{8,0},{9,1},... | collective-permute-start | bytes 614408 | tf_op jit(solution)/shard_map/ppermute | solution.py:343
  270.8 12.8 %collective-permute-start.34 = (f32[4,192,128]{2,1,0:T(8,128)S(1)}, f32[4,192,128]{2,1,0:T(8,128)S(1)}, u32[]{:S(2)}, u32[]{:S(2)}) collective-permute-start(f32[4,192,128]{2,1,0:T(8,128)S(1)} %pad_maximum_fusion.7), channel_id=1, source_target_pairs={{0,4},{1,3},{2,6},{3,1},{4,0},{5,7},{6,2},{7,5},{8,12},{9,11},{10,... | collective-permute-start | bytes 1179656 | tf_op jit(solution)/shard_map/ppermute | solution.py:343
  271.1 40.5 %collective-permute-start.46 = (f32[8,384,128]{2,1,0:T(8,128)S(1)}, f32[8,384,128]{2,1,0:T(8,128)S(1)}, u32[]{:S(2)}, u32[]{:S(2)}) collective-permute-start(f32[8,384,128]{2,1,0:T(8,128)S(1)} %pad_maximum_fusion.refs_0_), channel_id=1, source_target_pairs={{0,2},{1,5},{2,0},{3,7},{4,6},{5,1},{6,4},{7,3},{8,10},{9,13},{10,... | collective-permute-start | bytes 4718600 | tf_op jit(solution)/shard_map/ppermute | solution.py:343
  273.1 18.6 %collective-permute-start.12 = (f32[4,200,128]{2,1,0:T(8,128)S(1)}, f32[4,200,128]{2,1,0:T(8,128)S(1)}, u32[]{:S(2)}, u32[]{:S(2)}) collective-permute-start(f32[4,200,128]{2,1,0:T(8,128)S(1)} %pad_maximum_fusion.6), channel_id=1, source_target_pairs={{0,4},{1,3},{2,6},{3,1},{4,0},{5,7},{6,2},{7,5},{8,12},{9,11},{10,... | collective-permute-start | bytes 1228808 | tf_op jit(solution)/shard_map/ppermute | solution.py:343
  276.7 6.5 %collective-permute-start.21 = (f32[1,208,128]{2,1,0:T(8,128)S(1)}, f32[1,208,128]{2,1,0:T(8,128)S(1)}, u32[]{:S(2)}, u32[]{:S(2)}) collective-permute-start(f32[1,208,128]{2,1,0:T(8,128)S(1)} %fusion.1), channel_id=1, source_target_pairs={{0,16},{1,17},{2,18},{3,19},{4,20},{5,21},{6,22},{7,23},{8,24},{9,... | collective-permute-start | bytes 319496 | tf_op jit(solution)/shard_map/ppermute | solution.py:343
  283.3 8.5 %collective-permute-start.22 = (f32[2,208,128]{2,1,0:T(8,128)S(1)}, f32[2,208,128]{2,1,0:T(8,128)S(1)}, u32[]{:S(2)}, u32[]{:S(2)}) collective-permute-start(f32[2,208,128]{2,1,0:T(8,128)S(1)} %pad_maximum_fusion.9), channel_id=1, source_target_pairs={{0,8},{1,9},{2,10},{3,11},{4,12},{5,13},{6,14},{7,15},{8,0},{9,1},... | collective-permute-start | bytes 638984 | tf_op jit(solution)/shard_map/ppermute | solution.py:343
  283.7 21.2 %collective-permute-start.36 = (f32[8,192,128]{2,1,0:T(8,128)S(1)}, f32[8,192,128]{2,1,0:T(8,128)S(1)}, u32[]{:S(2)}, u32[]{:S(2)}) collective-permute-start(f32[8,192,128]{2,1,0:T(8,128)S(1)} %pad_maximum_fusion.3.refs_0_), channel_id=1, source_target_pairs={{0,1},{1,0},{2,3},{3,2},{4,5},{5,4},{6,7},{7,6},{8,9},{9,8},{10,11... | collective-permute-start | bytes 2359304 | tf_op jit(solution)/shard_map/ppermute | solution.py:343
  283.8 24.2 %collective-permute-start.35 = (f32[8,192,128]{2,1,0:T(8,128)S(1)}, f32[8,192,128]{2,1,0:T(8,128)S(1)}, u32[]{:S(2)}, u32[]{:S(2)}) collective-permute-start(f32[8,192,128]{2,1,0:T(8,128)S(1)} %pad_maximum_fusion.3.refs_0_), channel_id=1, source_target_pairs={{0,2},{1,5},{2,0},{3,7},{4,6},{5,1},{6,4},{7,3},{8,10},{9,13},{10,... | collective-permute-start | bytes 2359304 | tf_op jit(solution)/shard_map/ppermute | solution.py:343
  291.8 19.0 %collective-permute-start.14 = (f32[8,200,128]{2,1,0:T(8,128)S(1)}, f32[8,200,128]{2,1,0:T(8,128)S(1)}, u32[]{:S(2)}, u32[]{:S(2)}) collective-permute-start(f32[8,200,128]{2,1,0:T(8,128)S(1)} %pad_maximum_fusion.2.refs_0_), channel_id=1, source_target_pairs={{0,1},{1,0},{2,3},{3,2},{4,5},{5,4},{6,7},{7,6},{8,9},{9,8},{10,11... | collective-permute-start | bytes 2457608 | tf_op jit(solution)/shard_map/ppermute | solution.py:343
  291.9 12.8 %collective-permute-start.23 = (f32[4,208,128]{2,1,0:T(8,128)S(1)}, f32[4,208,128]{2,1,0:T(8,128)S(1)}, u32[]{:S(2)}, u32[]{:S(2)}) collective-permute-start(f32[4,208,128]{2,1,0:T(8,128)S(1)} %pad_maximum_fusion.5), channel_id=1, source_target_pairs={{0,4},{1,3},{2,6},{3,1},{4,0},{5,7},{6,2},{7,5},{8,12},{9,11},{10,... | collective-permute-start | bytes 1277960 | tf_op jit(solution)/shard_map/ppermute | solution.py:343
  304.8 34.3 %copy-start.8 = (s32[2]{0:T(128)S(1)}, s32[2]{0:T(128)}, u32[]{:S(2)}) copy-start(s32[2]{0:T(128)} %pad_add_fusion.code_ref) | copy-start | bytes 28
  304.8 22.8 %collective-permute-start.24 = (f32[8,208,128]{2,1,0:T(8,128)S(1)}, f32[8,208,128]{2,1,0:T(8,128)S(1)}, u32[]{:S(2)}, u32[]{:S(2)}) collective-permute-start(f32[8,208,128]{2,1,0:T(8,128)S(1)} %pad_maximum_fusion.1.refs_0_), channel_id=1, source_target_pairs={{0,2},{1,5},{2,0},{3,7},{4,6},{5,1},{6,4},{7,3},{8,10},{9,13},{10,... | collective-permute-start | bytes 2555912 | tf_op jit(solution)/shard_map/ppermute | solution.py:343
  304.9 0.9 copy-start.2
  305.8 20.7 %collective-permute-start.13 = (f32[8,200,128]{2,1,0:T(8,128)S(1)}, f32[8,200,128]{2,1,0:T(8,128)}, u32[]{:S(2)}, u32[]{:S(2)}) collective-permute-start(f32[8,200,128]{2,1,0:T(8,128)S(1)} %pad_maximum_fusion.2.refs_0_), channel_id=1, source_target_pairs={{0,2},{1,5},{2,0},{3,7},{4,6},{5,1},{6,4},{7,3},{8,10},{9,13},{10,... | collective-permute-start | bytes 2457608 | tf_op jit(solution)/shard_map/ppermute | solution.py:343
  307.9 19.6 %collective-permute-start.37 = (f32[8,192,128]{2,1,0:T(8,128)S(1)}, f32[8,192,128]{2,1,0:T(8,128)S(1)}, u32[]{:S(2)}, u32[]{:S(2)}) collective-permute-start(f32[8,192,128]{2,1,0:T(8,128)S(1)} %collective-permute-done.35.refs_1_), channel_id=1, source_target_pairs={{0,1},{1,0},{2,3},{3,2},{4,5},{5,4},{6,7},{7,6},{8,9},{9,8},{10,11... | collective-permute-start | bytes 2359304 | tf_op jit(solution)/shard_map/ppermute | solution.py:343
  309.9 0.9 copy-start.4
  310.7 0.9 copy-start
  311.6 41.2 %collective-permute-start.47 = (f32[8,384,128]{2,1,0:T(8,128)S(1)}, f32[8,384,128]{2,1,0:T(8,128)S(1)}, u32[]{:S(2)}, u32[]{:S(2)}) collective-permute-start(f32[8,384,128]{2,1,0:T(8,128)S(1)} %pad_maximum_fusion.refs_0_), channel_id=1, source_target_pairs={{0,1},{1,0},{2,3},{3,2},{4,5},{5,4},{6,7},{7,6},{8,9},{9,8},{10,11... | collective-permute-start | bytes 4718600 | tf_op jit(solution)/shard_map/ppermute | solution.py:343
  311.6 41.2 %collective-permute-start.48 = (f32[8,384,128]{2,1,0:T(8,128)S(1)}, f32[8,384,128]{2,1,0:T(8,128)}, u32[]{:S(2)}, u32[]{:S(2)}) collective-permute-start(f32[8,384,128]{2,1,0:T(8,128)S(1)} %collective-permute-done.46.refs_1_), channel_id=1, source_target_pairs={{0,1},{1,0},{2,3},{3,2},{4,5},{5,4},{6,7},{7,6},{8,9},{9,8},{10,11... | collective-permute-start | bytes 4718600 | tf_op jit(solution)/shard_map/ppermute | solution.py:343
  326.4 22.5 %collective-permute-start.25 = (f32[8,208,128]{2,1,0:T(8,128)S(1)}, f32[8,208,128]{2,1,0:T(8,128)}, u32[]{:S(2)}, u32[]{:S(2)}) collective-permute-start(f32[8,208,128]{2,1,0:T(8,128)S(1)} %pad_maximum_fusion.1.refs_0_), channel_id=1, source_target_pairs={{0,1},{1,0},{2,3},{3,2},{4,5},{5,4},{6,7},{7,6},{8,9},{9,8},{10,11... | collective-permute-start | bytes 2555912 | tf_op jit(solution)/shard_map/ppermute | solution.py:343
  327.6 21.4 %collective-permute-start.26 = (f32[8,208,128]{2,1,0:T(8,128)S(1)}, f32[8,208,128]{2,1,0:T(8,128)}, u32[]{:S(2)}, u32[]{:S(2)}) collective-permute-start(f32[8,208,128]{2,1,0:T(8,128)S(1)} %collective-permute-done.24.refs_1_), channel_id=1, source_target_pairs={{0,1},{1,0},{2,3},{3,2},{4,5},{5,4},{6,7},{7,6},{8,9},{9,8},{10,11... | collective-permute-start | bytes 2555912 | tf_op jit(solution)/shard_map/ppermute | solution.py:343
  327.6 0.9 copy-start.6
  328.5 16.8 %collective-permute-start.15 = (f32[8,200,128]{2,1,0:T(8,128)}, f32[8,200,128]{2,1,0:T(8,128)}, u32[]{:S(2)}, u32[]{:S(2)}) collective-permute-start(f32[8,200,128]{2,1,0:T(8,128)} %collective-permute-done.13.refs_1_), channel_id=1, source_target_pairs={{0,1},{1,0},{2,3},{3,2},{4,5},{5,4},{6,7},{7,6},{8,9},{9,8},{10,11... | collective-permute-start | bytes 2457608 | tf_op jit(solution)/shard_map/ppermute | solution.py:343
  339.1 1.1 copy-start.3
  340.3 1.1 copy-start.5
  341.4 1.1 copy-start.7
  342.5 2.8 copy-start.1
where the time goes:
time: 359 us; the launch traced here: 358 us
  waiting for transfers between devices  136 us (38%)
  Pallas kernels  130 us (36%)
  starting transfers between devices  61 us (17%)
  other arithmetic  15.8 us (4%)
  local copies, waits for them, and re-layouts  10.2 us (3%)
  between operations  5.65 us (2%)
    ppermute x49, waiting for transfers between devices, exchange(): lax.ppermute(values, 'dp', flips(count, first, first if second is None el...  136 us
    pallas_call x8, Pallas kernels, run(): pl.pallas_call(kernel, grid=(steps,), out_shape=[jax.ShapeDtypeStruct(s,...  114 us
    ppermute x49, starting transfers between devices, exchange(): lax.ppermute(values, 'dp', flips(count, first, first if second is None el...  61 us
    pallas_call x4, Pallas kernels, unpack(): pl.pallas_call(functools.partial(unpack_kernel, shapes, with_gains), out_...  15.4 us
    mul x8, other arithmetic, sum_blocks(): keep, got = (keep * own, got * other)  9.46 us
    unnamed x28, local copies, waits for them, and re-layouts  8.29 us
  transfers between devices with their start and end apart: 49, of which 21 were waited for; matrix products, arithmetic and copies ran while one was open for 4% of the time, Pallas kernels for 35%

commit v1 on v0

--- a/solution.py
+++ b/solution.py
@@ -166,7 +166,7 @@
 
 def feed_forward_kernel(
     len_ref, code_ref, x2_ref, cot_ref, g3_ref, wg_ref, wu_ref, wd_ref,
-    out_ref, dx2_ref, gain_ref, keep_ref, send_ref,
+    out_ref, dx2_ref, gain_ref, keep_low, keep_high, send_low, send_high,
     hid, dgate, dup, acc_down, acc_gate, acc_up, *, maxlen,
 ):
     step, steps = pl.program_id(0), pl.num_programs(0)
@@ -209,14 +209,31 @@
     @pl.when(step == steps - 1)
     def finish():
         items = [(acc_down, acc_down.shape, 0), (acc_gate, acc_gate.shape, 0), (acc_up, acc_up.shape, 0)]
-        pack(items, code_ref, keep_ref, send_ref)
-
-
-def cross_backward_kernel(
-    code_ref, dx2_ref, oc_ref, cq_ref, pt_ref, kv_ref, h2_ref, feat_ref, x1_ref, g2_ref,
-    wco_ref, wcq_ref, wck_ref, wcv_ref,
-    dfeat_ref, dx1_ref, gain_ref, bias_ref, keep_ref, send_ref,
-    joined, dcq, dkv, acc_out, acc_query, acc_kv,
+        pack(items, code_ref, keep_low, keep_high, send_low, send_high)
+
+
+def cross_attention_kernel(dx2_ref, cq_ref, pt_ref, kv_ref, wco_ref, dcq_ref, dkv_ref):
+    seqs, _, both, maxlen = pt_ref.shape
+    patches = both // 2
+    doc = dot_back(dx2_ref[...].astype(BF16), wco_ref[...]).astype(BF16)
+    for s in range(seqs):
+        rows, wide = pl.ds(s * maxlen, maxlen), pl.ds(s * patches, patches)
+        for p in range(PAIRS):
+            keys, values = pair_lanes(p), pair_lanes(p, INNER)
+            dcq_ref[rows, keys], dkv_ref[wide, keys], dkv_ref[wide, values] = pair_backward(
+                cq_ref[rows, keys],
+                kv_ref[wide, keys],
+                kv_ref[wide, values],
+                pt_ref[s, p],
+                doc[s * maxlen : (s + 1) * maxlen, p * PAIR : (p + 1) * PAIR],
+            )
+
+
+def cross_weights_kernel(
+    code_ref, dx2_ref, oc_ref, dcq_ref, dkv_ref, h2_ref, feat_ref, x1_ref, g2_ref,
+    wcq_ref, wck_ref, wcv_ref,
+    dfeat_ref, dx1_ref, gain_ref, bias_ref, keep_low, keep_high, send_low, send_high,
+    joined, acc_out, acc_query, acc_kv,
 ):
     step, steps = pl.program_id(0), pl.num_programs(0)
 
@@ -225,90 +242,76 @@
         joined[:, :INNER] = wck_ref[...]
         joined[:, INNER:] = wcv_ref[...]
 
-    seqs, _, both, maxlen = pt_ref.shape
-    patches = both // 2
     dx2 = dx2_ref[...]
-    dc = dx2.astype(BF16)
-    doc = dot_back(dc, wco_ref[...]).astype(BF16)
-    for s in range(seqs):
-        rows, wide = pl.ds(s * maxlen, maxlen), pl.ds(s * patches, patches)
-        for p in range(PAIRS):
-            dcq[rows, pair_lanes(p)], dkv[wide, pair_lanes(p)], dkv[wide, pair_lanes(p, INNER)] = (
-                pair_backward(
-                    cq_ref[rows, pair_lanes(p)],
-                    kv_ref[wide, pair_lanes(p)],
-                    kv_ref[wide, pair_lanes(p, INNER)],
-                    pt_ref[s, p],
-                    doc[s * maxlen : (s + 1) * maxlen, p * PAIR : (p + 1) * PAIR],
-                )
-            )
-    dh2 = dot_back(dcq[...], wcq_ref[...])
-    dfeat = dot_back(dkv[...], joined[...]).astype(BF16)
+    dfeat = dot_back(dkv_ref[...], joined[...]).astype(BF16)
     dfeat_ref[...] = dfeat
+    dh2 = dot_back(dcq_ref[...], wcq_ref[...])
     dx, gain = norm_backward(x1_ref[...], g2_ref[...], dh2)
     dx1_ref[...] = dx2 + dx
     add_to(gain_ref, step == 0, gain)
     add_to(bias_ref, step == 0, jnp.sum(dfeat.astype(F32), axis=0, keepdims=True))
-    add_to(acc_out, step == 0, dot_rows(oc_ref[...], dc))
-    add_to(acc_query, step == 0, dot_rows(h2_ref[...], dcq[...]))
-    add_to(acc_kv, step == 0, dot_rows(feat_ref[...], dkv[...]))
+    add_to(acc_out, step == 0, dot_rows(oc_ref[...], dx2.astype(BF16)))
+    add_to(acc_query, step == 0, dot_rows(h2_ref[...], dcq_ref[...]))
+    add_to(acc_kv, step == 0, dot_rows(feat_ref[...], dkv_ref[...]))
 
     @pl.when(step == steps - 1)
     def finish():
         small = acc_query.shape
         items = [(acc_out, acc_out.shape, 0), (acc_query, small, 0), (acc_kv, small, 0), (acc_kv, small, INNER)]
-        pack(items, code_ref, keep_ref, send_ref)
-
-
-def patch_weight_kernel(code_ref, patch_ref, dfeat_ref, keep_ref, send_ref, acc, turned):
+        pack(items, code_ref, keep_low, keep_high, send_low, send_high)
+
+
+def patch_weight_kernel(code_ref, patch_ref, dfeat_ref, keep_low, keep_high, send_low, send_high, acc, turned):
     step, steps = pl.program_id(0), pl.num_programs(0)
     add_to(acc, step == 0, dot_rows(dfeat_ref[...], patch_ref[...]))
 
     @pl.when(step == steps - 1)
     def finish():
         turned[...] = acc[...].T
-        pack([(turned, turned.shape, 0)], code_ref, keep_ref, send_ref)
-
-
-def patch_input_kernel(weight_ref, dfeat_ref, w_ref, out_ref):
-    out_ref[...] = dot_back(dfeat_ref[...], w_ref[...]) * weight_ref[0]
-
-
-def self_backward_kernel(
-    code_ref, weight_ref, dx1_ref, o_ref, qkv_ref, pt_ref, h1_ref, tok_ref, g1_ref,
-    wo_ref, wq_ref, wk_ref, wv_ref, gain_two_ref, gain_three_ref, bias_ref,
-    dtok_ref, keep_ref, send_ref,
-    joined, dqkv, acc_out, acc_qkv, gain, gain_block,
-):
-    step, steps = pl.program_id(0), pl.num_programs(0)
-
-    @pl.when(step == 0)
-    def join():
-        joined[:, :INNER] = wq_ref[...]
-        joined[:, INNER : 2 * INNER] = wk_ref[...]
-        joined[:, 2 * INNER :] = wv_ref[...]
-
+        pack([(turned, turned.shape, 0)], code_ref, keep_low, keep_high, send_low, send_high)
+
+
+def patch_input_kernel(weight_ref, dfeat_ref, w_ref, *refs):
+    refs[-1][...] = dot_back(dfeat_ref[...], w_ref[...]) * weight_ref[0]
+
+
+def self_attention_kernel(dx1_ref, qkv_ref, pt_ref, wo_ref, dqkv_ref):
     seqs, _, _, maxlen = pt_ref.shape
-    dx1 = dx1_ref[...]
-    da = dx1.astype(BF16)
-    do = dot_back(da, wo_ref[...]).astype(BF16)
+    do = dot_back(dx1_ref[...].astype(BF16), wo_ref[...]).astype(BF16)
     for s in range(seqs):
         rows = pl.ds(s * maxlen, maxlen)
         for p in range(PAIRS):
             lanes = [pair_lanes(p, k * INNER) for k in range(3)]
-            dqkv[rows, lanes[0]], dqkv[rows, lanes[1]], dqkv[rows, lanes[2]] = pair_backward(
+            dqkv_ref[rows, lanes[0]], dqkv_ref[rows, lanes[1]], dqkv_ref[rows, lanes[2]] = pair_backward(
                 qkv_ref[rows, lanes[0]],
                 qkv_ref[rows, lanes[1]],
                 qkv_ref[rows, lanes[2]],
                 pt_ref[s, p],
                 do[s * maxlen : (s + 1) * maxlen, p * PAIR : (p + 1) * PAIR],
             )
-    dh1 = dot_back(dqkv[...], joined[...])
+
+
+def self_weights_kernel(
+    code_ref, weight_ref, dx1_ref, o_ref, dqkv_ref, h1_ref, tok_ref, g1_ref,
+    wq_ref, wk_ref, wv_ref, gain_two_ref, gain_three_ref, bias_ref,
+    dtok_ref, keep_low, keep_high, send_low, send_high,
+    joined, acc_out, acc_qkv, gain, gain_block,
+):
+    step, steps = pl.program_id(0), pl.num_programs(0)
+
+    @pl.when(step == 0)
+    def join():
+        joined[:, :INNER] = wq_ref[...]
+        joined[:, INNER : 2 * INNER] = wk_ref[...]
+        joined[:, 2 * INNER :] = wv_ref[...]
+
+    dx1 = dx1_ref[...]
+    dh1 = dot_back(dqkv_ref[...], joined[...])
     dx, grad_gain = norm_backward(tok_ref[...].astype(F32), g1_ref[...], dh1)
     dtok_ref[...] = (dx1 + dx) * weight_ref[0]
     add_to(gain, step == 0, grad_gain)
-    add_to(acc_out, step == 0, dot_rows(o_ref[...], da))
-    add_to(acc_qkv, step == 0, dot_rows(h1_ref[...], dqkv[...]))
+    add_to(acc_out, step == 0, dot_rows(o_ref[...], dx1.astype(BF16)))
+    add_to(acc_qkv, step == 0, dot_rows(h1_ref[...], dqkv_ref[...]))
 
     @pl.when(step == steps - 1)
     def finish():
@@ -320,7 +323,7 @@
         items = [(acc_out, acc_out.shape, 0)]
         items += [(acc_qkv, small, k * INNER) for k in range(3)]
         items += [(gain_block, gain_block.shape, 0)]
-        pack(items, code_ref, keep_ref, send_ref)
+        pack(items, code_ref, keep_low, keep_high, send_low, send_high)
 
 
 def flips(count, first, second):
@@ -366,17 +369,18 @@
     ]
 
 
-def pack(items, code_ref, keep_ref, send_ref):
+def pack(items, code_ref, *out_refs):
     def step(p, carry):
-        for code, out_ref in ((code_ref[0], keep_ref), (code_ref[1], send_ref)):
+        for k, out_ref in enumerate(out_refs):
             start = 0
+            index = (p + 8 * (k % 2)) ^ code_ref[k // 2]
             for ref, shape, offset in items:
-                for rows, lanes in block_parts(shape, p ^ code, offset):
+                for rows, lanes in block_parts(shape, index, offset):
                     out_ref[p, pl.ds(start, rows.size), :] = ref[rows, lanes]
                     start += rows.size
         return carry
 
-    lax.fori_loop(0, HALF, step, 0)
+    lax.fori_loop(0, 8, step, 0)
 
 
 def unpack_kernel(shapes, with_gains, code_ref, *refs):
@@ -419,30 +423,68 @@
     )(codes, *pieces)
 
 
-def sum_blocks(packed, own, other):
-    keep, send = packed
-    got = exchange(send, 1)
-    keep, got = keep * own, got * other
-    for first, second in ((2, 4), (4, 2), (8, 8), (16, 16)):
-        half = keep.shape[0] // 2
-        send, keep = keep[half:] + got[half:], keep[:half] + got[:half]
-        got = exchange(send, first, second)
-    keep = keep + got
-    extra = BLOCKS
-    while extra < lax.axis_size("dp"):
-        keep = keep + exchange(keep, extra)
-        extra *= 2
-    return keep
-
-
-def spread_blocks(held):
-    held = jnp.concatenate([held, exchange(held, 16)])
-    held = jnp.concatenate([held, exchange(held, 8)])
-    held = jnp.concatenate([held, exchange(held, 4, 2)])
-    near = exchange(held, 1)
-    rest = exchange(held, 2, 4)
-    far = exchange(rest, 1)
-    return held, rest, near, far
+def after(values, *others):
+    return lax.optimization_barrier((values, others))[0]
+
+
+class Chunk:
+    def __init__(self, packed, shapes, weights, codes, with_gains=False):
+        self.keep_low, self.keep_high, self.send_low, self.send_high = packed
+        self.shapes, self.weights, self.codes, self.with_gains = shapes, weights, codes, with_gains
+
+    def start(self):
+        own, other = self.weights
+        high = exchange(self.send_high, 1)
+        low = exchange(self.send_low, 1)
+        self.send = self.keep_high * own + high * other
+        self.keep = self.keep_low * own + low * other
+
+    def halve(self, first, second=None, last=False):
+        got = exchange(self.send, first, second)
+        if last:
+            self.send = self.keep + got
+            return
+        half = got.shape[0] // 2
+        self.send, self.keep = self.keep[half:] + got[half:], self.keep[:half] + got[:half]
+
+    def first(self):
+        self.halve(2, 4)
+
+    def second(self):
+        self.halve(4, 2)
+
+    def third(self):
+        self.halve(8)
+
+    def fourth(self):
+        self.halve(16, last=True)
+        extra = BLOCKS
+        while extra < lax.axis_size("dp"):
+            self.send = self.send + exchange(self.send, extra)
+            extra *= 2
+
+    def double(self, first, second=None):
+        self.send = jnp.concatenate([self.send, exchange(self.send, first, second)])
+
+    def back_fourth(self):
+        self.double(16)
+
+    def back_third(self):
+        self.double(8)
+
+    def back_second(self):
+        self.double(4, 2)
+
+    def back_first(self):
+        self.near = exchange(self.send, 1)
+        self.rest = exchange(self.send, 2, 4)
+
+    def finish(self):
+        self.far = exchange(self.rest, 1)
+
+    def unpack(self):
+        pieces = (self.send, self.rest, self.near, self.far)
+        return unpack(pieces, self.shapes, self.codes, self.with_gains)
 
 
 def by_step(array_shape, steps):
@@ -521,23 +563,20 @@
     other_first = lax.dynamic_index_in_dim(members, 1 - (me & 1), keepdims=False) == 1
     own_count = jnp.sum(lengths).astype(F32)
     counts = own_count * jnp.where(in_first, jnp.array([1.0, 0.0], F32), jnp.array([0.0, 1.0], F32))
-    bit = 1
-    while bit < lax.axis_size("dp"):
-        counts = counts + exchange(counts, bit)
-        bit *= 2
-    group_weights = mix * jnp.sum(counts) / counts
-    weight_own = jnp.where(in_first, group_weights[0], group_weights[1])
-    weight_other = jnp.where(other_first, group_weights[0], group_weights[1])
-    weight_ref = weight_own[None]
+    bits = [1]
+    while 2 * bits[-1] < lax.axis_size("dp"):
+        bits.append(2 * bits[-1])
+    counts = counts + exchange(counts, bits.pop(0))
 
     feat, cross_kv = run(
-        features_kernel, "features", steps, [], [flat],
+        features_kernel, "features", steps, [], [after(flat, counts)],
         [w_patch, bias_patch, w_cross_key, w_cross_value], "rffff",
         [((image_rows, width), BF16, True), ((image_rows, 2 * INNER), BF16, True)],
         [((width, 2 * INNER), BF16)], 5.1,
     )
+    counts = counts + exchange(counts, bits.pop(0))
     h1, qkv, chances, mixed, x1, h2, cross_q = run(
-        self_forward_kernel, "self_forward", steps, [lengths], [tokens],
+        self_forward_kernel, "self_forward", steps, [lengths], [after(tokens, counts, feat)],
         [gain_one, w_query, w_key, w_value, w_out, gain_two, w_cross_query], "srfffffff",
         [
             ((rows, width), BF16, True),
@@ -550,8 +589,10 @@
         ],
         [((width, 3 * INNER), BF16), ((width, INNER), BF16)], 6.0,
     )
+    counts = counts + exchange(counts, bits.pop(0))
     cross_chances, cross_mixed, x2 = run(
-        cross_forward_kernel, "cross_forward", steps, [], [cross_q, cross_kv, x1], [w_cross_out], "rrrf",
+        cross_forward_kernel, "cross_forward", steps, [], [after(cross_q, counts), cross_kv, x1],
+        [w_cross_out], "rrrf",
         [
             ((seqs, PAIRS, 2 * images, maxlen), BF16, True),
             ((rows, INNER), BF16, True),
@@ -559,18 +600,18 @@
         ],
         [], 6.0,
     )
+    while len(bits) > 1:
+        counts = counts + exchange(counts, bits.pop(0))
     late_shapes = [w_down.shape, w_gate.shape, w_up.shape]
     late_rows = sum(block_rows(s) for s in late_shapes)
     result, dx2, gain3, *late = run(
         functools.partial(feed_forward_kernel, maxlen=maxlen), "feed_forward", steps,
-        [lengths, codes], [x2, cotangent], [gain_three, w_gate, w_up, w_down], "ssrrffff",
+        [lengths, codes], [after(x2, counts), cotangent], [gain_three, w_gate, w_up, w_down], "ssrrffff",
         [
             ((rows, width), BF16, True),
             ((rows, width), F32, True),
             ((1, width), F32, False),
-            ((HALF, late_rows, 128), F32, False),
-            ((HALF, late_rows, 128), F32, False),
-        ],
+        ] + [((8, late_rows, 128), F32, False)] * 4,
         [
             ((part, wide), BF16),
             ((part, wide), BF16),
@@ -581,51 +622,60 @@
         ],
         14.0,
     )
+    counts = counts + exchange(counts, bits.pop(0))
+    group_weights = mix * jnp.sum(counts) / counts
+    weight_own = jnp.where(in_first, group_weights[0], group_weights[1])
+    weight_other = jnp.where(other_first, group_weights[0], group_weights[1])
+    weight_ref = weight_own[None]
+    weights = (weight_own, weight_other)
+
+    late = Chunk(late, late_shapes, weights, codes)
+    late.start()
+    dcq, dkv = run(
+        cross_attention_kernel, "cross_attention", steps, [],
+        [after(dx2, late.send), cross_q, cross_chances, cross_kv], [w_cross_out], "rrrrf",
+        [((rows, INNER), BF16, True), ((image_rows, 2 * INNER), BF16, True)], [], 8.0,
+    )
+    late.first()
     cross_shapes = [w_cross_out.shape, w_cross_query.shape, w_cross_key.shape, w_cross_value.shape]
     cross_rows = sum(block_rows(s) for s in cross_shapes)
     dfeat, dx1, gain2, dbias, *cross = run(
-        cross_backward_kernel, "cross_backward", steps, [codes],
-        [dx2, cross_mixed, cross_q, cross_chances, cross_kv, h2, feat, x1],
-        [gain_two, w_cross_out, w_cross_query, w_cross_key, w_cross_value], "srrrrrrrrfffff",
+        cross_weights_kernel, "cross_weights", steps, [codes],
+        [after(dx2, late.send), cross_mixed, dcq, dkv, h2, feat, x1],
+        [gain_two, w_cross_query, w_cross_key, w_cross_value], "srrrrrrrffff",
         [
             ((image_rows, width), BF16, True),
             ((rows, width), F32, True),
             ((1, width), F32, False),
             ((1, width), F32, False),
-            ((HALF, cross_rows, 128), F32, False),
-            ((HALF, cross_rows, 128), F32, False),
-        ],
+        ] + [((8, cross_rows, 128), F32, False)] * 4,
         [
             ((width, 2 * INNER), BF16),
-            ((part, INNER), BF16),
-            ((image_rows // steps, 2 * INNER), BF16),
             (w_cross_out.shape, F32),
             (w_cross_query.shape, F32),
             ((width, 2 * INNER), F32),
         ],
-        10.0,
-    )
-    patch_shapes = [w_patch.shape]
-    patch_rows = block_rows(w_patch.shape)
-    patch = run(
-        patch_weight_kernel, "patch_weight", steps, [codes], [flat, dfeat], [], "srr",
-        [((HALF, patch_rows, 128), F32, False), ((HALF, patch_rows, 128), F32, False)],
-        [((width, patch_dim), F32), ((patch_dim, width), F32)], 5.0,
-    )
+        8.0,
+    )
+    late.second()
+    cross = Chunk(cross, cross_shapes, weights, codes)
+    cross.start()
+    (dqkv,) = run(
+        self_attention_kernel, "self_attention", steps, [],
+        [after(dx1, late.send, cross.send), qkv, chances], [w_out], "rrrf",
+        [((rows, 3 * INNER), BF16, True)], [], 8.0,
+    )
+    late.third()
+    cross.first()
     own_shapes = [w_out.shape, w_query.shape, w_key.shape, w_value.shape, (BLOCKS * 8, 128)]
     own_rows = sum(block_rows(s) for s in own_shapes)
     grad_tokens, *own = run(
-        self_backward_kernel, "self_backward", steps, [codes, weight_ref],
-        [dx1, mixed, qkv, chances, h1, tokens],
-        [gain_one, w_out, w_query, w_key, w_value, gain2, gain3, dbias], "ssrrrrrrffffffff",
-        [
-            ((rows, width), F32, True),
-            ((HALF, own_rows, 128), F32, False),
-            ((HALF, own_rows, 128), F32, False),
-        ],
+        self_weights_kernel, "self_weights", steps, [codes, weight_ref],
+        [after(dx1, late.send, cross.send), mixed, dqkv, h1, tokens],
+        [gain_one, w_query, w_key, w_value, gain2, gain3, dbias], "ssrrrrrfffffff",
+        [((rows, width), F32, True)] + [((8, own_rows, 128), F32, False)] * 4,
         [
             ((width, 3 * INNER), BF16),
-            ((part, 3 * INNER), BF16),
             (w_out.shape, F32),
             ((width, 3 * INNER), F32),
             ((1, width), F32),
@@ -633,16 +683,73 @@
         ],
         8.0,
     )
+    late.fourth()
+    cross.second()
+    own = Chunk(own, own_shapes, weights, codes, True)
+    own.start()
+    patch_shapes = [w_patch.shape]
+    patch_rows = block_rows(w_patch.shape)
+    patch = run(
+        patch_weight_kernel, "patch_weight", steps, [codes],
+        [flat, after(dfeat, late.send, cross.send, own.send)], [], "srr",
+        [((8, patch_rows, 128), F32, False)] * 4,
+        [((width, patch_dim), F32), ((patch_dim, width), F32)], 8.0,
+    )
+    late.back_fourth()
+    own.first()
+    patch = Chunk(patch, patch_shapes, weights, codes)
+    patch.start()
+    half = image_rows // 2
     (grad_patches,) = run(
-        patch_input_kernel, "patch_input", 2 * steps, [weight_ref], [dfeat], [w_patch], "srf",
-        [((image_rows, patch_dim), F32, True)], [], 4.0,
-    )
-
-    pieces = [spread_blocks(sum_blocks(v, weight_own, weight_other)) for v in (late, cross, patch, own)]
-    late = unpack(pieces[0], late_shapes, codes)
-    cross = unpack(pieces[1], cross_shapes, codes)
-    patch = unpack(pieces[2], patch_shapes, codes)
-    own = unpack(pieces[3], own_shapes, codes, True)
+        patch_input_kernel, "patch_input", 2 * steps, [weight_ref],
+        [after(dfeat, late.send, own.send, patch.send)], [w_patch], "srf",
+        [((image_rows, patch_dim), F32, True)], [], 8.0,
+    )
+    late.back_third()
+    own.second()
+    cross.third()
+    grad_patches, late.send, own.send, cross.send = lax.optimization_barrier(
+        (grad_patches, late.send, own.send, cross.send)
+    )
+    late.back_second()
+    cross.fourth()
+    cross.back_fourth()
+    late.send, cross.send = lax.optimization_barrier((late.send, cross.send))
+    late.back_first()
+    cross.back_third()
+    own.third()
+    own.fourth()
+    late.rest, cross.send, own.send, patch.send = lax.optimization_barrier(
+        (late.rest, cross.send, own.send, patch.send)
+    )
+    late.finish()
+    patch.first()
+    own.back_fourth()
+    own.back_third()
+    patch.send, own.send, cross.send = lax.optimization_barrier((patch.send, own.send, cross.send))
+    patch.second()
+    patch.send, cross.send = lax.optimization_barrier((patch.send, cross.send))
+    cross.back_second()
+    patch.third()
+    patch.send, cross.send = lax.optimization_barrier((patch.send, cross.send))
+    cross.back_first()
+    patch.fourth()
+    patch.back_fourth()
+    patch.send, cross.rest, own.send = lax.optimization_barrier((patch.send, cross.rest, own.send))
+    cross.finish()
+    own.back_second()
+    patch.back_third()
+    patch.send, own.send = lax.optimization_barrier((patch.send, own.send))
+    own.back_first()
+    own.rest, patch.send = lax.optimization_barrier((own.rest, patch.send))
+    own.finish()
+    patch.back_second()
+    patch.back_first()
+    patch.finish()
+    late = late.unpack()
+    cross = cross.unpack()
+    own = own.unpack()
+    patch = patch.unpack()
     gains = [g.reshape(width) for g in own[5:]]
     return (
         result,

time: 359 us -> 346 us (0.964)
  starting transfers between devices: 61 us -> 46.5 us
  waiting for transfers between devices: 136 us -> 149 us
  other arithmetic: 15.8 us -> 7.98 us
  local copies, waits for them, and re-layouts: 10.2 us -> 2.99 us
    ppermute x49 -> x53, starting transfers between devices: 61 us -> 46.5 us  [exchange(): lax.ppermute(values, 'dp', flips(count, first, first if second is None el...]
    ppermute x49 -> x53, waiting for transfers between devices: 136 us -> 149 us  [exchange(): lax.ppermute(values, 'dp', flips(count, first, first if second is None el...]
    mul x8 -> x0, other arithmetic: 9.46 us -> none  [sum_blocks(): keep, got = (keep * own, got * other)]
    unnamed x28 -> x19, local copies, waits for them, and re-layouts: 8.29 us -> 1.05 us
    pallas_call x8 -> x10, Pallas kernels: 114 us -> 120 us  [run(): pl.pallas_call(kernel, grid=(steps,), out_shape=[jax.ShapeDtypeStruct(s,...]
  transfers between devices with their start and end apart: 49 -> 53, of which waited for: 21 -> 28; matrix products, arithmetic and copies ran while one was open for 4% -> 2% of each run, Pallas kernels for 35% -> 26%
where the time goes in v1:
time: 346 us; the launch traced here: 345 us
  waiting for transfers between devices  149 us (43%)
  Pallas kernels  133 us (38%)
  starting transfers between devices  46.5 us (13%)
  other arithmetic  7.98 us (2%)
  between operations  5.73 us (2%)
    ppermute x53, waiting for transfers between devices, exchange(): lax.ppermute(values, 'dp', flips(count, first, first if second is None el...  149 us
    pallas_call x10, Pallas kernels, run(): pl.pallas_call(kernel, grid=(steps,), out_shape=[jax.ShapeDtypeStruct(s,...  120 us
    ppermute x53, starting transfers between devices, exchange(): lax.ppermute(values, 'dp', flips(count, first, first if second is None el...  46.5 us
    pallas_call x4, Pallas kernels, unpack(): pl.pallas_call(functools.partial(unpack_kernel, shapes, with_gains), out_...  12.8 us
  transfers between devices with their start and end apart: 53, of which 28 were waited for; matrix products, arithmetic and copies ran while one was open for 2% of the time, Pallas kernels for 26%

profile of v1, /device:TPU:0, one launch (start us, length us, event | category | flops | bytes accessed | tf_op | source)
XLA Modules:
  0.0 345.0 jit_solution(5057485155526415550)
XLA Ops:
  0.7 1.3 reduce_sum.18
  2.6 1.3 fusion.6
  6.0 2.9 collective-permute-start.1
  8.8 9.8 %features.1 = (bf16[2048,512]{1,0:T(8,128)(2,1)}, bf16[2048,768]{1,0:T(8,128)(2,1)}) custom-call(bf16[2048,1664]{1,0:T(8,128)(2,1)} %bitcast.17, bf16[1664,512]{1,0:T(8,128)(2,1)} %w_ref.1, f32[1,512]{1,0:T(1,128)} %bitcast.19, bf16[512,384]{1,0:T(8,128)(2,1)} %wck_ref.1, bf16[512,384]{1,0:T(8,128)(2,1)} %wcv_ref.1), custom_call_target="tpu_custom_call" | custom-call | flops 5100000256 | bytes 1048576 | tf_op jit(solution)/shard_map/features/pallas_call | solution.py:509
  18.7 1.6 collective-permute-start.2
  20.3 9.4 %self_forward.1 = (bf16[1024,512]{1,0:T(8,128)(2,1)}, bf16[1024,1152]{1,0:T(8,128)(2,1)}, bf16[8,3,256,128]{3,2,1,0:T(8,128)(2,1)}, bf16[1024,384]{1,0:T(8,128)(...) custom-call(s32[8]{0:T(128)} %len_ref.3, bf16[1024,512]{1,0:T(8,128)(2,1)} %tok_ref.2, ...), custom_call_target="tpu_custom_call" | custom-call | flops 6000000000 | bytes 1048576 | tf_op jit(solution)/shard_map/self_forward/pallas_call | solution.py:509
  29.7 2.8 collective-permute-start.3
  32.5 8.1 %cross_forward.1 = (bf16[8,3,512,128]{3,2,1,0:T(8,128)(2,1)}, bf16[1024,384]{1,0:T(8,128)(2,1)}, f32[1024,512]{1,0:T(8,128)}) custom-call(bf16[1024,384]{1,0:T(8,128)(2,1)} %get-tuple-element.110.cq_ref, bf16[2048,768]{1,0:T(8,128)(2,1)} %get-tuple-element.111.kv_ref, f32[1024,512]{1,0:T(8,128)} %get-tuple-element.112.x1_ref, bf16[384,512]{1,0:T(8,128)(2,1)} %wco_ref.3), custom_call_target="tpu_custom_call" | custom-call | flops 6000000000 | bytes 1048576 | tf_op jit(solution)/shard_map/cross_forward/pallas_call | solution.py:509
  40.6 23.4 %feed_forward.1 = (bf16[1024,512]{1,0:T(8,128)(2,1)}, f32[1024,512]{1,0:T(8,128)}, f32[1,512]{1,0:T(1,128)}, f32[8,384,128]{2,1,0:T(8,128)}, f32[8,384,128]{2,1,...) custom-call(s32[8]{0:T(128)} %len_ref.3, s32[2]{0:T(128)} %pad_add_fusion.code_ref, ...), custom_call_target="tpu_custom_call" | custom-call | flops 14000000000 | bytes 1048576 | tf_op jit(solution)/shard_map/feed_forward/pallas_call | solution.py:509
  65.2 1.5 collective-permute-start.4
  66.7 3.0 collective-permute-done.4
  74.2 1.7 multiply_add_fusion
  76.3 11.1 %cross_attention.1 = (bf16[1024,384]{1,0:T(8,128)(2,1)}, bf16[2048,768]{1,0:T(8,128)(2,1)}) custom-call(f32[1024,512]{1,0:T(8,128)} %get-tuple-element.123.dx2_ref, bf16[1024,384]{1,0:T(8,128)(2,1)} %get-tuple-element.110.cq_ref, bf16[8,3,512,128]{3,2,1,0:T(8,128)(2,1)} %get-tuple-element.124.pt_ref, bf16[2048,768]{1,0:T(8,128)(2,1)} %get-tuple-element.111.kv_ref, ...), custom_call_target="tpu_custom_call" | custom-call | flops 8000000000 | bytes 1048576 | tf_op jit(solution)/shard_map/cross_attention/pallas_call | solution.py:509
  87.4 9.0 %collective-permute-done.7 = f32[8,384,128]{2,1,0:T(8,128)S(1)} collective-permute-done((f32[8,384,128]{2,1,0:T(8,128)S(1)}, f32[8,384,128]{2,1,0:T(8,128)S(1)}, u32[]{:S(2)}, u32[]{:S(2)}) %collective-permute-start.7) | collective-permute-done | bytes 1572896 | tf_op jit(solution)/shard_map/ppermute | solution.py:346
  96.5 16.4 %cross_weights.1 = (bf16[2048,512]{1,0:T(8,128)(2,1)}, f32[1024,512]{1,0:T(8,128)}, f32[1,512]{1,0:T(1,128)}, f32[1,512]{1,0:T(1,128)}, f32[8,192,128]{2,1,0:T(8...) custom-call(s32[2]{0:T(128)} %pad_add_fusion.code_ref, ...), custom_call_target="tpu_custom_call" | custom-call | flops 8000000000 | bytes 1048576 | tf_op jit(solution)/shard_map/cross_weights/pallas_call | solution.py:509
  113.5 2.0 collective-permute-done.11
  115.5 1.2 multiply_add_fusion.6
  116.8 13.7 %collective-permute-done.8 = f32[4,384,128]{2,1,0:T(8,128)S(1)} collective-permute-done((f32[4,384,128]{2,1,0:T(8,128)S(1)}, f32[4,384,128]{2,1,0:T(8,128)S(1)}, u32[]{:S(2)}, u32[]{:S(2)}) %collective-permute-start.8) | collective-permute-done | bytes 786464 | tf_op jit(solution)/shard_map/ppermute | solution.py:346
  130.8 8.9 %self_attention.1.dqkv_ref = bf16[1024,1152]{1,0:T(8,128)(2,1)} custom-call(f32[1024,512]{1,0:T(8,128)} %get-tuple-element.135.dx1_ref, bf16[1024,1152]{1,0:T(8,128)(2,1)} %get-tuple-element.136.qkv_ref, bf16[8,3,256,128]{3,2,1,0:T(8,128)(2,1)} %get-tuple-element.137.pt_ref, bf16[384,512]{1,0:T(8,128)(2,1)} %wo_ref.3), custom_call_target="tpu_custom_call" | custom-call | flops 8000000000 | bytes 1048576 | tf_op jit(solution)/shard_map/self_attention/pallas_call | solution.py:509
  140.0 1.7 collective-permute-start.13
  141.8 12.3 %self_weights.1 = (f32[1024,512]{1,0:T(8,128)}, f32[8,200,128]{2,1,0:T(8,128)}, f32[8,200,128]{2,1,0:T(8,128)}, f32[8,200,128]{2,1,0:T(8,128)}, f32[8,200,128]{2,1,0:T(8,128)}) custom-call(s32[2]{0:T(128)} %pad_add_fusion.code_ref, f32[1]{0:T(128)} %bitcast.10.weight_ref, f32[1024,512]{1,0:T(8,128)} %get-tuple-element.135.dx1_ref, ...), custom_call_target="tpu_custom_call" | custom-call | flops 8000000000 | bytes 1048576 | tf_op jit(solution)/shard_map/self_weights/pallas_call | solution.py:509
  154.9 0.7 collective-permute-start.14
  156.0 10.9 %collective-permute-done.14 = f32[1,384,128]{2,1,0:T(8,128)S(1)} collective-permute-done((f32[1,384,128]{2,1,0:T(8,128)S(1)}, f32[1,384,128]{2,1,0:T(8,128)S(1)}, u32[]{:S(2)}, u32[]{:S(2)}) %collective-permute-start.14) | collective-permute-done | bytes 196640 | tf_op jit(solution)/shard_map/ppermute | solution.py:346
  167.1 2.1 collective-permute-start.22
  169.3 1.2 collective-permute-start.17
  170.5 10.8 %patch_weight.1 = (f32[8,208,128]{2,1,0:T(8,128)}, f32[8,208,128]{2,1,0:T(8,128)}, f32[8,208,128]{2,1,0:T(8,128)}, f32[8,208,128]{2,1,0:T(8,128)}) custom-call(s32[2]{0:T(128)} %pad_add_fusion.code_ref, bf16[2048,1664]{1,0:T(8,128)(2,1)} %bitcast.18, bf16[2048,512]{1,0:T(8,128)(2,1)} %get-tuple-element.151.dfeat_ref), custom_call_target="tpu_custom_call" | custom-call | flops 8000000000 | bytes 1048576 | tf_op jit(solution)/shard_map/patch_weight/pallas_call | solution.py:509
  181.5 0.9 copy-done.4
  182.6 1.0 collective-permute-start.21
  184.0 10.2 %patch_input.1 = f32[2048,1664]{1,0:T(8,128)} custom-call(f32[1]{0:T(128)} %bitcast.10.weight_ref, bf16[2048,512]{1,0:T(8,128)(2,1)} %get-tuple-element.151.dfeat_ref, bf16[1664,512]{1,0:T(8,128)(2,1)} %w_ref.1), custom_call_target="tpu_custom_call" | custom-call | flops 8000000000 | bytes 1048576 | tf_op jit(solution)/shard_map/patch_input/pallas_call | solution.py:509
  194.2 1.0 collective-permute-start.24
  195.2 0.8 collective-permute-start.25
  196.1 6.2 %collective-permute-done.25 = f32[1,192,128]{2,1,0:T(8,128)S(1)} collective-permute-done((f32[1,192,128]{2,1,0:T(8,128)S(1)}, f32[1,192,128]{2,1,0:T(8,128)S(1)}, u32[]{:S(2)}, u32[]{:S(2)}) %collective-permute-start.25) | collective-permute-done | bytes 98336 | tf_op jit(solution)/shard_map/ppermute | solution.py:346
  202.3 7.0 %collective-permute-done.26 = f32[1,192,128]{2,1,0:T(8,128)S(1)} collective-permute-done((f32[1,192,128]{2,1,0:T(8,128)S(1)}, f32[1,192,128]{2,1,0:T(8,128)S(1)}, u32[]{:S(2)}, u32[]{:S(2)}) %collective-permute-start.26) | collective-permute-done | bytes 98336 | tf_op jit(solution)/shard_map/ppermute | solution.py:346
  209.5 1.3 collective-permute-start.27
  210.8 5.8 %collective-permute-done.29 = f32[2,200,128]{2,1,0:T(8,128)S(1)} collective-permute-done((f32[2,200,128]{2,1,0:T(8,128)S(1)}, f32[2,200,128]{2,1,0:T(8,128)S(1)}, u32[]{:S(2)}, u32[]{:S(2)}) %collective-permute-start.29) | collective-permute-done | bytes 204832 | tf_op jit(solution)/shard_map/ppermute | solution.py:346
  216.6 0.8 collective-permute-start.30
  217.4 1.7 collective-permute-start.28
  219.2 4.0 %collective-permute-done.30 = f32[1,200,128]{2,1,0:T(8,128)S(1)} collective-permute-done((f32[1,200,128]{2,1,0:T(8,128)S(1)}, f32[1,200,128]{2,1,0:T(8,128)S(1)}, u32[]{:S(2)}, u32[]{:S(2)}) %collective-permute-start.30) | collective-permute-done | bytes 102432 | tf_op jit(solution)/shard_map/ppermute | solution.py:346
  223.2 2.6 collective-permute-done.28
  225.9 4.1 %collective-permute-done.27.refs_1_ = f32[8,384,128]{2,1,0:T(8,128)S(1)} collective-permute-done((f32[8,384,128]{2,1,0:T(8,128)S(1)}, f32[8,384,128]{2,1,0:T(8,128)S(1)}, u32[]{:S(2)}, u32[]{:S(2)}) %collective-permute-start.27) | collective-permute-done | bytes 1572896 | tf_op jit(solution)/shard_map/ppermute | solution.py:346
  230.0 1.3 collective-permute-start.31
  231.2 5.7 %collective-permute-done.32 = f32[1,200,128]{2,1,0:T(8,128)S(1)} collective-permute-done((f32[1,200,128]{2,1,0:T(8,128)S(1)}, f32[1,200,128]{2,1,0:T(8,128)S(1)}, u32[]{:S(2)}, u32[]{:S(2)}) %collective-permute-start.32) | collective-permute-done | bytes 102432 | tf_op jit(solution)/shard_map/ppermute | solution.py:346
  237.2 5.6 %collective-permute-done.33 = f32[2,200,128]{2,1,0:T(8,128)S(1)} collective-permute-done((f32[2,200,128]{2,1,0:T(8,128)S(1)}, f32[2,200,128]{2,1,0:T(8,128)S(1)}, u32[]{:S(2)}, u32[]{:S(2)}) %collective-permute-start.33) | collective-permute-done | bytes 204832 | tf_op jit(solution)/shard_map/ppermute | solution.py:346
  242.9 2.4 collective-permute-start.34
  245.3 6.1 %collective-permute-done.34 = f32[4,208,128]{2,1,0:T(8,128)S(1)} collective-permute-done((f32[4,208,128]{2,1,0:T(8,128)S(1)}, f32[4,208,128]{2,1,0:T(8,128)S(1)}, u32[]{:S(2)}, u32[]{:S(2)}) %collective-permute-start.34) | collective-permute-done | bytes 426016 | tf_op jit(solution)/shard_map/ppermute | solution.py:346
  251.8 2.0 collective-permute-start.36
  253.8 3.5 %collective-permute-done.35 = f32[2,208,128]{2,1,0:T(8,128)S(1)} collective-permute-done((f32[2,208,128]{2,1,0:T(8,128)S(1)}, f32[2,208,128]{2,1,0:T(8,128)S(1)}, u32[]{:S(2)}, u32[]{:S(2)}) %collective-permute-start.35) | collective-permute-done | bytes 213024 | tf_op jit(solution)/shard_map/ppermute | solution.py:346
  257.4 2.2 collective-permute-done.36
  259.6 1.4 collective-permute-start.39
  261.0 2.2 collective-permute-start.37
  263.2 3.4 collective-permute-done.37
  266.6 2.3 collective-permute-start.38
  268.9 3.4 collective-permute-done.38
  272.3 5.5 %collective-permute-start.41 = (f32[4,200,128]{2,1,0:T(8,128)S(1)}, f32[4,200,128]{2,1,0:T(8,128)S(1)}, u32[]{:S(2)}, u32[]{:S(2)}) collective-permute-start(f32[4,200,128]{2,1,0:T(8,128)S(1)} %pad_maximum_fusion.5), channel_id=1, source_target_pairs={{0,4},{1,3},{2,6},{3,1},{4,0},{5,7},{6,2},{7,5},{8,12},{9,11},{10,... | collective-permute-start | bytes 1228808 | tf_op jit(solution)/shard_map/ppermute | solution.py:346
  277.9 5.8 %collective-permute-done.40 = f32[2,208,128]{2,1,0:T(8,128)S(1)} collective-permute-done((f32[2,208,128]{2,1,0:T(8,128)S(1)}, f32[2,208,128]{2,1,0:T(8,128)S(1)}, u32[]{:S(2)}, u32[]{:S(2)}) %collective-permute-start.40) | collective-permute-done | bytes 213024 | tf_op jit(solution)/shard_map/ppermute | solution.py:346
  283.8 4.2 %collective-permute-done.41 = f32[4,200,128]{2,1,0:T(8,128)S(1)} collective-permute-done((f32[4,200,128]{2,1,0:T(8,128)S(1)}, f32[4,200,128]{2,1,0:T(8,128)S(1)}, u32[]{:S(2)}, u32[]{:S(2)}) %collective-permute-start.41) | collective-permute-done | bytes 409632 | tf_op jit(solution)/shard_map/ppermute | solution.py:346
  288.6 16.3 %collective-permute-done.42.refs_1_ = f32[8,200,128]{2,1,0:T(8,128)S(1)} collective-permute-done((f32[8,200,128]{2,1,0:T(8,128)S(1)}, f32[8,200,128]{2,1,0:T(8,128)S(1)}, u32[]{:S(2)}, u32[]{:S(2)}) %collective-permute-start.42) | collective-permute-done | bytes 819232 | tf_op jit(solution)/shard_map/ppermute | solution.py:346
  304.9 2.2 collective-permute-start.45
  307.2 10.7 %collective-permute-done.45 = f32[4,208,128]{2,1,0:T(8,128)S(1)} collective-permute-done((f32[4,208,128]{2,1,0:T(8,128)S(1)}, f32[4,208,128]{2,1,0:T(8,128)S(1)}, u32[]{:S(2)}, u32[]{:S(2)}) %collective-permute-start.45) | collective-permute-done | bytes 426016 | tf_op jit(solution)/shard_map/ppermute | solution.py:346
  318.5 12.1 %collective-permute-done.46.refs_1_ = f32[8,208,128]{2,1,0:T(8,128)S(1)} collective-permute-done((f32[8,208,128]{2,1,0:T(8,128)S(1)}, f32[8,208,128]{2,1,0:T(8,128)S(1)}, u32[]{:S(2)}, u32[]{:S(2)}) %collective-permute-start.46) | collective-permute-done | bytes 852000 | tf_op jit(solution)/shard_map/ppermute | solution.py:346
  331.7 4.3 %unpack.7 = (f32[1024,512]{1,0:T(8,128)}, f32[512,1024]{1,0:T(8,128)}, f32[512,1024]{1,0:T(8,128)}) custom-call(s32[2]{0:T(128)S(1)} %copy-done, f32[8,384,128]{2,1,0:T(8,128)S(1)} %pad_maximum_fusion.refs_0_, f32[8,384,128]{2,1,0:T(8,128)S(1)} %collective-permute-done.27.refs_1_, f32[8,384,128]{2,1,0:T(8,128)S(1)} %collective-permute-done.51.refs_2_, ...), custom_call_target="tpu_custom_call" | custom-call | tf_op jit(solution)/shard_map/unpack/pallas_call | solution.py:416
  336.5 2.8 unpack.6
  339.2 2.8 unpack.4
  342.1 3.0 unpack.5
  (122 shorter events, 11.9 us)
Async XLA Ops:
  4.6 1.3 collective-permute-start
  6.0 12.7 %collective-permute-start.1 = (f32[2]{0:T(128)S(1)}, f32[2]{0:T(128)S(1)}, u32[]{:S(2)}, u32[]{:S(2)}) collective-permute-start(f32[2]{0:T(128)S(1)} %fusion.8), channel_id=1, source_target_pairs={{0,2},{1,3},{2,0},{3,1},{4,6},{5,7},{6,4},{7,5},{8,10},{9,11},{10,... | collective-permute-start | bytes 32 | tf_op jit(solution)/shard_map/ppermute | solution.py:346
  18.7 11.0 %collective-permute-start.2 = (f32[2]{0:T(128)S(1)}, f32[2]{0:T(128)S(1)}, u32[]{:S(2)}, u32[]{:S(2)}) collective-permute-start(f32[2]{0:T(128)S(1)} %add.163), channel_id=1, source_target_pairs={{0,4},{1,5},{2,6},{3,7},{4,0},{5,1},{6,2},{7,3},{8,12},{9,13},{10,... | collective-permute-start | bytes 32 | tf_op jit(solution)/shard_map/ppermute | solution.py:346
  29.7 11.0 %collective-permute-start.3 = (f32[2]{0:T(128)S(1)}, f32[2]{0:T(128)S(1)}, u32[]{:S(2)}, u32[]{:S(2)}) collective-permute-start(f32[2]{0:T(128)S(1)} %add.164), channel_id=1, source_target_pairs={{0,8},{1,9},{2,10},{3,11},{4,12},{5,13},{6,14},{7,15},{8,0},{9,1},... | collective-permute-start | bytes 32 | tf_op jit(solution)/shard_map/ppermute | solution.py:346
  40.6 29.7 %copy-start.7 = (f32[2]{0:T(128)S(1)}, f32[2]{0:T(128)}, u32[]{:S(2)}) copy-start(f32[2]{0:T(128)} %param.29) | copy-start | bytes 28
  64.0 10.2 %collective-permute-start.6 = (f32[8,384,128]{2,1,0:T(8,128)}, f32[8,384,128]{2,1,0:T(8,128)S(1)}, u32[]{:S(2)}, u32[]{:S(2)}) collective-permute-start(f32[8,384,128]{2,1,0:T(8,128)} %get-tuple-element.120), channel_id=1, source_target_pairs={{0,1},{1,0},{2,3},{3,2},{4,5},{5,4},{6,7},{7,6},{8,9},{9,8},{10,11... | collective-permute-start | bytes 4718600 | tf_op jit(solution)/shard_map/ppermute | solution.py:346
  64.1 11.9 %collective-permute-start.5 = (f32[8,384,128]{2,1,0:T(8,128)}, f32[8,384,128]{2,1,0:T(8,128)S(1)}, u32[]{:S(2)}, u32[]{:S(2)}) collective-permute-start(f32[8,384,128]{2,1,0:T(8,128)} %get-tuple-element.118), channel_id=1, source_target_pairs={{0,1},{1,0},{2,3},{3,2},{4,5},{5,4},{6,7},{7,6},{8,9},{9,8},{10,11... | collective-permute-start | bytes 4718600 | tf_op jit(solution)/shard_map/ppermute | solution.py:346
  65.2 4.5 %collective-permute-start.4 = (f32[2]{0:T(128)S(1)}, f32[2]{0:T(128)S(1)}, u32[]{:S(2)}, u32[]{:S(2)}) collective-permute-start(f32[2]{0:T(128)S(1)} %add.165), channel_id=1, source_target_pairs={{0,16},{1,17},{2,18},{3,19},{4,20},{5,21},{6,22},{7,23},{8,24},{9,... | collective-permute-start | bytes 32 | tf_op jit(solution)/shard_map/ppermute | solution.py:346
  74.2 1.9 copy-start.1
  75.9 20.5 %collective-permute-start.7 = (f32[8,384,128]{2,1,0:T(8,128)S(1)}, f32[8,384,128]{2,1,0:T(8,128)S(1)}, u32[]{:S(2)}, u32[]{:S(2)}) collective-permute-start(f32[8,384,128]{2,1,0:T(8,128)S(1)} %multiply_add_fusion), channel_id=1, source_target_pairs={{0,2},{1,5},{2,0},{3,7},{4,6},{5,1},{6,4},{7,3},{8,10},{9,13},{10,... | collective-permute-start | bytes 4718600 | tf_op jit(solution)/shard_map/ppermute | solution.py:346
  113.0 2.6 collective-permute-start.11
  113.0 17.5 %collective-permute-start.8 = (f32[4,384,128]{2,1,0:T(8,128)S(1)}, f32[4,384,128]{2,1,0:T(8,128)S(1)}, u32[]{:S(2)}, u32[]{:S(2)}) collective-permute-start(f32[4,384,128]{2,1,0:T(8,128)S(1)} %get-tuple-element.196), channel_id=1, source_target_pairs={{0,4},{1,3},{2,6},{3,1},{4,0},{5,7},{6,2},{7,5},{8,12},{9,11},{10,... | collective-permute-start | bytes 2359304 | tf_op jit(solution)/shard_map/ppermute | solution.py:346
  113.1 26.5 %collective-permute-start.10 = (f32[8,192,128]{2,1,0:T(8,128)}, f32[8,192,128]{2,1,0:T(8,128)S(1)}, u32[]{:S(2)}, u32[]{:S(2)}) collective-permute-start(f32[8,192,128]{2,1,0:T(8,128)} %get-tuple-element.130), channel_id=1, source_target_pairs={{0,1},{1,0},{2,3},{3,2},{4,5},{5,4},{6,7},{7,6},{8,9},{9,8},{10,11... | collective-permute-start | bytes 2359304 | tf_op jit(solution)/shard_map/ppermute | solution.py:346
  116.8 25.0 %collective-permute-start.12 = (f32[8,192,128]{2,1,0:T(8,128)S(1)}, f32[8,192,128]{2,1,0:T(8,128)S(1)}, u32[]{:S(2)}, u32[]{:S(2)}) collective-permute-start(f32[8,192,128]{2,1,0:T(8,128)S(1)} %multiply_add_fusion.6), channel_id=1, source_target_pairs={{0,2},{1,5},{2,0},{3,7},{4,6},{5,1},{6,4},{7,3},{8,10},{9,13},{10,... | collective-permute-start | bytes 2359304 | tf_op jit(solution)/shard_map/ppermute | solution.py:346
  130.7 9.3 %collective-permute-start.9 = (f32[2,384,128]{2,1,0:T(8,128)S(1)}, f32[2,384,128]{2,1,0:T(8,128)S(1)}, u32[]{:S(2)}, u32[]{:S(2)}) collective-permute-start(f32[2,384,128]{2,1,0:T(8,128)S(1)} %get-tuple-element.204), channel_id=1, source_target_pairs={{0,8},{1,9},{2,10},{3,11},{4,12},{5,13},{6,14},{7,15},{8,0},{9,1},... | collective-permute-start | bytes 1179656 | tf_op jit(solution)/shard_map/ppermute | solution.py:346
  130.8 8.9 %copy-start.6 = (f32[8,192,128]{2,1,0:T(8,128)S(1)}, f32[8,192,128]{2,1,0:T(8,128)}, u32[]{:S(2)}) copy-start(f32[8,192,128]{2,1,0:T(8,128)} %get-tuple-element.129) | copy-start | bytes 2359300
  140.0 14.9 %collective-permute-start.13 = (f32[1,384,128]{2,1,0:T(8,128)S(1)}, f32[1,384,128]{2,1,0:T(8,128)S(1)}, u32[]{:S(2)}, u32[]{:S(2)}) collective-permute-start(f32[1,384,128]{2,1,0:T(8,128)S(1)} %slice_add_fusion.17), channel_id=1, source_target_pairs={{0,16},{1,17},{2,18},{3,19},{4,20},{5,21},{6,22},{7,23},{8,24},{9,... | collective-permute-start | bytes 589832 | tf_op jit(solution)/shard_map/ppermute | solution.py:346
  154.1 15.1 %copy-start.5 = (f32[8,200,128]{2,1,0:T(8,128)S(1)}, f32[8,200,128]{2,1,0:T(8,128)}, u32[]{:S(2)}) copy-start(f32[8,200,128]{2,1,0:T(8,128)} %get-tuple-element.146) | copy-start | bytes 2457604
  154.1 15.1 %collective-permute-start.16 = (f32[8,200,128]{2,1,0:T(8,128)}, f32[8,200,128]{2,1,0:T(8,128)S(1)}, u32[]{:S(2)}, u32[]{:S(2)}) collective-permute-start(f32[8,200,128]{2,1,0:T(8,128)} %get-tuple-element.147), channel_id=1, source_target_pairs={{0,1},{1,0},{2,3},{3,2},{4,5},{5,4},{6,7},{7,6},{8,9},{9,8},{10,11... | collective-permute-start | bytes 2457608 | tf_op jit(solution)/shard_map/ppermute | solution.py:346
  154.2 12.9 %collective-permute-start.18 = (f32[4,192,128]{2,1,0:T(8,128)S(1)}, f32[4,192,128]{2,1,0:T(8,128)S(1)}, u32[]{:S(2)}, u32[]{:S(2)}) collective-permute-start(f32[4,192,128]{2,1,0:T(8,128)S(1)} %get-tuple-element.202), channel_id=1, source_target_pairs={{0,4},{1,3},{2,6},{3,1},{4,0},{5,7},{6,2},{7,5},{8,12},{9,11},{10,... | collective-permute-start | bytes 1179656 | tf_op jit(solution)/shard_map/ppermute | solution.py:346
  154.9 12.0 %collective-permute-start.14 = (f32[1,384,128]{2,1,0:T(8,128)S(1)}, f32[1,384,128]{2,1,0:T(8,128)S(1)}, u32[]{:S(2)}, u32[]{:S(2)}) collective-permute-start(f32[1,384,128]{2,1,0:T(8,128)S(1)} %fusion), channel_id=1, source_target_pairs={{0,16},{1,17},{2,18},{3,19},{4,20},{5,21},{6,22},{7,23},{8,24},{9,... | collective-permute-start | bytes 589832 | tf_op jit(solution)/shard_map/ppermute | solution.py:346
  155.6 25.9 %collective-permute-start.15 = (f32[8,200,128]{2,1,0:T(8,128)}, f32[8,200,128]{2,1,0:T(8,128)S(1)}, u32[]{:S(2)}, u32[]{:S(2)}) collective-permute-start(f32[8,200,128]{2,1,0:T(8,128)} %get-tuple-element.145), channel_id=1, source_target_pairs={{0,1},{1,0},{2,3},{3,2},{4,5},{5,4},{6,7},{7,6},{8,9},{9,8},{10,11... | collective-permute-start | bytes 2457608 | tf_op jit(solution)/shard_map/ppermute | solution.py:346
  167.0 14.3 %collective-permute-start.20 = (f32[2,384,128]{2,1,0:T(8,128)S(1)}, f32[2,384,128]{2,1,0:T(8,128)S(1)}, u32[]{:S(2)}, u32[]{:S(2)}) collective-permute-start(f32[2,384,128]{2,1,0:T(8,128)S(1)} %pad_maximum_fusion.6), channel_id=1, source_target_pairs={{0,8},{1,9},{2,10},{3,11},{4,12},{5,13},{6,14},{7,15},{8,0},{9,1},... | collective-permute-start | bytes 1179656 | tf_op jit(solution)/shard_map/ppermute | solution.py:346
  167.1 14.4 %collective-permute-start.22 = (f32[2,192,128]{2,1,0:T(8,128)S(1)}, f32[2,192,128]{2,1,0:T(8,128)S(1)}, u32[]{:S(2)}, u32[]{:S(2)}) collective-permute-start(f32[2,192,128]{2,1,0:T(8,128)S(1)} %get-tuple-element.210), channel_id=1, source_target_pairs={{0,8},{1,9},{2,10},{3,11},{4,12},{5,13},{6,14},{7,15},{8,0},{9,1},... | collective-permute-start | bytes 589832 | tf_op jit(solution)/shard_map/ppermute | solution.py:346
  169.3 13.3 %collective-permute-start.17 = (f32[8,200,128]{2,1,0:T(8,128)S(1)}, f32[8,200,128]{2,1,0:T(8,128)S(1)}, u32[]{:S(2)}, u32[]{:S(2)}) collective-permute-start(f32[8,200,128]{2,1,0:T(8,128)S(1)} %multiply_add_fusion.4), channel_id=1, source_target_pairs={{0,2},{1,5},{2,0},{3,7},{4,6},{5,1},{6,4},{7,3},{8,10},{9,13},{10,... | collective-permute-start | bytes 2457608 | tf_op jit(solution)/shard_map/ppermute | solution.py:346
  181.3 1.1 copy-start.4
  181.3 2.6 collective-permute-start.19
  182.5 1.4 copy-start.3
  182.6 11.5 %collective-permute-start.21 = (f32[4,200,128]{2,1,0:T(8,128)S(1)}, f32[4,200,128]{2,1,0:T(8,128)S(1)}, u32[]{:S(2)}, u32[]{:S(2)}) collective-permute-start(f32[4,200,128]{2,1,0:T(8,128)S(1)} %get-tuple-element.200), channel_id=1, source_target_pairs={{0,4},{1,3},{2,6},{3,1},{4,0},{5,7},{6,2},{7,5},{8,12},{9,11},{10,... | collective-permute-start | bytes 1228808 | tf_op jit(solution)/shard_map/ppermute | solution.py:346
  194.2 15.1 %collective-permute-start.24 = (f32[4,384,128]{2,1,0:T(8,128)S(1)}, f32[4,384,128]{2,1,0:T(8,128)S(1)}, u32[]{:S(2)}, u32[]{:S(2)}) collective-permute-start(f32[4,384,128]{2,1,0:T(8,128)S(1)} %pad_maximum_fusion.2), channel_id=1, source_target_pairs={{0,4},{1,3},{2,6},{3,1},{4,0},{5,7},{6,2},{7,5},{8,12},{9,11},{10,... | collective-permute-start | bytes 2359304 | tf_op jit(solution)/shard_map/ppermute | solution.py:346
  195.2 7.0 %collective-permute-start.25 = (f32[1,192,128]{2,1,0:T(8,128)S(1)}, f32[1,192,128]{2,1,0:T(8,128)S(1)}, u32[]{:S(2)}, u32[]{:S(2)}) collective-permute-start(f32[1,192,128]{2,1,0:T(8,128)S(1)} %slice_add_fusion.23), channel_id=1, source_target_pairs={{0,16},{1,17},{2,18},{3,19},{4,20},{5,21},{6,22},{7,23},{8,24},{9,... | collective-permute-start | bytes 294920 | tf_op jit(solution)/shard_map/ppermute | solution.py:346
  202.2 7.1 %collective-permute-start.26 = (f32[1,192,128]{2,1,0:T(8,128)S(1)}, f32[1,192,128]{2,1,0:T(8,128)S(1)}, u32[]{:S(2)}, u32[]{:S(2)}) collective-permute-start(f32[1,192,128]{2,1,0:T(8,128)S(1)} %fusion.3), channel_id=1, source_target_pairs={{0,16},{1,17},{2,18},{3,19},{4,20},{5,21},{6,22},{7,23},{8,24},{9,... | collective-permute-start | bytes 294920 | tf_op jit(solution)/shard_map/ppermute | solution.py:346
  209.3 8.1 %copy-start.8 = (f32[8,208,128]{2,1,0:T(8,128)S(1)}, f32[8,208,128]{2,1,0:T(8,128)}, u32[]{:S(2)}) copy-start(f32[8,208,128]{2,1,0:T(8,128)} %get-tuple-element.154) | copy-start | bytes 2555908
  209.5 27.6 %copy-start.2 = (f32[8,208,128]{2,1,0:T(8,128)S(1)}, f32[8,208,128]{2,1,0:T(8,128)}, u32[]{:S(2)}) copy-start(f32[8,208,128]{2,1,0:T(8,128)} %get-tuple-element.153) | copy-start | bytes 2555908
  209.5 20.5 %collective-permute-start.27 = (f32[8,384,128]{2,1,0:T(8,128)S(1)}, f32[8,384,128]{2,1,0:T(8,128)S(1)}, u32[]{:S(2)}, u32[]{:S(2)}) collective-permute-start(f32[8,384,128]{2,1,0:T(8,128)S(1)} %pad_maximum_fusion.refs_0_), channel_id=1, source_target_pairs={{0,2},{1,5},{2,0},{3,7},{4,6},{5,1},{6,4},{7,3},{8,10},{9,13},{10,... | collective-permute-start | bytes 4718600 | tf_op jit(solution)/shard_map/ppermute | solution.py:346
  210.8 5.8 %collective-permute-start.29 = (f32[2,200,128]{2,1,0:T(8,128)S(1)}, f32[2,200,128]{2,1,0:T(8,128)S(1)}, u32[]{:S(2)}, u32[]{:S(2)}) collective-permute-start(f32[2,200,128]{2,1,0:T(8,128)S(1)} %get-tuple-element.159), channel_id=1, source_target_pairs={{0,8},{1,9},{2,10},{3,11},{4,12},{5,13},{6,14},{7,15},{8,0},{9,1},... | collective-permute-start | bytes 614408 | tf_op jit(solution)/shard_map/ppermute | solution.py:346
  216.6 6.6 %collective-permute-start.30 = (f32[1,200,128]{2,1,0:T(8,128)S(1)}, f32[1,200,128]{2,1,0:T(8,128)S(1)}, u32[]{:S(2)}, u32[]{:S(2)}) collective-permute-start(f32[1,200,128]{2,1,0:T(8,128)S(1)} %slice_add_fusion.20), channel_id=1, source_target_pairs={{0,16},{1,17},{2,18},{3,19},{4,20},{5,21},{6,22},{7,23},{8,24},{9,... | collective-permute-start | bytes 307208 | tf_op jit(solution)/shard_map/ppermute | solution.py:346
  217.4 19.6 %collective-permute-start.23 = (f32[8,208,128]{2,1,0:T(8,128)S(1)}, f32[8,208,128]{2,1,0:T(8,128)S(1)}, u32[]{:S(2)}, u32[]{:S(2)}) collective-permute-start(f32[8,208,128]{2,1,0:T(8,128)S(1)} %copy-done.8), channel_id=1, source_target_pairs={{0,1},{1,0},{2,3},{3,2},{4,5},{5,4},{6,7},{7,6},{8,9},{9,8},{10,11... | collective-permute-start | bytes 2555912 | tf_op jit(solution)/shard_map/ppermute | solution.py:346
  217.4 8.4 %collective-permute-start.28 = (f32[2,192,128]{2,1,0:T(8,128)S(1)}, f32[2,192,128]{2,1,0:T(8,128)S(1)}, u32[]{:S(2)}, u32[]{:S(2)}) collective-permute-start(f32[2,192,128]{2,1,0:T(8,128)S(1)} %pad_maximum_fusion.10), channel_id=1, source_target_pairs={{0,8},{1,9},{2,10},{3,11},{4,12},{5,13},{6,14},{7,15},{8,0},{9,1},... | collective-permute-start | bytes 589832 | tf_op jit(solution)/shard_map/ppermute | solution.py:346
  230.0 12.9 %collective-permute-start.31 = (f32[8,208,128]{2,1,0:T(8,128)S(1)}, f32[8,208,128]{2,1,0:T(8,128)S(1)}, u32[]{:S(2)}, u32[]{:S(2)}) collective-permute-start(f32[8,208,128]{2,1,0:T(8,128)S(1)} %multiply_add_fusion.3), channel_id=1, source_target_pairs={{0,2},{1,5},{2,0},{3,7},{4,6},{5,1},{6,4},{7,3},{8,10},{9,13},{10,... | collective-permute-start | bytes 2555912 | tf_op jit(solution)/shard_map/ppermute | solution.py:346
  231.2 5.7 %collective-permute-start.32 = (f32[1,200,128]{2,1,0:T(8,128)S(1)}, f32[1,200,128]{2,1,0:T(8,128)S(1)}, u32[]{:S(2)}, u32[]{:S(2)}) collective-permute-start(f32[1,200,128]{2,1,0:T(8,128)S(1)} %fusion.2), channel_id=1, source_target_pairs={{0,16},{1,17},{2,18},{3,19},{4,20},{5,21},{6,22},{7,23},{8,24},{9,... | collective-permute-start | bytes 307208 | tf_op jit(solution)/shard_map/ppermute | solution.py:346
  237.0 5.8 %collective-permute-start.33 = (f32[2,200,128]{2,1,0:T(8,128)S(1)}, f32[2,200,128]{2,1,0:T(8,128)S(1)}, u32[]{:S(2)}, u32[]{:S(2)}) collective-permute-start(f32[2,200,128]{2,1,0:T(8,128)S(1)} %pad_maximum_fusion.9), channel_id=1, source_target_pairs={{0,8},{1,9},{2,10},{3,11},{4,12},{5,13},{6,14},{7,15},{8,0},{9,1},... | collective-permute-start | bytes 614408 | tf_op jit(solution)/shard_map/ppermute | solution.py:346
  242.9 8.5 %collective-permute-start.34 = (f32[4,208,128]{2,1,0:T(8,128)S(1)}, f32[4,208,128]{2,1,0:T(8,128)S(1)}, u32[]{:S(2)}, u32[]{:S(2)}) collective-permute-start(f32[4,208,128]{2,1,0:T(8,128)S(1)} %get-tuple-element.163), channel_id=1, source_target_pairs={{0,4},{1,3},{2,6},{3,1},{4,0},{5,7},{6,2},{7,5},{8,12},{9,11},{10,... | collective-permute-start | bytes 1277960 | tf_op jit(solution)/shard_map/ppermute | solution.py:346
  251.4 5.9 %collective-permute-start.35 = (f32[2,208,128]{2,1,0:T(8,128)S(1)}, f32[2,208,128]{2,1,0:T(8,128)S(1)}, u32[]{:S(2)}, u32[]{:S(2)}) collective-permute-start(f32[2,208,128]{2,1,0:T(8,128)S(1)} %get-tuple-element.165), channel_id=1, source_target_pairs={{0,8},{1,9},{2,10},{3,11},{4,12},{5,13},{6,14},{7,15},{8,0},{9,1},... | collective-permute-start | bytes 638984 | tf_op jit(solution)/shard_map/ppermute | solution.py:346
  251.8 7.8 %collective-permute-start.36 = (f32[4,192,128]{2,1,0:T(8,128)S(1)}, f32[4,192,128]{2,1,0:T(8,128)S(1)}, u32[]{:S(2)}, u32[]{:S(2)}) collective-permute-start(f32[4,192,128]{2,1,0:T(8,128)S(1)} %pad_maximum_fusion.7), channel_id=1, source_target_pairs={{0,4},{1,3},{2,6},{3,1},{4,0},{5,7},{6,2},{7,5},{8,12},{9,11},{10,... | collective-permute-start | bytes 1179656 | tf_op jit(solution)/shard_map/ppermute | solution.py:346
  259.6 12.7 %collective-permute-start.39 = (f32[8,192,128]{2,1,0:T(8,128)S(1)}, f32[8,192,128]{2,1,0:T(8,128)S(1)}, u32[]{:S(2)}, u32[]{:S(2)}) collective-permute-start(f32[8,192,128]{2,1,0:T(8,128)S(1)} %pad_maximum_fusion.3.refs_0_), channel_id=1, source_target_pairs={{0,2},{1,5},{2,0},{3,7},{4,6},{5,1},{6,4},{7,3},{8,10},{9,13},{10,... | collective-permute-start | bytes 2359304 | tf_op jit(solution)/shard_map/ppermute | solution.py:346
  261.0 5.6 %collective-permute-start.37 = (f32[1,208,128]{2,1,0:T(8,128)S(1)}, f32[1,208,128]{2,1,0:T(8,128)S(1)}, u32[]{:S(2)}, u32[]{:S(2)}) collective-permute-start(f32[1,208,128]{2,1,0:T(8,128)S(1)} %slice_add_fusion.18), channel_id=1, source_target_pairs={{0,16},{1,17},{2,18},{3,19},{4,20},{5,21},{6,22},{7,23},{8,24},{9,... | collective-permute-start | bytes 319496 | tf_op jit(solution)/shard_map/ppermute | solution.py:346
  266.6 5.7 %collective-permute-start.38 = (f32[1,208,128]{2,1,0:T(8,128)S(1)}, f32[1,208,128]{2,1,0:T(8,128)S(1)}, u32[]{:S(2)}, u32[]{:S(2)}) collective-permute-start(f32[1,208,128]{2,1,0:T(8,128)S(1)} %fusion.1), channel_id=1, source_target_pairs={{0,16},{1,17},{2,18},{3,19},{4,20},{5,21},{6,22},{7,23},{8,24},{9,... | collective-permute-start | bytes 319496 | tf_op jit(solution)/shard_map/ppermute | solution.py:346
  272.3 15.6 %collective-permute-start.41 = (f32[4,200,128]{2,1,0:T(8,128)S(1)}, f32[4,200,128]{2,1,0:T(8,128)S(1)}, u32[]{:S(2)}, u32[]{:S(2)}) collective-permute-start(f32[4,200,128]{2,1,0:T(8,128)S(1)} %pad_maximum_fusion.5), channel_id=1, source_target_pairs={{0,4},{1,3},{2,6},{3,1},{4,0},{5,7},{6,2},{7,5},{8,12},{9,11},{10,... | collective-permute-start | bytes 1228808 | tf_op jit(solution)/shard_map/ppermute | solution.py:346
  277.9 5.8 %collective-permute-start.40 = (f32[2,208,128]{2,1,0:T(8,128)S(1)}, f32[2,208,128]{2,1,0:T(8,128)S(1)}, u32[]{:S(2)}, u32[]{:S(2)}) collective-permute-start(f32[2,208,128]{2,1,0:T(8,128)S(1)} %pad_maximum_fusion.8), channel_id=1, source_target_pairs={{0,8},{1,9},{2,10},{3,11},{4,12},{5,13},{6,14},{7,15},{8,0},{9,1},... | collective-permute-start | bytes 638984 | tf_op jit(solution)/shard_map/ppermute | solution.py:346
  283.7 47.9 %copy-start = (s32[2]{0:T(128)S(1)}, s32[2]{0:T(128)}, u32[]{:S(2)}) copy-start(s32[2]{0:T(128)} %pad_add_fusion.code_ref) | copy-start | bytes 28
  288.0 17.0 %collective-permute-start.42 = (f32[8,200,128]{2,1,0:T(8,128)S(1)}, f32[8,200,128]{2,1,0:T(8,128)S(1)}, u32[]{:S(2)}, u32[]{:S(2)}) collective-permute-start(f32[8,200,128]{2,1,0:T(8,128)S(1)} %pad_maximum_fusion.1.refs_0_), channel_id=1, source_target_pairs={{0,2},{1,5},{2,0},{3,7},{4,6},{5,1},{6,4},{7,3},{8,10},{9,13},{10,... | collective-permute-start | bytes 2457608 | tf_op jit(solution)/shard_map/ppermute | solution.py:346
  288.0 42.6 %collective-permute-start.51 = (f32[8,384,128]{2,1,0:T(8,128)S(1)}, f32[8,384,128]{2,1,0:T(8,128)S(1)}, u32[]{:S(2)}, u32[]{:S(2)}) collective-permute-start(f32[8,384,128]{2,1,0:T(8,128)S(1)} %pad_maximum_fusion.refs_0_), channel_id=1, source_target_pairs={{0,1},{1,0},{2,3},{3,2},{4,5},{5,4},{6,7},{7,6},{8,9},{9,8},{10,11... | collective-permute-start | bytes 4718600 | tf_op jit(solution)/shard_map/ppermute | solution.py:346
  288.1 43.0 %collective-permute-start.52 = (f32[8,384,128]{2,1,0:T(8,128)S(1)}, f32[8,384,128]{2,1,0:T(8,128)S(1)}, u32[]{:S(2)}, u32[]{:S(2)}) collective-permute-start(f32[8,384,128]{2,1,0:T(8,128)S(1)} %collective-permute-done.27.refs_1_), channel_id=1, source_target_pairs={{0,1},{1,0},{2,3},{3,2},{4,5},{5,4},{6,7},{7,6},{8,9},{9,8},{10,11... | collective-permute-start | bytes 4718600 | tf_op jit(solution)/shard_map/ppermute | solution.py:346
  304.9 12.9 %collective-permute-start.45 = (f32[4,208,128]{2,1,0:T(8,128)S(1)}, f32[4,208,128]{2,1,0:T(8,128)S(1)}, u32[]{:S(2)}, u32[]{:S(2)}) collective-permute-start(f32[4,208,128]{2,1,0:T(8,128)S(1)} %pad_maximum_fusion.4), channel_id=1, source_target_pairs={{0,4},{1,3},{2,6},{3,1},{4,0},{5,7},{6,2},{7,5},{8,12},{9,11},{10,... | collective-permute-start | bytes 1277960 | tf_op jit(solution)/shard_map/ppermute | solution.py:346
  317.9 12.8 %collective-permute-start.46 = (f32[8,208,128]{2,1,0:T(8,128)S(1)}, f32[8,208,128]{2,1,0:T(8,128)S(1)}, u32[]{:S(2)}, u32[]{:S(2)}) collective-permute-start(f32[8,208,128]{2,1,0:T(8,128)S(1)} %constant_dynamic-update-slice_fusion.refs_0_), channel_id=1, source_target_pairs={{0,2},{1,5},{2,0},{3,7},{4,6},{5,1},{6,4},{7,3},{8,10},{9,13},{10,... | collective-permute-start | bytes 2555912 | tf_op jit(solution)/shard_map/ppermute | solution.py:346
  317.9 13.3 %collective-permute-start.49 = (f32[8,192,128]{2,1,0:T(8,128)S(1)}, f32[8,192,128]{2,1,0:T(8,128)S(1)}, u32[]{:S(2)}, u32[]{:S(2)}) collective-permute-start(f32[8,192,128]{2,1,0:T(8,128)S(1)} %pad_maximum_fusion.3.refs_0_), channel_id=1, source_target_pairs={{0,1},{1,0},{2,3},{3,2},{4,5},{5,4},{6,7},{7,6},{8,9},{9,8},{10,11... | collective-permute-start | bytes 2359304 | tf_op jit(solution)/shard_map/ppermute | solution.py:346
  318.0 24.0 %collective-permute-start.47 = (f32[8,208,128]{2,1,0:T(8,128)S(1)}, f32[8,208,128]{2,1,0:T(8,128)S(1)}, u32[]{:S(2)}, u32[]{:S(2)}) collective-permute-start(f32[8,208,128]{2,1,0:T(8,128)S(1)} %constant_dynamic-update-slice_fusion.refs_0_), channel_id=1, source_target_pairs={{0,1},{1,0},{2,3},{3,2},{4,5},{5,4},{6,7},{7,6},{8,9},{9,8},{10,11... | collective-permute-start | bytes 2555912 | tf_op jit(solution)/shard_map/ppermute | solution.py:346
  330.6 11.4 %collective-permute-start.48 = (f32[8,208,128]{2,1,0:T(8,128)S(1)}, f32[8,208,128]{2,1,0:T(8,128)S(1)}, u32[]{:S(2)}, u32[]{:S(2)}) collective-permute-start(f32[8,208,128]{2,1,0:T(8,128)S(1)} %collective-permute-done.46.refs_1_), channel_id=1, source_target_pairs={{0,1},{1,0},{2,3},{3,2},{4,5},{5,4},{6,7},{7,6},{8,9},{9,8},{10,11... | collective-permute-start | bytes 2555912 | tf_op jit(solution)/shard_map/ppermute | solution.py:346
  330.6 8.6 %collective-permute-start.43 = (f32[8,200,128]{2,1,0:T(8,128)S(1)}, f32[8,200,128]{2,1,0:T(8,128)S(1)}, u32[]{:S(2)}, u32[]{:S(2)}) collective-permute-start(f32[8,200,128]{2,1,0:T(8,128)S(1)} %pad_maximum_fusion.1.refs_0_), channel_id=1, source_target_pairs={{0,1},{1,0},{2,3},{3,2},{4,5},{5,4},{6,7},{7,6},{8,9},{9,8},{10,11... | collective-permute-start | bytes 2457608 | tf_op jit(solution)/shard_map/ppermute | solution.py:346
  331.1 8.1 %collective-permute-start.44 = (f32[8,200,128]{2,1,0:T(8,128)S(1)}, f32[8,200,128]{2,1,0:T(8,128)S(1)}, u32[]{:S(2)}, u32[]{:S(2)}) collective-permute-start(f32[8,200,128]{2,1,0:T(8,128)S(1)} %collective-permute-done.42.refs_1_), channel_id=1, source_target_pairs={{0,1},{1,0},{2,3},{3,2},{4,5},{5,4},{6,7},{7,6},{8,9},{9,8},{10,11... | collective-permute-start | bytes 2457608 | tf_op jit(solution)/shard_map/ppermute | solution.py:346
  331.2 5.3 %collective-permute-start.50 = (f32[8,192,128]{2,1,0:T(8,128)S(1)}, f32[8,192,128]{2,1,0:T(8,128)S(1)}, u32[]{:S(2)}, u32[]{:S(2)}) collective-permute-start(f32[8,192,128]{2,1,0:T(8,128)S(1)} %collective-permute-done.39.refs_1_), channel_id=1, source_target_pairs={{0,1},{1,0},{2,3},{3,2},{4,5},{5,4},{6,7},{7,6},{8,9},{9,8},{10,11... | collective-permute-start | bytes 2359304 | tf_op jit(solution)/shard_map/ppermute | solution.py:346

commit v2 on v0

--- a/solution.py
+++ b/solution.py
@@ -91,9 +91,16 @@
     return pl.ds(offset + index * PAIR, PAIR)
 
 
-def features_kernel(patch_ref, weight_ref, bias_ref, wk_ref, wv_ref, feat_ref, kv_ref, joined):
+def features_kernel(
+    me_ref, len_ref, member_ref, patch_ref, weight_ref, bias_ref, wk_ref, wv_ref,
+    feat_ref, kv_ref, count_ref, joined,
+):
     @pl.when(pl.program_id(0) == 0)
     def join():
+        count = sum(len_ref[s] for s in range(len_ref.shape[0])).astype(F32)
+        in_first = member_ref[me_ref[0]] == 1
+        count_ref[0] = jnp.where(in_first, count, 0.0)
+        count_ref[1] = jnp.where(in_first, 0.0, count)
         joined[:, :INNER] = wk_ref[...]
         joined[:, INNER:] = wv_ref[...]
 
@@ -164,10 +171,19 @@
         ref[...] += value
 
 
+def gelu_parts(gate):
+    slant = 0.7978845608028654
+    square = gate * gate
+    tanh = jnp.tanh(gate * (slant + (slant * 0.044715) * square))
+    half = 0.5 + 0.5 * tanh
+    slope = half + (0.5 * gate) * (1.0 - tanh * tanh) * (slant + (3.0 * slant * 0.044715) * square)
+    return gate * half, slope
+
+
 def feed_forward_kernel(
     len_ref, code_ref, x2_ref, cot_ref, g3_ref, wg_ref, wu_ref, wd_ref,
-    out_ref, dx2_ref, gain_ref, keep_ref, send_ref,
-    hid, dgate, dup, acc_down, acc_gate, acc_up, *, maxlen,
+    hid_ref, dgate_ref, dup_ref, keep_low, keep_high, send_low, send_high,
+    h3_all, de_all, hid_all, dgate_all, dup_all, acc_down, acc_gate, acc_up, *, maxlen,
 ):
     step, steps = pl.program_id(0), pl.num_programs(0)
     x2 = x2_ref[...]
@@ -178,8 +194,10 @@
     keep = jnp.concatenate(
         [jnp.where(at < len_ref[step * seqs + s], 1.0, 0.0) for s in range(seqs)], axis=0
     )
-    e = cot_ref[...].astype(F32) * keep
-    de = e.astype(BF16)
+    de = (cot_ref[...].astype(F32) * keep).astype(BF16)
+    here = pl.ds(pl.multiple_of(step * rows, rows), rows)
+    h3_all[here, :] = h3
+    de_all[here, :] = de
     wide = wg_ref.shape[1]
     chunk = 256
     for c in range(wide // chunk):
@@ -187,38 +205,58 @@
         gate = dot_plain(h3, wg_ref[:, cols])
         up = dot_plain(h3, wu_ref[:, cols])
         grad = dot_back(de, wd_ref[cols, :])
-        square = gate * gate
-        tanh = jnp.tanh(gate * (0.7978845608028654 + (0.7978845608028654 * 0.044715) * square))
-        half = 0.5 * (1.0 + tanh)
-        gelu = gate * half
-        slope = half + (0.5 * gate) * (1.0 - tanh * tanh) * (
-            0.7978845608028654 + (3.0 * 0.7978845608028654 * 0.044715) * square
-        )
-        hid[:, cols] = (gelu * up).astype(BF16)
-        dgate[:, cols] = (grad * up * slope).astype(BF16)
-        dup[:, cols] = (grad * gelu).astype(BF16)
-    out_ref[...] = (x2 + dot_plain(hid[...], wd_ref[...])).astype(BF16)
-    dh3 = dot_back(dgate[...], wg_ref[...]) + dot_back(dup[...], wu_ref[...])
-    dx, gain = norm_backward(x2, g3_ref[...], dh3)
-    dx2_ref[...] = e + dx
-    add_to(gain_ref, step == 0, gain)
-    add_to(acc_down, step == 0, dot_rows(hid[...], de))
-    add_to(acc_gate, step == 0, dot_rows(h3, dgate[...]))
-    add_to(acc_up, step == 0, dot_rows(h3, dup[...]))
+        gelu, slope = gelu_parts(gate)
+        hid = (gelu * up).astype(BF16)
+        dgate = (grad * up * slope).astype(BF16)
+        dup = (grad * gelu).astype(BF16)
+        hid_ref[:, cols], hid_all[here, cols] = hid, hid
+        dgate_ref[:, cols], dgate_all[here, cols] = dgate, dgate
+        dup_ref[:, cols], dup_all[here, cols] = dup, dup
 
     @pl.when(step == steps - 1)
     def finish():
+        for c in range(wide // chunk):
+            cols = pl.ds(c * chunk, chunk)
+            acc_down[cols, :] = dot_rows(hid_all[:, cols], de_all[...])
+            acc_gate[:, cols] = dot_rows(h3_all[...], dgate_all[:, cols])
+            acc_up[:, cols] = dot_rows(h3_all[...], dup_all[:, cols])
         items = [(acc_down, acc_down.shape, 0), (acc_gate, acc_gate.shape, 0), (acc_up, acc_up.shape, 0)]
-        pack(items, code_ref, keep_ref, send_ref)
+        pack(items, code_ref, keep_low, keep_high, send_low, send_high)
+
+
+def feed_back_kernel(
+    me_ref, len_ref, member_ref, mix_ref, count_ref,
+    x2_ref, cot_ref, hid_ref, dgate_ref, dup_ref, g3_ref, wg_ref, wu_ref, wd_ref,
+    out_ref, dx2_ref, gain_ref, weight_ref, *, maxlen,
+):
+    step = pl.program_id(0)
+
+    @pl.when(step == 0)
+    def weigh():
+        total = count_ref[0] + count_ref[1]
+        first = mix_ref[0] * total / count_ref[0]
+        second = mix_ref[1] * total / count_ref[1]
+        weight_ref[0] = jnp.where(member_ref[me_ref[0]] == 1, first, second)
+        weight_ref[1] = jnp.where(member_ref[me_ref[0] ^ 1] == 1, first, second)
+
+    x2 = x2_ref[...]
+    seqs = x2.shape[0] // maxlen
+    at = lax.broadcasted_iota(jnp.int32, (maxlen, 1), 0)
+    keep = jnp.concatenate(
+        [jnp.where(at < len_ref[step * seqs + s], 1.0, 0.0) for s in range(seqs)], axis=0
+    )
+    out_ref[...] = (x2 + dot_plain(hid_ref[...], wd_ref[...])).astype(BF16)
+    dh3 = dot_back(dgate_ref[...], wg_ref[...]) + dot_back(dup_ref[...], wu_ref[...])
+    dx, gain = norm_backward(x2, g3_ref[...], dh3)
+    dx2_ref[...] = cot_ref[...].astype(F32) * keep + dx
+    add_to(gain_ref, step == 0, gain)
 
 
 def cross_backward_kernel(
-    code_ref, dx2_ref, oc_ref, cq_ref, pt_ref, kv_ref, h2_ref, feat_ref, x1_ref, g2_ref,
-    wco_ref, wcq_ref, wck_ref, wcv_ref,
-    dfeat_ref, dx1_ref, gain_ref, bias_ref, keep_ref, send_ref,
-    joined, dcq, dkv, acc_out, acc_query, acc_kv,
+    dx2_ref, cq_ref, pt_ref, kv_ref, x1_ref, g2_ref, wco_ref, wcq_ref, wck_ref, wcv_ref,
+    dcq_ref, dkv_ref, dfeat_ref, dx1_ref, dc_ref, gain_ref, bias_ref, joined,
 ):
-    step, steps = pl.program_id(0), pl.num_programs(0)
+    step = pl.program_id(0)
 
     @pl.when(step == 0)
     def join():
@@ -229,58 +267,59 @@
     patches = both // 2
     dx2 = dx2_ref[...]
     dc = dx2.astype(BF16)
+    dc_ref[...] = dc
     doc = dot_back(dc, wco_ref[...]).astype(BF16)
     for s in range(seqs):
         rows, wide = pl.ds(s * maxlen, maxlen), pl.ds(s * patches, patches)
         for p in range(PAIRS):
-            dcq[rows, pair_lanes(p)], dkv[wide, pair_lanes(p)], dkv[wide, pair_lanes(p, INNER)] = (
-                pair_backward(
-                    cq_ref[rows, pair_lanes(p)],
-                    kv_ref[wide, pair_lanes(p)],
-                    kv_ref[wide, pair_lanes(p, INNER)],
-                    pt_ref[s, p],
-                    doc[s * maxlen : (s + 1) * maxlen, p * PAIR : (p + 1) * PAIR],
-                )
+            keys, values = pair_lanes(p), pair_lanes(p, INNER)
+            dcq_ref[rows, keys], dkv_ref[wide, keys], dkv_ref[wide, values] = pair_backward(
+                cq_ref[rows, keys],
+                kv_ref[wide, keys],
+                kv_ref[wide, values],
+                pt_ref[s, p],
+                doc[s * maxlen : (s + 1) * maxlen, p * PAIR : (p + 1) * PAIR],
             )
-    dh2 = dot_back(dcq[...], wcq_ref[...])
-    dfeat = dot_back(dkv[...], joined[...]).astype(BF16)
+    dfeat = dot_back(dkv_ref[...], joined[...]).astype(BF16)
     dfeat_ref[...] = dfeat
+    dh2 = dot_back(dcq_ref[...], wcq_ref[...])
     dx, gain = norm_backward(x1_ref[...], g2_ref[...], dh2)
     dx1_ref[...] = dx2 + dx
     add_to(gain_ref, step == 0, gain)
     add_to(bias_ref, step == 0, jnp.sum(dfeat.astype(F32), axis=0, keepdims=True))
-    add_to(acc_out, step == 0, dot_rows(oc_ref[...], dc))
-    add_to(acc_query, step == 0, dot_rows(h2_ref[...], dcq[...]))
-    add_to(acc_kv, step == 0, dot_rows(feat_ref[...], dkv[...]))
-
-    @pl.when(step == steps - 1)
-    def finish():
-        small = acc_query.shape
-        items = [(acc_out, acc_out.shape, 0), (acc_query, small, 0), (acc_kv, small, 0), (acc_kv, small, INNER)]
-        pack(items, code_ref, keep_ref, send_ref)
-
-
-def patch_weight_kernel(code_ref, patch_ref, dfeat_ref, keep_ref, send_ref, acc, turned):
+
+
+def cross_weights_kernel(
+    code_ref, oc_ref, dc_ref, h2_ref, dcq_ref, feat_ref, dkv_ref,
+    keep_low, keep_high, send_low, send_high, acc_out, acc_query, acc_kv,
+):
+    acc_out[...] = dot_rows(oc_ref[...], dc_ref[...])
+    acc_query[...] = dot_rows(h2_ref[...], dcq_ref[...])
+    acc_kv[...] = dot_rows(feat_ref[...], dkv_ref[...])
+    small = acc_query.shape
+    items = [(acc_out, acc_out.shape, 0), (acc_query, small, 0), (acc_kv, small, 0), (acc_kv, small, INNER)]
+    pack(items, code_ref, keep_low, keep_high, send_low, send_high)
+
+
+def patch_weight_kernel(code_ref, patch_ref, dfeat_ref, keep_low, keep_high, send_low, send_high, acc, turned):
     step, steps = pl.program_id(0), pl.num_programs(0)
     add_to(acc, step == 0, dot_rows(dfeat_ref[...], patch_ref[...]))
 
     @pl.when(step == steps - 1)
     def finish():
         turned[...] = acc[...].T
-        pack([(turned, turned.shape, 0)], code_ref, keep_ref, send_ref)
-
-
-def patch_input_kernel(weight_ref, dfeat_ref, w_ref, out_ref):
-    out_ref[...] = dot_back(dfeat_ref[...], w_ref[...]) * weight_ref[0]
+        pack([(turned, turned.shape, 0)], code_ref, keep_low, keep_high, send_low, send_high)
+
+
+def patch_input_kernel(weight_ref, dfeat_ref, w_ref, *refs):
+    refs[-1][...] = dot_back(dfeat_ref[...], w_ref[...]) * weight_ref[0]
 
 
 def self_backward_kernel(
-    code_ref, weight_ref, dx1_ref, o_ref, qkv_ref, pt_ref, h1_ref, tok_ref, g1_ref,
-    wo_ref, wq_ref, wk_ref, wv_ref, gain_two_ref, gain_three_ref, bias_ref,
-    dtok_ref, keep_ref, send_ref,
-    joined, dqkv, acc_out, acc_qkv, gain, gain_block,
+    weight_ref, dx1_ref, qkv_ref, pt_ref, tok_ref, g1_ref, wo_ref, wq_ref, wk_ref, wv_ref,
+    dqkv_ref, da_ref, dtok_ref, gain_ref, joined,
 ):
-    step, steps = pl.program_id(0), pl.num_programs(0)
+    step = pl.program_id(0)
 
     @pl.when(step == 0)
     def join():
@@ -291,36 +330,40 @@
     seqs, _, _, maxlen = pt_ref.shape
     dx1 = dx1_ref[...]
     da = dx1.astype(BF16)
+    da_ref[...] = da
     do = dot_back(da, wo_ref[...]).astype(BF16)
     for s in range(seqs):
         rows = pl.ds(s * maxlen, maxlen)
         for p in range(PAIRS):
             lanes = [pair_lanes(p, k * INNER) for k in range(3)]
-            dqkv[rows, lanes[0]], dqkv[rows, lanes[1]], dqkv[rows, lanes[2]] = pair_backward(
+            dqkv_ref[rows, lanes[0]], dqkv_ref[rows, lanes[1]], dqkv_ref[rows, lanes[2]] = pair_backward(
                 qkv_ref[rows, lanes[0]],
                 qkv_ref[rows, lanes[1]],
                 qkv_ref[rows, lanes[2]],
                 pt_ref[s, p],
                 do[s * maxlen : (s + 1) * maxlen, p * PAIR : (p + 1) * PAIR],
             )
-    dh1 = dot_back(dqkv[...], joined[...])
-    dx, grad_gain = norm_backward(tok_ref[...].astype(F32), g1_ref[...], dh1)
+    dh1 = dot_back(dqkv_ref[...], joined[...])
+    dx, gain = norm_backward(tok_ref[...].astype(F32), g1_ref[...], dh1)
     dtok_ref[...] = (dx1 + dx) * weight_ref[0]
-    add_to(gain, step == 0, grad_gain)
-    add_to(acc_out, step == 0, dot_rows(o_ref[...], da))
-    add_to(acc_qkv, step == 0, dot_rows(h1_ref[...], dqkv[...]))
-
-    @pl.when(step == steps - 1)
-    def finish():
-        gain_block[...] = jnp.zeros_like(gain_block)
-        for k, ref in enumerate((gain, gain_two_ref, gain_three_ref, bias_ref)):
-            for t in range(4):
-                gain_block[pl.ds((4 * k + t) * 8, 1), :] = ref[:, pl.ds(t * 128, 128)]
-        small = (acc_qkv.shape[0], INNER)
-        items = [(acc_out, acc_out.shape, 0)]
-        items += [(acc_qkv, small, k * INNER) for k in range(3)]
-        items += [(gain_block, gain_block.shape, 0)]
-        pack(items, code_ref, keep_ref, send_ref)
+    add_to(gain_ref, step == 0, gain)
+
+
+def self_weights_kernel(
+    code_ref, o_ref, da_ref, h1_ref, dqkv_ref, gain_one_ref, gain_two_ref, gain_three_ref, bias_ref,
+    keep_low, keep_high, send_low, send_high, acc_out, acc_qkv, gain_block,
+):
+    acc_out[...] = dot_rows(o_ref[...], da_ref[...])
+    acc_qkv[...] = dot_rows(h1_ref[...], dqkv_ref[...])
+    gain_block[...] = jnp.zeros_like(gain_block)
+    for k, ref in enumerate((gain_one_ref, gain_two_ref, gain_three_ref, bias_ref)):
+        for t in range(4):
+            gain_block[pl.ds((4 * k + t) * 8, 1), :] = ref[:, pl.ds(t * 128, 128)]
+    small = (acc_qkv.shape[0], INNER)
+    items = [(acc_out, acc_out.shape, 0)]
+    items += [(acc_qkv, small, k * INNER) for k in range(3)]
+    items += [(gain_block, gain_block.shape, 0)]
+    pack(items, code_ref, keep_low, keep_high, send_low, send_high)
 
 
 def flips(count, first, second):
@@ -366,17 +409,18 @@
     ]
 
 
-def pack(items, code_ref, keep_ref, send_ref):
+def pack(items, code_ref, *out_refs):
     def step(p, carry):
-        for code, out_ref in ((code_ref[0], keep_ref), (code_ref[1], send_ref)):
+        for k, out_ref in enumerate(out_refs):
             start = 0
+            index = (p + 8 * (k % 2)) ^ code_ref[k // 2]
             for ref, shape, offset in items:
-                for rows, lanes in block_parts(shape, p ^ code, offset):
+                for rows, lanes in block_parts(shape, index, offset):
                     out_ref[p, pl.ds(start, rows.size), :] = ref[rows, lanes]
                     start += rows.size
         return carry
 
-    lax.fori_loop(0, HALF, step, 0)
+    lax.fori_loop(0, 8, step, 0)
 
 
 def unpack_kernel(shapes, with_gains, code_ref, *refs):
@@ -419,30 +463,82 @@
     )(codes, *pieces)
 
 
-def sum_blocks(packed, own, other):
-    keep, send = packed
-    got = exchange(send, 1)
-    keep, got = keep * own, got * other
-    for first, second in ((2, 4), (4, 2), (8, 8), (16, 16)):
+def fence(values, *chunks):
+    values, state = lax.optimization_barrier((values, [(c.held, c.got) for c in chunks]))
+    for c, (held, got) in zip(chunks, state):
+        c.held, c.got = held, got
+    return values
+
+
+class Chunk:
+    def __init__(self, packed, shapes, codes, with_gains=False):
+        self.held, self.got = tuple(packed), ()
+        self.shapes, self.codes, self.with_gains = shapes, codes, with_gains
+
+    def send_cores(self):
+        _, _, low, high = self.held
+        self.got = (exchange(high, 1), exchange(low, 1))
+
+    def take_cores(self, weights):
+        keep_low, keep_high, _, _ = self.held
+        high, low = self.got
+        self.held = (keep_high * weights[0] + high * weights[1], keep_low)
+        self.got, self.weights = (low,), weights
+
+    def send_first(self):
+        self.got += (exchange(self.held[0], 2, 4),)
+
+    def take_first(self):
+        (_, keep), (low, got), weights = self.held, self.got, self.weights
+        keep = keep * weights[0] + low * weights[1]
+        self.held, self.got = (keep[4:] + got[4:], keep[:4] + got[:4]), ()
+
+    def send(self, first, second=None):
+        self.got = (exchange(self.held[0], first, second),)
+
+    def take(self):
+        (_, keep), (got,) = self.held, self.got
         half = keep.shape[0] // 2
-        send, keep = keep[half:] + got[half:], keep[:half] + got[:half]
-        got = exchange(send, first, second)
-    keep = keep + got
-    extra = BLOCKS
-    while extra < lax.axis_size("dp"):
-        keep = keep + exchange(keep, extra)
-        extra *= 2
-    return keep
-
-
-def spread_blocks(held):
-    held = jnp.concatenate([held, exchange(held, 16)])
-    held = jnp.concatenate([held, exchange(held, 8)])
-    held = jnp.concatenate([held, exchange(held, 4, 2)])
-    near = exchange(held, 1)
-    rest = exchange(held, 2, 4)
-    far = exchange(rest, 1)
-    return held, rest, near, far
+        self.held, self.got = (keep[half:] + got[half:], keep[:half] + got[:half]), ()
+
+    def send_second(self):
+        self.send(4, 2)
+
+    def send_third(self):
+        self.send(8)
+
+    def send_fourth(self):
+        self.send(16)
+
+    def take_fourth(self):
+        total = self.held[1] + self.got[0]
+        extra = BLOCKS
+        while extra < lax.axis_size("dp"):
+            total = total + exchange(total, extra)
+            extra *= 2
+        self.held, self.got = (total,), ()
+
+    def send_back_fourth(self):
+        self.send(16)
+
+    def send_back_third(self):
+        self.send(8)
+
+    def send_back_second(self):
+        self.send(4, 2)
+
+    def take_back(self):
+        self.held, self.got = (jnp.concatenate([*self.held, *self.got]),), ()
+
+    def send_back_first(self):
+        self.got = (exchange(self.held[0], 2, 4), exchange(self.held[0], 1))
+
+    def send_back_cores(self):
+        self.held = (self.held[0], *self.got)
+        self.got = (exchange(self.held[1], 1),)
+
+    def unpack(self):
+        return unpack(self.held + self.got, self.shapes, self.codes, self.with_gains)
 
 
 def by_step(array_shape, steps):
@@ -469,7 +565,10 @@
         grid=(steps,),
         out_shape=[jax.ShapeDtypeStruct(s, d) for s, d, _ in outs],
         in_specs=in_specs,
-        out_specs=[by_step(s, steps) if moves else whole(s) for s, _, moves in outs],
+        out_specs=[
+            SCALARS if moves is None else by_step(s, steps) if moves else whole(s)
+            for s, _, moves in outs
+        ],
         scratch_shapes=[VMEM(s, d) for s, d in scratch],
         compiler_params=pltpu.CompilerParams(vmem_limit_bytes=56 * 2**20),
         cost_estimate=pl.CostEstimate(flops=int(cost * 1e9), bytes_accessed=2**20, transcendentals=0),
@@ -515,29 +614,19 @@
     )
 
     me = lax.axis_index("dp")
+    me_ref = me[None].astype(jnp.int32)
     codes = jnp.stack(code_pair(me))
-    members = lax.dynamic_slice_in_dim(group_member, me & ~1, 2)
-    in_first = lax.dynamic_index_in_dim(members, me & 1, keepdims=False) == 1
-    other_first = lax.dynamic_index_in_dim(members, 1 - (me & 1), keepdims=False) == 1
-    own_count = jnp.sum(lengths).astype(F32)
-    counts = own_count * jnp.where(in_first, jnp.array([1.0, 0.0], F32), jnp.array([0.0, 1.0], F32))
-    bit = 1
-    while bit < lax.axis_size("dp"):
-        counts = counts + exchange(counts, bit)
-        bit *= 2
-    group_weights = mix * jnp.sum(counts) / counts
-    weight_own = jnp.where(in_first, group_weights[0], group_weights[1])
-    weight_other = jnp.where(other_first, group_weights[0], group_weights[1])
-    weight_ref = weight_own[None]
-
-    feat, cross_kv = run(
-        features_kernel, "features", steps, [], [flat],
-        [w_patch, bias_patch, w_cross_key, w_cross_value], "rffff",
-        [((image_rows, width), BF16, True), ((image_rows, 2 * INNER), BF16, True)],
+    feat, cross_kv, counts = run(
+        features_kernel, "features", steps, [me_ref, lengths, group_member], [flat],
+        [w_patch, bias_patch, w_cross_key, w_cross_value], "sssrffff",
+        [((image_rows, width), BF16, True), ((image_rows, 2 * INNER), BF16, True), ((2,), F32, None)],
         [((width, 2 * INNER), BF16)], 5.1,
     )
+    counts = counts + exchange(counts, 1)
+    tokens_in, counts = lax.optimization_barrier((tokens, counts))
+    counts = counts + exchange(counts, 2)
     h1, qkv, chances, mixed, x1, h2, cross_q = run(
-        self_forward_kernel, "self_forward", steps, [lengths], [tokens],
+        self_forward_kernel, "self_forward", steps, [lengths], [tokens_in],
         [gain_one, w_query, w_key, w_value, w_out, gain_two, w_cross_query], "srfffffff",
         [
             ((rows, width), BF16, True),
@@ -550,8 +639,11 @@
         ],
         [((width, 3 * INNER), BF16), ((width, INNER), BF16)], 6.0,
     )
+    cross_q, counts = lax.optimization_barrier((cross_q, counts))
+    counts = counts + exchange(counts, 4)
     cross_chances, cross_mixed, x2 = run(
-        cross_forward_kernel, "cross_forward", steps, [], [cross_q, cross_kv, x1], [w_cross_out], "rrrf",
+        cross_forward_kernel, "cross_forward", steps, [], [cross_q, cross_kv, x1],
+        [w_cross_out], "rrrf",
         [
             ((seqs, PAIRS, 2 * images, maxlen), BF16, True),
             ((rows, INNER), BF16, True),
@@ -559,90 +651,194 @@
         ],
         [], 6.0,
     )
+    x2, counts = lax.optimization_barrier((x2, counts))
+    counts = counts + exchange(counts, 8) + exchange(counts, 16) + exchange(counts, 24)
+    bit = BLOCKS
+    while bit < lax.axis_size("dp"):
+        counts = counts + exchange(counts, bit)
+        bit *= 2
     late_shapes = [w_down.shape, w_gate.shape, w_up.shape]
     late_rows = sum(block_rows(s) for s in late_shapes)
-    result, dx2, gain3, *late = run(
+    hid, dgate, dup, *late = run(
         functools.partial(feed_forward_kernel, maxlen=maxlen), "feed_forward", steps,
         [lengths, codes], [x2, cotangent], [gain_three, w_gate, w_up, w_down], "ssrrffff",
+        [((rows, wide), BF16, True)] * 3 + [((8, late_rows, 128), F32, False)] * 4,
         [
-            ((rows, width), BF16, True),
-            ((rows, width), F32, True),
-            ((1, width), F32, False),
-            ((HALF, late_rows, 128), F32, False),
-            ((HALF, late_rows, 128), F32, False),
-        ],
-        [
-            ((part, wide), BF16),
-            ((part, wide), BF16),
-            ((part, wide), BF16),
+            ((rows, width), BF16),
+            ((rows, width), BF16),
+            ((rows, wide), BF16),
+            ((rows, wide), BF16),
+            ((rows, wide), BF16),
             (w_down.shape, F32),
             (w_gate.shape, F32),
             (w_up.shape, F32),
         ],
         14.0,
     )
+    hid, counts, late = lax.optimization_barrier((hid, counts, late))
+    late = Chunk(late, late_shapes, codes)
+    late.send_cores()
+    result, dx2, gain3, weights = run(
+        functools.partial(feed_back_kernel, maxlen=maxlen), "feed_back", steps,
+        [me_ref, lengths, group_member, mix, counts], [x2, cotangent, hid, dgate, dup],
+        [gain_three, w_gate, w_up, w_down], "sssssrrrrrffff",
+        [
+            ((rows, width), BF16, True),
+            ((rows, width), F32, True),
+            ((1, width), F32, False),
+            ((2,), F32, None),
+        ],
+        [], 8.0,
+    )
+    dx2 = fence(dx2, late)
+    late.take_cores(weights)
+    dx2 = fence(dx2, late)
+    late.send_first()
+    dcq, dkv, dfeat, dx1, dc, gain2, dbias = run(
+        cross_backward_kernel, "cross_backward", steps, [],
+        [dx2, cross_q, cross_chances, cross_kv, x1],
+        [gain_two, w_cross_out, w_cross_query, w_cross_key, w_cross_value], "rrrrrfffff",
+        [
+            ((rows, INNER), BF16, True),
+            ((image_rows, 2 * INNER), BF16, True),
+            ((image_rows, width), BF16, True),
+            ((rows, width), F32, True),
+            ((rows, width), BF16, True),
+            ((1, width), F32, False),
+            ((1, width), F32, False),
+        ],
+        [((width, 2 * INNER), BF16)], 14.0,
+    )
+    dcq = fence(dcq, late)
+    late.take_first()
+    dcq = fence(dcq, late)
+    late.send_second()
     cross_shapes = [w_cross_out.shape, w_cross_query.shape, w_cross_key.shape, w_cross_value.shape]
     cross_rows = sum(block_rows(s) for s in cross_shapes)
-    dfeat, dx1, gain2, dbias, *cross = run(
-        cross_backward_kernel, "cross_backward", steps, [codes],
-        [dx2, cross_mixed, cross_q, cross_chances, cross_kv, h2, feat, x1],
-        [gain_two, w_cross_out, w_cross_query, w_cross_key, w_cross_value], "srrrrrrrrfffff",
+    cross = run(
+        cross_weights_kernel, "cross_weights", 1, [codes], [],
+        [cross_mixed, dc, h2, dcq, feat, dkv], "sffffff",
+        [((8, cross_rows, 128), F32, False)] * 4,
+        [(w_cross_out.shape, F32), (w_cross_query.shape, F32), ((width, 2 * INNER), F32)], 8.0,
+    )
+    cross = Chunk(fence(cross, late), cross_shapes, codes)
+    late.take()
+    fence((), cross, late)
+    cross.send_cores()
+    late.send_third()
+    fence((), cross)
+    cross.take_cores(weights)
+    dx1 = fence(dx1, cross)
+    cross.send_first()
+    dqkv, da, grad_tokens, gain1 = run(
+        self_backward_kernel, "self_backward", steps, [weights], [dx1, qkv, chances, tokens],
+        [gain_one, w_out, w_query, w_key, w_value], "srrrrfffff",
         [
-            ((image_rows, width), BF16, True),
+            ((rows, 3 * INNER), BF16, True),
+            ((rows, width), BF16, True),
             ((rows, width), F32, True),
             ((1, width), F32, False),
-            ((1, width), F32, False),
-            ((HALF, cross_rows, 128), F32, False),
-            ((HALF, cross_rows, 128), F32, False),
         ],
-        [
-            ((width, 2 * INNER), BF16),
-            ((part, INNER), BF16),
-            ((image_rows // steps, 2 * INNER), BF16),
-            (w_cross_out.shape, F32),
-            (w_cross_query.shape, F32),
-            ((width, 2 * INNER), F32),
-        ],
-        10.0,
-    )
+        [((width, 3 * INNER), BF16)], 14.0,
+    )
+    dqkv = fence(dqkv, cross, late)
+    late.take()
+    cross.take_first()
+    dqkv = fence(dqkv, cross, late)
+    late.send_fourth()
+    cross.send_second()
+    own_shapes = [w_out.shape, w_query.shape, w_key.shape, w_value.shape, (BLOCKS * 8, 128)]
+    own_rows = sum(block_rows(s) for s in own_shapes)
+    own = run(
+        self_weights_kernel, "self_weights", 1, [codes], [],
+        [mixed, da, h1, dqkv, gain1, gain2, gain3, dbias], "sffffffff",
+        [((8, own_rows, 128), F32, False)] * 4,
+        [(w_out.shape, F32), ((width, 3 * INNER), F32), ((BLOCKS * 8, 128), F32)], 8.0,
+    )
+    own = Chunk(fence(own, late, cross), own_shapes, codes, True)
+    late.take_fourth()
+    cross.take()
+    fence((), own, late, cross)
+    own.send_cores()
+    late.send_back_fourth()
+    cross.send_third()
+    fence((), own)
+    own.take_cores(weights)
+    dfeat = fence(dfeat, own)
+    own.send_first()
     patch_shapes = [w_patch.shape]
     patch_rows = block_rows(w_patch.shape)
     patch = run(
         patch_weight_kernel, "patch_weight", steps, [codes], [flat, dfeat], [], "srr",
-        [((HALF, patch_rows, 128), F32, False), ((HALF, patch_rows, 128), F32, False)],
-        [((width, patch_dim), F32), ((patch_dim, width), F32)], 5.0,
-    )
-    own_shapes = [w_out.shape, w_query.shape, w_key.shape, w_value.shape, (BLOCKS * 8, 128)]
-    own_rows = sum(block_rows(s) for s in own_shapes)
-    grad_tokens, *own = run(
-        self_backward_kernel, "self_backward", steps, [codes, weight_ref],
-        [dx1, mixed, qkv, chances, h1, tokens],
-        [gain_one, w_out, w_query, w_key, w_value, gain2, gain3, dbias], "ssrrrrrrffffffff",
-        [
-            ((rows, width), F32, True),
-            ((HALF, own_rows, 128), F32, False),
-            ((HALF, own_rows, 128), F32, False),
-        ],
-        [
-            ((width, 3 * INNER), BF16),
-            ((part, 3 * INNER), BF16),
-            (w_out.shape, F32),
-            ((width, 3 * INNER), F32),
-            ((1, width), F32),
-            ((BLOCKS * 8, 128), F32),
-        ],
-        8.0,
-    )
+        [((8, patch_rows, 128), F32, False)] * 4,
+        [((width, patch_dim), F32), ((patch_dim, width), F32)], 12.0,
+    )
+    patch = Chunk(fence(patch, own, cross, late), patch_shapes, codes)
+    late.take_back()
+    cross.take()
+    own.take_first()
+    fence((), patch, own, cross, late)
+    patch.send_cores()
+    late.send_back_third()
+    cross.send_fourth()
+    own.send_second()
+    fence((), patch)
+    patch.take_cores(weights)
+    dfeat = fence(dfeat, patch)
+    patch.send_first()
     (grad_patches,) = run(
-        patch_input_kernel, "patch_input", 2 * steps, [weight_ref], [dfeat], [w_patch], "srf",
-        [((image_rows, patch_dim), F32, True)], [], 4.0,
-    )
-
-    pieces = [spread_blocks(sum_blocks(v, weight_own, weight_other)) for v in (late, cross, patch, own)]
-    late = unpack(pieces[0], late_shapes, codes)
-    cross = unpack(pieces[1], cross_shapes, codes)
-    patch = unpack(pieces[2], patch_shapes, codes)
-    own = unpack(pieces[3], own_shapes, codes, True)
+        patch_input_kernel, "patch_input", 2 * steps, [weights], [dfeat], [w_patch], "srf",
+        [((image_rows, patch_dim), F32, True)], [], 12.0,
+    )
+    grad_patches = fence(grad_patches, patch, own, cross, late)
+    late.take_back()
+    cross.take_fourth()
+    own.take()
+    patch.take_first()
+    fence((), patch, own, cross, late)
+    late.send_back_second()
+    cross.send_back_fourth()
+    own.send_third()
+    patch.send_second()
+    late.take_back()
+    late.send_back_first()
+    cross.take_back()
+    cross.send_back_third()
+    own.take()
+    own.send_fourth()
+    own.take_fourth()
+    patch.take()
+    patch.send_third()
+    cross.take_back()
+    cross.send_back_second()
+    own.send_back_fourth()
+    patch.take()
+    patch.send_fourth()
+    patch.take_fourth()
+    late.send_back_cores()
+    cross.take_back()
+    cross.send_back_first()
+    own.take_back()
+    own.send_back_third()
+    patch.send_back_fourth()
+    patch.take_back()
+    patch.send_back_third()
+    own.take_back()
+    own.send_back_second()
+    cross.send_back_cores()
+    patch.take_back()
+    patch.send_back_second()
+    own.take_back()
+    own.send_back_first()
+    patch.take_back()
+    late = fence(late.unpack(), patch)
+    patch.send_back_first()
+    own.send_back_cores()
+    cross = cross.unpack()
+    own = own.unpack()
+    cross, own, late = fence((cross, own, late), patch)
+    patch.send_back_cores()
+    patch = patch.unpack()
     gains = [g.reshape(width) for g in own[5:]]
     return (
         result,

time: 359 us -> 268 us (0.75)
  waiting for transfers between devices: 136 us -> 74.1 us
  starting transfers between devices: 61 us -> 44.5 us
  local copies, waits for them, and re-layouts: 10.2 us -> 3.32 us
  between operations: 5.65 us -> 1.2 us
    ppermute x49 -> x54, waiting for transfers between devices: 136 us -> 74.1 us  [exchange(): lax.ppermute(values, 'dp', flips(count, first, first if second is None el...]
    ppermute x49 -> x54, starting transfers between devices: 61 us -> 44.5 us  [exchange(): lax.ppermute(values, 'dp', flips(count, first, first if second is None el...]
    add x24 -> x28, other arithmetic: 1.99 us -> 13.9 us  [the longest x4 5.98 us: take_first(): keep = keep * weights[0] + low * weights[1]]
    mul x9 -> x0, other arithmetic: 10.1 us -> none  [the longest x8 9.46 us: sum_blocks(): keep, got = (keep * own, got * other)]
    unnamed x28 -> x32, local copies, waits for them, and re-layouts: 8.29 us -> 1.93 us
    pallas_call x8 -> x11, Pallas kernels: 114 us -> 116 us  [run(): pl.pallas_call(kernel, grid=(steps,), out_shape=[jax.ShapeDtypeStruct(s,...]
  transfers between devices with their start and end apart: 49 -> 54, of which waited for: 21 -> 24; matrix products, arithmetic and copies ran while one was open for 4% -> 3% of each run, Pallas kernels for 35% -> 43%
where the time goes in v2:
time: 268 us; the launch traced here: 267 us
  Pallas kernels  129 us (48%)
  waiting for transfers between devices  74.1 us (28%)
  starting transfers between devices  44.5 us (17%)
  other arithmetic  14.9 us (6%)
  local copies, waits for them, and re-layouts  3.32 us (1%)
    pallas_call x11, Pallas kernels, run(): pl.pallas_call(kernel, grid=(steps,), out_shape=[jax.ShapeDtypeStruct(s,...  116 us
    ppermute x54, waiting for transfers between devices, exchange(): lax.ppermute(values, 'dp', flips(count, first, first if second is None el...  74.1 us
    ppermute x54, starting transfers between devices, exchange(): lax.ppermute(values, 'dp', flips(count, first, first if second is None el...  44.5 us
    pallas_call x4, Pallas kernels, unpack(): pl.pallas_call(functools.partial(unpack_kernel, shapes, with_gains), out_...  12.8 us
    add x4, other arithmetic, take_first(): keep = keep * weights[0] + low * weights[1]  5.98 us
    add x4, other arithmetic, take_cores(): self.held = (keep_high * weights[0] + high * weights[1], keep_low)  5.86 us
  transfers between devices with their start and end apart: 54, of which 24 were waited for; matrix products, arithmetic and copies ran while one was open for 3% of the time, Pallas kernels for 43%

profile of v2, /device:TPU:0, one launch (start us, length us, event | category | flops | bytes accessed | tf_op | source)
XLA Modules:
  0.0 267.0 jit_solution(2424343349073458146)
XLA Ops:
  0.7 9.9 %features.1 = (bf16[2048,512]{1,0:T(8,128)(2,1)}, bf16[2048,768]{1,0:T(8,128)(2,1)}, f32[2]{0:T(128)}) custom-call(s32[1]{0:T(128)} %bitcast.me_ref, s32[8]{0:T(128)} %len_ref.7, s32[32]{0:T(128)} %member_ref.3, bf16[2048,1664]{1,0:T(8,128)(2,1)} %bitcast.15, bf16[1664,512]{1,0:T(8,128)(2,1)} %w_ref.1, f32[1,512]{1,0:T(1,128)} %bitcast.17, ...), custom_call_target="tpu_custom_call" | custom-call | flops 5100000256 | bytes 1048576 | tf_op jit(solution)/shard_map/features/pallas_call | solution.py:563
  12.6 2.8 %collective-permute-start.1 = (f32[2]{0:T(128)S(1)}, f32[2]{0:T(128)S(1)}, u32[]{:S(2)}, u32[]{:S(2)}) collective-permute-start(f32[2]{0:T(128)S(1)} %add.150), channel_id=1, source_target_pairs={{0,2},{1,3},{2,0},{3,1},{4,6},{5,7},{6,4},{7,5},{8,10},{9,11},{10,... | collective-permute-start | bytes 32 | tf_op jit(solution)/shard_map/ppermute | solution.py:386
  15.4 9.4 %self_forward.1 = (bf16[1024,512]{1,0:T(8,128)(2,1)}, bf16[1024,1152]{1,0:T(8,128)(2,1)}, bf16[8,3,256,128]{3,2,1,0:T(8,128)(2,1)}, bf16[1024,384]{1,0:T(8,128)(...) custom-call(s32[8]{0:T(128)} %len_ref.7, bf16[1024,512]{1,0:T(8,128)(2,1)} %tok_ref.2, ...), custom_call_target="tpu_custom_call" | custom-call | flops 6000000000 | bytes 1048576 | tf_op jit(solution)/shard_map/self_forward/pallas_call | solution.py:563
  24.8 1.6 collective-permute-start.2
  26.4 8.1 %cross_forward.1 = (bf16[8,3,512,128]{3,2,1,0:T(8,128)(2,1)}, bf16[1024,384]{1,0:T(8,128)(2,1)}, f32[1024,512]{1,0:T(8,128)}) custom-call(bf16[1024,384]{1,0:T(8,128)(2,1)} %get-tuple-element.233.cq_ref, bf16[2048,768]{1,0:T(8,128)(2,1)} %get-tuple-element.234.kv_ref, f32[1024,512]{1,0:T(8,128)} %get-tuple-element.235.x1_ref, bf16[384,512]{1,0:T(8,128)(2,1)} %wco_ref.3), custom_call_target="tpu_custom_call" | custom-call | flops 6000000000 | bytes 1048576 | tf_op jit(solution)/shard_map/cross_forward/pallas_call | solution.py:563
  34.6 3.7 %collective-permute-start.5 = (f32[2]{0:T(128)S(1)}, f32[2]{0:T(128)S(1)}, u32[]{:S(2)}, u32[]{:S(2)}) collective-permute-start(f32[2]{0:T(128)S(1)} %add.152), channel_id=1, source_target_pairs={{0,24},{1,25},{2,26},{3,27},{4,28},{5,29},{6,30},{7,31},{8,16},{9,... | collective-permute-start | bytes 32 | tf_op jit(solution)/shard_map/ppermute | solution.py:386
  38.2 0.8 collective-permute-start.3
  39.0 15.5 %feed_forward.1 = (bf16[1024,1024]{1,0:T(8,128)(2,1)}, bf16[1024,1024]{1,0:T(8,128)(2,1)}, bf16[1024,1024]{1,0:T(8,128)(2,1)}, f32[8,384,128]{2,1,0:T(8,128)}, f...) custom-call(s32[8]{0:T(128)} %len_ref.7, s32[2]{0:T(128)} %pad_add_fusion.code_ref, ...), custom_call_target="tpu_custom_call" | custom-call | flops 14000000000 | bytes 1048576 | tf_op jit(solution)/shard_map/feed_forward/pallas_call | solution.py:563
  55.6 9.5 %feed_back.1 = (bf16[1024,512]{1,0:T(8,128)(2,1)}, f32[1024,512]{1,0:T(8,128)}, f32[1,512]{1,0:T(1,128)}, f32[2]{0:T(128)}) custom-call(s32[1]{0:T(128)} %bitcast.me_ref, s32[8]{0:T(128)} %len_ref.7, s32[32]{0:T(128)} %member_ref.3, f32[2]{0:T(128)} %mix_ref.1, f32[2]{0:T(128)} %add_add_fusion.count_ref, f32[1024,512]{1,0:T(8,128)} %get-tuple-element.238.x2_ref, ...), custom_call_target="tpu_custom_call" | custom-call | flops 8000000000 | bytes 1048576 | tf_op jit(solution)/shard_map/feed_back/pallas_call | solution.py:563
  65.2 1.3 fusion.2
  66.5 1.5 multiply_add_fusion.1
  68.6 15.8 %cross_backward.1 = (bf16[1024,384]{1,0:T(8,128)(2,1)}, bf16[2048,768]{1,0:T(8,128)(2,1)}, bf16[2048,512]{1,0:T(8,128)(2,1)}, f32[1024,512]{1,0:T(8,128)}, bf16[...) custom-call(f32[1024,512]{1,0:T(8,128)} %get-tuple-element.261.dx2_ref, ...), custom_call_target="tpu_custom_call" | custom-call | flops 14000000000 | bytes 1048576 | tf_op jit(solution)/shard_map/cross_backward/pallas_call | solution.py:563
  84.4 4.1 %collective-permute-done.8 = f32[8,384,128]{2,1,0:T(8,128)S(1)} collective-permute-done((f32[8,384,128]{2,1,0:T(8,128)S(1)}, f32[8,384,128]{2,1,0:T(8,128)S(1)}, u32[]{:S(2)}, u32[]{:S(2)}) %collective-permute-start.8) | collective-permute-done | bytes 1572896 | tf_op jit(solution)/shard_map/ppermute | solution.py:386
  88.5 1.5 multiply_add_fusion
  90.9 8.4 %cross_weights.1 = (f32[8,192,128]{2,1,0:T(8,128)}, f32[8,192,128]{2,1,0:T(8,128)}, f32[8,192,128]{2,1,0:T(8,128)}, f32[8,192,128]{2,1,0:T(8,128)}) custom-call(s32[2]{0:T(128)} %pad_add_fusion.code_ref, bf16[1024,384]{1,0:T(8,128)(2,1)} %get-tuple-element.264.oc_ref, bf16[1024,512]{1,0:T(8,128)(2,1)} %get-tuple-element.265.dc_ref, ...), custom_call_target="tpu_custom_call" | custom-call | flops 8000000000 | bytes 1048576 | tf_op jit(solution)/shard_map/cross_weights/pallas_call | solution.py:563
  99.3 3.1 %collective-permute-done.9 = f32[4,384,128]{2,1,0:T(8,128)S(1)} collective-permute-done((f32[4,384,128]{2,1,0:T(8,128)S(1)}, f32[4,384,128]{2,1,0:T(8,128)S(1)}, u32[]{:S(2)}, u32[]{:S(2)}) %collective-permute-start.9) | collective-permute-done | bytes 786464 | tf_op jit(solution)/shard_map/ppermute | solution.py:386
  103.0 1.2 collective-permute-start.13
  104.8 1.1 collective-permute-done.10
  105.9 1.4 multiply_add_fusion.7
  108.0 11.9 %self_backward.1 = (bf16[1024,1152]{1,0:T(8,128)(2,1)}, bf16[1024,512]{1,0:T(8,128)(2,1)}, f32[1024,512]{1,0:T(8,128)}, f32[1,512]{1,0:T(1,128)}) custom-call(f32[2]{0:T(128)} %get-tuple-element.250.weight_ref, f32[1024,512]{1,0:T(8,128)} %get-tuple-element.298.dx1_ref, bf16[1024,1152]{1,0:T(8,128)(2,1)} %get-tuple-element.299.qkv_ref, ...), custom_call_target="tpu_custom_call" | custom-call | flops 14000000000 | bytes 1048576 | tf_op jit(solution)/shard_map/self_backward/pallas_call | solution.py:563
  120.0 1.1 copy-done.7
  121.0 1.4 multiply_add_fusion.6
  122.6 2.2 collective-permute-start.14
  125.3 6.6 %self_weights.1 = (f32[8,200,128]{2,1,0:T(8,128)}, f32[8,200,128]{2,1,0:T(8,128)}, f32[8,200,128]{2,1,0:T(8,128)}, f32[8,200,128]{2,1,0:T(8,128)}) custom-call(s32[2]{0:T(128)} %pad_add_fusion.code_ref, bf16[1024,384]{1,0:T(8,128)(2,1)} %get-tuple-element.303.o_ref, bf16[1024,512]{1,0:T(8,128)(2,1)} %get-tuple-element.304.da_ref, ...), custom_call_target="tpu_custom_call" | custom-call | flops 8000000000 | bytes 1048576 | tf_op jit(solution)/shard_map/self_weights/pallas_call | solution.py:563
  131.8 2.5 collective-permute-done.14
  135.3 3.4 %collective-permute-start.20 = (f32[1,384,128]{2,1,0:T(8,128)S(1)}, f32[1,384,128]{2,1,0:T(8,128)S(1)}, u32[]{:S(2)}, u32[]{:S(2)}) collective-permute-start(f32[1,384,128]{2,1,0:T(8,128)S(1)} %add.168), channel_id=1, source_target_pairs={{0,16},{1,17},{2,18},{3,19},{4,20},{5,21},{6,22},{7,23},{8,24},{9,... | collective-permute-start | bytes 589832 | tf_op jit(solution)/shard_map/ppermute | solution.py:386
  138.7 1.4 multiply_add_fusion.5
  140.7 10.8 %patch_weight.1 = (f32[8,208,128]{2,1,0:T(8,128)}, f32[8,208,128]{2,1,0:T(8,128)}, f32[8,208,128]{2,1,0:T(8,128)}, f32[8,208,128]{2,1,0:T(8,128)}) custom-call(s32[2]{0:T(128)} %pad_add_fusion.code_ref, bf16[2048,1664]{1,0:T(8,128)(2,1)} %bitcast.16, bf16[2048,512]{1,0:T(8,128)(2,1)} %get-tuple-element.377.dfeat_ref), custom_call_target="tpu_custom_call" | custom-call | flops 12000000000 | bytes 1048576 | tf_op jit(solution)/shard_map/patch_weight/pallas_call | solution.py:563
  151.5 1.0 collective-permute-done.18
  152.6 1.5 multiply_add_fusion.4
  155.9 3.3 %collective-permute-start.26 = (f32[2,384,128]{2,1,0:T(8,128)S(1)}, f32[2,384,128]{2,1,0:T(8,128)S(1)}, u32[]{:S(2)}, u32[]{:S(2)}) collective-permute-start(f32[2,384,128]{2,1,0:T(8,128)S(1)} %pad_maximum_fusion.5), channel_id=1, source_target_pairs={{0,8},{1,9},{2,10},{3,11},{4,12},{5,13},{6,14},{7,15},{8,0},{9,1},... | collective-permute-start | bytes 1179656 | tf_op jit(solution)/shard_map/ppermute | solution.py:386
  159.9 1.4 multiply_add_fusion.3
  161.3 1.6 collective-permute-start.23
  162.9 10.2 %patch_input.1 = f32[2048,1664]{1,0:T(8,128)} custom-call(f32[2]{0:T(128)} %get-tuple-element.250.weight_ref, bf16[2048,512]{1,0:T(8,128)(2,1)} %get-tuple-element.377.dfeat_ref, bf16[1664,512]{1,0:T(8,128)(2,1)} %w_ref.1), custom_call_target="tpu_custom_call" | custom-call | flops 12000000000 | bytes 1048576 | tf_op jit(solution)/shard_map/patch_input/pallas_call | solution.py:563
  173.1 1.6 collective-permute-done.23
  174.9 1.5 multiply_add_fusion.2
  176.4 1.2 collective-permute-start.41
  178.0 1.7 collective-permute-start.33
  180.2 8.3 %collective-permute-done.41 = f32[4,384,128]{2,1,0:T(8,128)S(1)} collective-permute-done((f32[4,384,128]{2,1,0:T(8,128)S(1)}, f32[4,384,128]{2,1,0:T(8,128)S(1)}, u32[]{:S(2)}, u32[]{:S(2)}) %collective-permute-start.41) | collective-permute-done | bytes 786464 | tf_op jit(solution)/shard_map/ppermute | solution.py:386
  188.5 1.2 collective-permute-start.42
  190.2 4.2 %collective-permute-done.45 = f32[4,208,128]{2,1,0:T(8,128)S(1)} collective-permute-done((f32[4,208,128]{2,1,0:T(8,128)S(1)}, f32[4,208,128]{2,1,0:T(8,128)S(1)}, u32[]{:S(2)}, u32[]{:S(2)}) %collective-permute-start.45) | collective-permute-done | bytes 426016 | tf_op jit(solution)/shard_map/ppermute | solution.py:386
  195.0 1.9 collective-permute-done.34
  197.0 6.3 %collective-permute-done.46 = f32[2,208,128]{2,1,0:T(8,128)S(1)} collective-permute-done((f32[2,208,128]{2,1,0:T(8,128)S(1)}, f32[2,208,128]{2,1,0:T(8,128)S(1)}, u32[]{:S(2)}, u32[]{:S(2)}) %collective-permute-start.46) | collective-permute-done | bytes 213024 | tf_op jit(solution)/shard_map/ppermute | solution.py:386
  203.5 0.9 collective-permute-done.35
  204.3 1.6 collective-permute-start.36
  205.9 4.1 %collective-permute-done.47 = f32[1,208,128]{2,1,0:T(8,128)S(1)} collective-permute-done((f32[1,208,128]{2,1,0:T(8,128)S(1)}, f32[1,208,128]{2,1,0:T(8,128)S(1)}, u32[]{:S(2)}, u32[]{:S(2)}) %collective-permute-start.47) | collective-permute-done | bytes 106528 | tf_op jit(solution)/shard_map/ppermute | solution.py:386
  210.3 2.6 collective-permute-start.28
  212.9 4.4 %collective-permute-done.48 = f32[1,208,128]{2,1,0:T(8,128)S(1)} collective-permute-done((f32[1,208,128]{2,1,0:T(8,128)S(1)}, f32[1,208,128]{2,1,0:T(8,128)S(1)}, u32[]{:S(2)}, u32[]{:S(2)}) %collective-permute-start.48) | collective-permute-done | bytes 106528 | tf_op jit(solution)/shard_map/ppermute | solution.py:386
  218.1 1.5 collective-permute-done.28
  219.6 1.9 collective-permute-start.29
  221.5 2.9 %collective-permute-done.49 = f32[2,208,128]{2,1,0:T(8,128)S(1)} collective-permute-done((f32[2,208,128]{2,1,0:T(8,128)S(1)}, f32[2,208,128]{2,1,0:T(8,128)S(1)}, u32[]{:S(2)}, u32[]{:S(2)}) %collective-permute-start.49) | collective-permute-done | bytes 213024 | tf_op jit(solution)/shard_map/ppermute | solution.py:386
  224.5 1.0 collective-permute-done.37
  225.7 1.5 collective-permute-start.38
  227.2 4.3 %collective-permute-done.29 = f32[4,192,128]{2,1,0:T(8,128)S(1)} collective-permute-done((f32[4,192,128]{2,1,0:T(8,128)S(1)}, f32[4,192,128]{2,1,0:T(8,128)S(1)}, u32[]{:S(2)}, u32[]{:S(2)}) %collective-permute-start.29) | collective-permute-done | bytes 393248 | tf_op jit(solution)/shard_map/ppermute | solution.py:386
  231.5 9.0 %collective-permute-done.50 = f32[4,208,128]{2,1,0:T(8,128)S(1)} collective-permute-done((f32[4,208,128]{2,1,0:T(8,128)S(1)}, f32[4,208,128]{2,1,0:T(8,128)S(1)}, u32[]{:S(2)}, u32[]{:S(2)}) %collective-permute-start.50) | collective-permute-done | bytes 426016 | tf_op jit(solution)/shard_map/ppermute | solution.py:386
  240.6 1.6 collective-permute-start.30
  242.2 4.3 %unpack.6 = (f32[1024,512]{1,0:T(8,128)}, f32[512,1024]{1,0:T(8,128)}, f32[512,1024]{1,0:T(8,128)}) custom-call(s32[2]{0:T(128)S(1)} %copy-done, f32[8,384,128]{2,1,0:T(8,128)S(1)} %constant_dynamic-update-slice_fusion.4.refs_0_, f32[8,384,128]{2,1,0:T(8,128)S(1)} %collective-permute-done.42.refs_1_, f32[8,384,128]{2,1,0:T(8,128)S(1)} %collective-permute-done.43.refs_2_, ...), custom_call_target="tpu_custom_call" | custom-call | tf_op jit(solution)/shard_map/unpack/pallas_call | solution.py:456
  247.6 5.0 %collective-permute-done.30.refs_1_ = f32[8,192,128]{2,1,0:T(8,128)S(1)} collective-permute-done((f32[8,192,128]{2,1,0:T(8,128)S(1)}, f32[8,192,128]{2,1,0:T(8,128)S(1)}, u32[]{:S(2)}, u32[]{:S(2)}) %collective-permute-start.30) | collective-permute-done | bytes 786464 | tf_op jit(solution)/shard_map/ppermute | solution.py:386
  252.6 2.3 collective-permute-done.32.refs_3_
  254.8 2.8 %unpack.4 = (f32[384,512]{1,0:T(8,128)}, f32[512,384]{1,0:T(8,128)}, f32[512,384]{1,0:T(8,128)}, f32[512,384]{1,0:T(8,128)}) custom-call(s32[2]{0:T(128)S(1)} %copy-done, f32[8,192,128]{2,1,0:T(8,128)S(1)} %constant_dynamic-update-slice_fusion.refs_0_, f32[8,192,128]{2,1,0:T(8,128)S(1)} %collective-permute-done.30.refs_1_, ...), custom_call_target="tpu_custom_call" | custom-call | tf_op jit(solution)/shard_map/unpack/pallas_call | solution.py:456
  257.6 2.8 %unpack.5 = (f32[384,512]{1,0:T(8,128)}, f32[512,384]{1,0:T(8,128)}, f32[512,384]{1,0:T(8,128)}, f32[512,384]{1,0:T(8,128)}, f32[256,128]{1,0:T(8,128)}, /*index...) custom-call(s32[2]{0:T(128)S(1)} %copy-done, ...), custom_call_target="tpu_custom_call" | custom-call | tf_op jit(solution)/shard_map/unpack/pallas_call | solution.py:456
  260.4 1.2 collective-permute-done.51.refs_1_
  261.7 2.4 collective-permute-done.53.refs_3_
  264.1 3.0 %unpack.7 = f32[1664,512]{1,0:T(8,128)} custom-call(s32[2]{0:T(128)S(1)} %copy-done, f32[8,208,128]{2,1,0:T(8,128)S(1)} %pad_maximum_fusion.refs_0_, f32[8,208,128]{2,1,0:T(8,128)S(1)} %collective-permute-done.51.refs_1_, f32[8,208,128]{2,1,0:T(8,128)S(1)} %collective-permute-done.52.refs_2_, f32[8,208,128]{2,1,0:T(8,128)S(1)} %collective-permute-done.53.refs_3_), custom_call_target="tpu_custom_call" | custom-call | tf_op jit(solution)/shard_map/unpack/pallas_call | solution.py:456
  (133 shorter events, 15.8 us)
Async XLA Ops:
  10.6 1.4 collective-permute-start
  12.6 12.2 %collective-permute-start.1 = (f32[2]{0:T(128)S(1)}, f32[2]{0:T(128)S(1)}, u32[]{:S(2)}, u32[]{:S(2)}) collective-permute-start(f32[2]{0:T(128)S(1)} %add.150), channel_id=1, source_target_pairs={{0,2},{1,3},{2,0},{3,1},{4,6},{5,7},{6,4},{7,5},{8,10},{9,11},{10,... | collective-permute-start | bytes 32 | tf_op jit(solution)/shard_map/ppermute | solution.py:386
  24.8 9.7 %collective-permute-start.2 = (f32[2]{0:T(128)S(1)}, f32[2]{0:T(128)S(1)}, u32[]{:S(2)}, u32[]{:S(2)}) collective-permute-start(f32[2]{0:T(128)S(1)} %add.151), channel_id=1, source_target_pairs={{0,4},{1,5},{2,6},{3,7},{4,0},{5,1},{6,2},{7,3},{8,12},{9,13},{10,... | collective-permute-start | bytes 32 | tf_op jit(solution)/shard_map/ppermute | solution.py:386
  34.6 20.0 %collective-permute-start.5 = (f32[2]{0:T(128)S(1)}, f32[2]{0:T(128)S(1)}, u32[]{:S(2)}, u32[]{:S(2)}) collective-permute-start(f32[2]{0:T(128)S(1)} %add.152), channel_id=1, source_target_pairs={{0,24},{1,25},{2,26},{3,27},{4,28},{5,29},{6,30},{7,31},{8,16},{9,... | collective-permute-start | bytes 32 | tf_op jit(solution)/shard_map/ppermute | solution.py:386
  38.2 16.3 %collective-permute-start.4 = (f32[2]{0:T(128)S(1)}, f32[2]{0:T(128)S(1)}, u32[]{:S(2)}, u32[]{:S(2)}) collective-permute-start(f32[2]{0:T(128)S(1)} %add.152), channel_id=1, source_target_pairs={{0,16},{1,17},{2,18},{3,19},{4,20},{5,21},{6,22},{7,23},{8,24},{9,... | collective-permute-start | bytes 32 | tf_op jit(solution)/shard_map/ppermute | solution.py:386
  38.2 16.4 %collective-permute-start.3 = (f32[2]{0:T(128)S(1)}, f32[2]{0:T(128)S(1)}, u32[]{:S(2)}, u32[]{:S(2)}) collective-permute-start(f32[2]{0:T(128)S(1)} %add.152), channel_id=1, source_target_pairs={{0,8},{1,9},{2,10},{3,11},{4,12},{5,13},{6,14},{7,15},{8,0},{9,1},... | collective-permute-start | bytes 32 | tf_op jit(solution)/shard_map/ppermute | solution.py:386
  55.1 11.4 %collective-permute-start.7 = (f32[8,384,128]{2,1,0:T(8,128)}, f32[8,384,128]{2,1,0:T(8,128)S(1)}, u32[]{:S(2)}, u32[]{:S(2)}) collective-permute-start(f32[8,384,128]{2,1,0:T(8,128)} %get-tuple-element.254), channel_id=1, source_target_pairs={{0,1},{1,0},{2,3},{3,2},{4,5},{5,4},{6,7},{7,6},{8,9},{9,8},{10,11... | collective-permute-start | bytes 4718600 | tf_op jit(solution)/shard_map/ppermute | solution.py:386
  55.1 11.4 %collective-permute-start.6 = (f32[8,384,128]{2,1,0:T(8,128)}, f32[8,384,128]{2,1,0:T(8,128)S(1)}, u32[]{:S(2)}, u32[]{:S(2)}) collective-permute-start(f32[8,384,128]{2,1,0:T(8,128)} %get-tuple-element.255), channel_id=1, source_target_pairs={{0,1},{1,0},{2,3},{3,2},{4,5},{5,4},{6,7},{7,6},{8,9},{9,8},{10,11... | collective-permute-start | bytes 4718600 | tf_op jit(solution)/shard_map/ppermute | solution.py:386
  55.6 10.9 %copy-start.2 = (f32[8,384,128]{2,1,0:T(8,128)S(1)}, f32[8,384,128]{2,1,0:T(8,128)}, u32[]{:S(2)}) copy-start(f32[8,384,128]{2,1,0:T(8,128)} %get-tuple-element.257) | copy-start | bytes 4718596
  68.0 20.5 %collective-permute-start.8 = (f32[8,384,128]{2,1,0:T(8,128)S(1)}, f32[8,384,128]{2,1,0:T(8,128)S(1)}, u32[]{:S(2)}, u32[]{:S(2)}) collective-permute-start(f32[8,384,128]{2,1,0:T(8,128)S(1)} %multiply_add_fusion.1), channel_id=1, source_target_pairs={{0,2},{1,5},{2,0},{3,7},{4,6},{5,1},{6,4},{7,3},{8,10},{9,13},{10,... | collective-permute-start | bytes 4718600 | tf_op jit(solution)/shard_map/ppermute | solution.py:386
  68.6 19.9 %copy-start.1 = (f32[8,384,128]{2,1,0:T(8,128)S(1)}, f32[8,384,128]{2,1,0:T(8,128)}, u32[]{:S(2)}) copy-start(f32[8,384,128]{2,1,0:T(8,128)} %get-tuple-element.272) | copy-start | bytes 4718596
  90.3 12.1 %collective-permute-start.9 = (f32[4,384,128]{2,1,0:T(8,128)S(1)}, f32[4,384,128]{2,1,0:T(8,128)S(1)}, u32[]{:S(2)}, u32[]{:S(2)}) collective-permute-start(f32[4,384,128]{2,1,0:T(8,128)S(1)} %get-tuple-element.282), channel_id=1, source_target_pairs={{0,4},{1,3},{2,6},{3,1},{4,0},{5,7},{6,2},{7,5},{8,12},{9,11},{10,... | collective-permute-start | bytes 2359304 | tf_op jit(solution)/shard_map/ppermute | solution.py:386
  99.3 3.2 %copy-start.13 = (f32[8,192,128]{2,1,0:T(8,128)S(1)}, f32[8,192,128]{2,1,0:T(8,128)}, u32[]{:S(2)}) copy-start(f32[8,192,128]{2,1,0:T(8,128)} %get-tuple-element.292) | copy-start | bytes 2359300
  99.3 3.2 %copy-start.12 = (f32[8,192,128]{2,1,0:T(8,128)S(1)}, f32[8,192,128]{2,1,0:T(8,128)}, u32[]{:S(2)}) copy-start(f32[8,192,128]{2,1,0:T(8,128)} %get-tuple-element.293) | copy-start | bytes 2359300
  99.3 6.6 %copy-start.8 = (f32[8,192,128]{2,1,0:T(8,128)S(1)}, f32[8,192,128]{2,1,0:T(8,128)}, u32[]{:S(2)}) copy-start(f32[8,192,128]{2,1,0:T(8,128)} %get-tuple-element.294) | copy-start | bytes 2359300
  102.4 2.4 collective-permute-start.11
  102.5 3.4 %collective-permute-start.10 = (f32[8,192,128]{2,1,0:T(8,128)S(1)}, f32[8,192,128]{2,1,0:T(8,128)S(1)}, u32[]{:S(2)}, u32[]{:S(2)}) collective-permute-start(f32[8,192,128]{2,1,0:T(8,128)S(1)} %copy-done.12), channel_id=1, source_target_pairs={{0,1},{1,0},{2,3},{3,2},{4,5},{5,4},{6,7},{7,6},{8,9},{9,8},{10,11... | collective-permute-start | bytes 2359304 | tf_op jit(solution)/shard_map/ppermute | solution.py:386
  103.0 16.9 %collective-permute-start.13 = (f32[2,384,128]{2,1,0:T(8,128)S(1)}, f32[2,384,128]{2,1,0:T(8,128)S(1)}, u32[]{:S(2)}, u32[]{:S(2)}) collective-permute-start(f32[2,384,128]{2,1,0:T(8,128)S(1)} %get-tuple-element.310), channel_id=1, source_target_pairs={{0,8},{1,9},{2,10},{3,11},{4,12},{5,13},{6,14},{7,15},{8,0},{9,1},... | collective-permute-start | bytes 1179656 | tf_op jit(solution)/shard_map/ppermute | solution.py:386
  107.4 12.6 %collective-permute-start.12 = (f32[8,192,128]{2,1,0:T(8,128)S(1)}, f32[8,192,128]{2,1,0:T(8,128)S(1)}, u32[]{:S(2)}, u32[]{:S(2)}) collective-permute-start(f32[8,192,128]{2,1,0:T(8,128)S(1)} %multiply_add_fusion.7), channel_id=1, source_target_pairs={{0,2},{1,5},{2,0},{3,7},{4,6},{5,1},{6,4},{7,3},{8,10},{9,13},{10,... | collective-permute-start | bytes 2359304 | tf_op jit(solution)/shard_map/ppermute | solution.py:386
  122.6 11.8 %collective-permute-start.14 = (f32[1,384,128]{2,1,0:T(8,128)S(1)}, f32[1,384,128]{2,1,0:T(8,128)S(1)}, u32[]{:S(2)}, u32[]{:S(2)}) collective-permute-start(f32[1,384,128]{2,1,0:T(8,128)S(1)} %get-tuple-element.327), channel_id=1, source_target_pairs={{0,16},{1,17},{2,18},{3,19},{4,20},{5,21},{6,22},{7,23},{8,24},{9,... | collective-permute-start | bytes 589832 | tf_op jit(solution)/shard_map/ppermute | solution.py:386
  124.8 9.6 %collective-permute-start.15 = (f32[4,192,128]{2,1,0:T(8,128)S(1)}, f32[4,192,128]{2,1,0:T(8,128)S(1)}, u32[]{:S(2)}, u32[]{:S(2)}) collective-permute-start(f32[4,192,128]{2,1,0:T(8,128)S(1)} %get-tuple-element.329), channel_id=1, source_target_pairs={{0,4},{1,3},{2,6},{3,1},{4,0},{5,7},{6,2},{7,5},{8,12},{9,11},{10,... | collective-permute-start | bytes 1179656 | tf_op jit(solution)/shard_map/ppermute | solution.py:386
  131.8 2.7 %copy-start.11 = (f32[8,200,128]{2,1,0:T(8,128)S(1)}, f32[8,200,128]{2,1,0:T(8,128)}, u32[]{:S(2)}) copy-start(f32[8,200,128]{2,1,0:T(8,128)} %get-tuple-element.342) | copy-start | bytes 2457604
  131.8 6.8 %copy-start.6 = (f32[8,200,128]{2,1,0:T(8,128)S(1)}, f32[8,200,128]{2,1,0:T(8,128)}, u32[]{:S(2)}) copy-start(f32[8,200,128]{2,1,0:T(8,128)} %get-tuple-element.343) | copy-start | bytes 2457604
  134.5 4.2 %collective-permute-start.17 = (f32[8,200,128]{2,1,0:T(8,128)}, f32[8,200,128]{2,1,0:T(8,128)S(1)}, u32[]{:S(2)}, u32[]{:S(2)}) collective-permute-start(f32[8,200,128]{2,1,0:T(8,128)} %get-tuple-element.341), channel_id=1, source_target_pairs={{0,1},{1,0},{2,3},{3,2},{4,5},{5,4},{6,7},{7,6},{8,9},{9,8},{10,11... | collective-permute-start | bytes 2457608 | tf_op jit(solution)/shard_map/ppermute | solution.py:386
  134.6 4.1 %collective-permute-start.16 = (f32[8,200,128]{2,1,0:T(8,128)S(1)}, f32[8,200,128]{2,1,0:T(8,128)S(1)}, u32[]{:S(2)}, u32[]{:S(2)}) collective-permute-start(f32[8,200,128]{2,1,0:T(8,128)S(1)} %copy-done.11), channel_id=1, source_target_pairs={{0,1},{1,0},{2,3},{3,2},{4,5},{5,4},{6,7},{7,6},{8,9},{9,8},{10,11... | collective-permute-start | bytes 2457608 | tf_op jit(solution)/shard_map/ppermute | solution.py:386
  135.1 16.4 %collective-permute-start.19 = (f32[2,192,128]{2,1,0:T(8,128)S(1)}, f32[2,192,128]{2,1,0:T(8,128)S(1)}, u32[]{:S(2)}, u32[]{:S(2)}) collective-permute-start(f32[2,192,128]{2,1,0:T(8,128)S(1)} %get-tuple-element.355), channel_id=1, source_target_pairs={{0,8},{1,9},{2,10},{3,11},{4,12},{5,13},{6,14},{7,15},{8,0},{9,1},... | collective-permute-start | bytes 589832 | tf_op jit(solution)/shard_map/ppermute | solution.py:386
  135.3 16.2 %collective-permute-start.20 = (f32[1,384,128]{2,1,0:T(8,128)S(1)}, f32[1,384,128]{2,1,0:T(8,128)S(1)}, u32[]{:S(2)}, u32[]{:S(2)}) collective-permute-start(f32[1,384,128]{2,1,0:T(8,128)S(1)} %add.168), channel_id=1, source_target_pairs={{0,16},{1,17},{2,18},{3,19},{4,20},{5,21},{6,22},{7,23},{8,24},{9,... | collective-permute-start | bytes 589832 | tf_op jit(solution)/shard_map/ppermute | solution.py:386
  140.1 12.4 %collective-permute-start.18 = (f32[8,200,128]{2,1,0:T(8,128)S(1)}, f32[8,200,128]{2,1,0:T(8,128)S(1)}, u32[]{:S(2)}, u32[]{:S(2)}) collective-permute-start(f32[8,200,128]{2,1,0:T(8,128)S(1)} %multiply_add_fusion.5), channel_id=1, source_target_pairs={{0,2},{1,5},{2,0},{3,7},{4,6},{5,1},{6,4},{7,3},{8,10},{9,13},{10,... | collective-permute-start | bytes 2457608 | tf_op jit(solution)/shard_map/ppermute | solution.py:386
  154.2 5.7 %copy-start.4 = (f32[8,208,128]{2,1,0:T(8,128)S(1)}, f32[8,208,128]{2,1,0:T(8,128)}, u32[]{:S(2)}) copy-start(f32[8,208,128]{2,1,0:T(8,128)} %get-tuple-element.373) | copy-start | bytes 2555908
  154.3 5.5 %collective-permute-start.22 = (f32[8,208,128]{2,1,0:T(8,128)S(1)}, f32[8,208,128]{2,1,0:T(8,128)S(1)}, u32[]{:S(2)}, u32[]{:S(2)}) collective-permute-start(f32[8,208,128]{2,1,0:T(8,128)S(1)} %copy-done.10), channel_id=1, source_target_pairs={{0,1},{1,0},{2,3},{3,2},{4,5},{5,4},{6,7},{7,6},{8,9},{9,8},{10,11... | collective-permute-start | bytes 2555912 | tf_op jit(solution)/shard_map/ppermute | solution.py:386
  155.3 4.5 %collective-permute-start.21 = (f32[8,208,128]{2,1,0:T(8,128)S(1)}, f32[8,208,128]{2,1,0:T(8,128)S(1)}, u32[]{:S(2)}, u32[]{:S(2)}) collective-permute-start(f32[8,208,128]{2,1,0:T(8,128)S(1)} %copy-done.9), channel_id=1, source_target_pairs={{0,1},{1,0},{2,3},{3,2},{4,5},{5,4},{6,7},{7,6},{8,9},{9,8},{10,11... | collective-permute-start | bytes 2555912 | tf_op jit(solution)/shard_map/ppermute | solution.py:386
  155.6 17.5 %collective-permute-start.25 = (f32[1,192,128]{2,1,0:T(8,128)S(1)}, f32[1,192,128]{2,1,0:T(8,128)S(1)}, u32[]{:S(2)}, u32[]{:S(2)}) collective-permute-start(f32[1,192,128]{2,1,0:T(8,128)S(1)} %get-tuple-element.383), channel_id=1, source_target_pairs={{0,16},{1,17},{2,18},{3,19},{4,20},{5,21},{6,22},{7,23},{8,24},{9,... | collective-permute-start | bytes 294920 | tf_op jit(solution)/shard_map/ppermute | solution.py:386
  155.9 17.2 %collective-permute-start.26 = (f32[2,384,128]{2,1,0:T(8,128)S(1)}, f32[2,384,128]{2,1,0:T(8,128)S(1)}, u32[]{:S(2)}, u32[]{:S(2)}) collective-permute-start(f32[2,384,128]{2,1,0:T(8,128)S(1)} %pad_maximum_fusion.5), channel_id=1, source_target_pairs={{0,8},{1,9},{2,10},{3,11},{4,12},{5,13},{6,14},{7,15},{8,0},{9,1},... | collective-permute-start | bytes 1179656 | tf_op jit(solution)/shard_map/ppermute | solution.py:386
  159.2 13.9 %collective-permute-start.24 = (f32[4,200,128]{2,1,0:T(8,128)S(1)}, f32[4,200,128]{2,1,0:T(8,128)S(1)}, u32[]{:S(2)}, u32[]{:S(2)}) collective-permute-start(f32[4,200,128]{2,1,0:T(8,128)S(1)} %get-tuple-element.381), channel_id=1, source_target_pairs={{0,4},{1,3},{2,6},{3,1},{4,0},{5,7},{6,2},{7,5},{8,12},{9,11},{10,... | collective-permute-start | bytes 1228808 | tf_op jit(solution)/shard_map/ppermute | solution.py:386
  161.3 13.4 %collective-permute-start.23 = (f32[8,208,128]{2,1,0:T(8,128)S(1)}, f32[8,208,128]{2,1,0:T(8,128)S(1)}, u32[]{:S(2)}, u32[]{:S(2)}) collective-permute-start(f32[8,208,128]{2,1,0:T(8,128)S(1)} %multiply_add_fusion.3), channel_id=1, source_target_pairs={{0,2},{1,5},{2,0},{3,7},{4,6},{5,1},{6,4},{7,3},{8,10},{9,13},{10,... | collective-permute-start | bytes 2555912 | tf_op jit(solution)/shard_map/ppermute | solution.py:386
  173.1 1.8 copy-start.3
  176.4 12.1 %collective-permute-start.41 = (f32[4,384,128]{2,1,0:T(8,128)S(1)}, f32[4,384,128]{2,1,0:T(8,128)S(1)}, u32[]{:S(2)}, u32[]{:S(2)}) collective-permute-start(f32[4,384,128]{2,1,0:T(8,128)S(1)} %pad_maximum_fusion.2), channel_id=1, source_target_pairs={{0,4},{1,3},{2,6},{3,1},{4,0},{5,7},{6,2},{7,5},{8,12},{9,11},{10,... | collective-permute-start | bytes 2359304 | tf_op jit(solution)/shard_map/ppermute | solution.py:386
  177.7 32.6 %collective-permute-start.27 = (f32[1,192,128]{2,1,0:T(8,128)S(1)}, f32[1,192,128]{2,1,0:T(8,128)S(1)}, u32[]{:S(2)}, u32[]{:S(2)}) collective-permute-start(f32[1,192,128]{2,1,0:T(8,128)S(1)} %add.183), channel_id=1, source_target_pairs={{0,16},{1,17},{2,18},{3,19},{4,20},{5,21},{6,22},{7,23},{8,24},{9,... | collective-permute-start | bytes 294920 | tf_op jit(solution)/shard_map/ppermute | solution.py:386
  178.0 11.8 %collective-permute-start.33 = (f32[2,200,128]{2,1,0:T(8,128)S(1)}, f32[2,200,128]{2,1,0:T(8,128)S(1)}, u32[]{:S(2)}, u32[]{:S(2)}) collective-permute-start(f32[2,200,128]{2,1,0:T(8,128)S(1)} %get-tuple-element.402), channel_id=1, source_target_pairs={{0,8},{1,9},{2,10},{3,11},{4,12},{5,13},{6,14},{7,15},{8,0},{9,1},... | collective-permute-start | bytes 614408 | tf_op jit(solution)/shard_map/ppermute | solution.py:386
  179.7 14.7 %collective-permute-start.45 = (f32[4,208,128]{2,1,0:T(8,128)S(1)}, f32[4,208,128]{2,1,0:T(8,128)S(1)}, u32[]{:S(2)}, u32[]{:S(2)}) collective-permute-start(f32[4,208,128]{2,1,0:T(8,128)S(1)} %get-tuple-element.416), channel_id=1, source_target_pairs={{0,4},{1,3},{2,6},{3,1},{4,0},{5,7},{6,2},{7,5},{8,12},{9,11},{10,... | collective-permute-start | bytes 1277960 | tf_op jit(solution)/shard_map/ppermute | solution.py:386
  188.5 28.9 %collective-permute-start.42 = (f32[8,384,128]{2,1,0:T(8,128)S(1)}, f32[8,384,128]{2,1,0:T(8,128)S(1)}, u32[]{:S(2)}, u32[]{:S(2)}) collective-permute-start(f32[8,384,128]{2,1,0:T(8,128)S(1)} %constant_dynamic-update-slice_fusion.4.refs_0_), channel_id=1, source_target_pairs={{0,2},{1,5},{2,0},{3,7},{4,6},{5,1},{6,4},{7,3},{8,10},{9,13},{10,... | collective-permute-start | bytes 4718600 | tf_op jit(solution)/shard_map/ppermute | solution.py:386
  189.8 7.1 %collective-permute-start.34 = (f32[1,200,128]{2,1,0:T(8,128)S(1)}, f32[1,200,128]{2,1,0:T(8,128)S(1)}, u32[]{:S(2)}, u32[]{:S(2)}) collective-permute-start(f32[1,200,128]{2,1,0:T(8,128)S(1)} %slice_add_fusion.20), channel_id=1, source_target_pairs={{0,16},{1,17},{2,18},{3,19},{4,20},{5,21},{6,22},{7,23},{8,24},{9,... | collective-permute-start | bytes 307208 | tf_op jit(solution)/shard_map/ppermute | solution.py:386
  194.4 9.0 %collective-permute-start.46 = (f32[2,208,128]{2,1,0:T(8,128)S(1)}, f32[2,208,128]{2,1,0:T(8,128)S(1)}, u32[]{:S(2)}, u32[]{:S(2)}) collective-permute-start(f32[2,208,128]{2,1,0:T(8,128)S(1)} %get-tuple-element.450), channel_id=1, source_target_pairs={{0,8},{1,9},{2,10},{3,11},{4,12},{5,13},{6,14},{7,15},{8,0},{9,1},... | collective-permute-start | bytes 638984 | tf_op jit(solution)/shard_map/ppermute | solution.py:386
  196.9 7.4 %collective-permute-start.35 = (f32[1,200,128]{2,1,0:T(8,128)S(1)}, f32[1,200,128]{2,1,0:T(8,128)S(1)}, u32[]{:S(2)}, u32[]{:S(2)}) collective-permute-start(f32[1,200,128]{2,1,0:T(8,128)S(1)} %fusion.1), channel_id=1, source_target_pairs={{0,16},{1,17},{2,18},{3,19},{4,20},{5,21},{6,22},{7,23},{8,24},{9,... | collective-permute-start | bytes 307208 | tf_op jit(solution)/shard_map/ppermute | solution.py:386
  203.4 6.6 %collective-permute-start.47 = (f32[1,208,128]{2,1,0:T(8,128)S(1)}, f32[1,208,128]{2,1,0:T(8,128)S(1)}, u32[]{:S(2)}, u32[]{:S(2)}) collective-permute-start(f32[1,208,128]{2,1,0:T(8,128)S(1)} %slice_add_fusion.18), channel_id=1, source_target_pairs={{0,16},{1,17},{2,18},{3,19},{4,20},{5,21},{6,22},{7,23},{8,24},{9,... | collective-permute-start | bytes 319496 | tf_op jit(solution)/shard_map/ppermute | solution.py:386
  204.3 13.2 %collective-permute-start.36 = (f32[2,200,128]{2,1,0:T(8,128)S(1)}, f32[2,200,128]{2,1,0:T(8,128)S(1)}, u32[]{:S(2)}, u32[]{:S(2)}) collective-permute-start(f32[2,200,128]{2,1,0:T(8,128)S(1)} %pad_maximum_fusion.8), channel_id=1, source_target_pairs={{0,8},{1,9},{2,10},{3,11},{4,12},{5,13},{6,14},{7,15},{8,0},{9,1},... | collective-permute-start | bytes 614408 | tf_op jit(solution)/shard_map/ppermute | solution.py:386
  210.1 7.3 %collective-permute-start.48 = (f32[1,208,128]{2,1,0:T(8,128)S(1)}, f32[1,208,128]{2,1,0:T(8,128)S(1)}, u32[]{:S(2)}, u32[]{:S(2)}) collective-permute-start(f32[1,208,128]{2,1,0:T(8,128)S(1)} %fusion), channel_id=1, source_target_pairs={{0,16},{1,17},{2,18},{3,19},{4,20},{5,21},{6,22},{7,23},{8,24},{9,... | collective-permute-start | bytes 319496 | tf_op jit(solution)/shard_map/ppermute | solution.py:386
  210.3 9.3 %collective-permute-start.28 = (f32[2,192,128]{2,1,0:T(8,128)S(1)}, f32[2,192,128]{2,1,0:T(8,128)S(1)}, u32[]{:S(2)}, u32[]{:S(2)}) collective-permute-start(f32[2,192,128]{2,1,0:T(8,128)S(1)} %pad_maximum_fusion.9), channel_id=1, source_target_pairs={{0,8},{1,9},{2,10},{3,11},{4,12},{5,13},{6,14},{7,15},{8,0},{9,1},... | collective-permute-start | bytes 589832 | tf_op jit(solution)/shard_map/ppermute | solution.py:386
  212.9 29.3 %collective-permute-start.43 = (f32[8,384,128]{2,1,0:T(8,128)S(1)}, f32[8,384,128]{2,1,0:T(8,128)S(1)}, u32[]{:S(2)}, u32[]{:S(2)}) collective-permute-start(f32[8,384,128]{2,1,0:T(8,128)S(1)} %constant_dynamic-update-slice_fusion.4.refs_0_), channel_id=1, source_target_pairs={{0,1},{1,0},{2,3},{3,2},{4,5},{5,4},{6,7},{7,6},{8,9},{9,8},{10,11... | collective-permute-start | bytes 4718600 | tf_op jit(solution)/shard_map/ppermute | solution.py:386
  217.3 7.0 %collective-permute-start.49 = (f32[2,208,128]{2,1,0:T(8,128)S(1)}, f32[2,208,128]{2,1,0:T(8,128)S(1)}, u32[]{:S(2)}, u32[]{:S(2)}) collective-permute-start(f32[2,208,128]{2,1,0:T(8,128)S(1)} %pad_maximum_fusion.7), channel_id=1, source_target_pairs={{0,8},{1,9},{2,10},{3,11},{4,12},{5,13},{6,14},{7,15},{8,0},{9,1},... | collective-permute-start | bytes 638984 | tf_op jit(solution)/shard_map/ppermute | solution.py:386
  217.4 24.8 %collective-permute-start.44 = (f32[8,384,128]{2,1,0:T(8,128)S(1)}, f32[8,384,128]{2,1,0:T(8,128)S(1)}, u32[]{:S(2)}, u32[]{:S(2)}) collective-permute-start(f32[8,384,128]{2,1,0:T(8,128)S(1)} %collective-permute-done.42.refs_1_), channel_id=1, source_target_pairs={{0,1},{1,0},{2,3},{3,2},{4,5},{5,4},{6,7},{7,6},{8,9},{9,8},{10,11... | collective-permute-start | bytes 4718600 | tf_op jit(solution)/shard_map/ppermute | solution.py:386
  217.6 8.0 %collective-permute-start.37 = (f32[4,200,128]{2,1,0:T(8,128)S(1)}, f32[4,200,128]{2,1,0:T(8,128)S(1)}, u32[]{:S(2)}, u32[]{:S(2)}) collective-permute-start(f32[4,200,128]{2,1,0:T(8,128)S(1)} %pad_maximum_fusion.4), channel_id=1, source_target_pairs={{0,4},{1,3},{2,6},{3,1},{4,0},{5,7},{6,2},{7,5},{8,12},{9,11},{10,... | collective-permute-start | bytes 1228808 | tf_op jit(solution)/shard_map/ppermute | solution.py:386
  219.6 11.8 %collective-permute-start.29 = (f32[4,192,128]{2,1,0:T(8,128)S(1)}, f32[4,192,128]{2,1,0:T(8,128)S(1)}, u32[]{:S(2)}, u32[]{:S(2)}) collective-permute-start(f32[4,192,128]{2,1,0:T(8,128)S(1)} %pad_maximum_fusion.6), channel_id=1, source_target_pairs={{0,4},{1,3},{2,6},{3,1},{4,0},{5,7},{6,2},{7,5},{8,12},{9,11},{10,... | collective-permute-start | bytes 1179656 | tf_op jit(solution)/shard_map/ppermute | solution.py:386
  224.4 16.1 %collective-permute-start.50 = (f32[4,208,128]{2,1,0:T(8,128)S(1)}, f32[4,208,128]{2,1,0:T(8,128)S(1)}, u32[]{:S(2)}, u32[]{:S(2)}) collective-permute-start(f32[4,208,128]{2,1,0:T(8,128)S(1)} %pad_maximum_fusion.3), channel_id=1, source_target_pairs={{0,4},{1,3},{2,6},{3,1},{4,0},{5,7},{6,2},{7,5},{8,12},{9,11},{10,... | collective-permute-start | bytes 1277960 | tf_op jit(solution)/shard_map/ppermute | solution.py:386
  225.6 16.6 %copy-start = (s32[2]{0:T(128)S(1)}, s32[2]{0:T(128)}, u32[]{:S(2)}) copy-start(s32[2]{0:T(128)} %pad_add_fusion.code_ref) | copy-start | bytes 28
  225.7 21.8 %collective-permute-start.38 = (f32[8,200,128]{2,1,0:T(8,128)S(1)}, f32[8,200,128]{2,1,0:T(8,128)S(1)}, u32[]{:S(2)}, u32[]{:S(2)}) collective-permute-start(f32[8,200,128]{2,1,0:T(8,128)S(1)} %pad_maximum_fusion.1.refs_0_), channel_id=1, source_target_pairs={{0,2},{1,5},{2,0},{3,7},{4,6},{5,1},{6,4},{7,3},{8,10},{9,13},{10,... | collective-permute-start | bytes 2457608 | tf_op jit(solution)/shard_map/ppermute | solution.py:386
  231.5 15.5 %collective-permute-start.31 = (f32[8,192,128]{2,1,0:T(8,128)S(1)}, f32[8,192,128]{2,1,0:T(8,128)S(1)}, u32[]{:S(2)}, u32[]{:S(2)}) collective-permute-start(f32[8,192,128]{2,1,0:T(8,128)S(1)} %constant_dynamic-update-slice_fusion.refs_0_), channel_id=1, source_target_pairs={{0,1},{1,0},{2,3},{3,2},{4,5},{5,4},{6,7},{7,6},{8,9},{9,8},{10,11... | collective-permute-start | bytes 2359304 | tf_op jit(solution)/shard_map/ppermute | solution.py:386
  240.6 12.0 %collective-permute-start.30 = (f32[8,192,128]{2,1,0:T(8,128)S(1)}, f32[8,192,128]{2,1,0:T(8,128)S(1)}, u32[]{:S(2)}, u32[]{:S(2)}) collective-permute-start(f32[8,192,128]{2,1,0:T(8,128)S(1)} %constant_dynamic-update-slice_fusion.refs_0_), channel_id=1, source_target_pairs={{0,2},{1,5},{2,0},{3,7},{4,6},{5,1},{6,4},{7,3},{8,10},{9,13},{10,... | collective-permute-start | bytes 2359304 | tf_op jit(solution)/shard_map/ppermute | solution.py:386
  246.5 14.0 %collective-permute-start.52 = (f32[8,208,128]{2,1,0:T(8,128)S(1)}, f32[8,208,128]{2,1,0:T(8,128)S(1)}, u32[]{:S(2)}, u32[]{:S(2)}) collective-permute-start(f32[8,208,128]{2,1,0:T(8,128)S(1)} %pad_maximum_fusion.refs_0_), channel_id=1, source_target_pairs={{0,1},{1,0},{2,3},{3,2},{4,5},{5,4},{6,7},{7,6},{8,9},{9,8},{10,11... | collective-permute-start | bytes 2555912 | tf_op jit(solution)/shard_map/ppermute | solution.py:386
  246.5 15.2 %collective-permute-start.51 = (f32[8,208,128]{2,1,0:T(8,128)S(1)}, f32[8,208,128]{2,1,0:T(8,128)S(1)}, u32[]{:S(2)}, u32[]{:S(2)}) collective-permute-start(f32[8,208,128]{2,1,0:T(8,128)S(1)} %pad_maximum_fusion.refs_0_), channel_id=1, source_target_pairs={{0,2},{1,5},{2,0},{3,7},{4,6},{5,1},{6,4},{7,3},{8,10},{9,13},{10,... | collective-permute-start | bytes 2555912 | tf_op jit(solution)/shard_map/ppermute | solution.py:386
  246.9 10.7 %collective-permute-start.39 = (f32[8,200,128]{2,1,0:T(8,128)S(1)}, f32[8,200,128]{2,1,0:T(8,128)S(1)}, u32[]{:S(2)}, u32[]{:S(2)}) collective-permute-start(f32[8,200,128]{2,1,0:T(8,128)S(1)} %pad_maximum_fusion.1.refs_0_), channel_id=1, source_target_pairs={{0,1},{1,0},{2,3},{3,2},{4,5},{5,4},{6,7},{7,6},{8,9},{9,8},{10,11... | collective-permute-start | bytes 2457608 | tf_op jit(solution)/shard_map/ppermute | solution.py:386
  247.5 10.1 %collective-permute-start.40 = (f32[8,200,128]{2,1,0:T(8,128)S(1)}, f32[8,200,128]{2,1,0:T(8,128)S(1)}, u32[]{:S(2)}, u32[]{:S(2)}) collective-permute-start(f32[8,200,128]{2,1,0:T(8,128)S(1)} %collective-permute-done.38.refs_1_), channel_id=1, source_target_pairs={{0,1},{1,0},{2,3},{3,2},{4,5},{5,4},{6,7},{7,6},{8,9},{9,8},{10,11... | collective-permute-start | bytes 2457608 | tf_op jit(solution)/shard_map/ppermute | solution.py:386
  252.5 2.3 collective-permute-start.32
  261.7 2.4 collective-permute-start.53
  (4 other events, 5.1 us)

commit v3 on v0

v3 whole, which is shorter than its diff:
```python
import functools

import jax
import jax.numpy as jnp
from jax import lax
from jax.experimental import pallas as pl
from jax.experimental.pallas import tpu as pltpu
from jax.sharding import PartitionSpec as P

HEADS = 6
HEAD_DIM = 64
PAIRS = HEADS // 2
PAIR = 2 * HEAD_DIM
INNER = HEADS * HEAD_DIM
BLOCKS = 32
HALF = 16
EPSILON = 1e-06
F32 = jnp.float32
BF16 = jnp.bfloat16
VMEM = pltpu.VMEM
SMEM = pltpu.SMEM


def dot_plain(left_op, right_op):
    return jnp.dot(left_op, right_op, preferred_element_type=F32)


def dot_rows(left_op, right_op):
    return lax.dot_general(left_op, right_op, (((0,), (0,)), ((), ())), preferred_element_type=F32)


def dot_back(left_op, right_op):
    return lax.dot_general(left_op, right_op, (((1,), (1,)), ((), ())), preferred_element_type=F32)


def inverse_rms(values):
    return lax.rsqrt(jnp.mean(values * values, axis=-1, keepdims=True) + EPSILON)


def norm_backward(values, gain, grad):
    inverse = inverse_rms(values)
    unit = values * inverse
    scaled = grad * gain
    along = jnp.mean(scaled * unit, axis=-1, keepdims=True)
    return inverse * (scaled - unit * along), jnp.sum(grad * unit, axis=0, keepdims=True)


def lane_masks():
    lane = lax.broadcasted_iota(jnp.int32, (1, PAIR), 1)
    first = jnp.where(lane < HEAD_DIM, 1.0, 0.0)
    return first.astype(BF16), (1.0 - first).astype(BF16)


def stack_heads(values):
    first, second = lane_masks()
    return jnp.concatenate([values * first, values * second], axis=0)


def fold_heads(values):
    half = values.shape[0] // 2
    lane = lax.broadcasted_iota(jnp.int32, (half, PAIR), 1)
    return jnp.where(lane < HEAD_DIM, values[:half], values[half:])


def pair_forward(queries, key_rows, value_rows, allowed):
    keys = key_rows.shape[0]
    scores = dot_back(stack_heads(key_rows), queries).reshape(2, keys, queries.shape[0])
    if allowed is not None:
        scores = jnp.where(allowed, scores, -1000000000.0)
    expo = jnp.exp(scores - jnp.max(scores, axis=1, keepdims=True))
    chances = expo * (1.0 / jnp.sum(expo, axis=1, keepdims=True))
    chances = chances.reshape(2 * keys, queries.shape[0]).astype(BF16)
    return chances, dot_rows(chances, stack_heads(value_rows)).astype(BF16)


def pair_backward(queries, key_rows, value_rows, chances, grad_mixed):
    keys, count = key_rows.shape[0], queries.shape[0]
    wide = chances.astype(F32)
    grad_chances = dot_back(stack_heads(value_rows), grad_mixed)
    product = wide * grad_chances
    inner = jnp.sum(product.reshape(2, keys, count), axis=1, keepdims=True)
    spread = (wide.reshape(2, keys, count) * inner).reshape(2 * keys, count)
    grad_scores = (product - spread).astype(BF16)
    grad_values = fold_heads(dot_plain(chances, grad_mixed))
    grad_keys = fold_heads(dot_plain(grad_scores, queries))
    grad_queries = dot_rows(grad_scores, stack_heads(key_rows)) * 0.125
    return grad_queries.astype(BF16), grad_keys.astype(BF16), grad_values.astype(BF16)


def pair_lanes(index, offset=0):
    return pl.ds(offset + index * PAIR, PAIR)


def count_kernel(me_ref, len_ref, member_ref, count_ref, code_ref):
    me = me_ref[0]
    count = sum(len_ref[s] for s in range(len_ref.shape[0])).astype(F32)
    in_first = member_ref[me] == 1
    count_ref[0] = jnp.where(in_first, count, 0.0)
    count_ref[1] = jnp.where(in_first, 0.0, count)
    code_ref[0], code_ref[1] = code_pair(me)


def weigh_kernel(me_ref, member_ref, mix_ref, *refs):
    me = me_ref[0]
    parts, (weight_ref, own_ref, other_ref) = refs[:-3], refs[-3:]
    count_one = sum(part[0] for part in parts)
    count_two = sum(part[1] for part in parts)
    total = count_one + count_two
    first = mix_ref[0] * total / count_one
    second = mix_ref[1] * total / count_two
    own = jnp.where(member_ref[me] == 1, first, second)
    other = jnp.where(member_ref[me ^ 1] == 1, first, second)
    weight_ref[0], weight_ref[1] = own, other
    own_ref[...] = jnp.full(own_ref.shape, own)
    other_ref[...] = jnp.full(other_ref.shape, other)


def add_to(ref, first, value):
    @pl.when(first)
    def fresh():
        ref[...] = value

    @pl.when(jnp.logical_not(first))
    def more():
        ref[...] += value


def gelu_parts(gate):
    slant = 0.7978845608028654
    square = gate * gate
    tanh = jnp.tanh(gate * (slant + (slant * 0.044715) * square))
    half = 0.5 + 0.5 * tanh
    slope = half + (0.5 * gate) * (1.0 - tanh * tanh) * (slant + (3.0 * slant * 0.044715) * square)
    return gate * half, slope


def forward_kernel(
    len_ref, code_ref,
    patch_ref, tok_ref, cot_ref,
    wp_ref, bias_ref, wck_ref, wcv_ref,
    g1_ref, wq_ref, wk_ref, wv_ref, wo_ref, g2_ref, wcq_ref, wco_ref, g3_ref, wg_ref, wu_ref, wd_ref,
    feat_ref, kv_ref, qkv_ref, pt_ref, o_ref, x1_ref, cq_ref, pc_ref, oc_ref,
    out_ref, dx2_ref, gain_ref, keep_low, keep_high, send_low, send_high,
    join_kv, join_qkv, wcq, h3_all, de_all, hid_all, dgate_all, dup_all, acc_down, acc_gate, acc_up,
):
    step, steps = pl.program_id(0), pl.num_programs(0)

    @pl.when(step == 0)
    def join():
        join_kv[:, :INNER] = wck_ref[...]
        join_kv[:, INNER:] = wcv_ref[...]
        join_qkv[:, :INNER] = wq_ref[...] * 0.125
        join_qkv[:, INNER : 2 * INNER] = wk_ref[...]
        join_qkv[:, 2 * INNER :] = wv_ref[...]
        wcq[...] = wcq_ref[...] * 0.125

    seqs, _, _, maxlen = pt_ref.shape
    patches = pc_ref.shape[2] // 2
    feat = (dot_plain(patch_ref[...], wp_ref[...]) + bias_ref[...]).astype(BF16)
    feat_ref[...] = feat
    kv_ref[...] = dot_plain(feat, join_kv[...]).astype(BF16)
    x = tok_ref[...].astype(F32)
    h1 = (x * inverse_rms(x) * g1_ref[...]).astype(BF16)
    qkv_ref[...] = dot_plain(h1, join_qkv[...]).astype(BF16)
    key_at = lax.broadcasted_iota(jnp.int32, (1, maxlen, maxlen), 1)
    query_at = lax.broadcasted_iota(jnp.int32, (1, maxlen, maxlen), 2)
    for s in range(seqs):
        rows = pl.ds(s * maxlen, maxlen)
        allowed = (key_at <= query_at) & (key_at < len_ref[step * seqs + s])
        for p in range(PAIRS):
            pt_ref[s, p], o_ref[rows, pair_lanes(p)] = pair_forward(
                qkv_ref[rows, pair_lanes(p)],
                qkv_ref[rows, pair_lanes(p, INNER)],
                qkv_ref[rows, pair_lanes(p, 2 * INNER)],
                allowed,
            )
    x1 = x + dot_plain(o_ref[...], wo_ref[...])
    x1_ref[...] = x1
    h2 = (x1 * inverse_rms(x1) * g2_ref[...]).astype(BF16)
    cq_ref[...] = dot_plain(h2, wcq[...]).astype(BF16)
    for s in range(seqs):
        rows, wide = pl.ds(s * maxlen, maxlen), pl.ds(s * patches, patches)
        for p in range(PAIRS):
            pc_ref[s, p], oc_ref[rows, pair_lanes(p)] = pair_forward(
                cq_ref[rows, pair_lanes(p)],
                kv_ref[wide, pair_lanes(p)],
                kv_ref[wide, pair_lanes(p, INNER)],
                None,
            )
    x2 = x1_ref[...] + dot_plain(oc_ref[...], wco_ref[...])
    h3 = (x2 * inverse_rms(x2) * g3_ref[...]).astype(BF16)
    at = lax.broadcasted_iota(jnp.int32, (maxlen, 1), 0)
    keep = jnp.concatenate(
        [jnp.where(at < len_ref[step * seqs + s], 1.0, 0.0) for s in range(seqs)], axis=0
    )
    e = cot_ref[...].astype(F32) * keep
    de = e.astype(BF16)
    count = x2.shape[0]
    here = pl.ds(pl.multiple_of(step * count, count), count)
    h3_all[here, :] = h3
    de_all[here, :] = de
    span = wg_ref.shape[1]
    chunk = 256
    for c in range(span // chunk):
        cols = pl.ds(c * chunk, chunk)
        gate = dot_plain(h3, wg_ref[:, cols])
        up = dot_plain(h3, wu_ref[:, cols])
        grad = dot_back(de, wd_ref[cols, :])
        gelu, slope = gelu_parts(gate)
        hid = (gelu * up).astype(BF16)
        dgate = (grad * up * slope).astype(BF16)
        dup = (grad * gelu).astype(BF16)
        hid_all[here, cols] = hid
        dgate_all[here, cols] = dgate
        dup_all[here, cols] = dup

    out_ref[...] = (x2 + dot_plain(hid_all[here, :], wd_ref[...])).astype(BF16)
    dh3 = dot_back(dgate_all[here, :], wg_ref[...]) + dot_back(dup_all[here, :], wu_ref[...])
    dx, gain = norm_backward(x2, g3_ref[...], dh3)
    dx2_ref[...] = e + dx
    add_to(gain_ref, step == 0, gain)

    @pl.when(step == steps - 1)
    def finish():
        for c in range(span // chunk):
            cols = pl.ds(c * chunk, chunk)
            acc_down[cols, :] = dot_rows(hid_all[:, cols], de_all[...])
            acc_gate[:, cols] = dot_rows(h3_all[...], dgate_all[:, cols])
            acc_up[:, cols] = dot_rows(h3_all[...], dup_all[:, cols])
        items = [(acc_down, acc_down.shape, 0), (acc_gate, acc_gate.shape, 0), (acc_up, acc_up.shape, 0)]
        pack(items, code_ref, keep_low, keep_high, send_low, send_high)


def cross_backward_kernel(
    code_ref, dx2_ref, cq_ref, pt_ref, kv_ref, x1_ref, oc_ref, feat_ref,
    g2_ref, wco_ref, wcq_ref, wck_ref, wcv_ref,
    dfeat_ref, dx1_ref, gain_ref, bias_ref, keep_low, keep_high, send_low, send_high,
    joined, dcq_all, dkv_all, dc_all, h2_all, oc_all, feat_all, acc_out, acc_query, acc_kv,
):
    step, steps = pl.program_id(0), pl.num_programs(0)

    @pl.when(step == 0)
    def join():
        joined[:, :INNER] = wck_ref[...]
        joined[:, INNER:] = wcv_ref[...]

    seqs, _, both, maxlen = pt_ref.shape
    patches = both // 2
    count, wide_count = seqs * maxlen, seqs * patches
    here = pl.ds(pl.multiple_of(step * count, count), count)
    wide_here = pl.ds(pl.multiple_of(step * wide_count, wide_count), wide_count)
    dx2 = dx2_ref[...]
    dc = dx2.astype(BF16)
    dc_all[here, :] = dc
    oc_all[here, :] = oc_ref[...]
    feat_all[wide_here, :] = feat_ref[...]
    doc = dot_back(dc, wco_ref[...]).astype(BF16)
    for s in range(seqs):
        rows, wide = pl.ds(s * maxlen, maxlen), pl.ds(s * patches, patches)
        at = pl.ds(pl.multiple_of(step * count + s * maxlen, maxlen), maxlen)
        wide_at = pl.ds(pl.multiple_of(step * wide_count + s * patches, patches), patches)
        for p in range(PAIRS):
            keys, values = pair_lanes(p), pair_lanes(p, INNER)
            dcq_all[at, keys], dkv_all[wide_at, keys], dkv_all[wide_at, values] = pair_backward(
                cq_ref[rows, keys],
                kv_ref[wide, keys],
                kv_ref[wide, values],
                pt_ref[s, p],
                doc[s * maxlen : (s + 1) * maxlen, p * PAIR : (p + 1) * PAIR],
            )
    dfeat = dot_back(dkv_all[wide_here, :], joined[...]).astype(BF16)
    dfeat_ref[...] = dfeat
    dh2 = dot_back(dcq_all[here, :], wcq_ref[...])
    x1 = x1_ref[...]
    h2_all[here, :] = (x1 * inverse_rms(x1) * g2_ref[...]).astype(BF16)
    dx, gain = norm_backward(x1, g2_ref[...], dh2)
    dx1_ref[...] = dx2 + dx
    add_to(gain_ref, step == 0, gain)
    add_to(bias_ref, step == 0, jnp.sum(dfeat.astype(F32), axis=0, keepdims=True))

    @pl.when(step == steps - 1)
    def finish():
        acc_out[...] = dot_rows(oc_all[...], dc_all[...])
        acc_query[...] = dot_rows(h2_all[...], dcq_all[...])
        acc_kv[...] = dot_rows(feat_all[...], dkv_all[...])
        small = acc_query.shape
        items = [(acc_out, acc_out.shape, 0), (acc_query, small, 0)]
        items += [(acc_kv, small, 0), (acc_kv, small, INNER)]
        pack(items, code_ref, keep_low, keep_high, send_low, send_high)


def patch_weight_kernel(code_ref, patch_ref, dfeat_ref, keep_low, keep_high, send_low, send_high, acc, turned):
    step, steps = pl.program_id(0), pl.num_programs(0)
    add_to(acc, step == 0, dot_rows(dfeat_ref[...], patch_ref[...]))

    @pl.when(step == steps - 1)
    def finish():
        turned[...] = acc[...].T
        pack([(turned, turned.shape, 0)], code_ref, keep_low, keep_high, send_low, send_high)


def patch_input_kernel(weight_ref, dfeat_ref, w_ref, *refs):
    refs[-1][...] = dot_back(dfeat_ref[...], w_ref[...]) * weight_ref[0]


def self_backward_kernel(
    code_ref, weight_ref, dx1_ref, qkv_ref, pt_ref, tok_ref, o_ref,
    g1_ref, wo_ref, wq_ref, wk_ref, wv_ref, gain_two_ref, gain_three_ref, bias_ref,
    dtok_ref, keep_low, keep_high, send_low, send_high,
    joined, dqkv_all, da_all, h1_all, o_all, acc_out, acc_qkv, gain_one, gain_block,
):
    step, steps = pl.program_id(0), pl.num_programs(0)

    @pl.when(step == 0)
    def join():
        joined[:, :INNER] = wq_ref[...]
        joined[:, INNER : 2 * INNER] = wk_ref[...]
        joined[:, 2 * INNER :] = wv_ref[...]

    seqs, _, _, maxlen = pt_ref.shape
    count = seqs * maxlen
    here = pl.ds(pl.multiple_of(step * count, count), count)
    dx1 = dx1_ref[...]
    da = dx1.astype(BF16)
    da_all[here, :] = da
    o_all[here, :] = o_ref[...]
    do = dot_back(da, wo_ref[...]).astype(BF16)
    for s in range(seqs):
        rows = pl.ds(s * maxlen, maxlen)
        at = pl.ds(pl.multiple_of(step * count + s * maxlen, maxlen), maxlen)
        for p in range(PAIRS):
            lanes = [pair_lanes(p, k * INNER) for k in range(3)]
            dqkv_all[at, lanes[0]], dqkv_all[at, lanes[1]], dqkv_all[at, lanes[2]] = pair_backward(
                qkv_ref[rows, lanes[0]],
                qkv_ref[rows, lanes[1]],
                qkv_ref[rows, lanes[2]],
                pt_ref[s, p],
                do[s * maxlen : (s + 1) * maxlen, p * PAIR : (p + 1) * PAIR],
            )
    dh1 = dot_back(dqkv_all[here, :], joined[...])
    x = tok_ref[...].astype(F32)
    h1_all[here, :] = (x * inverse_rms(x) * g1_ref[...]).astype(BF16)
    dx, gain = norm_backward(x, g1_ref[...], dh1)
    dtok_ref[...] = (dx1 + dx) * weight_ref[0]
    add_to(gain_one, step == 0, gain)

    @pl.when(step == steps - 1)
    def finish():
        acc_out[...] = dot_rows(o_all[...], da_all[...])
        acc_qkv[...] = dot_rows(h1_all[...], dqkv_all[...])
        gain_block[...] = jnp.zeros_like(gain_block)
        for k, ref in enumerate((gain_one, gain_two_ref, gain_three_ref, bias_ref)):
            for t in range(4):
                gain_block[pl.ds((4 * k + t) * 8, 1), :] = ref[:, pl.ds(t * 128, 128)]
        small = (acc_qkv.shape[0], INNER)
        items = [(acc_out, acc_out.shape, 0)]
        items += [(acc_qkv, small, k * INNER) for k in range(3)]
        items += [(gain_block, gain_block.shape, 0)]
        pack(items, code_ref, keep_low, keep_high, send_low, send_high)


def flips(count, first, second):
    return [(i, i ^ (first if i % 2 == 0 else second)) for i in range(count)]


def code_pair(me):
    core, ex, why = me & 1, (me >> 1) & 1, (me >> 2) & 1
    near, far = (me >> 3) & 1, (me >> 4) & 1
    even = ex * 8 + why * 4 + near * 2 + far
    odd = why * 8 + ex * 4 + far * 2 + near
    own = core * 16 + jnp.where(core == 0, even, odd)
    other = (1 - core) * 16 + jnp.where(core == 0, odd, even)
    return own, other


def exchange(values, first, second=None):
    count = lax.axis_size("dp")
    return lax.ppermute(values, "dp", flips(count, first, first if second is None else second))


def block_rows(shape):
    return shape[0] * shape[1] // (BLOCKS * 128)


def block_parts(shape, index, offset):
    rows, lanes = shape
    tiles = lanes // 128
    if BLOCKS % tiles:
        height = rows // BLOCKS
        return [
            (pl.ds(pl.multiple_of(index * height, 8), height), pl.ds(offset + t * 128, 128))
            for t in range(tiles)
        ]
    height = rows * tiles // BLOCKS
    row, lane = index // tiles, index % tiles
    return [
        (
            pl.ds(pl.multiple_of(row * height, 8), height),
            pl.ds(pl.multiple_of(offset + lane * 128, 128), 128),
        )
    ]


def pack(items, code_ref, *out_refs):
    def step(p, carry):
        for k, out_ref in enumerate(out_refs):
            start = 0
            index = (p + 8 * (k % 2)) ^ code_ref[k // 2]
            for ref, shape, offset in items:
                for rows, lanes in block_parts(shape, index, offset):
                    out_ref[p, pl.ds(start, rows.size), :] = ref[rows, lanes]
                    start += rows.size
        return carry

    lax.fori_loop(0, 8, step, 0)


def unpack_kernel(shapes, with_gains, code_ref, *refs):
    ins, outs = refs[:4], refs[4:]
    for k, piece in enumerate(ins):

        def step(p, carry, piece=piece, k=k):
            index = (p + 8 * (k % 2)) ^ code_ref[k // 2]
            start = 0
            for shape, out_ref in zip(shapes, outs):
                for rows, lanes in block_parts(shape, index, 0):
                    out_ref[rows, lanes] = piece[p, pl.ds(start, rows.size), :]
                    start += rows.size
            return carry

        lax.fori_loop(0, 8, step, 0)
    if with_gains:
        count = len(shapes)
        block = outs[count - 1]
        for k, out_ref in enumerate(outs[count:]):
            for t in range(4):
                out_ref[:, pl.ds(t * 128, 128)] = block[pl.ds((4 * k + t) * 8, 1), :]


def vmem(count):
    return [pl.BlockSpec(memory_space=VMEM)] * count


def unpack(pieces, shapes, codes, with_gains=False):
    outs = [jax.ShapeDtypeStruct(s, F32) for s in shapes]
    if with_gains:
        outs += [jax.ShapeDtypeStruct((1, 512), F32)] * 4
    return pl.pallas_call(
        functools.partial(unpack_kernel, shapes, with_gains),
        out_shape=outs,
        in_specs=[pl.BlockSpec(memory_space=SMEM)] + vmem(4),
        out_specs=vmem(len(outs)),
        compiler_params=pltpu.CompilerParams(vmem_limit_bytes=40 * 2**20),
        name="unpack",
    )(codes, *pieces)


class Chunk:
    def __init__(self, packed, shapes, codes, weights=None, with_gains=False):
        self.held, self.got, self.stage = tuple(packed), (), 0
        self.shapes, self.codes, self.weights, self.with_gains = shapes, codes, weights, with_gains

    def advance(self, token):
        (self.held, self.got), token = lax.optimization_barrier(((self.held, self.got), token))
        take, send = STAGES[self.stage]
        self.stage += 1
        if take is not None:
            take(self)
        send(self)
        return self.held[0]

    def send_cores(self):
        _, _, low, high = self.held
        self.got = (exchange(high, 1), exchange(low, 1))

    def take_cores(self):
        keep_low, keep_high, _, _ = self.held
        high, low = self.got
        self.held = (keep_high * self.weights[0] + high * self.weights[1], keep_low)
        self.got = (low,)

    def send_first(self):
        self.got += (exchange(self.held[0], 2, 4),)

    def take_first(self):
        (_, keep), (low, got) = self.held, self.got
        keep = keep * self.weights[0] + low * self.weights[1]
        self.held = (keep[4:] + got[4:], keep[:4] + got[:4])

    def take_half(self):
        (_, keep), (got,) = self.held, self.got
        half = keep.shape[0] // 2
        self.held = (keep[half:] + got[half:], keep[:half] + got[:half])

    def take_last(self):
        total = self.held[1] + self.got[0]
        extra = BLOCKS
        while extra < lax.axis_size("dp"):
            total = total + exchange(total, extra)
            extra *= 2
        self.held = (total,)

    def take_back(self):
        self.held = (jnp.concatenate([*self.held, *self.got]),)

    def send_second(self):
        self.got = (exchange(self.held[0], 4, 2),)

    def send_third(self):
        self.got = (exchange(self.held[0], 8, 16),)

    def send_fourth(self):
        self.got = (exchange(self.held[0], 16, 8),)

    def send_back_first(self):
        self.got = (exchange(self.held[0], 2, 4), exchange(self.held[0], 1))

    def send_back_cores(self):
        self.held = (self.held[0], *self.got)
        self.got = (exchange(self.held[1], 1),)

    def unpack(self, token):
        (held, got), token = lax.optimization_barrier(((self.held, self.got), token))
        return unpack(held + got, self.shapes, self.codes, self.with_gains)


STAGES = (
    (None, Chunk.send_cores),
    (Chunk.take_cores, Chunk.send_first),
    (Chunk.take_first, Chunk.send_second),
    (Chunk.take_half, Chunk.send_third),
    (Chunk.take_half, Chunk.send_fourth),
    (Chunk.take_last, Chunk.send_fourth),
    (Chunk.take_back, Chunk.send_third),
    (Chunk.take_back, Chunk.send_second),
    (Chunk.take_back, Chunk.send_back_first),
    (None, Chunk.send_back_cores),
)


def by_step(array_shape, steps):
    block = (array_shape[0] // steps,) + tuple(array_shape[1:])
    return pl.BlockSpec(block, lambda i: (i,) + (0,) * (len(block) - 1))


def whole(array_shape):
    return pl.BlockSpec(tuple(array_shape), lambda i: (0,) * len(array_shape))


SCALARS = pl.BlockSpec(memory_space=SMEM)


def run_small(kernel, name, operands, outs, ins=None):
    return pl.pallas_call(
        kernel,
        out_shape=[jax.ShapeDtypeStruct(s, d) for s, d, _ in outs],
        in_specs=ins or [SCALARS] * len(operands),
        out_specs=[spec for _, _, spec in outs],
        name=name,
    )(*operands)


def run(kernel, name, steps, scalars, stepped, fixed, order, outs, scratch, cost):
    lists = {"s": iter(scalars), "r": iter(stepped), "f": iter(fixed)}
    operands = [next(lists[c]) for c in order]
    in_specs = [
        SCALARS if c == "s" else by_step(v.shape, steps) if c == "r" else whole(v.shape)
        for c, v in zip(order, operands)
    ]
    return pl.pallas_call(
        kernel,
        grid=(steps,),
        out_shape=[jax.ShapeDtypeStruct(s, d) for s, d, _ in outs],
        in_specs=in_specs,
        out_specs=[
            SCALARS if moves is None else by_step(s, steps) if moves else whole(s)
            for s, _, moves in outs
        ],
        scratch_shapes=[VMEM(s, d) for s, d in scratch],
        compiler_params=pltpu.CompilerParams(vmem_limit_bytes=56 * 2**20),
        cost_estimate=pl.CostEstimate(flops=int(cost * 1e9), bytes_accessed=2**20, transcendentals=0),
        name=name,
    )(*operands)


def local(
    tokens,
    cotangent,
    patches,
    lengths,
    group_member,
    mix,
    gain_one,
    w_query,
    w_key,
    w_value,
    w_out,
    gain_two,
    w_patch,
    bias_patch,
    w_cross_query,
    w_cross_key,
    w_cross_value,
    w_cross_out,
    gain_three,
    w_gate,
    w_up,
    w_down,
):
    seqs = lengths.shape[0]
    rows, width = tokens.shape
    maxlen = rows // seqs
    images, patch_dim = patches.shape[1], patches.shape[2]
    image_rows = seqs * images
    wide = w_gate.shape[1]
    steps = seqs // 2
    part = rows // steps
    flat = patches.reshape(image_rows, patch_dim)
    gain_one, gain_two, gain_three, bias_patch = (
        g.reshape(1, width) for g in (gain_one, gain_two, gain_three, bias_patch)
    )

    me_ref = lax.axis_index("dp")[None].astype(jnp.int32)
    in_vmem = pl.BlockSpec(memory_space=VMEM)
    counts, codes = run_small(
        count_kernel, "count", [me_ref, lengths, group_member],
        [((2,), F32, SCALARS), ((2,), jnp.int32, SCALARS)],
    )
    devices = lax.axis_size("dp")
    counts = counts + exchange(counts, 1)
    flat, counts = lax.optimization_barrier((flat, counts))
    column = [counts] + [exchange(counts, bit) for bit in (8, 16, 24)]
    late_shapes = [w_down.shape, w_gate.shape, w_up.shape]
    late_rows = sum(block_rows(s) for s in late_shapes)
    (
        feat, cross_kv, qkv, chances, mixed, x1, cross_q, cross_chances, cross_mixed, result, dx2, gain3, *late
    ) = run(
        forward_kernel, "forward", steps, [lengths, codes], [flat, tokens, cotangent],
        [
            w_patch, bias_patch, w_cross_key, w_cross_value,
            gain_one, w_query, w_key, w_value, w_out, gain_two, w_cross_query, w_cross_out,
            gain_three, w_gate, w_up, w_down,
        ],
        "ssrrr" + "f" * 16,
        [
            ((image_rows, width), BF16, True),
            ((image_rows, 2 * INNER), BF16, True),
            ((rows, 3 * INNER), BF16, True),
            ((seqs, PAIRS, 2 * maxlen, maxlen), BF16, True),
            ((rows, INNER), BF16, True),
            ((rows, width), F32, True),
            ((rows, INNER), BF16, True),
            ((seqs, PAIRS, 2 * images, maxlen), BF16, True),
            ((rows, INNER), BF16, True),
            ((rows, width), BF16, True),
            ((rows, width), F32, True),
            ((1, width), F32, False),
        ] + [((8, late_rows, 128), F32, False)] * 4,
        [
            ((width, 2 * INNER), BF16),
            ((width, 3 * INNER), BF16),
            ((width, INNER), BF16),
            ((rows, width), BF16),
            ((rows, width), BF16),
            ((rows, wide), BF16),
            ((rows, wide), BF16),
            ((rows, wide), BF16),
            (w_down.shape, F32),
            (w_gate.shape, F32),
            (w_up.shape, F32),
        ],
        40.0,
    )
    late, column = lax.optimization_barrier((late, column))
    late = Chunk(late, late_shapes, codes)
    token = late.advance(dx2)
    column, token = lax.optimization_barrier((column, token))
    counts = sum(column)
    bit = BLOCKS
    while bit < devices:
        counts = counts + exchange(counts, bit)
        bit *= 2
    counts = counts + exchange(counts, 2)
    parts = [counts, exchange(counts, 4)]
    row = (1, 1, 128)
    weights, *rows_of_weights = run_small(
        weigh_kernel, "weigh", [me_ref, group_member, mix, *parts],
        [((2,), F32, SCALARS), (row, F32, in_vmem), (row, F32, in_vmem)],
    )
    late.weights = rows_of_weights
    token = weights

    def cross_backward(token):
        tied, token = lax.optimization_barrier((dx2, token))
        cross_shapes = [w_cross_out.shape, w_cross_query.shape, w_cross_key.shape, w_cross_value.shape]
        cross_rows = sum(block_rows(s) for s in cross_shapes)
        dfeat, dx1, gain2, dbias, *cross = run(
            cross_backward_kernel, "cross_backward", steps, [codes],
            [tied, cross_q, cross_chances, cross_kv, x1, cross_mixed, feat],
            [gain_two, w_cross_out, w_cross_query, w_cross_key, w_cross_value], "srrrrrrrfffff",
            [
                ((image_rows, width), BF16, True),
                ((rows, width), F32, True),
                ((1, width), F32, False),
                ((1, width), F32, False),
            ] + [((8, cross_rows, 128), F32, False)] * 4,
            [
                ((width, 2 * INNER), BF16),
                ((rows, INNER), BF16),
                ((image_rows, 2 * INNER), BF16),
                ((rows, width), BF16),
                ((rows, width), BF16),
                ((rows, INNER), BF16),
                ((image_rows, width), BF16),
                (w_cross_out.shape, F32),
                (w_cross_query.shape, F32),
                ((width, 2 * INNER), F32),
            ],
            20.0,
        )
        return (dfeat, dx1, gain2, dbias), Chunk(cross, cross_shapes, codes, late.weights)

    def self_backward(token, dx1, gain2, dbias):
        tied, token = lax.optimization_barrier((dx1, token))
        own_shapes = [w_out.shape, w_query.shape, w_key.shape, w_value.shape, (BLOCKS * 8, 128)]
        own_rows = sum(block_rows(s) for s in own_shapes)
        grad_tokens, *own = run(
            self_backward_kernel, "self_backward", steps, [codes, weights],
            [tied, qkv, chances, tokens, mixed],
            [gain_one, w_out, w_query, w_key, w_value, gain2, gain3, dbias], "ssrrrrr" + "f" * 8,
            [((rows, width), F32, True)] + [((8, own_rows, 128), F32, False)] * 4,
            [
                ((width, 3 * INNER), BF16),
                ((rows, 3 * INNER), BF16),
                ((rows, width), BF16),
                ((rows, width), BF16),
                ((rows, INNER), BF16),
                (w_out.shape, F32),
                ((width, 3 * INNER), F32),
                ((1, width), F32),
                ((BLOCKS * 8, 128), F32),
            ],
            16.0,
        )
        return grad_tokens, Chunk(own, own_shapes, codes, late.weights, True)

    def patch_weight(token, dfeat):
        tied, token = lax.optimization_barrier((dfeat, token))
        patch_shapes = [w_patch.shape]
        patch_rows = block_rows(w_patch.shape)
        patch = run(
            patch_weight_kernel, "patch_weight", steps, [codes], [flat, tied], [], "srr",
            [((8, patch_rows, 128), F32, False)] * 4,
            [((width, patch_dim), F32), ((patch_dim, width), F32)], 12.0,
        )
        return Chunk(patch, patch_shapes, codes, late.weights)

    def patch_input(token, dfeat, half, out):
        tied, token = lax.optimization_barrier((dfeat, token))
        return pl.pallas_call(
            patch_input_kernel,
            grid=(steps,),
            out_shape=jax.ShapeDtypeStruct((image_rows, patch_dim), F32),
            in_specs=[
                SCALARS,
                pl.BlockSpec((image_rows // (2 * steps), width), lambda i: (i + half * steps, 0)),
                whole(w_patch.shape),
            ]
            + [pl.BlockSpec(memory_space=pl.ANY)] * len(out),
            out_specs=pl.BlockSpec((image_rows // (2 * steps), patch_dim), lambda i: (i + half * steps, 0)),
            input_output_aliases={3: 0} if out else {},
            compiler_params=pltpu.CompilerParams(vmem_limit_bytes=32 * 2**20),
            cost_estimate=pl.CostEstimate(flops=6 * 10**9, bytes_accessed=2**20, transcendentals=0),
            name="patch_input",
        )(weights, tied, w_patch, *out)

    chunks, done, grad_patches = {"late": late}, {}, ()
    for name in (
        "late", "cross kernel", "late", "cross", "self kernel", "cross", "own", "late",
        "patch kernel", "late", "own", "patch", "cross", "patch", "late", "input kernel",
        "cross", "own", "late", "input kernel", "cross", "patch", "own", "late", "cross",
        "patch", "own", "cross", "late", "patch", "own", "cross", "patch", "own", "cross",
        "late", "patch", "own", "late", "cross", "patch", "own", "cross", "patch", "own", "own",
        "patch", "patch",
    ):
        if name == "cross kernel":
            (dfeat, dx1, gain2, dbias), chunks["cross"] = cross_backward(token)
            token = dx1
        elif name == "self kernel":
            grad_tokens, chunks["own"] = self_backward(token, dx1, gain2, dbias)
            token = grad_tokens
        elif name == "patch kernel":
            chunks["patch"] = patch_weight(token, dfeat)
            token = chunks["patch"].held
        elif name == "input kernel":
            half = len(grad_patches)
            grad_patches = (patch_input(token, dfeat, half, grad_patches),)
            token = grad_patches
        elif chunks[name].stage < len(STAGES):
            token = chunks[name].advance(token)
        else:
            done[name] = chunks[name].unpack(token)
            token = done[name]
    (grad_patches,) = grad_patches
    late, cross, own, patch = (done[name] for name in ("late", "cross", "own", "patch"))
    gains = [g.reshape(width) for g in own[5:]]
    return (
        result,
        grad_tokens,
        grad_patches.reshape(seqs, images, patch_dim),
        gains[0],
        own[1],
        own[2],
        own[3],
        own[0],
        gains[1],
        patch[0],
        gains[3],
        cross[1],
        cross[2],
        cross[3],
        cross[0],
        gains[2],
        late[1],
        late[2],
        late[0],
    )


def solution(mesh):
    split = P("dp", None)
    images = P("dp", None, None)
    return jax.shard_map(
        local,
        mesh=mesh,
        in_specs=(split, split, images, P("dp")) + (P(),) * 18,
        out_specs=(split, split, images) + (P(),) * 16,
        check_vma=False,
    )
```

time: 359 us -> 243 us (0.68)
  waiting for transfers between devices: 136 us -> 69.3 us
  Pallas kernels: 130 us -> 111 us
  other arithmetic: 15.8 us -> 4.02 us
  local copies, waits for them, and re-layouts: 10.2 us -> 2.33 us
  starting transfers between devices: 61 us -> 55.2 us
  between operations: 5.65 us -> 1.27 us
    ppermute x49 -> x54, waiting for transfers between devices: 136 us -> 69.3 us  [exchange(): lax.ppermute(values, 'dp', flips(count, first, first if second is None el...]
    pallas_call x8 -> x4, Pallas kernels: 114 us -> 85.4 us  [run(): pl.pallas_call(kernel, grid=(steps,), out_shape=[jax.ShapeDtypeStruct(s,...]
    pallas_call x0 -> x4, Pallas kernels: none -> 12.7 us  [the longest x2 10.2 us: patch_input(): pl.pallas_call(patch_input_kernel, grid=(steps,), out_shape=jax.ShapeDtyp...]
    mul x9 -> x0, other arithmetic: 10.1 us -> none  [the longest x8 9.46 us: sum_blocks(): keep, got = (keep * own, got * other)]
    unnamed x28 -> x54, local copies, waits for them, and re-layouts: 8.29 us -> 2.07 us
    ppermute x49 -> x54, starting transfers between devices: 61 us -> 55.2 us  [exchange(): lax.ppermute(values, 'dp', flips(count, first, first if second is None el...]
  transfers between devices with their start and end apart: 49 -> 54, of which waited for: 21 -> 23; matrix products, arithmetic and copies ran while one was open for 4% -> 1% of each run, Pallas kernels for 35% -> 44%
where the time goes in v3:
time: 243 us
  Pallas kernels  111 us (46%)
  waiting for transfers between devices  69.3 us (29%)
  starting transfers between devices  55.2 us (23%)
  other arithmetic  4.02 us (2%)
    pallas_call x4, Pallas kernels, run(): pl.pallas_call(kernel, grid=(steps,), out_shape=[jax.ShapeDtypeStruct(s,...  85.4 us
    ppermute x54, waiting for transfers between devices, exchange(): lax.ppermute(values, 'dp', flips(count, first, first if second is None el...  69.3 us
    ppermute x54, starting transfers between devices, exchange(): lax.ppermute(values, 'dp', flips(count, first, first if second is None el...  55.2 us
    pallas_call x4, Pallas kernels, unpack(): pl.pallas_call(functools.partial(unpack_kernel, shapes, with_gains), out_...  12.8 us
    pallas_call x2, Pallas kernels, patch_input(): pl.pallas_call(patch_input_kernel, grid=(steps,), out_shape=jax.ShapeDtyp...  10.2 us
  transfers between devices with their start and end apart: 54, of which 23 were waited for; matrix products, arithmetic and copies ran while one was open for 1% of the time, Pallas kernels for 44%

profile of v3, /device:TPU:0, one launch (start us, length us, event | category | flops | bytes accessed | tf_op | source)
XLA Modules:
  0.0 243.0 jit_solution(7756325636214823545)
XLA Ops:
  0.7 1.2 count.1
  2.4 1.0 collective-permute-done
  3.3 0.7 add.123
  4.0 2.9 %collective-permute-start.1 = (f32[2]{0:T(128)S(1)}, f32[2]{0:T(128)S(1)}, u32[]{:S(2)}, u32[]{:S(2)}) collective-permute-start(f32[2]{0:T(128)S(1)} %add.123), channel_id=1, source_target_pairs={{0,8},{1,9},{2,10},{3,11},{4,12},{5,13},{6,14},{7,15},{8,0},{9,1},... | collective-permute-start | bytes 32 | tf_op jit(solution)/shard_map/ppermute | solution.py:378
  6.9 2.6 %collective-permute-start.2 = (f32[2]{0:T(128)S(1)}, f32[2]{0:T(128)S(1)}, u32[]{:S(2)}, u32[]{:S(2)}) collective-permute-start(f32[2]{0:T(128)S(1)} %add.123), channel_id=1, source_target_pairs={{0,16},{1,17},{2,18},{3,19},{4,20},{5,21},{6,22},{7,23},{8,24},{9,... | collective-permute-start | bytes 32 | tf_op jit(solution)/shard_map/ppermute | solution.py:378
  9.5 38.6 %forward.1 = (bf16[2048,512]{1,0:T(8,128)(2,1)}, bf16[2048,768]{1,0:T(8,128)(2,1)}, bf16[1024,1152]{1,0:T(8,128)(2,1)}, bf16[8,3,256,128]{3,2,1,0:T(8,128)(2,1)}...) custom-call(s32[8]{0:T(128)} %len_ref.3, ...), custom_call_target="tpu_custom_call" | custom-call | flops 40000000000 | bytes 1048576 | tf_op jit(solution)/shard_map/forward/pallas_call | solution.py:570
  48.7 1.7 collective-permute-start.4
  50.4 1.8 collective-permute-done.4
  52.3 1.7 collective-permute-start.5
  54.0 1.8 collective-permute-done.5.refs_1_
  56.3 1.3 weigh.1
  57.7 1.6 multiply_add_fusion.1
  59.3 1.8 collective-permute-start.8
  61.1 20.4 %cross_backward.1 = (bf16[2048,512]{1,0:T(8,128)(2,1)}, f32[1024,512]{1,0:T(8,128)}, f32[1,512]{1,0:T(1,128)}, f32[1,512]{1,0:T(1,128)}, f32[8,192,128]{2,1,0:T(...) custom-call(s32[2]{0:T(128)} %get-tuple-element.211.code_ref, ...), custom_call_target="tpu_custom_call" | custom-call | flops 20000000000 | bytes 1048576 | tf_op jit(solution)/shard_map/cross_backward/pallas_call | solution.py:570
  81.9 1.6 collective-permute-start.9
  84.0 15.6 %self_backward.1 = (f32[1024,512]{1,0:T(8,128)}, f32[8,200,128]{2,1,0:T(8,128)}, f32[8,200,128]{2,1,0:T(8,128)}, f32[8,200,128]{2,1,0:T(8,128)}, f32[8,200,128]{2,1,0:T(8,128)}) custom-call(s32[2]{0:T(128)} %get-tuple-element.211.code_ref, f32[2]{0:T(128)} %get-tuple-element.234.weight_ref, f32[1024,512]{1,0:T(8,128)} %get-tuple-element.260.dx1_ref, ...), custom_call_target="tpu_custom_call" | custom-call | flops 16000000000 | bytes 1048576 | tf_op jit(solution)/shard_map/self_backward/pallas_call | solution.py:570
  99.8 0.6 collective-permute-start.18
  100.5 0.8 collective-permute-start.12
  101.2 1.0 collective-permute-start.14
  102.3 10.8 %patch_weight.1 = (f32[8,208,128]{2,1,0:T(8,128)}, f32[8,208,128]{2,1,0:T(8,128)}, f32[8,208,128]{2,1,0:T(8,128)}, f32[8,208,128]{2,1,0:T(8,128)}) custom-call(s32[2]{0:T(128)} %get-tuple-element.211.code_ref, bf16[2048,1664]{1,0:T(8,128)(2,1)} %bitcast.31, bf16[2048,512]{1,0:T(8,128)(2,1)} %get-tuple-element.316.dfeat_ref), custom_call_target="tpu_custom_call" | custom-call | flops 12000000000 | bytes 1048576 | tf_op jit(solution)/shard_map/patch_weight/pallas_call | solution.py:570
  113.2 1.0 copy-done.8
  115.1 2.8 %collective-permute-start.13 = (f32[1,384,128]{2,1,0:T(8,128)S(1)}, f32[1,384,128]{2,1,0:T(8,128)S(1)}, u32[]{:S(2)}, u32[]{:S(2)}) collective-permute-start(f32[1,384,128]{2,1,0:T(8,128)S(1)} %get-tuple-element.420), channel_id=1, source_target_pairs={{0,16},{1,9},{2,18},{3,11},{4,20},{5,13},{6,22},{7,15},{8,24},{9,1... | collective-permute-start | bytes 589832 | tf_op jit(solution)/shard_map/ppermute | solution.py:378
  117.9 1.5 collective-permute-start.20
  119.7 0.9 collective-permute-start.21
  120.7 1.5 collective-permute-done.13
  122.2 3.4 %collective-permute-start.19 = (f32[1,384,128]{2,1,0:T(8,128)S(1)}, f32[1,384,128]{2,1,0:T(8,128)S(1)}, u32[]{:S(2)}, u32[]{:S(2)}) collective-permute-start(f32[1,384,128]{2,1,0:T(8,128)S(1)} %add.141), channel_id=1, source_target_pairs={{0,16},{1,9},{2,18},{3,11},{4,20},{5,13},{6,22},{7,15},{8,24},{9,1... | collective-permute-start | bytes 589832 | tf_op jit(solution)/shard_map/ppermute | solution.py:378
  125.7 0.6 collective-permute-start.23
  126.3 5.2 %patch_input.2.refs_0_ = f32[2048,1664]{1,0:T(8,128)} custom-call(f32[2]{0:T(128)S(1)} %copy-done.3, bf16[2048,512]{1,0:T(8,128)(2,1)S(1)} %copy-done, bf16[1664,512]{1,0:T(8,128)(2,1)S(1)} %copy-done.1), custom_call_target="tpu_custom_call" | custom-call | flops 6000000000 | bytes 1048576 | tf_op jit(solution)/shard_map/patch_input/pallas_call | solution.py:760
  131.9 1.8 collective-permute-start.24
  134.5 1.0 collective-permute-start.22
  136.0 5.0 %patch_input.3 = f32[2048,1664]{1,0:T(8,128)} custom-call(f32[2]{0:T(128)S(1)} %copy-done.3, bf16[2048,512]{1,0:T(8,128)(2,1)S(1)} %copy-done, bf16[1664,512]{1,0:T(8,128)(2,1)S(1)} %copy-done.1, f32[2048,1664]{1,0:T(8,128)} %patch_input.2.refs_0_), custom_call_target="tpu_custom_call", output_to_operand_aliasing={{}: (3, {})} | custom-call | flops 6000000000 | bytes 1048576 | tf_op jit(solution)/shard_map/patch_input/pallas_call | solution.py:760
  141.0 3.0 %collective-permute-start.27 = (f32[1,192,128]{2,1,0:T(8,128)S(1)}, f32[1,192,128]{2,1,0:T(8,128)S(1)}, u32[]{:S(2)}, u32[]{:S(2)}) collective-permute-start(f32[1,192,128]{2,1,0:T(8,128)S(1)} %get-tuple-element.426), channel_id=1, source_target_pairs={{0,16},{1,9},{2,18},{3,11},{4,20},{5,13},{6,22},{7,15},{8,24},{9,1... | collective-permute-start | bytes 294920 | tf_op jit(solution)/shard_map/ppermute | solution.py:378
  144.0 3.8 %collective-permute-done.23 = f32[8,208,128]{2,1,0:T(8,128)S(1)} collective-permute-done((f32[8,208,128]{2,1,0:T(8,128)S(1)}, f32[8,208,128]{2,1,0:T(8,128)S(1)}, u32[]{:S(2)}, u32[]{:S(2)}) %collective-permute-start.23) | collective-permute-done | bytes 852000 | tf_op jit(solution)/shard_map/ppermute | solution.py:378
  148.0 1.0 collective-permute-start.26
  149.7 0.8 collective-permute-start.31
  150.6 2.8 %collective-permute-start.32 = (f32[1,192,128]{2,1,0:T(8,128)S(1)}, f32[1,192,128]{2,1,0:T(8,128)S(1)}, u32[]{:S(2)}, u32[]{:S(2)}) collective-permute-start(f32[1,192,128]{2,1,0:T(8,128)S(1)} %add.155), channel_id=1, source_target_pairs={{0,16},{1,9},{2,18},{3,11},{4,20},{5,13},{6,22},{7,15},{8,24},{9,1... | collective-permute-start | bytes 294920 | tf_op jit(solution)/shard_map/ppermute | solution.py:378
  153.4 2.8 %collective-permute-done.26 = f32[4,208,128]{2,1,0:T(8,128)S(1)} collective-permute-done((f32[4,208,128]{2,1,0:T(8,128)S(1)}, f32[4,208,128]{2,1,0:T(8,128)S(1)}, u32[]{:S(2)}, u32[]{:S(2)}) %collective-permute-start.26) | collective-permute-done | bytes 426016 | tf_op jit(solution)/shard_map/ppermute | solution.py:378
  156.2 2.9 %collective-permute-done.25 = f32[2,200,128]{2,1,0:T(8,128)S(1)} collective-permute-done((f32[2,200,128]{2,1,0:T(8,128)S(1)}, f32[2,200,128]{2,1,0:T(8,128)S(1)}, u32[]{:S(2)}, u32[]{:S(2)}) %collective-permute-start.25) | collective-permute-done | bytes 204832 | tf_op jit(solution)/shard_map/ppermute | solution.py:378
  159.2 5.4 %collective-permute-done.31 = f32[4,384,128]{2,1,0:T(8,128)S(1)} collective-permute-done((f32[4,384,128]{2,1,0:T(8,128)S(1)}, f32[4,384,128]{2,1,0:T(8,128)S(1)}, u32[]{:S(2)}, u32[]{:S(2)}) %collective-permute-start.31) | collective-permute-done | bytes 786464 | tf_op jit(solution)/shard_map/ppermute | solution.py:378
  164.7 0.6 collective-permute-start.38
  165.6 2.5 %collective-permute-start.29 = (f32[1,200,128]{2,1,0:T(8,128)S(1)}, f32[1,200,128]{2,1,0:T(8,128)S(1)}, u32[]{:S(2)}, u32[]{:S(2)}) collective-permute-start(f32[1,200,128]{2,1,0:T(8,128)S(1)} %get-tuple-element.424), channel_id=1, source_target_pairs={{0,16},{1,9},{2,18},{3,11},{4,20},{5,13},{6,22},{7,15},{8,24},{9,1... | collective-permute-start | bytes 307208 | tf_op jit(solution)/shard_map/ppermute | solution.py:378
  168.5 7.2 %collective-permute-done.30 = f32[2,208,128]{2,1,0:T(8,128)S(1)} collective-permute-done((f32[2,208,128]{2,1,0:T(8,128)S(1)}, f32[2,208,128]{2,1,0:T(8,128)S(1)}, u32[]{:S(2)}, u32[]{:S(2)}) %collective-permute-start.30) | collective-permute-done | bytes 213024 | tf_op jit(solution)/shard_map/ppermute | solution.py:378
  175.8 3.5 %collective-permute-done.35 = f32[2,192,128]{2,1,0:T(8,128)S(1)} collective-permute-done((f32[2,192,128]{2,1,0:T(8,128)S(1)}, f32[2,192,128]{2,1,0:T(8,128)S(1)}, u32[]{:S(2)}, u32[]{:S(2)}) %collective-permute-start.35) | collective-permute-done | bytes 196640 | tf_op jit(solution)/shard_map/ppermute | solution.py:378
  179.4 1.1 collective-permute-start.40
  180.5 1.2 collective-permute-start.34
  181.7 1.8 collective-permute-start.33
  183.4 4.8 %collective-permute-done.34 = f32[1,208,128]{2,1,0:T(8,128)S(1)} collective-permute-done((f32[1,208,128]{2,1,0:T(8,128)S(1)}, f32[1,208,128]{2,1,0:T(8,128)S(1)}, u32[]{:S(2)}, u32[]{:S(2)}) %collective-permute-start.34) | collective-permute-done | bytes 106528 | tf_op jit(solution)/shard_map/ppermute | solution.py:378
  188.3 1.1 collective-permute-done.33
  189.6 1.4 collective-permute-start.43
  191.1 2.3 collective-permute-start.36
  193.4 7.3 %collective-permute-done.37 = f32[1,208,128]{2,1,0:T(8,128)S(1)} collective-permute-done((f32[1,208,128]{2,1,0:T(8,128)S(1)}, f32[1,208,128]{2,1,0:T(8,128)S(1)}, u32[]{:S(2)}, u32[]{:S(2)}) %collective-permute-start.37) | collective-permute-done | bytes 106528 | tf_op jit(solution)/shard_map/ppermute | solution.py:378
  200.9 0.8 collective-permute-start.41
  201.7 4.3 %unpack.4 = (f32[1024,512]{1,0:T(8,128)}, f32[512,1024]{1,0:T(8,128)}, f32[512,1024]{1,0:T(8,128)}) custom-call(s32[2]{0:T(128)S(1)} %copy-done.2, f32[8,384,128]{2,1,0:T(8,128)S(1)} %constant_dynamic-update-slice_fusion.6.refs_0_, f32[8,384,128]{2,1,0:T(8,128)S(1)} %collective-permute-done.38.refs_1_, f32[8,384,128]{2,1,0:T(8,128)S(1)} %collective-permute-done.39.refs_2_, ...), custom_call_target="tpu_custom_call" | custom-call | tf_op jit(solution)/shard_map/unpack/pallas_call | solution.py:448
  205.9 2.3 collective-permute-done.42
  209.0 3.1 %collective-permute-start.46 = (f32[8,200,128]{2,1,0:T(8,128)S(1)}, f32[8,200,128]{2,1,0:T(8,128)S(1)}, u32[]{:S(2)}, u32[]{:S(2)}) collective-permute-start(f32[8,200,128]{2,1,0:T(8,128)S(1)} %constant_dynamic-update-slice_fusion.20.refs_0_), channel_id=1, source_target_pairs={{0,2},{1,5},{2,0},{3,7},{4,6},{5,1},{6,4},{7,3},{8,10},{9,13},{10,... | collective-permute-start | bytes 2457608 | tf_op jit(solution)/shard_map/ppermute | solution.py:378
  212.1 1.3 collective-permute-start.48
  213.3 2.8 %unpack.5 = (f32[384,512]{1,0:T(8,128)}, f32[512,384]{1,0:T(8,128)}, f32[512,384]{1,0:T(8,128)}, f32[512,384]{1,0:T(8,128)}) custom-call(s32[2]{0:T(128)S(1)} %copy-done.2, f32[8,192,128]{2,1,0:T(8,128)S(1)} %constant_dynamic-update-slice_fusion.12.refs_0_, f32[8,192,128]{2,1,0:T(8,128)S(1)} %collective-permute-done.43.refs_1_, ...), custom_call_target="tpu_custom_call" | custom-call | tf_op jit(solution)/shard_map/unpack/pallas_call | solution.py:448
  216.1 8.7 %collective-permute-done.48 = f32[4,208,128]{2,1,0:T(8,128)S(1)} collective-permute-done((f32[4,208,128]{2,1,0:T(8,128)S(1)}, f32[4,208,128]{2,1,0:T(8,128)S(1)}, u32[]{:S(2)}, u32[]{:S(2)}) %collective-permute-start.48) | collective-permute-done | bytes 426016 | tf_op jit(solution)/shard_map/ppermute | solution.py:378
  225.6 1.4 collective-permute-done.46.refs_1_
  227.0 2.3 collective-permute-done.50.refs_3_
  229.3 2.8 %unpack.6 = (f32[384,512]{1,0:T(8,128)}, f32[512,384]{1,0:T(8,128)}, f32[512,384]{1,0:T(8,128)}, f32[512,384]{1,0:T(8,128)}, f32[256,128]{1,0:T(8,128)}, /*index...) custom-call(s32[2]{0:T(128)S(1)} %copy-done.2, ...), custom_call_target="tpu_custom_call" | custom-call | tf_op jit(solution)/shard_map/unpack/pallas_call | solution.py:448
  232.1 5.5 %collective-permute-done.51.refs_1_ = f32[8,208,128]{2,1,0:T(8,128)S(1)} collective-permute-done((f32[8,208,128]{2,1,0:T(8,128)S(1)}, f32[8,208,128]{2,1,0:T(8,128)S(1)}, u32[]{:S(2)}, u32[]{:S(2)}) %collective-permute-start.51) | collective-permute-done | bytes 852000 | tf_op jit(solution)/shard_map/ppermute | solution.py:378
  237.7 2.4 collective-permute-done.53.refs_3_
  240.0 3.0 %unpack.7 = f32[1664,512]{1,0:T(8,128)} custom-call(s32[2]{0:T(128)S(1)} %copy-done.2, f32[8,208,128]{2,1,0:T(8,128)S(1)} %constant_dynamic-update-slice_fusion.22.refs_0_, f32[8,208,128]{2,1,0:T(8,128)S(1)} %collective-permute-done.51.refs_1_, f32[8,208,128]{2,1,0:T(8,128)S(1)} %collective-permute-done.52.refs_2_, ...), custom_call_target="tpu_custom_call" | custom-call | tf_op jit(solution)/shard_map/unpack/pallas_call | solution.py:448
  (149 shorter events, 9.7 us)
Async XLA Ops:
  1.9 1.5 collective-permute-start
  4.0 44.1 %collective-permute-start.1 = (f32[2]{0:T(128)S(1)}, f32[2]{0:T(128)S(1)}, u32[]{:S(2)}, u32[]{:S(2)}) collective-permute-start(f32[2]{0:T(128)S(1)} %add.123), channel_id=1, source_target_pairs={{0,8},{1,9},{2,10},{3,11},{4,12},{5,13},{6,14},{7,15},{8,0},{9,1},... | collective-permute-start | bytes 32 | tf_op jit(solution)/shard_map/ppermute | solution.py:378
  6.9 41.3 %collective-permute-start.2 = (f32[2]{0:T(128)S(1)}, f32[2]{0:T(128)S(1)}, u32[]{:S(2)}, u32[]{:S(2)}) collective-permute-start(f32[2]{0:T(128)S(1)} %add.123), channel_id=1, source_target_pairs={{0,16},{1,17},{2,18},{3,19},{4,20},{5,21},{6,22},{7,23},{8,24},{9,... | collective-permute-start | bytes 32 | tf_op jit(solution)/shard_map/ppermute | solution.py:378
  9.5 38.7 %collective-permute-start.3 = (f32[2]{0:T(128)S(1)}, f32[2]{0:T(128)S(1)}, u32[]{:S(2)}, u32[]{:S(2)}) collective-permute-start(f32[2]{0:T(128)S(1)} %add.123), channel_id=1, source_target_pairs={{0,24},{1,25},{2,26},{3,27},{4,28},{5,29},{6,30},{7,31},{8,16},{9,... | collective-permute-start | bytes 32 | tf_op jit(solution)/shard_map/ppermute | solution.py:378
  48.2 9.5 %collective-permute-start.6 = (f32[8,384,128]{2,1,0:T(8,128)}, f32[8,384,128]{2,1,0:T(8,128)S(1)}, u32[]{:S(2)}, u32[]{:S(2)}) collective-permute-start(f32[8,384,128]{2,1,0:T(8,128)} %get-tuple-element.237), channel_id=1, source_target_pairs={{0,1},{1,0},{2,3},{3,2},{4,5},{5,4},{6,7},{7,6},{8,9},{9,8},{10,11... | collective-permute-start | bytes 4718600 | tf_op jit(solution)/shard_map/ppermute | solution.py:378
  48.2 9.5 %collective-permute-start.7 = (f32[8,384,128]{2,1,0:T(8,128)}, f32[8,384,128]{2,1,0:T(8,128)S(1)}, u32[]{:S(2)}, u32[]{:S(2)}) collective-permute-start(f32[8,384,128]{2,1,0:T(8,128)} %get-tuple-element.236), channel_id=1, source_target_pairs={{0,1},{1,0},{2,3},{3,2},{4,5},{5,4},{6,7},{7,6},{8,9},{9,8},{10,11... | collective-permute-start | bytes 4718600 | tf_op jit(solution)/shard_map/ppermute | solution.py:378
  48.7 3.5 %collective-permute-start.4 = (f32[2]{0:T(128)S(1)}, f32[2]{0:T(128)S(1)}, u32[]{:S(2)}, u32[]{:S(2)}) collective-permute-start(f32[2]{0:T(128)S(1)} %add_add_fusion), channel_id=1, source_target_pairs={{0,2},{1,3},{2,0},{3,1},{4,6},{5,7},{6,4},{7,5},{8,10},{9,11},{10,... | collective-permute-start | bytes 32 | tf_op jit(solution)/shard_map/ppermute | solution.py:378
  52.3 3.5 %collective-permute-start.5 = (f32[2]{0:T(128)S(1)}, f32[2]{0:T(128)S(1)}, u32[]{:S(2)}, u32[]{:S(2)}) collective-permute-start(f32[2]{0:T(128)S(1)} %add.127.refs_0_), channel_id=1, source_target_pairs={{0,4},{1,5},{2,6},{3,7},{4,0},{5,1},{6,2},{7,3},{8,12},{9,13},{10,... | collective-permute-start | bytes 32 | tf_op jit(solution)/shard_map/ppermute | solution.py:378
  59.3 22.1 %collective-permute-start.8 = (f32[8,384,128]{2,1,0:T(8,128)S(1)}, f32[8,384,128]{2,1,0:T(8,128)S(1)}, u32[]{:S(2)}, u32[]{:S(2)}) collective-permute-start(f32[8,384,128]{2,1,0:T(8,128)S(1)} %multiply_add_fusion.1), channel_id=1, source_target_pairs={{0,2},{1,5},{2,0},{3,7},{4,6},{5,1},{6,4},{7,3},{8,10},{9,13},{10,... | collective-permute-start | bytes 4718600 | tf_op jit(solution)/shard_map/ppermute | solution.py:378
  61.0 20.4 %copy-start.4 = (f32[8,384,128]{2,1,0:T(8,128)S(1)}, f32[8,384,128]{2,1,0:T(8,128)}, u32[]{:S(2)}) copy-start(f32[8,384,128]{2,1,0:T(8,128)} %get-tuple-element.256) | copy-start | bytes 4718596
  61.1 20.4 %copy-start.11 = (f32[1,1,128]{2,1,0:T(1,128)S(1)}, f32[1,1,128]{2,1,0:T(1,128)}, u32[]{:S(2)}) copy-start(f32[1,1,128]{2,1,0:T(1,128)} %get-tuple-element.239) | copy-start | bytes 1540
  61.1 20.4 %copy-start.12 = (f32[1,1,128]{2,1,0:T(1,128)S(1)}, f32[1,1,128]{2,1,0:T(1,128)}, u32[]{:S(2)}) copy-start(f32[1,1,128]{2,1,0:T(1,128)} %get-tuple-element.241) | copy-start | bytes 1540
  81.9 18.5 %collective-permute-start.9 = (f32[4,384,128]{2,1,0:T(8,128)S(1)}, f32[4,384,128]{2,1,0:T(8,128)S(1)}, u32[]{:S(2)}, u32[]{:S(2)}) collective-permute-start(f32[4,384,128]{2,1,0:T(8,128)S(1)} %get-tuple-element.404), channel_id=1, source_target_pairs={{0,4},{1,3},{2,6},{3,1},{4,0},{5,7},{6,2},{7,5},{8,12},{9,11},{10,... | collective-permute-start | bytes 2359304 | tf_op jit(solution)/shard_map/ppermute | solution.py:378
  83.5 16.2 %collective-permute-start.10 = (f32[8,192,128]{2,1,0:T(8,128)S(1)}, f32[8,192,128]{2,1,0:T(8,128)S(1)}, u32[]{:S(2)}, u32[]{:S(2)}) collective-permute-start(f32[8,192,128]{2,1,0:T(8,128)S(1)} %copy-done.20), channel_id=1, source_target_pairs={{0,1},{1,0},{2,3},{3,2},{4,5},{5,4},{6,7},{7,6},{8,9},{9,8},{10,11... | collective-permute-start | bytes 2359304 | tf_op jit(solution)/shard_map/ppermute | solution.py:378
  83.5 16.2 %collective-permute-start.11 = (f32[8,192,128]{2,1,0:T(8,128)S(1)}, f32[8,192,128]{2,1,0:T(8,128)S(1)}, u32[]{:S(2)}, u32[]{:S(2)}) collective-permute-start(f32[8,192,128]{2,1,0:T(8,128)S(1)} %copy-done.19), channel_id=1, source_target_pairs={{0,1},{1,0},{2,3},{3,2},{4,5},{5,4},{6,7},{7,6},{8,9},{9,8},{10,11... | collective-permute-start | bytes 2359304 | tf_op jit(solution)/shard_map/ppermute | solution.py:378
  84.0 15.7 %copy-start.10 = (f32[8,192,128]{2,1,0:T(8,128)S(1)}, f32[8,192,128]{2,1,0:T(8,128)}, u32[]{:S(2)}) copy-start(f32[8,192,128]{2,1,0:T(8,128)} %get-tuple-element.276) | copy-start | bytes 2359300
  99.8 19.6 %collective-permute-start.18 = (f32[8,192,128]{2,1,0:T(8,128)S(1)}, f32[8,192,128]{2,1,0:T(8,128)S(1)}, u32[]{:S(2)}, u32[]{:S(2)}) collective-permute-start(f32[8,192,128]{2,1,0:T(8,128)S(1)} %multiply_add_fusion.7), channel_id=1, source_target_pairs={{0,2},{1,5},{2,0},{3,7},{4,6},{5,1},{6,4},{7,3},{8,10},{9,13},{10,... | collective-permute-start | bytes 2359304 | tf_op jit(solution)/shard_map/ppermute | solution.py:378
  100.5 12.6 %collective-permute-start.12 = (f32[2,384,128]{2,1,0:T(8,128)S(1)}, f32[2,384,128]{2,1,0:T(8,128)S(1)}, u32[]{:S(2)}, u32[]{:S(2)}) collective-permute-start(f32[2,384,128]{2,1,0:T(8,128)S(1)} %get-tuple-element.412), channel_id=1, source_target_pairs={{0,8},{1,17},{2,10},{3,19},{4,12},{5,21},{6,14},{7,23},{8,0},{9,25... | collective-permute-start | bytes 1179656 | tf_op jit(solution)/shard_map/ppermute | solution.py:378
  101.2 11.9 %collective-permute-start.14 = (f32[8,200,128]{2,1,0:T(8,128)S(1)}, f32[8,200,128]{2,1,0:T(8,128)S(1)}, u32[]{:S(2)}, u32[]{:S(2)}) collective-permute-start(f32[8,200,128]{2,1,0:T(8,128)S(1)} %copy-done.18), channel_id=1, source_target_pairs={{0,1},{1,0},{2,3},{3,2},{4,5},{5,4},{6,7},{7,6},{8,9},{9,8},{10,11... | collective-permute-start | bytes 2457608 | tf_op jit(solution)/shard_map/ppermute | solution.py:378
  102.2 11.0 %collective-permute-start.15 = (f32[8,200,128]{2,1,0:T(8,128)S(1)}, f32[8,200,128]{2,1,0:T(8,128)S(1)}, u32[]{:S(2)}, u32[]{:S(2)}) collective-permute-start(f32[8,200,128]{2,1,0:T(8,128)S(1)} %copy-done.17), channel_id=1, source_target_pairs={{0,1},{1,0},{2,3},{3,2},{4,5},{5,4},{6,7},{7,6},{8,9},{9,8},{10,11... | collective-permute-start | bytes 2457608 | tf_op jit(solution)/shard_map/ppermute | solution.py:378
  113.1 6.4 %copy-start.9 = (f32[8,192,128]{2,1,0:T(8,128)S(1)}, f32[8,192,128]{2,1,0:T(8,128)}, u32[]{:S(2)}) copy-start(f32[8,192,128]{2,1,0:T(8,128)} %get-tuple-element.299) | copy-start | bytes 2359300
  114.4 6.1 %collective-permute-start.16 = (f32[8,208,128]{2,1,0:T(8,128)S(1)}, f32[8,208,128]{2,1,0:T(8,128)S(1)}, u32[]{:S(2)}, u32[]{:S(2)}) collective-permute-start(f32[8,208,128]{2,1,0:T(8,128)S(1)} %copy-done.16), channel_id=1, source_target_pairs={{0,1},{1,0},{2,3},{3,2},{4,5},{5,4},{6,7},{7,6},{8,9},{9,8},{10,11... | collective-permute-start | bytes 2555912 | tf_op jit(solution)/shard_map/ppermute | solution.py:378
  114.9 5.7 %collective-permute-start.17 = (f32[8,208,128]{2,1,0:T(8,128)S(1)}, f32[8,208,128]{2,1,0:T(8,128)S(1)}, u32[]{:S(2)}, u32[]{:S(2)}) collective-permute-start(f32[8,208,128]{2,1,0:T(8,128)S(1)} %copy-done.15), channel_id=1, source_target_pairs={{0,1},{1,0},{2,3},{3,2},{4,5},{5,4},{6,7},{7,6},{8,9},{9,8},{10,11... | collective-permute-start | bytes 2555912 | tf_op jit(solution)/shard_map/ppermute | solution.py:378
  115.1 7.1 %collective-permute-start.13 = (f32[1,384,128]{2,1,0:T(8,128)S(1)}, f32[1,384,128]{2,1,0:T(8,128)S(1)}, u32[]{:S(2)}, u32[]{:S(2)}) collective-permute-start(f32[1,384,128]{2,1,0:T(8,128)S(1)} %get-tuple-element.420), channel_id=1, source_target_pairs={{0,16},{1,9},{2,18},{3,11},{4,20},{5,13},{6,22},{7,15},{8,24},{9,1... | collective-permute-start | bytes 589832 | tf_op jit(solution)/shard_map/ppermute | solution.py:378
  117.9 16.3 %collective-permute-start.20 = (f32[8,200,128]{2,1,0:T(8,128)S(1)}, f32[8,200,128]{2,1,0:T(8,128)S(1)}, u32[]{:S(2)}, u32[]{:S(2)}) collective-permute-start(f32[8,200,128]{2,1,0:T(8,128)S(1)} %multiply_add_fusion.5), channel_id=1, source_target_pairs={{0,2},{1,5},{2,0},{3,7},{4,6},{5,1},{6,4},{7,3},{8,10},{9,13},{10,... | collective-permute-start | bytes 2457608 | tf_op jit(solution)/shard_map/ppermute | solution.py:378
  119.6 6.8 %copy-start.1 = (bf16[1664,512]{1,0:T(8,128)(2,1)S(1)}, bf16[1664,512]{1,0:T(8,128)(2,1)}, u32[]{:S(2)}) copy-start(bf16[1664,512]{1,0:T(8,128)(2,1)} %w_ref.3) | copy-start | bytes 5111812
  119.7 6.7 %copy-start = (bf16[2048,512]{1,0:T(8,128)(2,1)S(1)}, bf16[2048,512]{1,0:T(8,128)(2,1)}, u32[]{:S(2)}) copy-start(bf16[2048,512]{1,0:T(8,128)(2,1)} %get-tuple-element.316.dfeat_ref) | copy-start | bytes 6291460
  119.7 6.6 %copy-start.3 = (f32[2]{0:T(128)S(1)}, f32[2]{0:T(128)}, u32[]{:S(2)}) copy-start(f32[2]{0:T(128)} %get-tuple-element.234.weight_ref) | copy-start | bytes 28
  119.7 12.1 %collective-permute-start.21 = (f32[4,192,128]{2,1,0:T(8,128)S(1)}, f32[4,192,128]{2,1,0:T(8,128)S(1)}, u32[]{:S(2)}, u32[]{:S(2)}) collective-permute-start(f32[4,192,128]{2,1,0:T(8,128)S(1)} %get-tuple-element.410), channel_id=1, source_target_pairs={{0,4},{1,3},{2,6},{3,1},{4,0},{5,7},{6,2},{7,5},{8,12},{9,11},{10,... | collective-permute-start | bytes 1179656 | tf_op jit(solution)/shard_map/ppermute | solution.py:378
  122.2 13.3 %collective-permute-start.19 = (f32[1,384,128]{2,1,0:T(8,128)S(1)}, f32[1,384,128]{2,1,0:T(8,128)S(1)}, u32[]{:S(2)}, u32[]{:S(2)}) collective-permute-start(f32[1,384,128]{2,1,0:T(8,128)S(1)} %add.141), channel_id=1, source_target_pairs={{0,16},{1,9},{2,18},{3,11},{4,20},{5,13},{6,22},{7,15},{8,24},{9,1... | collective-permute-start | bytes 589832 | tf_op jit(solution)/shard_map/ppermute | solution.py:378
  125.7 22.1 %collective-permute-start.23 = (f32[8,208,128]{2,1,0:T(8,128)S(1)}, f32[8,208,128]{2,1,0:T(8,128)S(1)}, u32[]{:S(2)}, u32[]{:S(2)}) collective-permute-start(f32[8,208,128]{2,1,0:T(8,128)S(1)} %multiply_add_fusion.3), channel_id=1, source_target_pairs={{0,2},{1,5},{2,0},{3,7},{4,6},{5,1},{6,4},{7,3},{8,10},{9,13},{10,... | collective-permute-start | bytes 2555912 | tf_op jit(solution)/shard_map/ppermute | solution.py:378
  131.9 9.1 %collective-permute-start.24 = (f32[2,192,128]{2,1,0:T(8,128)S(1)}, f32[2,192,128]{2,1,0:T(8,128)S(1)}, u32[]{:S(2)}, u32[]{:S(2)}) collective-permute-start(f32[2,192,128]{2,1,0:T(8,128)S(1)} %get-tuple-element.418), channel_id=1, source_target_pairs={{0,8},{1,17},{2,10},{3,19},{4,12},{5,21},{6,14},{7,23},{8,0},{9,25... | collective-permute-start | bytes 589832 | tf_op jit(solution)/shard_map/ppermute | solution.py:378
  134.5 14.5 %collective-permute-start.22 = (f32[4,200,128]{2,1,0:T(8,128)S(1)}, f32[4,200,128]{2,1,0:T(8,128)S(1)}, u32[]{:S(2)}, u32[]{:S(2)}) collective-permute-start(f32[4,200,128]{2,1,0:T(8,128)S(1)} %get-tuple-element.408), channel_id=1, source_target_pairs={{0,4},{1,3},{2,6},{3,1},{4,0},{5,7},{6,2},{7,5},{8,12},{9,11},{10,... | collective-permute-start | bytes 1228808 | tf_op jit(solution)/shard_map/ppermute | solution.py:378
  135.6 12.2 %copy-start.5 = (f32[8,208,128]{2,1,0:T(8,128)S(1)}, f32[8,208,128]{2,1,0:T(8,128)}, u32[]{:S(2)}) copy-start(f32[8,208,128]{2,1,0:T(8,128)} %get-tuple-element.321) | copy-start | bytes 2555908
  135.6 14.1 %collective-permute-start.28 = (f32[2,384,128]{2,1,0:T(8,128)S(1)}, f32[2,384,128]{2,1,0:T(8,128)S(1)}, u32[]{:S(2)}, u32[]{:S(2)}) collective-permute-start(f32[2,384,128]{2,1,0:T(8,128)S(1)} %constant_dynamic-update-slice_fusion), channel_id=1, source_target_pairs={{0,8},{1,17},{2,10},{3,19},{4,12},{5,21},{6,14},{7,23},{8,0},{9,25... | collective-permute-start | bytes 1179656 | tf_op jit(solution)/shard_map/ppermute | solution.py:378
  141.0 9.6 %collective-permute-start.27 = (f32[1,192,128]{2,1,0:T(8,128)S(1)}, f32[1,192,128]{2,1,0:T(8,128)S(1)}, u32[]{:S(2)}, u32[]{:S(2)}) collective-permute-start(f32[1,192,128]{2,1,0:T(8,128)S(1)} %get-tuple-element.426), channel_id=1, source_target_pairs={{0,16},{1,9},{2,18},{3,11},{4,20},{5,13},{6,22},{7,15},{8,24},{9,1... | collective-permute-start | bytes 294920 | tf_op jit(solution)/shard_map/ppermute | solution.py:378
  148.0 8.2 %collective-permute-start.26 = (f32[4,208,128]{2,1,0:T(8,128)S(1)}, f32[4,208,128]{2,1,0:T(8,128)S(1)}, u32[]{:S(2)}, u32[]{:S(2)}) collective-permute-start(f32[4,208,128]{2,1,0:T(8,128)S(1)} %get-tuple-element.406), channel_id=1, source_target_pairs={{0,4},{1,3},{2,6},{3,1},{4,0},{5,7},{6,2},{7,5},{8,12},{9,11},{10,... | collective-permute-start | bytes 1277960 | tf_op jit(solution)/shard_map/ppermute | solution.py:378
  149.7 14.9 %collective-permute-start.31 = (f32[4,384,128]{2,1,0:T(8,128)S(1)}, f32[4,384,128]{2,1,0:T(8,128)S(1)}, u32[]{:S(2)}, u32[]{:S(2)}) collective-permute-start(f32[4,384,128]{2,1,0:T(8,128)S(1)} %constant_dynamic-update-slice_fusion.2), channel_id=1, source_target_pairs={{0,4},{1,3},{2,6},{3,1},{4,0},{5,7},{6,2},{7,5},{8,12},{9,11},{10,... | collective-permute-start | bytes 2359304 | tf_op jit(solution)/shard_map/ppermute | solution.py:378
  150.6 8.6 %collective-permute-start.25 = (f32[2,200,128]{2,1,0:T(8,128)S(1)}, f32[2,200,128]{2,1,0:T(8,128)S(1)}, u32[]{:S(2)}, u32[]{:S(2)}) collective-permute-start(f32[2,200,128]{2,1,0:T(8,128)S(1)} %get-tuple-element.416), channel_id=1, source_target_pairs={{0,8},{1,17},{2,10},{3,19},{4,12},{5,21},{6,14},{7,23},{8,0},{9,25... | collective-permute-start | bytes 614408 | tf_op jit(solution)/shard_map/ppermute | solution.py:378
  150.6 8.6 %collective-permute-start.32 = (f32[1,192,128]{2,1,0:T(8,128)S(1)}, f32[1,192,128]{2,1,0:T(8,128)S(1)}, u32[]{:S(2)}, u32[]{:S(2)}) collective-permute-start(f32[1,192,128]{2,1,0:T(8,128)S(1)} %add.155), channel_id=1, source_target_pairs={{0,16},{1,9},{2,18},{3,11},{4,20},{5,13},{6,22},{7,15},{8,24},{9,1... | collective-permute-start | bytes 294920 | tf_op jit(solution)/shard_map/ppermute | solution.py:378
  164.7 24.7 %collective-permute-start.38 = (f32[8,384,128]{2,1,0:T(8,128)S(1)}, f32[8,384,128]{2,1,0:T(8,128)S(1)}, u32[]{:S(2)}, u32[]{:S(2)}) collective-permute-start(f32[8,384,128]{2,1,0:T(8,128)S(1)} %constant_dynamic-update-slice_fusion.6.refs_0_), channel_id=1, source_target_pairs={{0,2},{1,5},{2,0},{3,7},{4,6},{5,1},{6,4},{7,3},{8,10},{9,13},{10,... | collective-permute-start | bytes 4718600 | tf_op jit(solution)/shard_map/ppermute | solution.py:378
  165.3 24.1 %collective-permute-start.39 = (f32[8,384,128]{2,1,0:T(8,128)S(1)}, f32[8,384,128]{2,1,0:T(8,128)S(1)}, u32[]{:S(2)}, u32[]{:S(2)}) collective-permute-start(f32[8,384,128]{2,1,0:T(8,128)S(1)} %constant_dynamic-update-slice_fusion.6.refs_0_), channel_id=1, source_target_pairs={{0,1},{1,0},{2,3},{3,2},{4,5},{5,4},{6,7},{7,6},{8,9},{9,8},{10,11... | collective-permute-start | bytes 4718600 | tf_op jit(solution)/shard_map/ppermute | solution.py:378
  165.3 10.4 %collective-permute-start.30 = (f32[2,208,128]{2,1,0:T(8,128)S(1)}, f32[2,208,128]{2,1,0:T(8,128)S(1)}, u32[]{:S(2)}, u32[]{:S(2)}) collective-permute-start(f32[2,208,128]{2,1,0:T(8,128)S(1)} %get-tuple-element.414), channel_id=1, source_target_pairs={{0,8},{1,17},{2,10},{3,19},{4,12},{5,21},{6,14},{7,23},{8,0},{9,25... | collective-permute-start | bytes 638984 | tf_op jit(solution)/shard_map/ppermute | solution.py:378
  165.6 10.2 %collective-permute-start.29 = (f32[1,200,128]{2,1,0:T(8,128)S(1)}, f32[1,200,128]{2,1,0:T(8,128)S(1)}, u32[]{:S(2)}, u32[]{:S(2)}) collective-permute-start(f32[1,200,128]{2,1,0:T(8,128)S(1)} %get-tuple-element.424), channel_id=1, source_target_pairs={{0,16},{1,9},{2,18},{3,11},{4,20},{5,13},{6,22},{7,15},{8,24},{9,1... | collective-permute-start | bytes 307208 | tf_op jit(solution)/shard_map/ppermute | solution.py:378
  168.2 11.2 %collective-permute-start.35 = (f32[2,192,128]{2,1,0:T(8,128)S(1)}, f32[2,192,128]{2,1,0:T(8,128)S(1)}, u32[]{:S(2)}, u32[]{:S(2)}) collective-permute-start(f32[2,192,128]{2,1,0:T(8,128)S(1)} %constant_dynamic-update-slice_fusion.4), channel_id=1, source_target_pairs={{0,8},{1,17},{2,10},{3,19},{4,12},{5,21},{6,14},{7,23},{8,0},{9,25... | collective-permute-start | bytes 589832 | tf_op jit(solution)/shard_map/ppermute | solution.py:378
  179.4 10.0 %collective-permute-start.40 = (f32[4,192,128]{2,1,0:T(8,128)S(1)}, f32[4,192,128]{2,1,0:T(8,128)S(1)}, u32[]{:S(2)}, u32[]{:S(2)}) collective-permute-start(f32[4,192,128]{2,1,0:T(8,128)S(1)} %constant_dynamic-update-slice_fusion.8), channel_id=1, source_target_pairs={{0,4},{1,3},{2,6},{3,1},{4,0},{5,7},{6,2},{7,5},{8,12},{9,11},{10,... | collective-permute-start | bytes 1179656 | tf_op jit(solution)/shard_map/ppermute | solution.py:378
  180.5 7.7 %collective-permute-start.34 = (f32[1,208,128]{2,1,0:T(8,128)S(1)}, f32[1,208,128]{2,1,0:T(8,128)S(1)}, u32[]{:S(2)}, u32[]{:S(2)}) collective-permute-start(f32[1,208,128]{2,1,0:T(8,128)S(1)} %get-tuple-element.422), channel_id=1, source_target_pairs={{0,16},{1,9},{2,18},{3,11},{4,20},{5,13},{6,22},{7,15},{8,24},{9,1... | collective-permute-start | bytes 319496 | tf_op jit(solution)/shard_map/ppermute | solution.py:378
  181.7 7.7 %collective-permute-start.33 = (f32[1,200,128]{2,1,0:T(8,128)S(1)}, f32[1,200,128]{2,1,0:T(8,128)S(1)}, u32[]{:S(2)}, u32[]{:S(2)}) collective-permute-start(f32[1,200,128]{2,1,0:T(8,128)S(1)} %add.161), channel_id=1, source_target_pairs={{0,16},{1,9},{2,18},{3,11},{4,20},{5,13},{6,22},{7,15},{8,24},{9,1... | collective-permute-start | bytes 307208 | tf_op jit(solution)/shard_map/ppermute | solution.py:378
  188.3 13.4 %copy-start.2 = (s32[2]{0:T(128)S(1)}, s32[2]{0:T(128)}, u32[]{:S(2)}) copy-start(s32[2]{0:T(128)} %get-tuple-element.211.code_ref) | copy-start | bytes 28
  189.5 12.2 %collective-permute-start.45 = (f32[8,384,128]{2,1,0:T(8,128)S(1)}, f32[8,384,128]{2,1,0:T(8,128)S(1)}, u32[]{:S(2)}, u32[]{:S(2)}) collective-permute-start(f32[8,384,128]{2,1,0:T(8,128)S(1)} %collective-permute-done.38.refs_1_), channel_id=1, source_target_pairs={{0,1},{1,0},{2,3},{3,2},{4,5},{5,4},{6,7},{7,6},{8,9},{9,8},{10,11... | collective-permute-start | bytes 4718600 | tf_op jit(solution)/shard_map/ppermute | solution.py:378
  189.6 16.3 %collective-permute-start.43 = (f32[8,192,128]{2,1,0:T(8,128)S(1)}, f32[8,192,128]{2,1,0:T(8,128)S(1)}, u32[]{:S(2)}, u32[]{:S(2)}) collective-permute-start(f32[8,192,128]{2,1,0:T(8,128)S(1)} %constant_dynamic-update-slice_fusion.12.refs_0_), channel_id=1, source_target_pairs={{0,2},{1,5},{2,0},{3,7},{4,6},{5,1},{6,4},{7,3},{8,10},{9,13},{10,... | collective-permute-start | bytes 2359304 | tf_op jit(solution)/shard_map/ppermute | solution.py:378
  191.0 14.9 %collective-permute-start.44 = (f32[8,192,128]{2,1,0:T(8,128)S(1)}, f32[8,192,128]{2,1,0:T(8,128)S(1)}, u32[]{:S(2)}, u32[]{:S(2)}) collective-permute-start(f32[8,192,128]{2,1,0:T(8,128)S(1)} %constant_dynamic-update-slice_fusion.12.refs_0_), channel_id=1, source_target_pairs={{0,1},{1,0},{2,3},{3,2},{4,5},{5,4},{6,7},{7,6},{8,9},{9,8},{10,11... | collective-permute-start | bytes 2359304 | tf_op jit(solution)/shard_map/ppermute | solution.py:378
  191.0 9.7 %collective-permute-start.37 = (f32[1,208,128]{2,1,0:T(8,128)S(1)}, f32[1,208,128]{2,1,0:T(8,128)S(1)}, u32[]{:S(2)}, u32[]{:S(2)}) collective-permute-start(f32[1,208,128]{2,1,0:T(8,128)S(1)} %add.163), channel_id=1, source_target_pairs={{0,16},{1,9},{2,18},{3,11},{4,20},{5,13},{6,22},{7,15},{8,24},{9,1... | collective-permute-start | bytes 319496 | tf_op jit(solution)/shard_map/ppermute | solution.py:378
  191.1 9.7 %collective-permute-start.36 = (f32[2,200,128]{2,1,0:T(8,128)S(1)}, f32[2,200,128]{2,1,0:T(8,128)S(1)}, u32[]{:S(2)}, u32[]{:S(2)}) collective-permute-start(f32[2,200,128]{2,1,0:T(8,128)S(1)} %constant_dynamic-update-slice_fusion.10), channel_id=1, source_target_pairs={{0,8},{1,17},{2,10},{3,19},{4,12},{5,21},{6,14},{7,23},{8,0},{9,25... | collective-permute-start | bytes 614408 | tf_op jit(solution)/shard_map/ppermute | solution.py:378
  200.7 7.5 %collective-permute-start.42 = (f32[2,208,128]{2,1,0:T(8,128)S(1)}, f32[2,208,128]{2,1,0:T(8,128)S(1)}, u32[]{:S(2)}, u32[]{:S(2)}) collective-permute-start(f32[2,208,128]{2,1,0:T(8,128)S(1)} %constant_dynamic-update-slice_fusion.14), channel_id=1, source_target_pairs={{0,8},{1,17},{2,10},{3,19},{4,12},{5,21},{6,14},{7,23},{8,0},{9,25... | collective-permute-start | bytes 638984 | tf_op jit(solution)/shard_map/ppermute | solution.py:378
  200.9 8.0 %collective-permute-start.41 = (f32[4,200,128]{2,1,0:T(8,128)S(1)}, f32[4,200,128]{2,1,0:T(8,128)S(1)}, u32[]{:S(2)}, u32[]{:S(2)}) collective-permute-start(f32[4,200,128]{2,1,0:T(8,128)S(1)} %constant_dynamic-update-slice_fusion.16), channel_id=1, source_target_pairs={{0,4},{1,3},{2,6},{3,1},{4,0},{5,7},{6,2},{7,5},{8,12},{9,11},{10,... | collective-permute-start | bytes 1228808 | tf_op jit(solution)/shard_map/ppermute | solution.py:378
  208.2 5.1 %collective-permute-start.49 = (f32[8,192,128]{2,1,0:T(8,128)S(1)}, f32[8,192,128]{2,1,0:T(8,128)S(1)}, u32[]{:S(2)}, u32[]{:S(2)}) collective-permute-start(f32[8,192,128]{2,1,0:T(8,128)S(1)} %collective-permute-done.43.refs_1_), channel_id=1, source_target_pairs={{0,1},{1,0},{2,3},{3,2},{4,5},{5,4},{6,7},{7,6},{8,9},{9,8},{10,11... | collective-permute-start | bytes 2359304 | tf_op jit(solution)/shard_map/ppermute | solution.py:378
  209.0 18.0 %collective-permute-start.46 = (f32[8,200,128]{2,1,0:T(8,128)S(1)}, f32[8,200,128]{2,1,0:T(8,128)S(1)}, u32[]{:S(2)}, u32[]{:S(2)}) collective-permute-start(f32[8,200,128]{2,1,0:T(8,128)S(1)} %constant_dynamic-update-slice_fusion.20.refs_0_), channel_id=1, source_target_pairs={{0,2},{1,5},{2,0},{3,7},{4,6},{5,1},{6,4},{7,3},{8,10},{9,13},{10,... | collective-permute-start | bytes 2457608 | tf_op jit(solution)/shard_map/ppermute | solution.py:378
  212.1 14.9 %collective-permute-start.47 = (f32[8,200,128]{2,1,0:T(8,128)S(1)}, f32[8,200,128]{2,1,0:T(8,128)S(1)}, u32[]{:S(2)}, u32[]{:S(2)}) collective-permute-start(f32[8,200,128]{2,1,0:T(8,128)S(1)} %constant_dynamic-update-slice_fusion.20.refs_0_), channel_id=1, source_target_pairs={{0,1},{1,0},{2,3},{3,2},{4,5},{5,4},{6,7},{7,6},{8,9},{9,8},{10,11... | collective-permute-start | bytes 2457608 | tf_op jit(solution)/shard_map/ppermute | solution.py:378
  212.1 12.8 %collective-permute-start.48 = (f32[4,208,128]{2,1,0:T(8,128)S(1)}, f32[4,208,128]{2,1,0:T(8,128)S(1)}, u32[]{:S(2)}, u32[]{:S(2)}) collective-permute-start(f32[4,208,128]{2,1,0:T(8,128)S(1)} %constant_dynamic-update-slice_fusion.18), channel_id=1, source_target_pairs={{0,4},{1,3},{2,6},{3,1},{4,0},{5,7},{6,2},{7,5},{8,12},{9,11},{10,... | collective-permute-start | bytes 1277960 | tf_op jit(solution)/shard_map/ppermute | solution.py:378
  224.9 12.8 %collective-permute-start.51 = (f32[8,208,128]{2,1,0:T(8,128)S(1)}, f32[8,208,128]{2,1,0:T(8,128)S(1)}, u32[]{:S(2)}, u32[]{:S(2)}) collective-permute-start(f32[8,208,128]{2,1,0:T(8,128)S(1)} %constant_dynamic-update-slice_fusion.22.refs_0_), channel_id=1, source_target_pairs={{0,2},{1,5},{2,0},{3,7},{4,6},{5,1},{6,4},{7,3},{8,10},{9,13},{10,... | collective-permute-start | bytes 2555912 | tf_op jit(solution)/shard_map/ppermute | solution.py:378
  225.3 12.3 %collective-permute-start.52 = (f32[8,208,128]{2,1,0:T(8,128)S(1)}, f32[8,208,128]{2,1,0:T(8,128)S(1)}, u32[]{:S(2)}, u32[]{:S(2)}) collective-permute-start(f32[8,208,128]{2,1,0:T(8,128)S(1)} %constant_dynamic-update-slice_fusion.22.refs_0_), channel_id=1, source_target_pairs={{0,1},{1,0},{2,3},{3,2},{4,5},{5,4},{6,7},{7,6},{8,9},{9,8},{10,11... | collective-permute-start | bytes 2555912 | tf_op jit(solution)/shard_map/ppermute | solution.py:378
  227.0 2.3 collective-permute-start.50
  237.7 2.4 collective-permute-start.53
  (11 other events, 19.9 us)

commit v4 on v3

--- a/solution.py
+++ b/solution.py
@@ -17,6 +17,14 @@
 EPSILON = 1e-06
 F32 = jnp.float32
 BF16 = jnp.bfloat16
+PLACES = {"late": 0, "cross": 2, "own": 4, "patch": 6}
+AXES = {
+    "late": ((1, 2, 3, 4), (2, 1, 4, 3)),
+    "cross": ((1, 2, 3, 4), (2, 1, 4, 3)),
+    "own": ((1, 2, 3, 4), (2, 1, 4, 3)),
+    "patch": ((1, 2, 3, 4), (2, 1, 4, 3)),
+}
+EARLY = ("late", "patch",)
 VMEM = pltpu.VMEM
 SMEM = pltpu.SMEM
 
@@ -97,7 +105,8 @@
     in_first = member_ref[me] == 1
     count_ref[0] = jnp.where(in_first, count, 0.0)
     count_ref[1] = jnp.where(in_first, 0.0, count)
-    code_ref[0], code_ref[1] = code_pair(me)
+    for name, place in PLACES.items():
+        code_ref[place], code_ref[place + 1] = code_pair(me, AXES[name])
 
 
 def weigh_kernel(me_ref, member_ref, mix_ref, *refs):
@@ -140,7 +149,7 @@
     wp_ref, bias_ref, wck_ref, wcv_ref,
     g1_ref, wq_ref, wk_ref, wv_ref, wo_ref, g2_ref, wcq_ref, wco_ref, g3_ref, wg_ref, wu_ref, wd_ref,
     feat_ref, kv_ref, qkv_ref, pt_ref, o_ref, x1_ref, cq_ref, pc_ref, oc_ref,
-    out_ref, dx2_ref, gain_ref, keep_low, keep_high, send_low, send_high,
+    out_ref, dx2_ref, gain_ref, keep_ref, send_ref,
     join_kv, join_qkv, wcq, h3_all, de_all, hid_all, dgate_all, dup_all, acc_down, acc_gate, acc_up,
 ):
     step, steps = pl.program_id(0), pl.num_programs(0)
@@ -228,13 +237,13 @@
             acc_gate[:, cols] = dot_rows(h3_all[...], dgate_all[:, cols])
             acc_up[:, cols] = dot_rows(h3_all[...], dup_all[:, cols])
         items = [(acc_down, acc_down.shape, 0), (acc_gate, acc_gate.shape, 0), (acc_up, acc_up.shape, 0)]
-        pack(items, code_ref, keep_low, keep_high, send_low, send_high)
+        pack(items, code_ref, PLACES["late"], keep_ref, send_ref)
 
 
 def cross_backward_kernel(
     code_ref, dx2_ref, cq_ref, pt_ref, kv_ref, x1_ref, oc_ref, feat_ref,
     g2_ref, wco_ref, wcq_ref, wck_ref, wcv_ref,
-    dfeat_ref, dx1_ref, gain_ref, bias_ref, keep_low, keep_high, send_low, send_high,
+    dfeat_ref, dx1_ref, gain_ref, bias_ref, keep_ref, send_ref,
     joined, dcq_all, dkv_all, dc_all, h2_all, oc_all, feat_all, acc_out, acc_query, acc_kv,
 ):
     step, steps = pl.program_id(0), pl.num_programs(0)
@@ -286,17 +295,17 @@
         small = acc_query.shape
         items = [(acc_out, acc_out.shape, 0), (acc_query, small, 0)]
         items += [(acc_kv, small, 0), (acc_kv, small, INNER)]
-        pack(items, code_ref, keep_low, keep_high, send_low, send_high)
-
-
-def patch_weight_kernel(code_ref, patch_ref, dfeat_ref, keep_low, keep_high, send_low, send_high, acc, turned):
+        pack(items, code_ref, PLACES["cross"], keep_ref, send_ref)
+
+
+def patch_weight_kernel(code_ref, patch_ref, dfeat_ref, keep_ref, send_ref, acc, turned):
     step, steps = pl.program_id(0), pl.num_programs(0)
     add_to(acc, step == 0, dot_rows(dfeat_ref[...], patch_ref[...]))
 
     @pl.when(step == steps - 1)
     def finish():
         turned[...] = acc[...].T
-        pack([(turned, turned.shape, 0)], code_ref, keep_low, keep_high, send_low, send_high)
+        pack([(turned, turned.shape, 0)], code_ref, PLACES["patch"], keep_ref, send_ref)
 
 
 def patch_input_kernel(weight_ref, dfeat_ref, w_ref, *refs):
@@ -306,7 +315,7 @@
 def self_backward_kernel(
     code_ref, weight_ref, dx1_ref, qkv_ref, pt_ref, tok_ref, o_ref,
     g1_ref, wo_ref, wq_ref, wk_ref, wv_ref, gain_two_ref, gain_three_ref, bias_ref,
-    dtok_ref, keep_low, keep_high, send_low, send_high,
+    dtok_ref, keep_ref, send_ref,
     joined, dqkv_all, da_all, h1_all, o_all, acc_out, acc_qkv, gain_one, gain_block,
 ):
     step, steps = pl.program_id(0), pl.num_programs(0)
@@ -356,21 +365,26 @@
         items = [(acc_out, acc_out.shape, 0)]
         items += [(acc_qkv, small, k * INNER) for k in range(3)]
         items += [(gain_block, gain_block.shape, 0)]
-        pack(items, code_ref, keep_low, keep_high, send_low, send_high)
+        pack(items, code_ref, PLACES["own"], keep_ref, send_ref)
 
 
 def flips(count, first, second):
     return [(i, i ^ (first if i % 2 == 0 else second)) for i in range(count)]
 
 
-def code_pair(me):
-    core, ex, why = me & 1, (me >> 1) & 1, (me >> 2) & 1
-    near, far = (me >> 3) & 1, (me >> 4) & 1
-    even = ex * 8 + why * 4 + near * 2 + far
-    odd = why * 8 + ex * 4 + far * 2 + near
-    own = core * 16 + jnp.where(core == 0, even, odd)
-    other = (1 - core) * 16 + jnp.where(core == 0, odd, even)
-    return own, other
+def code_of(me, core, axes):
+    code = core
+    for axis in axes:
+        code = code * 2 + ((me >> axis) & 1)
+    return code
+
+
+def code_pair(me, axes):
+    core = me & 1
+    even, odd = code_of(me, core, axes[0]), code_of(me, core, axes[1])
+    own = jnp.where(core == 0, even, odd)
+    other = jnp.where(core == 0, odd, even)
+    return own, other ^ HALF
 
 
 def exchange(values, first, second=None):
@@ -401,26 +415,25 @@
     ]
 
 
-def pack(items, code_ref, *out_refs):
+def pack(items, code_ref, place, keep_ref, send_ref):
     def step(p, carry):
-        for k, out_ref in enumerate(out_refs):
+        for code, out_ref in ((code_ref[place], keep_ref), (code_ref[place + 1], send_ref)):
             start = 0
-            index = (p + 8 * (k % 2)) ^ code_ref[k // 2]
             for ref, shape, offset in items:
-                for rows, lanes in block_parts(shape, index, offset):
+                for rows, lanes in block_parts(shape, p ^ code, offset):
                     out_ref[p, pl.ds(start, rows.size), :] = ref[rows, lanes]
                     start += rows.size
         return carry
 
-    lax.fori_loop(0, 8, step, 0)
-
-
-def unpack_kernel(shapes, with_gains, code_ref, *refs):
+    lax.fori_loop(0, HALF, step, 0)
+
+
+def unpack_kernel(shapes, with_gains, place, code_ref, *refs):
     ins, outs = refs[:4], refs[4:]
     for k, piece in enumerate(ins):
 
         def step(p, carry, piece=piece, k=k):
-            index = (p + 8 * (k % 2)) ^ code_ref[k // 2]
+            index = (p + 8 * (k % 2)) ^ code_ref[place + k // 2]
             start = 0
             for shape, out_ref in zip(shapes, outs):
                 for rows, lanes in block_parts(shape, index, 0):
@@ -441,12 +454,12 @@
     return [pl.BlockSpec(memory_space=VMEM)] * count
 
 
-def unpack(pieces, shapes, codes, with_gains=False):
+def unpack(pieces, shapes, codes, place, with_gains=False):
     outs = [jax.ShapeDtypeStruct(s, F32) for s in shapes]
     if with_gains:
         outs += [jax.ShapeDtypeStruct((1, 512), F32)] * 4
     return pl.pallas_call(
-        functools.partial(unpack_kernel, shapes, with_gains),
+        functools.partial(unpack_kernel, shapes, with_gains, place),
         out_shape=outs,
         in_specs=[pl.BlockSpec(memory_space=SMEM)] + vmem(4),
         out_specs=vmem(len(outs)),
@@ -456,35 +469,41 @@
 
 
 class Chunk:
-    def __init__(self, packed, shapes, codes, weights=None, with_gains=False):
+    def __init__(self, name, packed, shapes, codes, weights=None, with_gains=False):
         self.held, self.got, self.stage = tuple(packed), (), 0
-        self.shapes, self.codes, self.weights, self.with_gains = shapes, codes, weights, with_gains
+        self.name, self.shapes, self.codes = name, shapes, codes
+        self.weights, self.with_gains = weights, with_gains
 
     def advance(self, token):
         (self.held, self.got), token = lax.optimization_barrier(((self.held, self.got), token))
-        take, send = STAGES[self.stage]
+        take, send, axis = STAGES[self.stage]
         self.stage += 1
         if take is not None:
             take(self)
-        send(self)
+        send(self, axis)
         return self.held[0]
 
-    def send_cores(self):
-        _, _, low, high = self.held
-        self.got = (exchange(high, 1), exchange(low, 1))
+    def land(self, token):
+        self.got, token = lax.optimization_barrier((self.got, token))
+        return token
+
+    def over(self, values, axis):
+        even, odd = AXES[self.name]
+        return exchange(values, 1 << even[axis], 1 << odd[axis])
+
+    def send_cores(self, axis):
+        self.got = (exchange(self.held[1], 1),)
 
     def take_cores(self):
-        keep_low, keep_high, _, _ = self.held
-        high, low = self.got
-        self.held = (keep_high * self.weights[0] + high * self.weights[1], keep_low)
-        self.got = (low,)
-
-    def send_first(self):
-        self.got += (exchange(self.held[0], 2, 4),)
+        (keep, _), (got,), (own, other) = self.held, self.got, self.weights
+        self.held = (keep[8:] * own + got[8:] * other, keep)
+
+    def send_first(self, axis):
+        self.got += (self.over(self.held[0], axis),)
 
     def take_first(self):
-        (_, keep), (low, got) = self.held, self.got
-        keep = keep * self.weights[0] + low * self.weights[1]
+        (_, keep), (low, got), (own, other) = self.held, self.got, self.weights
+        keep = keep[:8] * own + low[:8] * other
         self.held = (keep[4:] + got[4:], keep[:4] + got[:4])
 
     def take_half(self):
@@ -503,38 +522,37 @@
     def take_back(self):
         self.held = (jnp.concatenate([*self.held, *self.got]),)
 
-    def send_second(self):
-        self.got = (exchange(self.held[0], 4, 2),)
-
-    def send_third(self):
-        self.got = (exchange(self.held[0], 8, 16),)
-
-    def send_fourth(self):
-        self.got = (exchange(self.held[0], 16, 8),)
-
-    def send_back_first(self):
-        self.got = (exchange(self.held[0], 2, 4), exchange(self.held[0], 1))
-
-    def send_back_cores(self):
-        self.held = (self.held[0], *self.got)
-        self.got = (exchange(self.held[1], 1),)
+    def send(self, axis):
+        self.got = (self.over(self.held[0], axis),)
+
+    def send_back_first(self, axis):
+        self.send(axis)
+        if self.name in EARLY:
+            self.got += (exchange(self.held[0], 1),)
+
+    def send_back_cores(self, axis):
+        rest = self.got[0]
+        self.held += self.got
+        self.got = (exchange(rest, 1),)
+        if len(self.held) < 3:
+            self.held += (exchange(self.held[0], 1),)
 
     def unpack(self, token):
         (held, got), token = lax.optimization_barrier(((self.held, self.got), token))
-        return unpack(held + got, self.shapes, self.codes, self.with_gains)
+        return unpack(held + got, self.shapes, self.codes, PLACES[self.name], self.with_gains)
 
 
 STAGES = (
-    (None, Chunk.send_cores),
-    (Chunk.take_cores, Chunk.send_first),
-    (Chunk.take_first, Chunk.send_second),
-    (Chunk.take_half, Chunk.send_third),
-    (Chunk.take_half, Chunk.send_fourth),
-    (Chunk.take_last, Chunk.send_fourth),
-    (Chunk.take_back, Chunk.send_third),
-    (Chunk.take_back, Chunk.send_second),
-    (Chunk.take_back, Chunk.send_back_first),
-    (None, Chunk.send_back_cores),
+    (None, Chunk.send_cores, 0),
+    (Chunk.take_cores, Chunk.send_first, 0),
+    (Chunk.take_first, Chunk.send, 1),
+    (Chunk.take_half, Chunk.send, 2),
+    (Chunk.take_half, Chunk.send, 3),
+    (Chunk.take_last, Chunk.send, 3),
+    (Chunk.take_back, Chunk.send, 2),
+    (Chunk.take_back, Chunk.send, 1),
+    (Chunk.take_back, Chunk.send_back_first, 0),
+    (None, Chunk.send_back_cores, 0),
 )
 
 
@@ -548,6 +566,7 @@
 
 
 SCALARS = pl.BlockSpec(memory_space=SMEM)
+IN_VMEM = pl.BlockSpec(memory_space=VMEM)
 
 
 def run_small(kernel, name, operands, outs, ins=None):
@@ -573,14 +592,23 @@
         out_shape=[jax.ShapeDtypeStruct(s, d) for s, d, _ in outs],
         in_specs=in_specs,
         out_specs=[
-            SCALARS if moves is None else by_step(s, steps) if moves else whole(s)
+            SCALARS if moves is None else by_step(s, steps) if moves else IN_VMEM if name != "forward" else whole(s)
             for s, _, moves in outs
         ],
         scratch_shapes=[VMEM(s, d) for s, d in scratch],
-        compiler_params=pltpu.CompilerParams(vmem_limit_bytes=56 * 2**20),
+        compiler_params=pltpu.CompilerParams(vmem_limit_bytes=(56 if name == "forward" else 44) * 2**20),
         cost_estimate=pl.CostEstimate(flops=int(cost * 1e9), bytes_accessed=2**20, transcendentals=0),
         name=name,
     )(*operands)
+
+
+ORDER = (
+    "late", "cross kernel", "late", "cross", "self kernel", "cross", "own", "late",
+    "patch kernel", "own", "late", "patch", "cross", "input kernel", "late", "cross", "patch",
+    "own", "late", "cross", "input kernel", "patch", "late", "own", "patch", "cross", "own",
+    "cross", "late", "patch", "own", "cross", "patch", "own", "patch", "cross", "late", "own",
+    "late", "patch", "cross", "own", "cross", "patch", "own", "own", "patch", "patch",
+)
 
 
 def local(
@@ -624,7 +652,7 @@
     in_vmem = pl.BlockSpec(memory_space=VMEM)
     counts, codes = run_small(
         count_kernel, "count", [me_ref, lengths, group_member],
-        [((2,), F32, SCALARS), ((2,), jnp.int32, SCALARS)],
+        [((2,), F32, SCALARS), ((8,), jnp.int32, SCALARS)],
     )
     devices = lax.axis_size("dp")
     counts = counts + exchange(counts, 1)
@@ -655,7 +683,7 @@
             ((rows, width), BF16, True),
             ((rows, width), F32, True),
             ((1, width), F32, False),
-        ] + [((8, late_rows, 128), F32, False)] * 4,
+        ] + [((HALF, late_rows, 128), F32, False)] * 2,
         [
             ((width, 2 * INNER), BF16),
             ((width, 3 * INNER), BF16),
@@ -672,7 +700,7 @@
         40.0,
     )
     late, column = lax.optimization_barrier((late, column))
-    late = Chunk(late, late_shapes, codes)
+    late = Chunk("late", late, late_shapes, codes)
     token = late.advance(dx2)
     column, token = lax.optimization_barrier((column, token))
     counts = sum(column)
@@ -680,8 +708,7 @@
     while bit < devices:
         counts = counts + exchange(counts, bit)
         bit *= 2
-    counts = counts + exchange(counts, 2)
-    parts = [counts, exchange(counts, 4)]
+    parts = [counts] + [exchange(counts, bit) for bit in (2, 4, 6)]
     row = (1, 1, 128)
     weights, *rows_of_weights = run_small(
         weigh_kernel, "weigh", [me_ref, group_member, mix, *parts],
@@ -703,7 +730,7 @@
                 ((rows, width), F32, True),
                 ((1, width), F32, False),
                 ((1, width), F32, False),
-            ] + [((8, cross_rows, 128), F32, False)] * 4,
+            ] + [((HALF, cross_rows, 128), F32, False)] * 2,
             [
                 ((width, 2 * INNER), BF16),
                 ((rows, INNER), BF16),
@@ -718,7 +745,7 @@
             ],
             20.0,
         )
-        return (dfeat, dx1, gain2, dbias), Chunk(cross, cross_shapes, codes, late.weights)
+        return (dfeat, dx1, gain2, dbias), Chunk("cross", cross, cross_shapes, codes, late.weights)
 
     def self_backward(token, dx1, gain2, dbias):
         tied, token = lax.optimization_barrier((dx1, token))
@@ -728,7 +755,7 @@
             self_backward_kernel, "self_backward", steps, [codes, weights],
             [tied, qkv, chances, tokens, mixed],
             [gain_one, w_out, w_query, w_key, w_value, gain2, gain3, dbias], "ssrrrrr" + "f" * 8,
-            [((rows, width), F32, True)] + [((8, own_rows, 128), F32, False)] * 4,
+            [((rows, width), F32, True)] + [((HALF, own_rows, 128), F32, False)] * 2,
             [
                 ((width, 3 * INNER), BF16),
                 ((rows, 3 * INNER), BF16),
@@ -742,7 +769,7 @@
             ],
             16.0,
         )
-        return grad_tokens, Chunk(own, own_shapes, codes, late.weights, True)
+        return grad_tokens, Chunk("own", own, own_shapes, codes, late.weights, True)
 
     def patch_weight(token, dfeat):
         tied, token = lax.optimization_barrier((dfeat, token))
@@ -750,10 +777,10 @@
         patch_rows = block_rows(w_patch.shape)
         patch = run(
             patch_weight_kernel, "patch_weight", steps, [codes], [flat, tied], [], "srr",
-            [((8, patch_rows, 128), F32, False)] * 4,
+            [((HALF, patch_rows, 128), F32, False)] * 2,
             [((width, patch_dim), F32), ((patch_dim, width), F32)], 12.0,
         )
-        return Chunk(patch, patch_shapes, codes, late.weights)
+        return Chunk("patch", patch, patch_shapes, codes, late.weights)
 
     def patch_input(token, dfeat, half, out):
         tied, token = lax.optimization_barrier((dfeat, token))
@@ -775,14 +802,7 @@
         )(weights, tied, w_patch, *out)
 
     chunks, done, grad_patches = {"late": late}, {}, ()
-    for name in (
-        "late", "cross kernel", "late", "cross", "self kernel", "cross", "own", "late",
-        "patch kernel", "late", "own", "patch", "cross", "patch", "late", "input kernel",
-        "cross", "own", "late", "input kernel", "cross", "patch", "own", "late", "cross",
-        "patch", "own", "cross", "late", "patch", "own", "cross", "patch", "own", "cross",
-        "late", "patch", "own", "late", "cross", "patch", "own", "cross", "patch", "own", "own",
-        "patch", "patch",
-    ):
+    for name in ORDER:
         if name == "cross kernel":
             (dfeat, dx1, gain2, dbias), chunks["cross"] = cross_backward(token)
             token = dx1
@@ -796,6 +816,8 @@
             half = len(grad_patches)
             grad_patches = (patch_input(token, dfeat, half, grad_patches),)
             token = grad_patches
+        elif name.endswith(" lands"):
+            token = chunks[name[:-6]].land(token)
         elif chunks[name].stage < len(STAGES):
             token = chunks[name].advance(token)
         else:

time: 243 us -> 236 us (0.971)
  starting transfers between devices: 55.2 us -> 47 us
  Pallas kernels: 111 us -> 105 us
  waiting for transfers between devices: 69.3 us -> 74.4 us
    ppermute x54 -> x51, starting transfers between devices: 55.2 us -> 47 us  [exchange(): lax.ppermute(values, 'dp', flips(count, first, first if second is None el...]
    pallas_call x4, Pallas kernels: 85.4 us -> 79.6 us  [run(): pl.pallas_call(kernel, grid=(steps,), out_shape=[jax.ShapeDtypeStruct(s,...]
    ppermute x54 -> x51, waiting for transfers between devices: 69.3 us -> 74.4 us  [exchange(): lax.ppermute(values, 'dp', flips(count, first, first if second is None el...]
  transfers between devices with their start and end apart: 54 -> 51, of which waited for: 23 -> 30; matrix products, arithmetic and copies ran while one was open for 1% -> 1% of each run, Pallas kernels for 44% -> 43%
where the time goes in v4:
time: 236 us
  Pallas kernels  105 us (44%)
  waiting for transfers between devices  74.4 us (32%)
  starting transfers between devices  47 us (20%)
  other arithmetic  4.22 us (2%)
  local copies, waits for them, and re-layouts  4.04 us (2%)
    pallas_call x4, Pallas kernels, run(): pl.pallas_call(kernel, grid=(steps,), out_shape=[jax.ShapeDtypeStruct(s,...  79.6 us
    ppermute x51, waiting for transfers between devices, exchange(): lax.ppermute(values, 'dp', flips(count, first, first if second is None el...  74.4 us
    ppermute x51, starting transfers between devices, exchange(): lax.ppermute(values, 'dp', flips(count, first, first if second is None el...  47 us
    pallas_call x4, Pallas kernels, unpack(): pl.pallas_call(functools.partial(unpack_kernel, shapes, with_gains, place...  12.8 us
    pallas_call x2, Pallas kernels, patch_input(): pl.pallas_call(patch_input_kernel, grid=(steps,), out_shape=jax.ShapeDtyp...  9.93 us
  transfers between devices with their start and end apart: 51, of which 30 were waited for; matrix products, arithmetic and copies ran while one was open for 1% of the time, Pallas kernels for 43%

profile of v4, /device:TPU:0, one launch (start us, length us, event | category | flops | bytes accessed | tf_op | source)
XLA Modules:
  0.0 235.8 jit_solution(12778730700287411097)
XLA Ops:
  0.7 1.2 count.1
  2.4 1.0 collective-permute-done
  4.0 4.9 %collective-permute-start.3 = (f32[2]{0:T(128)S(1)}, f32[2]{0:T(128)S(1)}, u32[]{:S(2)}, u32[]{:S(2)}) collective-permute-start(f32[2]{0:T(128)S(1)} %add.120), channel_id=1, source_target_pairs={{0,24},{1,25},{2,26},{3,27},{4,28},{5,29},{6,30},{7,31},{8,16},{9,... | collective-permute-start | bytes 32 | tf_op jit(solution)/shard_map/ppermute | solution.py:392
  9.5 38.9 %forward.1 = (bf16[2048,512]{1,0:T(8,128)(2,1)}, bf16[2048,768]{1,0:T(8,128)(2,1)}, bf16[1024,1152]{1,0:T(8,128)(2,1)}, bf16[8,3,256,128]{3,2,1,0:T(8,128)(2,1)}...) custom-call(s32[8]{0:T(128)} %len_ref.3, ...), custom_call_target="tpu_custom_call" | custom-call | flops 40000000000 | bytes 1048576 | tf_op jit(solution)/shard_map/forward/pallas_call | solution.py:589
  48.5 2.7 %collective-permute-start.6 = (f32[2]{0:T(128)S(1)}, f32[2]{0:T(128)S(1)}, u32[]{:S(2)}, u32[]{:S(2)}) collective-permute-start(f32[2]{0:T(128)S(1)} %add_add_fusion.refs_0_), channel_id=1, source_target_pairs={{0,6},{1,7},{2,4},{3,5},{4,2},{5,3},{6,0},{7,1},{8,14},{9,15},{10,... | collective-permute-start | bytes 32 | tf_op jit(solution)/shard_map/ppermute | solution.py:392
  52.1 0.9 collective-permute-done.6.refs_3_
  53.0 1.8 collective-permute-done.5.refs_2_
  55.8 1.3 weigh.1
  57.2 1.9 multiply_add_fusion.1
  59.8 18.2 %cross_backward.1 = (bf16[2048,512]{1,0:T(8,128)(2,1)S(1)}, f32[1024,512]{1,0:T(8,128)}, f32[1,512]{1,0:T(1,128)S(1)}, f32[1,512]{1,0:T(1,128)S(1)}, f32[16,192,...) custom-call(s32[8]{0:T(128)S(1)} %copy-done.1, f32[1024,512]{1,0:T(8,128)} %get-tuple-element.208.dx2_ref, ...), custom_call_target="tpu_custom_call" | custom-call | flops 20000000000 | bytes 1048576 | tf_op jit(solution)/shard_map/cross_backward/pallas_call | solution.py:589
  78.0 1.6 collective-permute-done.8
  79.6 1.1 copy-done.21
  81.0 1.1 copy-done.22
  82.5 1.6 collective-permute-start.11
  84.7 13.4 %self_backward.1 = (f32[1024,512]{1,0:T(8,128)}, f32[16,200,128]{2,1,0:T(8,128)S(1)}, f32[16,200,128]{2,1,0:T(8,128)S(1)}) custom-call(s32[8]{0:T(128)S(1)} %copy-done.1, f32[2]{0:T(128)S(1)} %copy-done.2, f32[1024,512]{1,0:T(8,128)S(1)} %copy-done.14, bf16[1024,1152]{1,0:T(8,128)(2,1)} %get-tuple-element.223.qkv_ref, ...), custom_call_target="tpu_custom_call" | custom-call | flops 16000000000 | bytes 1048576 | tf_op jit(solution)/shard_map/self_backward/pallas_call | solution.py:589
  99.0 1.3 collective-permute-start.12
  100.3 9.1 %patch_weight.1 = (f32[16,208,128]{2,1,0:T(8,128)S(1)}, f32[16,208,128]{2,1,0:T(8,128)S(1)}) custom-call(s32[8]{0:T(128)S(1)} %copy-done.1, bf16[2048,1664]{1,0:T(8,128)(2,1)} %bitcast.35, bf16[2048,512]{1,0:T(8,128)(2,1)S(1)} %get-tuple-element.266.dfeat_ref), custom_call_target="tpu_custom_call" | custom-call | flops 12000000000 | bytes 1048576 | tf_op jit(solution)/shard_map/patch_weight/pallas_call | solution.py:589
  109.5 1.3 collective-permute-done.12
  111.4 1.9 collective-permute-start.15
  113.5 1.6 collective-permute-start.14
  115.0 0.9 collective-permute-start.18
  115.9 5.0 %patch_input.2.refs_0_ = f32[2048,1664]{1,0:T(8,128)} custom-call(f32[2]{0:T(128)S(1)} %copy-done.2, bf16[2048,512]{1,0:T(8,128)(2,1)S(1)} %get-tuple-element.266.dfeat_ref, bf16[1664,512]{1,0:T(8,128)(2,1)S(1)} %copy-done), custom_call_target="tpu_custom_call" | custom-call | flops 6000000000 | bytes 1048576 | tf_op jit(solution)/shard_map/patch_input/pallas_call | solution.py:787
  121.4 4.1 %collective-permute-done.14 = f32[4,192,128]{2,1,0:T(8,128)S(1)} collective-permute-done((f32[4,192,128]{2,1,0:T(8,128)S(1)}, f32[4,192,128]{2,1,0:T(8,128)S(1)}, u32[]{:S(2)}, u32[]{:S(2)}) %collective-permute-start.14) | collective-permute-done | bytes 393248 | tf_op jit(solution)/shard_map/ppermute | solution.py:392
  125.5 2.9 %collective-permute-start.16 = (f32[2,192,128]{2,1,0:T(8,128)S(1)}, f32[2,192,128]{2,1,0:T(8,128)S(1)}, u32[]{:S(2)}, u32[]{:S(2)}) collective-permute-start(f32[2,192,128]{2,1,0:T(8,128)S(1)} %get-tuple-element.362), channel_id=1, source_target_pairs={{0,8},{1,17},{2,10},{3,19},{4,12},{5,21},{6,14},{7,23},{8,0},{9,25... | collective-permute-start | bytes 589832 | tf_op jit(solution)/shard_map/ppermute | solution.py:392
  128.5 1.0 collective-permute-start.22
  129.7 2.5 %collective-permute-done.17 = f32[1,384,128]{2,1,0:T(8,128)S(1)} collective-permute-done((f32[1,384,128]{2,1,0:T(8,128)S(1)}, f32[1,384,128]{2,1,0:T(8,128)S(1)}, u32[]{:S(2)}, u32[]{:S(2)}) %collective-permute-start.17) | collective-permute-done | bytes 196640 | tf_op jit(solution)/shard_map/ppermute | solution.py:392
  132.2 2.2 collective-permute-done.16
  134.5 2.2 collective-permute-start.21
  136.7 0.8 collective-permute-start.20
  137.5 5.0 %patch_input.3 = f32[2048,1664]{1,0:T(8,128)} custom-call(f32[2]{0:T(128)S(1)} %copy-done.2, bf16[2048,512]{1,0:T(8,128)(2,1)S(1)} %get-tuple-element.266.dfeat_ref, bf16[1664,512]{1,0:T(8,128)(2,1)S(1)} %copy-done, f32[2048,1664]{1,0:T(8,128)} %patch_input.2.refs_0_), custom_call_target="tpu_custom_call", output_to_operand_aliasing={{}: (3, {})} | custom-call | flops 6000000000 | bytes 1048576 | tf_op jit(solution)/shard_map/patch_input/pallas_call | solution.py:787
  142.4 2.1 collective-permute-done.22
  145.2 1.7 collective-permute-start.28
  147.0 2.1 collective-permute-start.23
  149.1 3.8 %collective-permute-done.25 = f32[4,208,128]{2,1,0:T(8,128)S(1)} collective-permute-done((f32[4,208,128]{2,1,0:T(8,128)S(1)}, f32[4,208,128]{2,1,0:T(8,128)S(1)}, u32[]{:S(2)}, u32[]{:S(2)}) %collective-permute-start.25) | collective-permute-done | bytes 426016 | tf_op jit(solution)/shard_map/ppermute | solution.py:392
  153.1 1.5 collective-permute-done.23
  154.6 4.7 %collective-permute-done.29 = f32[1,192,128]{2,1,0:T(8,128)S(1)} collective-permute-done((f32[1,192,128]{2,1,0:T(8,128)S(1)}, f32[1,192,128]{2,1,0:T(8,128)S(1)}, u32[]{:S(2)}, u32[]{:S(2)}) %collective-permute-start.29) | collective-permute-done | bytes 98336 | tf_op jit(solution)/shard_map/ppermute | solution.py:392
  159.3 2.1 collective-permute-done.28
  161.9 1.6 collective-permute-start.26
  164.0 6.9 %collective-permute-done.27 = f32[2,208,128]{2,1,0:T(8,128)S(1)} collective-permute-done((f32[2,208,128]{2,1,0:T(8,128)S(1)}, f32[2,208,128]{2,1,0:T(8,128)S(1)}, u32[]{:S(2)}, u32[]{:S(2)}) %collective-permute-start.27) | collective-permute-done | bytes 213024 | tf_op jit(solution)/shard_map/ppermute | solution.py:392
  170.9 0.9 collective-permute-start.31
  171.8 2.2 collective-permute-start.30
  174.0 0.8 collective-permute-done.32
  174.9 1.7 collective-permute-start.36
  176.6 1.9 collective-permute-done.31
  178.5 1.2 collective-permute-start.37
  179.7 0.9 collective-permute-done.30
  180.6 4.6 %collective-permute-done.37 = f32[1,208,128]{2,1,0:T(8,128)S(1)} collective-permute-done((f32[1,208,128]{2,1,0:T(8,128)S(1)}, f32[1,208,128]{2,1,0:T(8,128)S(1)}, u32[]{:S(2)}, u32[]{:S(2)}) %collective-permute-start.37) | collective-permute-done | bytes 106528 | tf_op jit(solution)/shard_map/ppermute | solution.py:392
  185.8 1.1 collective-permute-start.41
  187.0 1.7 collective-permute-start.39
  188.7 2.0 collective-permute-start.40
  190.7 4.2 %collective-permute-done.33 = f32[2,200,128]{2,1,0:T(8,128)S(1)} collective-permute-done((f32[2,200,128]{2,1,0:T(8,128)S(1)}, f32[2,200,128]{2,1,0:T(8,128)S(1)}, u32[]{:S(2)}, u32[]{:S(2)}) %collective-permute-start.33) | collective-permute-done | bytes 204832 | tf_op jit(solution)/shard_map/ppermute | solution.py:392
  195.0 4.3 %unpack.4 = (f32[1024,512]{1,0:T(8,128)}, f32[512,1024]{1,0:T(8,128)}, f32[512,1024]{1,0:T(8,128)}) custom-call(s32[8]{0:T(128)S(1)} %copy-done.1, f32[8,384,128]{2,1,0:T(8,128)S(1)} %constant_dynamic-update-slice_fusion.6.refs_0_, f32[8,384,128]{2,1,0:T(8,128)S(1)} %collective-permute-done.34.refs_1_, f32[8,384,128]{2,1,0:T(8,128)S(1)} %collective-permute-done.35.refs_2_, ...), custom_call_target="tpu_custom_call" | custom-call | tf_op jit(solution)/shard_map/unpack/pallas_call | solution.py:461
  199.5 0.9 collective-permute-done.39.refs_1_
  200.9 2.1 collective-permute-done.38
  203.0 1.8 collective-permute-start.42
  204.8 2.8 %unpack.5 = (f32[384,512]{1,0:T(8,128)}, f32[512,384]{1,0:T(8,128)}, f32[512,384]{1,0:T(8,128)}, f32[512,384]{1,0:T(8,128)}) custom-call(s32[8]{0:T(128)S(1)} %copy-done.1, f32[8,192,128]{2,1,0:T(8,128)S(1)} %constant_dynamic-update-slice_fusion.14.refs_0_, f32[8,192,128]{2,1,0:T(8,128)S(1)} %collective-permute-done.39.refs_1_, ...), custom_call_target="tpu_custom_call" | custom-call | tf_op jit(solution)/shard_map/unpack/pallas_call | solution.py:461
  207.6 10.0 %collective-permute-done.43 = f32[4,208,128]{2,1,0:T(8,128)S(1)} collective-permute-done((f32[4,208,128]{2,1,0:T(8,128)S(1)}, f32[4,208,128]{2,1,0:T(8,128)S(1)}, u32[]{:S(2)}, u32[]{:S(2)}) %collective-permute-start.43) | collective-permute-done | bytes 426016 | tf_op jit(solution)/shard_map/ppermute | solution.py:392
  218.0 1.3 collective-permute-done.42.refs_1_
  219.8 1.8 collective-permute-done.46.refs_2_
  221.6 1.2 collective-permute-done.47.refs_3_
  222.8 2.8 %unpack.6 = (f32[384,512]{1,0:T(8,128)}, f32[512,384]{1,0:T(8,128)}, f32[512,384]{1,0:T(8,128)}, f32[512,384]{1,0:T(8,128)}, f32[256,128]{1,0:T(8,128)}, /*index...) custom-call(s32[8]{0:T(128)S(1)} %copy-done.1, ...), custom_call_target="tpu_custom_call" | custom-call | tf_op jit(solution)/shard_map/unpack/pallas_call | solution.py:461
  225.6 4.9 %collective-permute-done.48.refs_1_ = f32[8,208,128]{2,1,0:T(8,128)S(1)} collective-permute-done((f32[8,208,128]{2,1,0:T(8,128)S(1)}, f32[8,208,128]{2,1,0:T(8,128)S(1)}, u32[]{:S(2)}, u32[]{:S(2)}) %collective-permute-start.48) | collective-permute-done | bytes 852000 | tf_op jit(solution)/shard_map/ppermute | solution.py:392
  230.5 2.4 %collective-permute-done.50.refs_3_ = f32[8,208,128]{2,1,0:T(8,128)S(1)} collective-permute-done((f32[8,208,128]{2,1,0:T(8,128)S(1)}, f32[8,208,128]{2,1,0:T(8,128)S(1)}, u32[]{:S(2)}, u32[]{:S(2)}) %collective-permute-start.50) | collective-permute-done | bytes 852000 | tf_op jit(solution)/shard_map/ppermute | solution.py:392
  232.9 3.0 %unpack.7 = f32[1664,512]{1,0:T(8,128)} custom-call(s32[8]{0:T(128)S(1)} %copy-done.1, f32[8,208,128]{2,1,0:T(8,128)S(1)} %constant_dynamic-update-slice_fusion.22.refs_0_, f32[8,208,128]{2,1,0:T(8,128)S(1)} %collective-permute-done.48.refs_1_, f32[8,208,128]{2,1,0:T(8,128)S(1)} %collective-permute-done.49.refs_2_, ...), custom_call_target="tpu_custom_call" | custom-call | tf_op jit(solution)/shard_map/unpack/pallas_call | solution.py:461
  (158 shorter events, 12.4 us)
Async XLA Ops:
  1.9 1.5 collective-permute-start
  4.0 44.4 %collective-permute-start.3 = (f32[2]{0:T(128)S(1)}, f32[2]{0:T(128)S(1)}, u32[]{:S(2)}, u32[]{:S(2)}) collective-permute-start(f32[2]{0:T(128)S(1)} %add.120), channel_id=1, source_target_pairs={{0,24},{1,25},{2,26},{3,27},{4,28},{5,29},{6,30},{7,31},{8,16},{9,... | collective-permute-start | bytes 32 | tf_op jit(solution)/shard_map/ppermute | solution.py:392
  8.9 39.5 %collective-permute-start.2 = (f32[2]{0:T(128)S(1)}, f32[2]{0:T(128)S(1)}, u32[]{:S(2)}, u32[]{:S(2)}) collective-permute-start(f32[2]{0:T(128)S(1)} %add.120), channel_id=1, source_target_pairs={{0,16},{1,17},{2,18},{3,19},{4,20},{5,21},{6,22},{7,23},{8,24},{9,... | collective-permute-start | bytes 32 | tf_op jit(solution)/shard_map/ppermute | solution.py:392
  8.9 39.5 %collective-permute-start.1 = (f32[2]{0:T(128)S(1)}, f32[2]{0:T(128)S(1)}, u32[]{:S(2)}, u32[]{:S(2)}) collective-permute-start(f32[2]{0:T(128)S(1)} %add.120), channel_id=1, source_target_pairs={{0,8},{1,9},{2,10},{3,11},{4,12},{5,13},{6,14},{7,15},{8,0},{9,1},... | collective-permute-start | bytes 32 | tf_op jit(solution)/shard_map/ppermute | solution.py:392
  48.4 8.7 %collective-permute-start.7 = (f32[16,384,128]{2,1,0:T(8,128)}, f32[16,384,128]{2,1,0:T(8,128)S(1)}, u32[]{:S(2)}, u32[]{:S(2)}) collective-permute-start(f32[16,384,128]{2,1,0:T(8,128)} %get-tuple-element.203), channel_id=1, source_target_pairs={{0,1},{1,0},{2,3},{3,2},{4,5},{5,4},{6,7},{7,6},{8,9},{9,8},{10,11... | collective-permute-start | bytes 9437192 | tf_op jit(solution)/shard_map/ppermute | solution.py:392
  48.5 6.8 %copy-start.25 = (f32[2]{0:T(128)}, f32[2]{0:T(128)S(1)}, u32[]{:S(2)}) copy-start(f32[2]{0:T(128)S(1)} %add_add_fusion.refs_0_) | copy-start | bytes 28
  48.5 4.5 %collective-permute-start.6 = (f32[2]{0:T(128)S(1)}, f32[2]{0:T(128)S(1)}, u32[]{:S(2)}, u32[]{:S(2)}) collective-permute-start(f32[2]{0:T(128)S(1)} %add_add_fusion.refs_0_), channel_id=1, source_target_pairs={{0,6},{1,7},{2,4},{3,5},{4,2},{5,3},{6,0},{7,1},{8,14},{9,15},{10,... | collective-permute-start | bytes 32 | tf_op jit(solution)/shard_map/ppermute | solution.py:392
  51.3 3.5 %collective-permute-start.5 = (f32[2]{0:T(128)S(1)}, f32[2]{0:T(128)S(1)}, u32[]{:S(2)}, u32[]{:S(2)}) collective-permute-start(f32[2]{0:T(128)S(1)} %add_add_fusion.refs_0_), channel_id=1, source_target_pairs={{0,4},{1,5},{2,6},{3,7},{4,0},{5,1},{6,2},{7,3},{8,12},{9,13},{10,... | collective-permute-start | bytes 32 | tf_op jit(solution)/shard_map/ppermute | solution.py:392
  51.8 3.5 %collective-permute-start.4 = (f32[2]{0:T(128)S(1)}, f32[2]{0:T(128)S(1)}, u32[]{:S(2)}, u32[]{:S(2)}) collective-permute-start(f32[2]{0:T(128)S(1)} %add_add_fusion.refs_0_), channel_id=1, source_target_pairs={{0,2},{1,3},{2,0},{3,1},{4,6},{5,7},{6,4},{7,5},{8,10},{9,11},{10,... | collective-permute-start | bytes 32 | tf_op jit(solution)/shard_map/ppermute | solution.py:392
  57.1 2.6 %copy-start.1 = (s32[8]{0:T(128)S(1)}, s32[8]{0:T(128)}, u32[]{:S(2)}) copy-start(s32[8]{0:T(128)} %get-tuple-element.183.code_ref) | copy-start | bytes 100
  57.1 2.5 %copy-start.4 = (bf16[512,384]{1,0:T(8,128)(2,1)S(1)}, bf16[512,384]{1,0:T(8,128)(2,1)}, u32[]{:S(2)}) copy-start(bf16[512,384]{1,0:T(8,128)(2,1)} %wck_ref.3) | copy-start | bytes 1179652
  57.1 2.5 %copy-start.5 = (bf16[512,384]{1,0:T(8,128)(2,1)S(1)}, bf16[512,384]{1,0:T(8,128)(2,1)}, u32[]{:S(2)}) copy-start(bf16[512,384]{1,0:T(8,128)(2,1)} %wcv_ref.3) | copy-start | bytes 1179652
  57.2 2.5 %copy-start.6 = (bf16[512,384]{1,0:T(8,128)(2,1)S(1)}, bf16[512,384]{1,0:T(8,128)(2,1)}, u32[]{:S(2)}) copy-start(bf16[512,384]{1,0:T(8,128)(2,1)} %wcq_ref.3) | copy-start | bytes 1179652
  57.2 2.5 %copy-start.7 = (bf16[384,512]{1,0:T(8,128)(2,1)S(1)}, bf16[384,512]{1,0:T(8,128)(2,1)}, u32[]{:S(2)}) copy-start(bf16[384,512]{1,0:T(8,128)(2,1)} %wco_ref.3) | copy-start | bytes 1179652
  59.1 20.5 %collective-permute-start.8 = (f32[8,384,128]{2,1,0:T(8,128)S(1)}, f32[8,384,128]{2,1,0:T(8,128)S(1)}, u32[]{:S(2)}, u32[]{:S(2)}) collective-permute-start(f32[8,384,128]{2,1,0:T(8,128)S(1)} %multiply_add_fusion.1), channel_id=1, source_target_pairs={{0,2},{1,5},{2,0},{3,7},{4,6},{5,1},{6,4},{7,3},{8,10},{9,13},{10,... | collective-permute-start | bytes 4718600 | tf_op jit(solution)/shard_map/ppermute | solution.py:392
  59.7 21.0 %copy-start.20 = (f32[16,384,128]{2,1,0:T(8,128)S(1)}, f32[16,384,128]{2,1,0:T(8,128)}, u32[]{:S(2)}) copy-start(f32[16,384,128]{2,1,0:T(8,128)} %get-tuple-element.218) | copy-start | bytes 9437188
  59.7 21.0 %copy-start.23 = (f32[1,1,128]{2,1,0:T(1,128)S(1)}, f32[1,1,128]{2,1,0:T(1,128)}, u32[]{:S(2)}) copy-start(f32[1,1,128]{2,1,0:T(1,128)} %get-tuple-element.205) | copy-start | bytes 1540
  59.8 21.0 %copy-start.24 = (f32[1,1,128]{2,1,0:T(1,128)S(1)}, f32[1,1,128]{2,1,0:T(1,128)}, u32[]{:S(2)}) copy-start(f32[1,1,128]{2,1,0:T(1,128)} %get-tuple-element.207) | copy-start | bytes 1540
  80.7 3.3 %copy-start.15 = (bf16[8,3,256,128]{3,2,1,0:T(8,128)(2,1)S(1)}, bf16[8,3,256,128]{3,2,1,0:T(8,128)(2,1)}, u32[]{:S(2)}) copy-start(bf16[8,3,256,128]{3,2,1,0:T(8,128)(2,1)} %get-tuple-element.224.pt_ref) | copy-start | bytes 4718596
  80.7 3.3 %copy-start.16 = (bf16[1024,384]{1,0:T(8,128)(2,1)S(1)}, bf16[1024,384]{1,0:T(8,128)(2,1)}, u32[]{:S(2)}) copy-start(bf16[1024,384]{1,0:T(8,128)(2,1)} %get-tuple-element.225.o_ref) | copy-start | bytes 2359300
  82.2 2.5 %copy-start.14 = (f32[1024,512]{1,0:T(8,128)S(1)}, f32[1024,512]{1,0:T(8,128)}, u32[]{:S(2)}) copy-start(f32[1024,512]{1,0:T(8,128)} %get-tuple-element.222.dx1_ref) | copy-start | bytes 6291460
  82.4 15.8 %collective-permute-start.9 = (f32[16,192,128]{2,1,0:T(8,128)S(1)}, f32[16,192,128]{2,1,0:T(8,128)S(1)}, u32[]{:S(2)}, u32[]{:S(2)}) collective-permute-start(f32[16,192,128]{2,1,0:T(8,128)S(1)} %get-tuple-element.231), channel_id=1, source_target_pairs={{0,1},{1,0},{2,3},{3,2},{4,5},{5,4},{6,7},{7,6},{8,9},{9,8},{10,11... | collective-permute-start | bytes 4718600 | tf_op jit(solution)/shard_map/ppermute | solution.py:392
  82.5 16.4 %collective-permute-start.11 = (f32[4,384,128]{2,1,0:T(8,128)S(1)}, f32[4,384,128]{2,1,0:T(8,128)S(1)}, u32[]{:S(2)}, u32[]{:S(2)}) collective-permute-start(f32[4,384,128]{2,1,0:T(8,128)S(1)} %get-tuple-element.348), channel_id=1, source_target_pairs={{0,4},{1,3},{2,6},{3,1},{4,0},{5,7},{6,2},{7,5},{8,12},{9,11},{10,... | collective-permute-start | bytes 2359304 | tf_op jit(solution)/shard_map/ppermute | solution.py:392
  98.2 11.2 %collective-permute-start.13 = (f32[16,200,128]{2,1,0:T(8,128)S(1)}, f32[16,200,128]{2,1,0:T(8,128)S(1)}, u32[]{:S(2)}, u32[]{:S(2)}) collective-permute-start(f32[16,200,128]{2,1,0:T(8,128)S(1)} %get-tuple-element.242), channel_id=1, source_target_pairs={{0,1},{1,0},{2,3},{3,2},{4,5},{5,4},{6,7},{7,6},{8,9},{9,8},{10,11... | collective-permute-start | bytes 4915208 | tf_op jit(solution)/shard_map/ppermute | solution.py:392
  98.3 14.9 %collective-permute-start.10 = (f32[8,192,128]{2,1,0:T(8,128)S(1)}, f32[8,192,128]{2,1,0:T(8,128)S(1)}, u32[]{:S(2)}, u32[]{:S(2)}) collective-permute-start(f32[8,192,128]{2,1,0:T(8,128)S(1)} %multiply_add_fusion.7), channel_id=1, source_target_pairs={{0,2},{1,5},{2,0},{3,7},{4,6},{5,1},{6,4},{7,3},{8,10},{9,13},{10,... | collective-permute-start | bytes 2359304 | tf_op jit(solution)/shard_map/ppermute | solution.py:392
  99.0 11.9 %collective-permute-start.12 = (f32[2,384,128]{2,1,0:T(8,128)S(1)}, f32[2,384,128]{2,1,0:T(8,128)S(1)}, u32[]{:S(2)}, u32[]{:S(2)}) collective-permute-start(f32[2,384,128]{2,1,0:T(8,128)S(1)} %get-tuple-element.356), channel_id=1, source_target_pairs={{0,8},{1,17},{2,10},{3,19},{4,12},{5,21},{6,14},{7,23},{8,0},{9,25... | collective-permute-start | bytes 1179656 | tf_op jit(solution)/shard_map/ppermute | solution.py:392
  110.9 17.5 %collective-permute-start.19 = (f32[16,208,128]{2,1,0:T(8,128)S(1)}, f32[16,208,128]{2,1,0:T(8,128)S(1)}, u32[]{:S(2)}, u32[]{:S(2)}) collective-permute-start(f32[16,208,128]{2,1,0:T(8,128)S(1)} %get-tuple-element.256), channel_id=1, source_target_pairs={{0,1},{1,0},{2,3},{3,2},{4,5},{5,4},{6,7},{7,6},{8,9},{9,8},{10,11... | collective-permute-start | bytes 5111816 | tf_op jit(solution)/shard_map/ppermute | solution.py:392
  111.4 9.6 %collective-permute-start.15 = (f32[1,384,128]{2,1,0:T(8,128)S(1)}, f32[1,384,128]{2,1,0:T(8,128)S(1)}, u32[]{:S(2)}, u32[]{:S(2)}) collective-permute-start(f32[1,384,128]{2,1,0:T(8,128)S(1)} %get-tuple-element.364), channel_id=1, source_target_pairs={{0,16},{1,9},{2,18},{3,11},{4,20},{5,13},{6,22},{7,15},{8,24},{9,1... | collective-permute-start | bytes 589832 | tf_op jit(solution)/shard_map/ppermute | solution.py:392
  113.3 2.6 %copy-start = (bf16[1664,512]{1,0:T(8,128)(2,1)S(1)}, bf16[1664,512]{1,0:T(8,128)(2,1)}, u32[]{:S(2)}) copy-start(bf16[1664,512]{1,0:T(8,128)(2,1)} %w_ref.3) | copy-start | bytes 5111812
  113.5 12.0 %collective-permute-start.14 = (f32[4,192,128]{2,1,0:T(8,128)S(1)}, f32[4,192,128]{2,1,0:T(8,128)S(1)}, u32[]{:S(2)}, u32[]{:S(2)}) collective-permute-start(f32[4,192,128]{2,1,0:T(8,128)S(1)} %get-tuple-element.354), channel_id=1, source_target_pairs={{0,4},{1,3},{2,6},{3,1},{4,0},{5,7},{6,2},{7,5},{8,12},{9,11},{10,... | collective-permute-start | bytes 1179656 | tf_op jit(solution)/shard_map/ppermute | solution.py:392
  115.0 14.5 %collective-permute-start.18 = (f32[8,200,128]{2,1,0:T(8,128)S(1)}, f32[8,200,128]{2,1,0:T(8,128)S(1)}, u32[]{:S(2)}, u32[]{:S(2)}) collective-permute-start(f32[8,200,128]{2,1,0:T(8,128)S(1)} %multiply_add_fusion.5), channel_id=1, source_target_pairs={{0,2},{1,5},{2,0},{3,7},{4,6},{5,1},{6,4},{7,3},{8,10},{9,13},{10,... | collective-permute-start | bytes 2457608 | tf_op jit(solution)/shard_map/ppermute | solution.py:392
  120.9 11.3 %collective-permute-start.17 = (f32[1,384,128]{2,1,0:T(8,128)S(1)}, f32[1,384,128]{2,1,0:T(8,128)S(1)}, u32[]{:S(2)}, u32[]{:S(2)}) collective-permute-start(f32[1,384,128]{2,1,0:T(8,128)S(1)} %add.137), channel_id=1, source_target_pairs={{0,16},{1,9},{2,18},{3,11},{4,20},{5,13},{6,22},{7,15},{8,24},{9,1... | collective-permute-start | bytes 589832 | tf_op jit(solution)/shard_map/ppermute | solution.py:392
  125.5 8.9 %collective-permute-start.16 = (f32[2,192,128]{2,1,0:T(8,128)S(1)}, f32[2,192,128]{2,1,0:T(8,128)S(1)}, u32[]{:S(2)}, u32[]{:S(2)}) collective-permute-start(f32[2,192,128]{2,1,0:T(8,128)S(1)} %get-tuple-element.362), channel_id=1, source_target_pairs={{0,8},{1,17},{2,10},{3,19},{4,12},{5,21},{6,14},{7,23},{8,0},{9,25... | collective-permute-start | bytes 589832 | tf_op jit(solution)/shard_map/ppermute | solution.py:392
  128.5 16.0 %collective-permute-start.22 = (f32[8,208,128]{2,1,0:T(8,128)S(1)}, f32[8,208,128]{2,1,0:T(8,128)S(1)}, u32[]{:S(2)}, u32[]{:S(2)}) collective-permute-start(f32[8,208,128]{2,1,0:T(8,128)S(1)} %multiply_add_fusion.3), channel_id=1, source_target_pairs={{0,2},{1,5},{2,0},{3,7},{4,6},{5,1},{6,4},{7,3},{8,10},{9,13},{10,... | collective-permute-start | bytes 2555912 | tf_op jit(solution)/shard_map/ppermute | solution.py:392
  134.4 18.6 %collective-permute-start.24 = (f32[1,192,128]{2,1,0:T(8,128)S(1)}, f32[1,192,128]{2,1,0:T(8,128)S(1)}, u32[]{:S(2)}, u32[]{:S(2)}) collective-permute-start(f32[1,192,128]{2,1,0:T(8,128)S(1)} %get-tuple-element.370), channel_id=1, source_target_pairs={{0,16},{1,9},{2,18},{3,11},{4,20},{5,13},{6,22},{7,15},{8,24},{9,1... | collective-permute-start | bytes 294920 | tf_op jit(solution)/shard_map/ppermute | solution.py:392
  134.5 10.7 %collective-permute-start.21 = (f32[2,384,128]{2,1,0:T(8,128)S(1)}, f32[2,384,128]{2,1,0:T(8,128)S(1)}, u32[]{:S(2)}, u32[]{:S(2)}) collective-permute-start(f32[2,384,128]{2,1,0:T(8,128)S(1)} %constant_dynamic-update-slice_fusion), channel_id=1, source_target_pairs={{0,8},{1,17},{2,10},{3,19},{4,12},{5,21},{6,14},{7,23},{8,0},{9,25... | collective-permute-start | bytes 1179656 | tf_op jit(solution)/shard_map/ppermute | solution.py:392
  136.7 10.3 %collective-permute-start.20 = (f32[4,200,128]{2,1,0:T(8,128)S(1)}, f32[4,200,128]{2,1,0:T(8,128)S(1)}, u32[]{:S(2)}, u32[]{:S(2)}) collective-permute-start(f32[4,200,128]{2,1,0:T(8,128)S(1)} %get-tuple-element.352), channel_id=1, source_target_pairs={{0,4},{1,3},{2,6},{3,1},{4,0},{5,7},{6,2},{7,5},{8,12},{9,11},{10,... | collective-permute-start | bytes 1228808 | tf_op jit(solution)/shard_map/ppermute | solution.py:392
  144.7 8.2 %collective-permute-start.25 = (f32[4,208,128]{2,1,0:T(8,128)S(1)}, f32[4,208,128]{2,1,0:T(8,128)S(1)}, u32[]{:S(2)}, u32[]{:S(2)}) collective-permute-start(f32[4,208,128]{2,1,0:T(8,128)S(1)} %get-tuple-element.350), channel_id=1, source_target_pairs={{0,4},{1,3},{2,6},{3,1},{4,0},{5,7},{6,2},{7,5},{8,12},{9,11},{10,... | collective-permute-start | bytes 1277960 | tf_op jit(solution)/shard_map/ppermute | solution.py:392
  145.2 16.1 %collective-permute-start.28 = (f32[4,384,128]{2,1,0:T(8,128)S(1)}, f32[4,384,128]{2,1,0:T(8,128)S(1)}, u32[]{:S(2)}, u32[]{:S(2)}) collective-permute-start(f32[4,384,128]{2,1,0:T(8,128)S(1)} %constant_dynamic-update-slice_fusion.2), channel_id=1, source_target_pairs={{0,4},{1,3},{2,6},{3,1},{4,0},{5,7},{6,2},{7,5},{8,12},{9,11},{10,... | collective-permute-start | bytes 2359304 | tf_op jit(solution)/shard_map/ppermute | solution.py:392
  147.0 7.6 %collective-permute-start.23 = (f32[2,200,128]{2,1,0:T(8,128)S(1)}, f32[2,200,128]{2,1,0:T(8,128)S(1)}, u32[]{:S(2)}, u32[]{:S(2)}) collective-permute-start(f32[2,200,128]{2,1,0:T(8,128)S(1)} %get-tuple-element.360), channel_id=1, source_target_pairs={{0,8},{1,17},{2,10},{3,19},{4,12},{5,21},{6,14},{7,23},{8,0},{9,25... | collective-permute-start | bytes 614408 | tf_op jit(solution)/shard_map/ppermute | solution.py:392
  153.0 6.3 %collective-permute-start.29 = (f32[1,192,128]{2,1,0:T(8,128)S(1)}, f32[1,192,128]{2,1,0:T(8,128)S(1)}, u32[]{:S(2)}, u32[]{:S(2)}) collective-permute-start(f32[1,192,128]{2,1,0:T(8,128)S(1)} %add.152), channel_id=1, source_target_pairs={{0,16},{1,9},{2,18},{3,11},{4,20},{5,13},{6,22},{7,15},{8,24},{9,1... | collective-permute-start | bytes 294920 | tf_op jit(solution)/shard_map/ppermute | solution.py:392
  161.5 24.3 %collective-permute-start.35 = (f32[8,384,128]{2,1,0:T(8,128)S(1)}, f32[8,384,128]{2,1,0:T(8,128)S(1)}, u32[]{:S(2)}, u32[]{:S(2)}) collective-permute-start(f32[8,384,128]{2,1,0:T(8,128)S(1)} %constant_dynamic-update-slice_fusion.6.refs_0_), channel_id=1, source_target_pairs={{0,1},{1,0},{2,3},{3,2},{4,5},{5,4},{6,7},{7,6},{8,9},{9,8},{10,11... | collective-permute-start | bytes 4718600 | tf_op jit(solution)/shard_map/ppermute | solution.py:392
  161.6 24.2 %collective-permute-start.34 = (f32[8,384,128]{2,1,0:T(8,128)S(1)}, f32[8,384,128]{2,1,0:T(8,128)S(1)}, u32[]{:S(2)}, u32[]{:S(2)}) collective-permute-start(f32[8,384,128]{2,1,0:T(8,128)S(1)} %constant_dynamic-update-slice_fusion.6.refs_0_), channel_id=1, source_target_pairs={{0,2},{1,5},{2,0},{3,7},{4,6},{5,1},{6,4},{7,3},{8,10},{9,13},{10,... | collective-permute-start | bytes 4718600 | tf_op jit(solution)/shard_map/ppermute | solution.py:392
  161.9 8.9 %collective-permute-start.27 = (f32[2,208,128]{2,1,0:T(8,128)S(1)}, f32[2,208,128]{2,1,0:T(8,128)S(1)}, u32[]{:S(2)}, u32[]{:S(2)}) collective-permute-start(f32[2,208,128]{2,1,0:T(8,128)S(1)} %get-tuple-element.358), channel_id=1, source_target_pairs={{0,8},{1,17},{2,10},{3,19},{4,12},{5,21},{6,14},{7,23},{8,0},{9,25... | collective-permute-start | bytes 638984 | tf_op jit(solution)/shard_map/ppermute | solution.py:392
  161.9 9.8 %collective-permute-start.26 = (f32[1,200,128]{2,1,0:T(8,128)S(1)}, f32[1,200,128]{2,1,0:T(8,128)S(1)}, u32[]{:S(2)}, u32[]{:S(2)}) collective-permute-start(f32[1,200,128]{2,1,0:T(8,128)S(1)} %get-tuple-element.368), channel_id=1, source_target_pairs={{0,16},{1,9},{2,18},{3,11},{4,20},{5,13},{6,22},{7,15},{8,24},{9,1... | collective-permute-start | bytes 307208 | tf_op jit(solution)/shard_map/ppermute | solution.py:392
  163.5 11.3 %collective-permute-start.32 = (f32[2,192,128]{2,1,0:T(8,128)S(1)}, f32[2,192,128]{2,1,0:T(8,128)S(1)}, u32[]{:S(2)}, u32[]{:S(2)}) collective-permute-start(f32[2,192,128]{2,1,0:T(8,128)S(1)} %constant_dynamic-update-slice_fusion.4), channel_id=1, source_target_pairs={{0,8},{1,17},{2,10},{3,19},{4,12},{5,21},{6,14},{7,23},{8,0},{9,25... | collective-permute-start | bytes 589832 | tf_op jit(solution)/shard_map/ppermute | solution.py:392
  170.9 7.6 %collective-permute-start.31 = (f32[1,208,128]{2,1,0:T(8,128)S(1)}, f32[1,208,128]{2,1,0:T(8,128)S(1)}, u32[]{:S(2)}, u32[]{:S(2)}) collective-permute-start(f32[1,208,128]{2,1,0:T(8,128)S(1)} %get-tuple-element.366), channel_id=1, source_target_pairs={{0,16},{1,9},{2,18},{3,11},{4,20},{5,13},{6,22},{7,15},{8,24},{9,1... | collective-permute-start | bytes 319496 | tf_op jit(solution)/shard_map/ppermute | solution.py:392
  171.8 8.8 %collective-permute-start.30 = (f32[1,200,128]{2,1,0:T(8,128)S(1)}, f32[1,200,128]{2,1,0:T(8,128)S(1)}, u32[]{:S(2)}, u32[]{:S(2)}) collective-permute-start(f32[1,200,128]{2,1,0:T(8,128)S(1)} %add.157), channel_id=1, source_target_pairs={{0,16},{1,9},{2,18},{3,11},{4,20},{5,13},{6,22},{7,15},{8,24},{9,1... | collective-permute-start | bytes 307208 | tf_op jit(solution)/shard_map/ppermute | solution.py:392
  174.9 10.9 %collective-permute-start.36 = (f32[4,192,128]{2,1,0:T(8,128)S(1)}, f32[4,192,128]{2,1,0:T(8,128)S(1)}, u32[]{:S(2)}, u32[]{:S(2)}) collective-permute-start(f32[4,192,128]{2,1,0:T(8,128)S(1)} %constant_dynamic-update-slice_fusion.8), channel_id=1, source_target_pairs={{0,4},{1,3},{2,6},{3,1},{4,0},{5,7},{6,2},{7,5},{8,12},{9,11},{10,... | collective-permute-start | bytes 1179656 | tf_op jit(solution)/shard_map/ppermute | solution.py:392
  178.5 6.7 %collective-permute-start.37 = (f32[1,208,128]{2,1,0:T(8,128)S(1)}, f32[1,208,128]{2,1,0:T(8,128)S(1)}, u32[]{:S(2)}, u32[]{:S(2)}) collective-permute-start(f32[1,208,128]{2,1,0:T(8,128)S(1)} %add.159), channel_id=1, source_target_pairs={{0,16},{1,9},{2,18},{3,11},{4,20},{5,13},{6,22},{7,15},{8,24},{9,1... | collective-permute-start | bytes 319496 | tf_op jit(solution)/shard_map/ppermute | solution.py:392
  185.8 9.2 %collective-permute-start.41 = (f32[8,384,128]{2,1,0:T(8,128)S(1)}, f32[8,384,128]{2,1,0:T(8,128)S(1)}, u32[]{:S(2)}, u32[]{:S(2)}) collective-permute-start(f32[8,384,128]{2,1,0:T(8,128)S(1)} %collective-permute-done.34.refs_1_), channel_id=1, source_target_pairs={{0,1},{1,0},{2,3},{3,2},{4,5},{5,4},{6,7},{7,6},{8,9},{9,8},{10,11... | collective-permute-start | bytes 4718600 | tf_op jit(solution)/shard_map/ppermute | solution.py:392
  187.0 7.9 %collective-permute-start.33 = (f32[2,200,128]{2,1,0:T(8,128)S(1)}, f32[2,200,128]{2,1,0:T(8,128)S(1)}, u32[]{:S(2)}, u32[]{:S(2)}) collective-permute-start(f32[2,200,128]{2,1,0:T(8,128)S(1)} %constant_dynamic-update-slice_fusion.10), channel_id=1, source_target_pairs={{0,8},{1,17},{2,10},{3,19},{4,12},{5,21},{6,14},{7,23},{8,0},{9,25... | collective-permute-start | bytes 614408 | tf_op jit(solution)/shard_map/ppermute | solution.py:392
  187.0 13.4 %collective-permute-start.39 = (f32[8,192,128]{2,1,0:T(8,128)S(1)}, f32[8,192,128]{2,1,0:T(8,128)S(1)}, u32[]{:S(2)}, u32[]{:S(2)}) collective-permute-start(f32[8,192,128]{2,1,0:T(8,128)S(1)} %constant_dynamic-update-slice_fusion.14.refs_0_), channel_id=1, source_target_pairs={{0,2},{1,5},{2,0},{3,7},{4,6},{5,1},{6,4},{7,3},{8,10},{9,13},{10,... | collective-permute-start | bytes 2359304 | tf_op jit(solution)/shard_map/ppermute | solution.py:392
  188.7 10.8 %collective-permute-start.40 = (f32[2,208,128]{2,1,0:T(8,128)S(1)}, f32[2,208,128]{2,1,0:T(8,128)S(1)}, u32[]{:S(2)}, u32[]{:S(2)}) collective-permute-start(f32[2,208,128]{2,1,0:T(8,128)S(1)} %constant_dynamic-update-slice_fusion.12), channel_id=1, source_target_pairs={{0,8},{1,17},{2,10},{3,19},{4,12},{5,21},{6,14},{7,23},{8,0},{9,25... | collective-permute-start | bytes 638984 | tf_op jit(solution)/shard_map/ppermute | solution.py:392
  194.9 8.0 %collective-permute-start.38 = (f32[4,200,128]{2,1,0:T(8,128)S(1)}, f32[4,200,128]{2,1,0:T(8,128)S(1)}, u32[]{:S(2)}, u32[]{:S(2)}) collective-permute-start(f32[4,200,128]{2,1,0:T(8,128)S(1)} %constant_dynamic-update-slice_fusion.16), channel_id=1, source_target_pairs={{0,4},{1,3},{2,6},{3,1},{4,0},{5,7},{6,2},{7,5},{8,12},{9,11},{10,... | collective-permute-start | bytes 1228808 | tf_op jit(solution)/shard_map/ppermute | solution.py:392
  200.4 4.4 %collective-permute-start.45 = (f32[8,192,128]{2,1,0:T(8,128)S(1)}, f32[8,192,128]{2,1,0:T(8,128)S(1)}, u32[]{:S(2)}, u32[]{:S(2)}) collective-permute-start(f32[8,192,128]{2,1,0:T(8,128)S(1)} %collective-permute-done.39.refs_1_), channel_id=1, source_target_pairs={{0,1},{1,0},{2,3},{3,2},{4,5},{5,4},{6,7},{7,6},{8,9},{9,8},{10,11... | collective-permute-start | bytes 2359304 | tf_op jit(solution)/shard_map/ppermute | solution.py:392
  200.7 4.2 %collective-permute-start.44 = (f32[8,192,128]{2,1,0:T(8,128)S(1)}, f32[8,192,128]{2,1,0:T(8,128)S(1)}, u32[]{:S(2)}, u32[]{:S(2)}) collective-permute-start(f32[8,192,128]{2,1,0:T(8,128)S(1)} %constant_dynamic-update-slice_fusion.14.refs_0_), channel_id=1, source_target_pairs={{0,1},{1,0},{2,3},{3,2},{4,5},{5,4},{6,7},{7,6},{8,9},{9,8},{10,11... | collective-permute-start | bytes 2359304 | tf_op jit(solution)/shard_map/ppermute | solution.py:392
  203.0 16.3 %collective-permute-start.42 = (f32[8,200,128]{2,1,0:T(8,128)S(1)}, f32[8,200,128]{2,1,0:T(8,128)S(1)}, u32[]{:S(2)}, u32[]{:S(2)}) collective-permute-start(f32[8,200,128]{2,1,0:T(8,128)S(1)} %constant_dynamic-update-slice_fusion.20.refs_0_), channel_id=1, source_target_pairs={{0,2},{1,5},{2,0},{3,7},{4,6},{5,1},{6,4},{7,3},{8,10},{9,13},{10,... | collective-permute-start | bytes 2457608 | tf_op jit(solution)/shard_map/ppermute | solution.py:392
  204.8 12.8 %collective-permute-start.43 = (f32[4,208,128]{2,1,0:T(8,128)S(1)}, f32[4,208,128]{2,1,0:T(8,128)S(1)}, u32[]{:S(2)}, u32[]{:S(2)}) collective-permute-start(f32[4,208,128]{2,1,0:T(8,128)S(1)} %constant_dynamic-update-slice_fusion.18), channel_id=1, source_target_pairs={{0,4},{1,3},{2,6},{3,1},{4,0},{5,7},{6,2},{7,5},{8,12},{9,11},{10,... | collective-permute-start | bytes 1277960 | tf_op jit(solution)/shard_map/ppermute | solution.py:392
  217.7 8.0 %collective-permute-start.49 = (f32[8,208,128]{2,1,0:T(8,128)S(1)}, f32[8,208,128]{2,1,0:T(8,128)S(1)}, u32[]{:S(2)}, u32[]{:S(2)}) collective-permute-start(f32[8,208,128]{2,1,0:T(8,128)S(1)} %constant_dynamic-update-slice_fusion.22.refs_0_), channel_id=1, source_target_pairs={{0,1},{1,0},{2,3},{3,2},{4,5},{5,4},{6,7},{7,6},{8,9},{9,8},{10,11... | collective-permute-start | bytes 2555912 | tf_op jit(solution)/shard_map/ppermute | solution.py:392
  217.7 12.8 %collective-permute-start.48 = (f32[8,208,128]{2,1,0:T(8,128)S(1)}, f32[8,208,128]{2,1,0:T(8,128)S(1)}, u32[]{:S(2)}, u32[]{:S(2)}) collective-permute-start(f32[8,208,128]{2,1,0:T(8,128)S(1)} %constant_dynamic-update-slice_fusion.22.refs_0_), channel_id=1, source_target_pairs={{0,2},{1,5},{2,0},{3,7},{4,6},{5,1},{6,4},{7,3},{8,10},{9,13},{10,... | collective-permute-start | bytes 2555912 | tf_op jit(solution)/shard_map/ppermute | solution.py:392
  219.3 2.3 collective-permute-start.46
  219.3 3.5 %collective-permute-start.47 = (f32[8,200,128]{2,1,0:T(8,128)S(1)}, f32[8,200,128]{2,1,0:T(8,128)S(1)}, u32[]{:S(2)}, u32[]{:S(2)}) collective-permute-start(f32[8,200,128]{2,1,0:T(8,128)S(1)} %collective-permute-done.42.refs_1_), channel_id=1, source_target_pairs={{0,1},{1,0},{2,3},{3,2},{4,5},{5,4},{6,7},{7,6},{8,9},{9,8},{10,11... | collective-permute-start | bytes 2457608 | tf_op jit(solution)/shard_map/ppermute | solution.py:392
  230.5 2.4 %collective-permute-start.50 = (f32[8,208,128]{2,1,0:T(8,128)S(1)}, f32[8,208,128]{2,1,0:T(8,128)S(1)}, u32[]{:S(2)}, u32[]{:S(2)}) collective-permute-start(f32[8,208,128]{2,1,0:T(8,128)S(1)} %collective-permute-done.48.refs_1_), channel_id=1, source_target_pairs={{0,1},{1,0},{2,3},{3,2},{4,5},{5,4},{6,7},{7,6},{8,9},{9,8},{10,11... | collective-permute-start | bytes 2555912 | tf_op jit(solution)/shard_map/ppermute | solution.py:392
  (16 other events, 29.4 us)

commit v5 on v4

--- a/solution.py
+++ b/solution.py
@@ -605,8 +605,8 @@
 ORDER = (
     "late", "cross kernel", "late", "cross", "self kernel", "cross", "own", "late",
     "patch kernel", "own", "late", "patch", "cross", "input kernel", "late", "cross", "patch",
-    "own", "late", "cross", "input kernel", "patch", "late", "own", "patch", "cross", "own",
-    "cross", "late", "patch", "own", "cross", "patch", "own", "patch", "cross", "late", "own",
+    "late", "cross", "own", "input kernel", "patch", "late", "own", "patch", "cross", "own",
+    "late", "patch", "cross", "own", "cross", "patch", "own", "patch", "cross", "late", "own",
     "late", "patch", "cross", "own", "cross", "patch", "own", "own", "patch", "patch",
 )
 

time: 236 us -> 235 us (level)
  waiting for transfers between devices: 74.4 us -> 65.4 us
  starting transfers between devices: 47 us -> 55 us
  local copies, waits for them, and re-layouts: 4.04 us -> 1.61 us
    ppermute x51, waiting for transfers between devices: 74.4 us -> 65.4 us  [exchange(): lax.ppermute(values, 'dp', flips(count, first, first if second is None el...]
    ppermute x51, starting transfers between devices: 47 us -> 55 us  [exchange(): lax.ppermute(values, 'dp', flips(count, first, first if second is None el...]
    unnamed x70 -> x66, local copies, waits for them, and re-layouts: 3.78 us -> 1.35 us
  transfers between devices with their start and end apart: 51 -> 51, of which waited for: 30 -> 28; matrix products, arithmetic and copies ran while one was open for 1% -> 1% of each run, Pallas kernels for 43% -> 43%
where the time goes in v5:
time: 235 us
  Pallas kernels  105 us (45%)
  waiting for transfers between devices  65.4 us (28%)
  starting transfers between devices  55 us (23%)
  other arithmetic  6.14 us (3%)
    pallas_call x4, Pallas kernels, run(): pl.pallas_call(kernel, grid=(steps,), out_shape=[jax.ShapeDtypeStruct(s,...  79.6 us
    ppermute x51, waiting for transfers between devices, exchange(): lax.ppermute(values, 'dp', flips(count, first, first if second is None el...  65.4 us
    ppermute x51, starting transfers between devices, exchange(): lax.ppermute(values, 'dp', flips(count, first, first if second is None el...  55 us
    pallas_call x4, Pallas kernels, unpack(): pl.pallas_call(functools.partial(unpack_kernel, shapes, with_gains, place...  12.8 us
    pallas_call x2, Pallas kernels, patch_input(): pl.pallas_call(patch_input_kernel, grid=(steps,), out_shape=jax.ShapeDtyp...  10.1 us
  transfers between devices with their start and end apart: 51, of which 28 were waited for; matrix products, arithmetic and copies ran while one was open for 1% of the time, Pallas kernels for 43%

profile of v5, /device:TPU:0, one launch (start us, length us, event | category | flops | bytes accessed | tf_op | source)
XLA Modules:
  0.0 234.5 jit_solution(16524991320725548669)
XLA Ops:
  0.7 1.2 count.1
  2.4 1.0 collective-permute-done
  4.0 4.9 %collective-permute-start.3 = (f32[2]{0:T(128)S(1)}, f32[2]{0:T(128)S(1)}, u32[]{:S(2)}, u32[]{:S(2)}) collective-permute-start(f32[2]{0:T(128)S(1)} %add.120), channel_id=1, source_target_pairs={{0,24},{1,25},{2,26},{3,27},{4,28},{5,29},{6,30},{7,31},{8,16},{9,... | collective-permute-start | bytes 32 | tf_op jit(solution)/shard_map/ppermute | solution.py:392
  9.5 38.9 %forward.1 = (bf16[2048,512]{1,0:T(8,128)(2,1)}, bf16[2048,768]{1,0:T(8,128)(2,1)}, bf16[1024,1152]{1,0:T(8,128)(2,1)}, bf16[8,3,256,128]{3,2,1,0:T(8,128)(2,1)}...) custom-call(s32[8]{0:T(128)} %len_ref.3, ...), custom_call_target="tpu_custom_call" | custom-call | flops 40000000000 | bytes 1048576 | tf_op jit(solution)/shard_map/forward/pallas_call | solution.py:589
  48.5 2.7 %collective-permute-start.6 = (f32[2]{0:T(128)S(1)}, f32[2]{0:T(128)S(1)}, u32[]{:S(2)}, u32[]{:S(2)}) collective-permute-start(f32[2]{0:T(128)S(1)} %add_add_fusion.refs_0_), channel_id=1, source_target_pairs={{0,6},{1,7},{2,4},{3,5},{4,2},{5,3},{6,0},{7,1},{8,14},{9,15},{10,... | collective-permute-start | bytes 32 | tf_op jit(solution)/shard_map/ppermute | solution.py:392
  52.1 0.9 collective-permute-done.6.refs_3_
  53.0 1.8 collective-permute-done.5.refs_2_
  55.8 1.4 weigh.1
  57.3 2.2 multiply_add_fusion.1
  60.2 18.2 %cross_backward.1 = (bf16[2048,512]{1,0:T(8,128)(2,1)S(1)}, f32[1024,512]{1,0:T(8,128)}, f32[1,512]{1,0:T(1,128)S(1)}, f32[1,512]{1,0:T(1,128)S(1)}, f32[16,192,...) custom-call(s32[8]{0:T(128)S(1)} %copy-done.1, f32[1024,512]{1,0:T(8,128)} %get-tuple-element.208.dx2_ref, ...), custom_call_target="tpu_custom_call" | custom-call | flops 20000000000 | bytes 1048576 | tf_op jit(solution)/shard_map/cross_backward/pallas_call | solution.py:589
  78.4 1.6 collective-permute-done.8
  80.0 1.9 multiply_add_fusion
  82.2 1.6 collective-permute-start.11
  84.3 13.4 %self_backward.1 = (f32[1024,512]{1,0:T(8,128)}, f32[16,200,128]{2,1,0:T(8,128)S(1)}, f32[16,200,128]{2,1,0:T(8,128)S(1)}) custom-call(s32[8]{0:T(128)S(1)} %copy-done.1, f32[2]{0:T(128)S(1)} %copy-done.2, f32[1024,512]{1,0:T(8,128)S(1)} %copy-done.14, bf16[1024,1152]{1,0:T(8,128)(2,1)} %get-tuple-element.223.qkv_ref, ...), custom_call_target="tpu_custom_call" | custom-call | flops 16000000000 | bytes 1048576 | tf_op jit(solution)/shard_map/self_backward/pallas_call | solution.py:589
  98.6 1.3 collective-permute-start.14
  99.9 9.1 %patch_weight.1 = (f32[16,208,128]{2,1,0:T(8,128)S(1)}, f32[16,208,128]{2,1,0:T(8,128)S(1)}) custom-call(s32[8]{0:T(128)S(1)} %copy-done.1, bf16[2048,1664]{1,0:T(8,128)(2,1)} %bitcast.35, bf16[2048,512]{1,0:T(8,128)(2,1)S(1)} %get-tuple-element.266.dfeat_ref), custom_call_target="tpu_custom_call" | custom-call | flops 12000000000 | bytes 1048576 | tf_op jit(solution)/shard_map/patch_weight/pallas_call | solution.py:589
  109.1 1.3 collective-permute-done.14
  111.0 1.8 collective-permute-start.16
  113.0 1.6 collective-permute-start.15
  114.6 0.9 collective-permute-start.12
  115.5 5.0 %patch_input.2.refs_0_ = f32[2048,1664]{1,0:T(8,128)} custom-call(f32[2]{0:T(128)S(1)} %copy-done.2, bf16[2048,512]{1,0:T(8,128)(2,1)S(1)} %get-tuple-element.266.dfeat_ref, bf16[1664,512]{1,0:T(8,128)(2,1)S(1)} %copy-done), custom_call_target="tpu_custom_call" | custom-call | flops 6000000000 | bytes 1048576 | tf_op jit(solution)/shard_map/patch_input/pallas_call | solution.py:787
  121.0 4.0 %collective-permute-done.15 = f32[4,192,128]{2,1,0:T(8,128)S(1)} collective-permute-done((f32[4,192,128]{2,1,0:T(8,128)S(1)}, f32[4,192,128]{2,1,0:T(8,128)S(1)}, u32[]{:S(2)}, u32[]{:S(2)}) %collective-permute-start.15) | collective-permute-done | bytes 393248 | tf_op jit(solution)/shard_map/ppermute | solution.py:392
  125.0 2.9 %collective-permute-start.17 = (f32[2,192,128]{2,1,0:T(8,128)S(1)}, f32[2,192,128]{2,1,0:T(8,128)S(1)}, u32[]{:S(2)}, u32[]{:S(2)}) collective-permute-start(f32[2,192,128]{2,1,0:T(8,128)S(1)} %get-tuple-element.362), channel_id=1, source_target_pairs={{0,8},{1,17},{2,10},{3,19},{4,12},{5,21},{6,14},{7,23},{8,0},{9,25... | collective-permute-start | bytes 589832 | tf_op jit(solution)/shard_map/ppermute | solution.py:392
  128.1 1.0 collective-permute-start.22
  129.1 3.6 %collective-permute-done.18 = f32[1,384,128]{2,1,0:T(8,128)S(1)} collective-permute-done((f32[1,384,128]{2,1,0:T(8,128)S(1)}, f32[1,384,128]{2,1,0:T(8,128)S(1)}, u32[]{:S(2)}, u32[]{:S(2)}) %collective-permute-start.18) | collective-permute-done | bytes 196640 | tf_op jit(solution)/shard_map/ppermute | solution.py:392
  132.7 1.9 collective-permute-start.21
  135.3 5.0 %patch_input.3 = f32[2048,1664]{1,0:T(8,128)} custom-call(f32[2]{0:T(128)S(1)} %copy-done.2, bf16[2048,512]{1,0:T(8,128)(2,1)S(1)} %get-tuple-element.266.dfeat_ref, bf16[1664,512]{1,0:T(8,128)(2,1)S(1)} %copy-done, f32[2048,1664]{1,0:T(8,128)} %patch_input.2.refs_0_), custom_call_target="tpu_custom_call", output_to_operand_aliasing={{}: (3, {})} | custom-call | flops 6000000000 | bytes 1048576 | tf_op jit(solution)/shard_map/patch_input/pallas_call | solution.py:787
  141.2 1.1 collective-permute-start.25
  142.3 2.8 %collective-permute-done.21 = f32[2,384,128]{2,1,0:T(8,128)S(1)} collective-permute-done((f32[2,384,128]{2,1,0:T(8,128)S(1)}, f32[2,384,128]{2,1,0:T(8,128)S(1)}, u32[]{:S(2)}, u32[]{:S(2)}) %collective-permute-start.21) | collective-permute-done | bytes 393248 | tf_op jit(solution)/shard_map/ppermute | solution.py:392
  145.2 2.0 collective-permute-start.29
  147.2 1.0 collective-permute-start.24
  148.2 2.5 %collective-permute-start.23 = (f32[2,200,128]{2,1,0:T(8,128)S(1)}, f32[2,200,128]{2,1,0:T(8,128)S(1)}, u32[]{:S(2)}, u32[]{:S(2)}) collective-permute-start(f32[2,200,128]{2,1,0:T(8,128)S(1)} %get-tuple-element.360), channel_id=1, source_target_pairs={{0,8},{1,17},{2,10},{3,19},{4,12},{5,21},{6,14},{7,23},{8,0},{9,25... | collective-permute-start | bytes 614408 | tf_op jit(solution)/shard_map/ppermute | solution.py:392
  150.8 1.0 collective-permute-start.28
  151.8 6.4 %collective-permute-done.24 = f32[1,192,128]{2,1,0:T(8,128)S(1)} collective-permute-done((f32[1,192,128]{2,1,0:T(8,128)S(1)}, f32[1,192,128]{2,1,0:T(8,128)S(1)}, u32[]{:S(2)}, u32[]{:S(2)}) %collective-permute-start.24) | collective-permute-done | bytes 98336 | tf_op jit(solution)/shard_map/ppermute | solution.py:392
  158.4 1.6 collective-permute-start.35
  160.0 0.9 collective-permute-start.34
  160.9 1.2 collective-permute-done.28
  162.1 1.7 collective-permute-done.27
  163.9 2.0 collective-permute-start.26
  165.8 1.0 collective-permute-start.31
  166.8 4.4 %collective-permute-done.26 = f32[1,200,128]{2,1,0:T(8,128)S(1)} collective-permute-done((f32[1,200,128]{2,1,0:T(8,128)S(1)}, f32[1,200,128]{2,1,0:T(8,128)S(1)}, u32[]{:S(2)}, u32[]{:S(2)}) %collective-permute-start.26) | collective-permute-done | bytes 102432 | tf_op jit(solution)/shard_map/ppermute | solution.py:392
  171.3 3.4 %collective-permute-start.30 = (f32[1,200,128]{2,1,0:T(8,128)S(1)}, f32[1,200,128]{2,1,0:T(8,128)S(1)}, u32[]{:S(2)}, u32[]{:S(2)}) collective-permute-start(f32[1,200,128]{2,1,0:T(8,128)S(1)} %add.157), channel_id=1, source_target_pairs={{0,16},{1,9},{2,18},{3,11},{4,20},{5,13},{6,22},{7,15},{8,24},{9,1... | collective-permute-start | bytes 307208 | tf_op jit(solution)/shard_map/ppermute | solution.py:392
  174.9 0.8 collective-permute-start.36
  175.7 0.9 collective-permute-start.37
  176.6 1.2 collective-permute-done.30
  177.8 4.4 %collective-permute-done.37 = f32[1,208,128]{2,1,0:T(8,128)S(1)} collective-permute-done((f32[1,208,128]{2,1,0:T(8,128)S(1)}, f32[1,208,128]{2,1,0:T(8,128)S(1)}, u32[]{:S(2)}, u32[]{:S(2)}) %collective-permute-start.37) | collective-permute-done | bytes 106528 | tf_op jit(solution)/shard_map/ppermute | solution.py:392
  182.3 1.4 collective-permute-done.36
  183.8 0.8 collective-permute-done.34.refs_1_
  185.2 1.9 collective-permute-start.39
  187.6 3.4 %collective-permute-done.33 = f32[2,200,128]{2,1,0:T(8,128)S(1)} collective-permute-done((f32[2,200,128]{2,1,0:T(8,128)S(1)}, f32[2,200,128]{2,1,0:T(8,128)S(1)}, u32[]{:S(2)}, u32[]{:S(2)}) %collective-permute-start.33) | collective-permute-done | bytes 204832 | tf_op jit(solution)/shard_map/ppermute | solution.py:392
  191.6 4.3 %unpack.4 = (f32[1024,512]{1,0:T(8,128)}, f32[512,1024]{1,0:T(8,128)}, f32[512,1024]{1,0:T(8,128)}) custom-call(s32[8]{0:T(128)S(1)} %copy-done.1, f32[8,384,128]{2,1,0:T(8,128)S(1)} %constant_dynamic-update-slice_fusion.4.refs_0_, f32[8,384,128]{2,1,0:T(8,128)S(1)} %collective-permute-done.34.refs_1_, f32[8,384,128]{2,1,0:T(8,128)S(1)} %collective-permute-done.35.refs_2_, ...), custom_call_target="tpu_custom_call" | custom-call | tf_op jit(solution)/shard_map/unpack/pallas_call | solution.py:461
  195.9 3.1 %collective-permute-done.39.refs_1_ = f32[8,192,128]{2,1,0:T(8,128)S(1)} collective-permute-done((f32[8,192,128]{2,1,0:T(8,128)S(1)}, f32[8,192,128]{2,1,0:T(8,128)S(1)}, u32[]{:S(2)}, u32[]{:S(2)}) %collective-permute-start.39) | collective-permute-done | bytes 786464 | tf_op jit(solution)/shard_map/ppermute | solution.py:392
  199.0 3.0 %collective-permute-start.45 = (f32[8,192,128]{2,1,0:T(8,128)S(1)}, f32[8,192,128]{2,1,0:T(8,128)S(1)}, u32[]{:S(2)}, u32[]{:S(2)}) collective-permute-start(f32[8,192,128]{2,1,0:T(8,128)S(1)} %collective-permute-done.39.refs_1_), channel_id=1, source_target_pairs={{0,1},{1,0},{2,3},{3,2},{4,5},{5,4},{6,7},{7,6},{8,9},{9,8},{10,11... | collective-permute-start | bytes 2359304 | tf_op jit(solution)/shard_map/ppermute | solution.py:392
  203.0 2.0 collective-permute-start.43
  205.0 2.8 %unpack.5 = (f32[384,512]{1,0:T(8,128)}, f32[512,384]{1,0:T(8,128)}, f32[512,384]{1,0:T(8,128)}, f32[512,384]{1,0:T(8,128)}) custom-call(s32[8]{0:T(128)S(1)} %copy-done.1, f32[8,192,128]{2,1,0:T(8,128)S(1)} %constant_dynamic-update-slice_fusion.14.refs_0_, f32[8,192,128]{2,1,0:T(8,128)S(1)} %collective-permute-done.39.refs_1_, ...), custom_call_target="tpu_custom_call" | custom-call | tf_op jit(solution)/shard_map/unpack/pallas_call | solution.py:461
  207.8 7.9 %collective-permute-done.43 = f32[4,208,128]{2,1,0:T(8,128)S(1)} collective-permute-done((f32[4,208,128]{2,1,0:T(8,128)S(1)}, f32[4,208,128]{2,1,0:T(8,128)S(1)}, u32[]{:S(2)}, u32[]{:S(2)}) %collective-permute-start.43) | collective-permute-done | bytes 426016 | tf_op jit(solution)/shard_map/ppermute | solution.py:392
  216.5 1.3 collective-permute-start.48
  217.7 1.9 collective-permute-done.42.refs_1_
  220.1 1.8 collective-permute-done.46.refs_2_
  222.0 1.2 collective-permute-done.47.refs_3_
  223.1 2.8 %unpack.6 = (f32[384,512]{1,0:T(8,128)}, f32[512,384]{1,0:T(8,128)}, f32[512,384]{1,0:T(8,128)}, f32[512,384]{1,0:T(8,128)}, f32[256,128]{1,0:T(8,128)}, /*index...) custom-call(s32[8]{0:T(128)S(1)} %copy-done.1, ...), custom_call_target="tpu_custom_call" | custom-call | tf_op jit(solution)/shard_map/unpack/pallas_call | solution.py:461
  226.0 3.2 %collective-permute-done.48.refs_1_ = f32[8,208,128]{2,1,0:T(8,128)S(1)} collective-permute-done((f32[8,208,128]{2,1,0:T(8,128)S(1)}, f32[8,208,128]{2,1,0:T(8,128)S(1)}, u32[]{:S(2)}, u32[]{:S(2)}) %collective-permute-start.48) | collective-permute-done | bytes 852000 | tf_op jit(solution)/shard_map/ppermute | solution.py:392
  229.2 2.4 %collective-permute-done.50.refs_3_ = f32[8,208,128]{2,1,0:T(8,128)S(1)} collective-permute-done((f32[8,208,128]{2,1,0:T(8,128)S(1)}, f32[8,208,128]{2,1,0:T(8,128)S(1)}, u32[]{:S(2)}, u32[]{:S(2)}) %collective-permute-start.50) | collective-permute-done | bytes 852000 | tf_op jit(solution)/shard_map/ppermute | solution.py:392
  231.5 3.0 %unpack.7 = f32[1664,512]{1,0:T(8,128)} custom-call(s32[8]{0:T(128)S(1)} %copy-done.1, f32[8,208,128]{2,1,0:T(8,128)S(1)} %constant_dynamic-update-slice_fusion.22.refs_0_, f32[8,208,128]{2,1,0:T(8,128)S(1)} %collective-permute-done.48.refs_1_, f32[8,208,128]{2,1,0:T(8,128)S(1)} %collective-permute-done.49.refs_2_, ...), custom_call_target="tpu_custom_call" | custom-call | tf_op jit(solution)/shard_map/unpack/pallas_call | solution.py:461
  (154 shorter events, 13.7 us)
Async XLA Ops:
  1.9 1.5 collective-permute-start
  4.0 44.4 %collective-permute-start.3 = (f32[2]{0:T(128)S(1)}, f32[2]{0:T(128)S(1)}, u32[]{:S(2)}, u32[]{:S(2)}) collective-permute-start(f32[2]{0:T(128)S(1)} %add.120), channel_id=1, source_target_pairs={{0,24},{1,25},{2,26},{3,27},{4,28},{5,29},{6,30},{7,31},{8,16},{9,... | collective-permute-start | bytes 32 | tf_op jit(solution)/shard_map/ppermute | solution.py:392
  8.9 39.5 %collective-permute-start.2 = (f32[2]{0:T(128)S(1)}, f32[2]{0:T(128)S(1)}, u32[]{:S(2)}, u32[]{:S(2)}) collective-permute-start(f32[2]{0:T(128)S(1)} %add.120), channel_id=1, source_target_pairs={{0,16},{1,17},{2,18},{3,19},{4,20},{5,21},{6,22},{7,23},{8,24},{9,... | collective-permute-start | bytes 32 | tf_op jit(solution)/shard_map/ppermute | solution.py:392
  8.9 39.5 %collective-permute-start.1 = (f32[2]{0:T(128)S(1)}, f32[2]{0:T(128)S(1)}, u32[]{:S(2)}, u32[]{:S(2)}) collective-permute-start(f32[2]{0:T(128)S(1)} %add.120), channel_id=1, source_target_pairs={{0,8},{1,9},{2,10},{3,11},{4,12},{5,13},{6,14},{7,15},{8,0},{9,1},... | collective-permute-start | bytes 32 | tf_op jit(solution)/shard_map/ppermute | solution.py:392
  48.4 8.8 %collective-permute-start.7 = (f32[16,384,128]{2,1,0:T(8,128)}, f32[16,384,128]{2,1,0:T(8,128)}, u32[]{:S(2)}, u32[]{:S(2)}) collective-permute-start(f32[16,384,128]{2,1,0:T(8,128)} %get-tuple-element.203), channel_id=1, source_target_pairs={{0,1},{1,0},{2,3},{3,2},{4,5},{5,4},{6,7},{7,6},{8,9},{9,8},{10,11... | collective-permute-start | bytes 9437192 | tf_op jit(solution)/shard_map/ppermute | solution.py:392
  48.5 6.8 %copy-start.23 = (f32[2]{0:T(128)}, f32[2]{0:T(128)S(1)}, u32[]{:S(2)}) copy-start(f32[2]{0:T(128)S(1)} %add_add_fusion.refs_0_) | copy-start | bytes 28
  48.5 4.5 %collective-permute-start.6 = (f32[2]{0:T(128)S(1)}, f32[2]{0:T(128)S(1)}, u32[]{:S(2)}, u32[]{:S(2)}) collective-permute-start(f32[2]{0:T(128)S(1)} %add_add_fusion.refs_0_), channel_id=1, source_target_pairs={{0,6},{1,7},{2,4},{3,5},{4,2},{5,3},{6,0},{7,1},{8,14},{9,15},{10,... | collective-permute-start | bytes 32 | tf_op jit(solution)/shard_map/ppermute | solution.py:392
  51.2 3.5 %collective-permute-start.5 = (f32[2]{0:T(128)S(1)}, f32[2]{0:T(128)S(1)}, u32[]{:S(2)}, u32[]{:S(2)}) collective-permute-start(f32[2]{0:T(128)S(1)} %add_add_fusion.refs_0_), channel_id=1, source_target_pairs={{0,4},{1,5},{2,6},{3,7},{4,0},{5,1},{6,2},{7,3},{8,12},{9,13},{10,... | collective-permute-start | bytes 32 | tf_op jit(solution)/shard_map/ppermute | solution.py:392
  51.7 3.5 %collective-permute-start.4 = (f32[2]{0:T(128)S(1)}, f32[2]{0:T(128)S(1)}, u32[]{:S(2)}, u32[]{:S(2)}) collective-permute-start(f32[2]{0:T(128)S(1)} %add_add_fusion.refs_0_), channel_id=1, source_target_pairs={{0,2},{1,3},{2,0},{3,1},{4,6},{5,7},{6,4},{7,5},{8,10},{9,11},{10,... | collective-permute-start | bytes 32 | tf_op jit(solution)/shard_map/ppermute | solution.py:392
  57.2 2.9 %copy-start.1 = (s32[8]{0:T(128)S(1)}, s32[8]{0:T(128)}, u32[]{:S(2)}) copy-start(s32[8]{0:T(128)} %get-tuple-element.183.code_ref) | copy-start | bytes 100
  57.2 2.9 %copy-start.4 = (bf16[512,384]{1,0:T(8,128)(2,1)S(1)}, bf16[512,384]{1,0:T(8,128)(2,1)}, u32[]{:S(2)}) copy-start(bf16[512,384]{1,0:T(8,128)(2,1)} %wck_ref.3) | copy-start | bytes 1179652
  57.2 2.9 %copy-start.5 = (bf16[512,384]{1,0:T(8,128)(2,1)S(1)}, bf16[512,384]{1,0:T(8,128)(2,1)}, u32[]{:S(2)}) copy-start(bf16[512,384]{1,0:T(8,128)(2,1)} %wcv_ref.3) | copy-start | bytes 1179652
  57.2 2.9 %copy-start.6 = (bf16[512,384]{1,0:T(8,128)(2,1)S(1)}, bf16[512,384]{1,0:T(8,128)(2,1)}, u32[]{:S(2)}) copy-start(bf16[512,384]{1,0:T(8,128)(2,1)} %wcq_ref.3) | copy-start | bytes 1179652
  57.2 2.9 %copy-start.7 = (bf16[384,512]{1,0:T(8,128)(2,1)S(1)}, bf16[384,512]{1,0:T(8,128)(2,1)}, u32[]{:S(2)}) copy-start(bf16[384,512]{1,0:T(8,128)(2,1)} %wco_ref.3) | copy-start | bytes 1179652
  57.2 2.9 %copy-start.12 = (f32[512]{0:T(512)S(1)}, f32[512]{0:T(512)}, u32[]{:S(2)}) copy-start(f32[512]{0:T(512)} %param.33) | copy-start | bytes 6148
  57.3 2.9 %copy-start.17 = (bf16[1024,384]{1,0:T(8,128)(2,1)S(1)}, bf16[1024,384]{1,0:T(8,128)(2,1)}, u32[]{:S(2)}) copy-start(bf16[1024,384]{1,0:T(8,128)(2,1)} %get-tuple-element.209.cq_ref) | copy-start | bytes 2359300
  59.5 20.5 %collective-permute-start.8 = (f32[8,384,128]{2,1,0:T(8,128)S(1)}, f32[8,384,128]{2,1,0:T(8,128)S(1)}, u32[]{:S(2)}, u32[]{:S(2)}) collective-permute-start(f32[8,384,128]{2,1,0:T(8,128)S(1)} %multiply_add_fusion.1), channel_id=1, source_target_pairs={{0,2},{1,5},{2,0},{3,7},{4,6},{5,1},{6,4},{7,3},{8,10},{9,13},{10,... | collective-permute-start | bytes 4718600 | tf_op jit(solution)/shard_map/ppermute | solution.py:392
  60.1 19.8 %copy-start.20 = (f32[16,384,128]{2,1,0:T(8,128)S(1)}, f32[16,384,128]{2,1,0:T(8,128)}, u32[]{:S(2)}) copy-start(f32[16,384,128]{2,1,0:T(8,128)} %get-tuple-element.218) | copy-start | bytes 9437188
  60.1 19.8 %copy-start.21 = (f32[1,1,128]{2,1,0:T(1,128)S(1)}, f32[1,1,128]{2,1,0:T(1,128)}, u32[]{:S(2)}) copy-start(f32[1,1,128]{2,1,0:T(1,128)} %get-tuple-element.205) | copy-start | bytes 1540
  60.2 19.8 %copy-start.22 = (f32[1,1,128]{2,1,0:T(1,128)S(1)}, f32[1,1,128]{2,1,0:T(1,128)}, u32[]{:S(2)}) copy-start(f32[1,1,128]{2,1,0:T(1,128)} %get-tuple-element.207) | copy-start | bytes 1540
  80.0 3.8 %copy-start.15 = (bf16[8,3,256,128]{3,2,1,0:T(8,128)(2,1)S(1)}, bf16[8,3,256,128]{3,2,1,0:T(8,128)(2,1)}, u32[]{:S(2)}) copy-start(bf16[8,3,256,128]{3,2,1,0:T(8,128)(2,1)} %get-tuple-element.224.pt_ref) | copy-start | bytes 4718596
  80.0 3.8 %copy-start.16 = (bf16[1024,384]{1,0:T(8,128)(2,1)S(1)}, bf16[1024,384]{1,0:T(8,128)(2,1)}, u32[]{:S(2)}) copy-start(bf16[1024,384]{1,0:T(8,128)(2,1)} %get-tuple-element.225.o_ref) | copy-start | bytes 2359300
  82.2 15.6 %collective-permute-start.9 = (f32[16,192,128]{2,1,0:T(8,128)S(1)}, f32[16,192,128]{2,1,0:T(8,128)S(1)}, u32[]{:S(2)}, u32[]{:S(2)}) collective-permute-start(f32[16,192,128]{2,1,0:T(8,128)S(1)} %get-tuple-element.233), channel_id=1, source_target_pairs={{0,1},{1,0},{2,3},{3,2},{4,5},{5,4},{6,7},{7,6},{8,9},{9,8},{10,11... | collective-permute-start | bytes 4718600 | tf_op jit(solution)/shard_map/ppermute | solution.py:392
  82.2 16.3 %collective-permute-start.11 = (f32[4,384,128]{2,1,0:T(8,128)S(1)}, f32[4,384,128]{2,1,0:T(8,128)S(1)}, u32[]{:S(2)}, u32[]{:S(2)}) collective-permute-start(f32[4,384,128]{2,1,0:T(8,128)S(1)} %get-tuple-element.348), channel_id=1, source_target_pairs={{0,4},{1,3},{2,6},{3,1},{4,0},{5,7},{6,2},{7,5},{8,12},{9,11},{10,... | collective-permute-start | bytes 2359304 | tf_op jit(solution)/shard_map/ppermute | solution.py:392
  97.8 11.2 %collective-permute-start.10 = (f32[16,200,128]{2,1,0:T(8,128)S(1)}, f32[16,200,128]{2,1,0:T(8,128)S(1)}, u32[]{:S(2)}, u32[]{:S(2)}) collective-permute-start(f32[16,200,128]{2,1,0:T(8,128)S(1)} %get-tuple-element.237), channel_id=1, source_target_pairs={{0,1},{1,0},{2,3},{3,2},{4,5},{5,4},{6,7},{7,6},{8,9},{9,8},{10,11... | collective-permute-start | bytes 4915208 | tf_op jit(solution)/shard_map/ppermute | solution.py:392
  97.9 14.9 %collective-permute-start.13 = (f32[8,192,128]{2,1,0:T(8,128)S(1)}, f32[8,192,128]{2,1,0:T(8,128)S(1)}, u32[]{:S(2)}, u32[]{:S(2)}) collective-permute-start(f32[8,192,128]{2,1,0:T(8,128)S(1)} %multiply_add_fusion.7), channel_id=1, source_target_pairs={{0,2},{1,5},{2,0},{3,7},{4,6},{5,1},{6,4},{7,3},{8,10},{9,13},{10,... | collective-permute-start | bytes 2359304 | tf_op jit(solution)/shard_map/ppermute | solution.py:392
  98.6 11.9 %collective-permute-start.14 = (f32[2,384,128]{2,1,0:T(8,128)S(1)}, f32[2,384,128]{2,1,0:T(8,128)S(1)}, u32[]{:S(2)}, u32[]{:S(2)}) collective-permute-start(f32[2,384,128]{2,1,0:T(8,128)S(1)} %get-tuple-element.356), channel_id=1, source_target_pairs={{0,8},{1,17},{2,10},{3,19},{4,12},{5,21},{6,14},{7,23},{8,0},{9,25... | collective-permute-start | bytes 1179656 | tf_op jit(solution)/shard_map/ppermute | solution.py:392
  110.5 17.5 %collective-permute-start.19 = (f32[16,208,128]{2,1,0:T(8,128)S(1)}, f32[16,208,128]{2,1,0:T(8,128)S(1)}, u32[]{:S(2)}, u32[]{:S(2)}) collective-permute-start(f32[16,208,128]{2,1,0:T(8,128)S(1)} %get-tuple-element.256), channel_id=1, source_target_pairs={{0,1},{1,0},{2,3},{3,2},{4,5},{5,4},{6,7},{7,6},{8,9},{9,8},{10,11... | collective-permute-start | bytes 5111816 | tf_op jit(solution)/shard_map/ppermute | solution.py:392
  111.0 9.6 %collective-permute-start.16 = (f32[1,384,128]{2,1,0:T(8,128)S(1)}, f32[1,384,128]{2,1,0:T(8,128)S(1)}, u32[]{:S(2)}, u32[]{:S(2)}) collective-permute-start(f32[1,384,128]{2,1,0:T(8,128)S(1)} %get-tuple-element.364), channel_id=1, source_target_pairs={{0,16},{1,9},{2,18},{3,11},{4,20},{5,13},{6,22},{7,15},{8,24},{9,1... | collective-permute-start | bytes 589832 | tf_op jit(solution)/shard_map/ppermute | solution.py:392
  113.0 12.0 %collective-permute-start.15 = (f32[4,192,128]{2,1,0:T(8,128)S(1)}, f32[4,192,128]{2,1,0:T(8,128)S(1)}, u32[]{:S(2)}, u32[]{:S(2)}) collective-permute-start(f32[4,192,128]{2,1,0:T(8,128)S(1)} %get-tuple-element.354), channel_id=1, source_target_pairs={{0,4},{1,3},{2,6},{3,1},{4,0},{5,7},{6,2},{7,5},{8,12},{9,11},{10,... | collective-permute-start | bytes 1179656 | tf_op jit(solution)/shard_map/ppermute | solution.py:392
  114.6 20.1 %collective-permute-start.12 = (f32[8,200,128]{2,1,0:T(8,128)S(1)}, f32[8,200,128]{2,1,0:T(8,128)S(1)}, u32[]{:S(2)}, u32[]{:S(2)}) collective-permute-start(f32[8,200,128]{2,1,0:T(8,128)S(1)} %multiply_add_fusion.5), channel_id=1, source_target_pairs={{0,2},{1,5},{2,0},{3,7},{4,6},{5,1},{6,4},{7,3},{8,10},{9,13},{10,... | collective-permute-start | bytes 2457608 | tf_op jit(solution)/shard_map/ppermute | solution.py:392
  120.6 12.1 %collective-permute-start.18 = (f32[1,384,128]{2,1,0:T(8,128)S(1)}, f32[1,384,128]{2,1,0:T(8,128)S(1)}, u32[]{:S(2)}, u32[]{:S(2)}) collective-permute-start(f32[1,384,128]{2,1,0:T(8,128)S(1)} %add.137), channel_id=1, source_target_pairs={{0,16},{1,9},{2,18},{3,11},{4,20},{5,13},{6,22},{7,15},{8,24},{9,1... | collective-permute-start | bytes 589832 | tf_op jit(solution)/shard_map/ppermute | solution.py:392
  125.0 9.6 %collective-permute-start.17 = (f32[2,192,128]{2,1,0:T(8,128)S(1)}, f32[2,192,128]{2,1,0:T(8,128)S(1)}, u32[]{:S(2)}, u32[]{:S(2)}) collective-permute-start(f32[2,192,128]{2,1,0:T(8,128)S(1)} %get-tuple-element.362), channel_id=1, source_target_pairs={{0,8},{1,17},{2,10},{3,19},{4,12},{5,21},{6,14},{7,23},{8,0},{9,25... | collective-permute-start | bytes 589832 | tf_op jit(solution)/shard_map/ppermute | solution.py:392
  128.1 13.0 %collective-permute-start.22 = (f32[8,208,128]{2,1,0:T(8,128)S(1)}, f32[8,208,128]{2,1,0:T(8,128)S(1)}, u32[]{:S(2)}, u32[]{:S(2)}) collective-permute-start(f32[8,208,128]{2,1,0:T(8,128)S(1)} %multiply_add_fusion.3), channel_id=1, source_target_pairs={{0,2},{1,5},{2,0},{3,7},{4,6},{5,1},{6,4},{7,3},{8,10},{9,13},{10,... | collective-permute-start | bytes 2555912 | tf_op jit(solution)/shard_map/ppermute | solution.py:392
  132.7 12.4 %collective-permute-start.21 = (f32[2,384,128]{2,1,0:T(8,128)S(1)}, f32[2,384,128]{2,1,0:T(8,128)S(1)}, u32[]{:S(2)}, u32[]{:S(2)}) collective-permute-start(f32[2,384,128]{2,1,0:T(8,128)S(1)} %constant_dynamic-update-slice_fusion), channel_id=1, source_target_pairs={{0,8},{1,17},{2,10},{3,19},{4,12},{5,21},{6,14},{7,23},{8,0},{9,25... | collective-permute-start | bytes 1179656 | tf_op jit(solution)/shard_map/ppermute | solution.py:392
  134.9 13.2 %collective-permute-start.20 = (f32[4,200,128]{2,1,0:T(8,128)S(1)}, f32[4,200,128]{2,1,0:T(8,128)S(1)}, u32[]{:S(2)}, u32[]{:S(2)}) collective-permute-start(f32[4,200,128]{2,1,0:T(8,128)S(1)} %get-tuple-element.352), channel_id=1, source_target_pairs={{0,4},{1,3},{2,6},{3,1},{4,0},{5,7},{6,2},{7,5},{8,12},{9,11},{10,... | collective-permute-start | bytes 1228808 | tf_op jit(solution)/shard_map/ppermute | solution.py:392
  141.2 9.5 %collective-permute-start.25 = (f32[4,208,128]{2,1,0:T(8,128)S(1)}, f32[4,208,128]{2,1,0:T(8,128)S(1)}, u32[]{:S(2)}, u32[]{:S(2)}) collective-permute-start(f32[4,208,128]{2,1,0:T(8,128)S(1)} %get-tuple-element.350), channel_id=1, source_target_pairs={{0,4},{1,3},{2,6},{3,1},{4,0},{5,7},{6,2},{7,5},{8,12},{9,11},{10,... | collective-permute-start | bytes 1277960 | tf_op jit(solution)/shard_map/ppermute | solution.py:392
  145.2 13.1 %collective-permute-start.29 = (f32[4,384,128]{2,1,0:T(8,128)S(1)}, f32[4,384,128]{2,1,0:T(8,128)S(1)}, u32[]{:S(2)}, u32[]{:S(2)}) collective-permute-start(f32[4,384,128]{2,1,0:T(8,128)S(1)} %constant_dynamic-update-slice_fusion.2), channel_id=1, source_target_pairs={{0,4},{1,3},{2,6},{3,1},{4,0},{5,7},{6,2},{7,5},{8,12},{9,11},{10,... | collective-permute-start | bytes 2359304 | tf_op jit(solution)/shard_map/ppermute | solution.py:392
  147.2 11.0 %collective-permute-start.24 = (f32[1,192,128]{2,1,0:T(8,128)S(1)}, f32[1,192,128]{2,1,0:T(8,128)S(1)}, u32[]{:S(2)}, u32[]{:S(2)}) collective-permute-start(f32[1,192,128]{2,1,0:T(8,128)S(1)} %get-tuple-element.370), channel_id=1, source_target_pairs={{0,16},{1,9},{2,18},{3,11},{4,20},{5,13},{6,22},{7,15},{8,24},{9,1... | collective-permute-start | bytes 294920 | tf_op jit(solution)/shard_map/ppermute | solution.py:392
  148.2 10.1 %collective-permute-start.23 = (f32[2,200,128]{2,1,0:T(8,128)S(1)}, f32[2,200,128]{2,1,0:T(8,128)S(1)}, u32[]{:S(2)}, u32[]{:S(2)}) collective-permute-start(f32[2,200,128]{2,1,0:T(8,128)S(1)} %get-tuple-element.360), channel_id=1, source_target_pairs={{0,8},{1,17},{2,10},{3,19},{4,12},{5,21},{6,14},{7,23},{8,0},{9,25... | collective-permute-start | bytes 614408 | tf_op jit(solution)/shard_map/ppermute | solution.py:392
  150.8 11.3 %collective-permute-start.28 = (f32[2,208,128]{2,1,0:T(8,128)S(1)}, f32[2,208,128]{2,1,0:T(8,128)S(1)}, u32[]{:S(2)}, u32[]{:S(2)}) collective-permute-start(f32[2,208,128]{2,1,0:T(8,128)S(1)} %get-tuple-element.358), channel_id=1, source_target_pairs={{0,8},{1,17},{2,10},{3,19},{4,12},{5,21},{6,14},{7,23},{8,0},{9,25... | collective-permute-start | bytes 638984 | tf_op jit(solution)/shard_map/ppermute | solution.py:392
  158.2 5.6 %collective-permute-start.27 = (f32[1,192,128]{2,1,0:T(8,128)S(1)}, f32[1,192,128]{2,1,0:T(8,128)S(1)}, u32[]{:S(2)}, u32[]{:S(2)}) collective-permute-start(f32[1,192,128]{2,1,0:T(8,128)S(1)} %add.152), channel_id=1, source_target_pairs={{0,16},{1,9},{2,18},{3,11},{4,20},{5,13},{6,22},{7,15},{8,24},{9,1... | collective-permute-start | bytes 294920 | tf_op jit(solution)/shard_map/ppermute | solution.py:392
  158.4 25.4 %collective-permute-start.35 = (f32[8,384,128]{2,1,0:T(8,128)S(1)}, f32[8,384,128]{2,1,0:T(8,128)S(1)}, u32[]{:S(2)}, u32[]{:S(2)}) collective-permute-start(f32[8,384,128]{2,1,0:T(8,128)S(1)} %constant_dynamic-update-slice_fusion.4.refs_0_), channel_id=1, source_target_pairs={{0,1},{1,0},{2,3},{3,2},{4,5},{5,4},{6,7},{7,6},{8,9},{9,8},{10,11... | collective-permute-start | bytes 4718600 | tf_op jit(solution)/shard_map/ppermute | solution.py:392
  160.0 24.6 %collective-permute-start.34 = (f32[8,384,128]{2,1,0:T(8,128)S(1)}, f32[8,384,128]{2,1,0:T(8,128)S(1)}, u32[]{:S(2)}, u32[]{:S(2)}) collective-permute-start(f32[8,384,128]{2,1,0:T(8,128)S(1)} %constant_dynamic-update-slice_fusion.4.refs_0_), channel_id=1, source_target_pairs={{0,2},{1,5},{2,0},{3,7},{4,6},{5,1},{6,4},{7,3},{8,10},{9,13},{10,... | collective-permute-start | bytes 4718600 | tf_op jit(solution)/shard_map/ppermute | solution.py:392
  163.8 11.1 %collective-permute-start.32 = (f32[2,192,128]{2,1,0:T(8,128)S(1)}, f32[2,192,128]{2,1,0:T(8,128)S(1)}, u32[]{:S(2)}, u32[]{:S(2)}) collective-permute-start(f32[2,192,128]{2,1,0:T(8,128)S(1)} %constant_dynamic-update-slice_fusion.6), channel_id=1, source_target_pairs={{0,8},{1,17},{2,10},{3,19},{4,12},{5,21},{6,14},{7,23},{8,0},{9,25... | collective-permute-start | bytes 589832 | tf_op jit(solution)/shard_map/ppermute | solution.py:392
  163.9 7.4 %collective-permute-start.26 = (f32[1,200,128]{2,1,0:T(8,128)S(1)}, f32[1,200,128]{2,1,0:T(8,128)S(1)}, u32[]{:S(2)}, u32[]{:S(2)}) collective-permute-start(f32[1,200,128]{2,1,0:T(8,128)S(1)} %get-tuple-element.368), channel_id=1, source_target_pairs={{0,16},{1,9},{2,18},{3,11},{4,20},{5,13},{6,22},{7,15},{8,24},{9,1... | collective-permute-start | bytes 307208 | tf_op jit(solution)/shard_map/ppermute | solution.py:392
  165.8 9.9 %collective-permute-start.31 = (f32[1,208,128]{2,1,0:T(8,128)S(1)}, f32[1,208,128]{2,1,0:T(8,128)S(1)}, u32[]{:S(2)}, u32[]{:S(2)}) collective-permute-start(f32[1,208,128]{2,1,0:T(8,128)S(1)} %get-tuple-element.366), channel_id=1, source_target_pairs={{0,16},{1,9},{2,18},{3,11},{4,20},{5,13},{6,22},{7,15},{8,24},{9,1... | collective-permute-start | bytes 319496 | tf_op jit(solution)/shard_map/ppermute | solution.py:392
  171.3 6.5 %collective-permute-start.30 = (f32[1,200,128]{2,1,0:T(8,128)S(1)}, f32[1,200,128]{2,1,0:T(8,128)S(1)}, u32[]{:S(2)}, u32[]{:S(2)}) collective-permute-start(f32[1,200,128]{2,1,0:T(8,128)S(1)} %add.157), channel_id=1, source_target_pairs={{0,16},{1,9},{2,18},{3,11},{4,20},{5,13},{6,22},{7,15},{8,24},{9,1... | collective-permute-start | bytes 307208 | tf_op jit(solution)/shard_map/ppermute | solution.py:392
  174.9 8.8 %collective-permute-start.36 = (f32[4,192,128]{2,1,0:T(8,128)S(1)}, f32[4,192,128]{2,1,0:T(8,128)S(1)}, u32[]{:S(2)}, u32[]{:S(2)}) collective-permute-start(f32[4,192,128]{2,1,0:T(8,128)S(1)} %constant_dynamic-update-slice_fusion.8), channel_id=1, source_target_pairs={{0,4},{1,3},{2,6},{3,1},{4,0},{5,7},{6,2},{7,5},{8,12},{9,11},{10,... | collective-permute-start | bytes 1179656 | tf_op jit(solution)/shard_map/ppermute | solution.py:392
  175.7 6.5 %collective-permute-start.37 = (f32[1,208,128]{2,1,0:T(8,128)S(1)}, f32[1,208,128]{2,1,0:T(8,128)S(1)}, u32[]{:S(2)}, u32[]{:S(2)}) collective-permute-start(f32[1,208,128]{2,1,0:T(8,128)S(1)} %add.159), channel_id=1, source_target_pairs={{0,16},{1,9},{2,18},{3,11},{4,20},{5,13},{6,22},{7,15},{8,24},{9,1... | collective-permute-start | bytes 319496 | tf_op jit(solution)/shard_map/ppermute | solution.py:392
  184.6 7.0 %collective-permute-start.41 = (f32[8,384,128]{2,1,0:T(8,128)S(1)}, f32[8,384,128]{2,1,0:T(8,128)S(1)}, u32[]{:S(2)}, u32[]{:S(2)}) collective-permute-start(f32[8,384,128]{2,1,0:T(8,128)S(1)} %collective-permute-done.34.refs_1_), channel_id=1, source_target_pairs={{0,1},{1,0},{2,3},{3,2},{4,5},{5,4},{6,7},{7,6},{8,9},{9,8},{10,11... | collective-permute-start | bytes 4718600 | tf_op jit(solution)/shard_map/ppermute | solution.py:392
  184.6 6.4 %collective-permute-start.33 = (f32[2,200,128]{2,1,0:T(8,128)S(1)}, f32[2,200,128]{2,1,0:T(8,128)S(1)}, u32[]{:S(2)}, u32[]{:S(2)}) collective-permute-start(f32[2,200,128]{2,1,0:T(8,128)S(1)} %constant_dynamic-update-slice_fusion.10), channel_id=1, source_target_pairs={{0,8},{1,17},{2,10},{3,19},{4,12},{5,21},{6,14},{7,23},{8,0},{9,25... | collective-permute-start | bytes 614408 | tf_op jit(solution)/shard_map/ppermute | solution.py:392
  185.2 13.8 %collective-permute-start.39 = (f32[8,192,128]{2,1,0:T(8,128)S(1)}, f32[8,192,128]{2,1,0:T(8,128)S(1)}, u32[]{:S(2)}, u32[]{:S(2)}) collective-permute-start(f32[8,192,128]{2,1,0:T(8,128)S(1)} %constant_dynamic-update-slice_fusion.14.refs_0_), channel_id=1, source_target_pairs={{0,2},{1,5},{2,0},{3,7},{4,6},{5,1},{6,4},{7,3},{8,10},{9,13},{10,... | collective-permute-start | bytes 2359304 | tf_op jit(solution)/shard_map/ppermute | solution.py:392
  187.1 8.8 %collective-permute-start.40 = (f32[2,208,128]{2,1,0:T(8,128)S(1)}, f32[2,208,128]{2,1,0:T(8,128)S(1)}, u32[]{:S(2)}, u32[]{:S(2)}) collective-permute-start(f32[2,208,128]{2,1,0:T(8,128)S(1)} %constant_dynamic-update-slice_fusion.12), channel_id=1, source_target_pairs={{0,8},{1,17},{2,10},{3,19},{4,12},{5,21},{6,14},{7,23},{8,0},{9,25... | collective-permute-start | bytes 638984 | tf_op jit(solution)/shard_map/ppermute | solution.py:392
  191.0 11.6 %collective-permute-start.38 = (f32[4,200,128]{2,1,0:T(8,128)S(1)}, f32[4,200,128]{2,1,0:T(8,128)S(1)}, u32[]{:S(2)}, u32[]{:S(2)}) collective-permute-start(f32[4,200,128]{2,1,0:T(8,128)S(1)} %constant_dynamic-update-slice_fusion.16), channel_id=1, source_target_pairs={{0,4},{1,3},{2,6},{3,1},{4,0},{5,7},{6,2},{7,5},{8,12},{9,11},{10,... | collective-permute-start | bytes 1228808 | tf_op jit(solution)/shard_map/ppermute | solution.py:392
  199.0 6.0 %collective-permute-start.45 = (f32[8,192,128]{2,1,0:T(8,128)S(1)}, f32[8,192,128]{2,1,0:T(8,128)S(1)}, u32[]{:S(2)}, u32[]{:S(2)}) collective-permute-start(f32[8,192,128]{2,1,0:T(8,128)S(1)} %collective-permute-done.39.refs_1_), channel_id=1, source_target_pairs={{0,1},{1,0},{2,3},{3,2},{4,5},{5,4},{6,7},{7,6},{8,9},{9,8},{10,11... | collective-permute-start | bytes 2359304 | tf_op jit(solution)/shard_map/ppermute | solution.py:392
  202.0 3.1 %collective-permute-start.44 = (f32[8,192,128]{2,1,0:T(8,128)S(1)}, f32[8,192,128]{2,1,0:T(8,128)S(1)}, u32[]{:S(2)}, u32[]{:S(2)}) collective-permute-start(f32[8,192,128]{2,1,0:T(8,128)S(1)} %constant_dynamic-update-slice_fusion.14.refs_0_), channel_id=1, source_target_pairs={{0,1},{1,0},{2,3},{3,2},{4,5},{5,4},{6,7},{7,6},{8,9},{9,8},{10,11... | collective-permute-start | bytes 2359304 | tf_op jit(solution)/shard_map/ppermute | solution.py:392
  202.7 17.0 %collective-permute-start.42 = (f32[8,200,128]{2,1,0:T(8,128)S(1)}, f32[8,200,128]{2,1,0:T(8,128)S(1)}, u32[]{:S(2)}, u32[]{:S(2)}) collective-permute-start(f32[8,200,128]{2,1,0:T(8,128)S(1)} %constant_dynamic-update-slice_fusion.20.refs_0_), channel_id=1, source_target_pairs={{0,2},{1,5},{2,0},{3,7},{4,6},{5,1},{6,4},{7,3},{8,10},{9,13},{10,... | collective-permute-start | bytes 2457608 | tf_op jit(solution)/shard_map/ppermute | solution.py:392
  203.0 12.7 %collective-permute-start.43 = (f32[4,208,128]{2,1,0:T(8,128)S(1)}, f32[4,208,128]{2,1,0:T(8,128)S(1)}, u32[]{:S(2)}, u32[]{:S(2)}) collective-permute-start(f32[4,208,128]{2,1,0:T(8,128)S(1)} %constant_dynamic-update-slice_fusion.18), channel_id=1, source_target_pairs={{0,4},{1,3},{2,6},{3,1},{4,0},{5,7},{6,2},{7,5},{8,12},{9,11},{10,... | collective-permute-start | bytes 1277960 | tf_op jit(solution)/shard_map/ppermute | solution.py:392
  215.7 10.2 %collective-permute-start.49 = (f32[8,208,128]{2,1,0:T(8,128)S(1)}, f32[8,208,128]{2,1,0:T(8,128)S(1)}, u32[]{:S(2)}, u32[]{:S(2)}) collective-permute-start(f32[8,208,128]{2,1,0:T(8,128)S(1)} %constant_dynamic-update-slice_fusion.22.refs_0_), channel_id=1, source_target_pairs={{0,1},{1,0},{2,3},{3,2},{4,5},{5,4},{6,7},{7,6},{8,9},{9,8},{10,11... | collective-permute-start | bytes 2555912 | tf_op jit(solution)/shard_map/ppermute | solution.py:392
  216.5 12.7 %collective-permute-start.48 = (f32[8,208,128]{2,1,0:T(8,128)S(1)}, f32[8,208,128]{2,1,0:T(8,128)S(1)}, u32[]{:S(2)}, u32[]{:S(2)}) collective-permute-start(f32[8,208,128]{2,1,0:T(8,128)S(1)} %constant_dynamic-update-slice_fusion.22.refs_0_), channel_id=1, source_target_pairs={{0,2},{1,5},{2,0},{3,7},{4,6},{5,1},{6,4},{7,3},{8,10},{9,13},{10,... | collective-permute-start | bytes 2555912 | tf_op jit(solution)/shard_map/ppermute | solution.py:392
  219.6 2.3 collective-permute-start.46
  219.6 3.5 %collective-permute-start.47 = (f32[8,200,128]{2,1,0:T(8,128)S(1)}, f32[8,200,128]{2,1,0:T(8,128)S(1)}, u32[]{:S(2)}, u32[]{:S(2)}) collective-permute-start(f32[8,200,128]{2,1,0:T(8,128)S(1)} %collective-permute-done.42.refs_1_), channel_id=1, source_target_pairs={{0,1},{1,0},{2,3},{3,2},{4,5},{5,4},{6,7},{7,6},{8,9},{9,8},{10,11... | collective-permute-start | bytes 2457608 | tf_op jit(solution)/shard_map/ppermute | solution.py:392
  229.2 2.4 %collective-permute-start.50 = (f32[8,208,128]{2,1,0:T(8,128)S(1)}, f32[8,208,128]{2,1,0:T(8,128)S(1)}, u32[]{:S(2)}, u32[]{:S(2)}) collective-permute-start(f32[8,208,128]{2,1,0:T(8,128)S(1)} %collective-permute-done.48.refs_1_), channel_id=1, source_target_pairs={{0,1},{1,0},{2,3},{3,2},{4,5},{5,4},{6,7},{7,6},{8,9},{9,8},{10,11... | collective-permute-start | bytes 2555912 | tf_op jit(solution)/shard_map/ppermute | solution.py:392
  (14 other events, 27.0 us)

commit v6 on v5

--- a/solution.py
+++ b/solution.py
@@ -604,7 +604,7 @@
 
 ORDER = (
     "late", "cross kernel", "late", "cross", "self kernel", "cross", "own", "late",
-    "patch kernel", "own", "late", "patch", "cross", "input kernel", "late", "cross", "patch",
+    "patch kernel", "own", "late", "patch", "cross", "input kernel", "late", "patch", "cross",
     "late", "cross", "own", "input kernel", "patch", "late", "own", "patch", "cross", "own",
     "late", "patch", "cross", "own", "cross", "patch", "own", "patch", "cross", "late", "own",
     "late", "patch", "cross", "own", "cross", "patch", "own", "own", "patch", "patch",

time: 235 us -> 234 us (level)
  transfers between devices with their start and end apart: 51 -> 51, of which waited for: 28 -> 27; matrix products, arithmetic and copies ran while one was open for 1% -> 1% of each run, Pallas kernels for 43% -> 43%
where the time goes in v6:
time: 234 us
  Pallas kernels  105 us (45%)
  waiting for transfers between devices  66.1 us (28%)
  starting transfers between devices  53.8 us (23%)
  other arithmetic  6.14 us (3%)
    pallas_call x4, Pallas kernels, run(): pl.pallas_call(kernel, grid=(steps,), out_shape=[jax.ShapeDtypeStruct(s,...  79.5 us
    ppermute x51, waiting for transfers between devices, exchange(): lax.ppermute(values, 'dp', flips(count, first, first if second is None el...  66.1 us
    ppermute x51, starting transfers between devices, exchange(): lax.ppermute(values, 'dp', flips(count, first, first if second is None el...  53.8 us
    pallas_call x4, Pallas kernels, unpack(): pl.pallas_call(functools.partial(unpack_kernel, shapes, with_gains, place...  12.8 us
    pallas_call x2, Pallas kernels, patch_input(): pl.pallas_call(patch_input_kernel, grid=(steps,), out_shape=jax.ShapeDtyp...  10.1 us
  transfers between devices with their start and end apart: 51, of which 27 were waited for; matrix products, arithmetic and copies ran while one was open for 1% of the time, Pallas kernels for 43%

profile of v6, /device:TPU:0, one launch (start us, length us, event | category | flops | bytes accessed | tf_op | source)
XLA Modules:
  0.0 234.1 jit_solution(5916246924968033428)
XLA Ops:
  0.7 1.2 count.1
  2.4 1.0 collective-permute-done
  4.0 4.9 %collective-permute-start.3 = (f32[2]{0:T(128)S(1)}, f32[2]{0:T(128)S(1)}, u32[]{:S(2)}, u32[]{:S(2)}) collective-permute-start(f32[2]{0:T(128)S(1)} %add.120), channel_id=1, source_target_pairs={{0,24},{1,25},{2,26},{3,27},{4,28},{5,29},{6,30},{7,31},{8,16},{9,... | collective-permute-start | bytes 32 | tf_op jit(solution)/shard_map/ppermute | solution.py:392
  9.5 38.9 %forward.1 = (bf16[2048,512]{1,0:T(8,128)(2,1)}, bf16[2048,768]{1,0:T(8,128)(2,1)}, bf16[1024,1152]{1,0:T(8,128)(2,1)}, bf16[8,3,256,128]{3,2,1,0:T(8,128)(2,1)}...) custom-call(s32[8]{0:T(128)} %len_ref.3, ...), custom_call_target="tpu_custom_call" | custom-call | flops 40000000000 | bytes 1048576 | tf_op jit(solution)/shard_map/forward/pallas_call | solution.py:589
  48.5 2.7 %collective-permute-start.6 = (f32[2]{0:T(128)S(1)}, f32[2]{0:T(128)S(1)}, u32[]{:S(2)}, u32[]{:S(2)}) collective-permute-start(f32[2]{0:T(128)S(1)} %add_add_fusion.refs_0_), channel_id=1, source_target_pairs={{0,6},{1,7},{2,4},{3,5},{4,2},{5,3},{6,0},{7,1},{8,14},{9,15},{10,... | collective-permute-start | bytes 32 | tf_op jit(solution)/shard_map/ppermute | solution.py:392
  52.1 0.9 collective-permute-done.6.refs_3_
  53.0 1.8 collective-permute-done.5.refs_2_
  55.8 1.4 weigh.1
  57.3 2.2 multiply_add_fusion.1
  60.2 18.2 %cross_backward.1 = (bf16[2048,512]{1,0:T(8,128)(2,1)S(1)}, f32[1024,512]{1,0:T(8,128)}, f32[1,512]{1,0:T(1,128)S(1)}, f32[1,512]{1,0:T(1,128)S(1)}, f32[16,192,...) custom-call(s32[8]{0:T(128)S(1)} %copy-done.1, f32[1024,512]{1,0:T(8,128)} %get-tuple-element.208.dx2_ref, ...), custom_call_target="tpu_custom_call" | custom-call | flops 20000000000 | bytes 1048576 | tf_op jit(solution)/shard_map/cross_backward/pallas_call | solution.py:589
  78.4 1.6 collective-permute-done.8
  80.0 1.9 multiply_add_fusion
  82.2 1.6 collective-permute-start.11
  84.3 13.4 %self_backward.1 = (f32[1024,512]{1,0:T(8,128)}, f32[16,200,128]{2,1,0:T(8,128)S(1)}, f32[16,200,128]{2,1,0:T(8,128)S(1)}) custom-call(s32[8]{0:T(128)S(1)} %copy-done.1, f32[2]{0:T(128)S(1)} %copy-done.2, f32[1024,512]{1,0:T(8,128)S(1)} %copy-done.14, bf16[1024,1152]{1,0:T(8,128)(2,1)} %get-tuple-element.223.qkv_ref, ...), custom_call_target="tpu_custom_call" | custom-call | flops 16000000000 | bytes 1048576 | tf_op jit(solution)/shard_map/self_backward/pallas_call | solution.py:589
  98.6 1.3 collective-permute-start.14
  99.9 9.1 %patch_weight.1 = (f32[16,208,128]{2,1,0:T(8,128)S(1)}, f32[16,208,128]{2,1,0:T(8,128)S(1)}) custom-call(s32[8]{0:T(128)S(1)} %copy-done.1, bf16[2048,1664]{1,0:T(8,128)(2,1)} %bitcast.35, bf16[2048,512]{1,0:T(8,128)(2,1)S(1)} %get-tuple-element.266.dfeat_ref), custom_call_target="tpu_custom_call" | custom-call | flops 12000000000 | bytes 1048576 | tf_op jit(solution)/shard_map/patch_weight/pallas_call | solution.py:589
  109.1 1.3 collective-permute-done.14
  111.0 1.8 collective-permute-start.17
  113.0 1.6 collective-permute-start.15
  114.6 0.9 collective-permute-start.12
  115.5 5.0 %patch_input.2.refs_0_ = f32[2048,1664]{1,0:T(8,128)} custom-call(f32[2]{0:T(128)S(1)} %copy-done.2, bf16[2048,512]{1,0:T(8,128)(2,1)S(1)} %get-tuple-element.266.dfeat_ref, bf16[1664,512]{1,0:T(8,128)(2,1)S(1)} %copy-done), custom_call_target="tpu_custom_call" | custom-call | flops 6000000000 | bytes 1048576 | tf_op jit(solution)/shard_map/patch_input/pallas_call | solution.py:787
  121.1 1.8 collective-permute-start.22
  122.9 2.1 collective-permute-done.15
  125.0 2.9 %collective-permute-start.18 = (f32[2,192,128]{2,1,0:T(8,128)S(1)}, f32[2,192,128]{2,1,0:T(8,128)S(1)}, u32[]{:S(2)}, u32[]{:S(2)}) collective-permute-start(f32[2,192,128]{2,1,0:T(8,128)S(1)} %get-tuple-element.362), channel_id=1, source_target_pairs={{0,8},{1,17},{2,10},{3,19},{4,12},{5,21},{6,14},{7,23},{8,0},{9,25... | collective-permute-start | bytes 589832 | tf_op jit(solution)/shard_map/ppermute | solution.py:392
  128.0 4.7 %collective-permute-done.19 = f32[1,384,128]{2,1,0:T(8,128)S(1)} collective-permute-done((f32[1,384,128]{2,1,0:T(8,128)S(1)}, f32[1,384,128]{2,1,0:T(8,128)S(1)}, u32[]{:S(2)}, u32[]{:S(2)}) %collective-permute-start.19) | collective-permute-done | bytes 196640 | tf_op jit(solution)/shard_map/ppermute | solution.py:392
  132.7 1.9 collective-permute-start.21
  135.3 5.0 %patch_input.3 = f32[2048,1664]{1,0:T(8,128)} custom-call(f32[2]{0:T(128)S(1)} %copy-done.2, bf16[2048,512]{1,0:T(8,128)(2,1)S(1)} %get-tuple-element.266.dfeat_ref, bf16[1664,512]{1,0:T(8,128)(2,1)S(1)} %copy-done, f32[2048,1664]{1,0:T(8,128)} %patch_input.2.refs_0_), custom_call_target="tpu_custom_call", output_to_operand_aliasing={{}: (3, {})} | custom-call | flops 6000000000 | bytes 1048576 | tf_op jit(solution)/shard_map/patch_input/pallas_call | solution.py:787
  140.5 1.8 collective-permute-start.25
  142.3 2.8 %collective-permute-done.21 = f32[2,384,128]{2,1,0:T(8,128)S(1)} collective-permute-done((f32[2,384,128]{2,1,0:T(8,128)S(1)}, f32[2,384,128]{2,1,0:T(8,128)S(1)}, u32[]{:S(2)}, u32[]{:S(2)}) %collective-permute-start.21) | collective-permute-done | bytes 393248 | tf_op jit(solution)/shard_map/ppermute | solution.py:392
  145.2 1.9 collective-permute-start.29
  147.1 1.0 collective-permute-start.24
  148.2 2.5 %collective-permute-start.23 = (f32[2,200,128]{2,1,0:T(8,128)S(1)}, f32[2,200,128]{2,1,0:T(8,128)S(1)}, u32[]{:S(2)}, u32[]{:S(2)}) collective-permute-start(f32[2,200,128]{2,1,0:T(8,128)S(1)} %get-tuple-element.360), channel_id=1, source_target_pairs={{0,8},{1,17},{2,10},{3,19},{4,12},{5,21},{6,14},{7,23},{8,0},{9,25... | collective-permute-start | bytes 614408 | tf_op jit(solution)/shard_map/ppermute | solution.py:392
  150.9 7.3 %collective-permute-done.24 = f32[1,192,128]{2,1,0:T(8,128)S(1)} collective-permute-done((f32[1,192,128]{2,1,0:T(8,128)S(1)}, f32[1,192,128]{2,1,0:T(8,128)S(1)}, u32[]{:S(2)}, u32[]{:S(2)}) %collective-permute-start.24) | collective-permute-done | bytes 98336 | tf_op jit(solution)/shard_map/ppermute | solution.py:392
  158.4 1.5 collective-permute-start.35
  160.0 0.9 collective-permute-start.34
  160.9 1.2 collective-permute-done.28
  162.1 1.7 collective-permute-done.27
  163.9 1.9 collective-permute-start.26
  165.8 1.0 collective-permute-start.31
  166.9 4.4 %collective-permute-done.26 = f32[1,200,128]{2,1,0:T(8,128)S(1)} collective-permute-done((f32[1,200,128]{2,1,0:T(8,128)S(1)}, f32[1,200,128]{2,1,0:T(8,128)S(1)}, u32[]{:S(2)}, u32[]{:S(2)}) %collective-permute-start.26) | collective-permute-done | bytes 102432 | tf_op jit(solution)/shard_map/ppermute | solution.py:392
  171.3 3.4 %collective-permute-start.30 = (f32[1,200,128]{2,1,0:T(8,128)S(1)}, f32[1,200,128]{2,1,0:T(8,128)S(1)}, u32[]{:S(2)}, u32[]{:S(2)}) collective-permute-start(f32[1,200,128]{2,1,0:T(8,128)S(1)} %add.157), channel_id=1, source_target_pairs={{0,16},{1,9},{2,18},{3,11},{4,20},{5,13},{6,22},{7,15},{8,24},{9,1... | collective-permute-start | bytes 307208 | tf_op jit(solution)/shard_map/ppermute | solution.py:392
  175.7 0.9 collective-permute-start.37
  176.6 1.3 collective-permute-done.30
  177.9 3.5 %collective-permute-done.37 = f32[1,208,128]{2,1,0:T(8,128)S(1)} collective-permute-done((f32[1,208,128]{2,1,0:T(8,128)S(1)}, f32[1,208,128]{2,1,0:T(8,128)S(1)}, u32[]{:S(2)}, u32[]{:S(2)}) %collective-permute-start.37) | collective-permute-done | bytes 106528 | tf_op jit(solution)/shard_map/ppermute | solution.py:392
  181.5 2.2 collective-permute-done.36
  183.8 0.8 collective-permute-done.34.refs_1_
  184.6 0.9 collective-permute-start.39
  185.5 2.0 collective-permute-start.40
  187.6 5.3 %collective-permute-done.33 = f32[2,200,128]{2,1,0:T(8,128)S(1)} collective-permute-done((f32[2,200,128]{2,1,0:T(8,128)S(1)}, f32[2,200,128]{2,1,0:T(8,128)S(1)}, u32[]{:S(2)}, u32[]{:S(2)}) %collective-permute-start.33) | collective-permute-done | bytes 204832 | tf_op jit(solution)/shard_map/ppermute | solution.py:392
  193.0 4.3 %unpack.4 = (f32[1024,512]{1,0:T(8,128)}, f32[512,1024]{1,0:T(8,128)}, f32[512,1024]{1,0:T(8,128)}) custom-call(s32[8]{0:T(128)S(1)} %copy-done.1, f32[8,384,128]{2,1,0:T(8,128)S(1)} %constant_dynamic-update-slice_fusion.4.refs_0_, f32[8,384,128]{2,1,0:T(8,128)S(1)} %collective-permute-done.34.refs_1_, f32[8,384,128]{2,1,0:T(8,128)S(1)} %collective-permute-done.35.refs_2_, ...), custom_call_target="tpu_custom_call" | custom-call | tf_op jit(solution)/shard_map/unpack/pallas_call | solution.py:461
  197.3 1.1 collective-permute-done.39.refs_1_
  198.4 2.5 %collective-permute-start.45 = (f32[8,192,128]{2,1,0:T(8,128)S(1)}, f32[8,192,128]{2,1,0:T(8,128)S(1)}, u32[]{:S(2)}, u32[]{:S(2)}) collective-permute-start(f32[8,192,128]{2,1,0:T(8,128)S(1)} %collective-permute-done.39.refs_1_), channel_id=1, source_target_pairs={{0,1},{1,0},{2,3},{3,2},{4,5},{5,4},{6,7},{7,6},{8,9},{9,8},{10,11... | collective-permute-start | bytes 2359304 | tf_op jit(solution)/shard_map/ppermute | solution.py:392
  200.9 1.7 collective-permute-done.38
  202.7 1.8 collective-permute-start.43
  204.5 2.8 %unpack.5 = (f32[384,512]{1,0:T(8,128)}, f32[512,384]{1,0:T(8,128)}, f32[512,384]{1,0:T(8,128)}, f32[512,384]{1,0:T(8,128)}) custom-call(s32[8]{0:T(128)S(1)} %copy-done.1, f32[8,192,128]{2,1,0:T(8,128)S(1)} %constant_dynamic-update-slice_fusion.14.refs_0_, f32[8,192,128]{2,1,0:T(8,128)S(1)} %collective-permute-done.39.refs_1_, ...), custom_call_target="tpu_custom_call" | custom-call | tf_op jit(solution)/shard_map/unpack/pallas_call | solution.py:461
  207.3 8.2 %collective-permute-done.43 = f32[4,208,128]{2,1,0:T(8,128)S(1)} collective-permute-done((f32[4,208,128]{2,1,0:T(8,128)S(1)}, f32[4,208,128]{2,1,0:T(8,128)S(1)}, u32[]{:S(2)}, u32[]{:S(2)}) %collective-permute-start.43) | collective-permute-done | bytes 426016 | tf_op jit(solution)/shard_map/ppermute | solution.py:392
  215.7 2.0 collective-permute-start.48
  217.7 1.9 collective-permute-done.42.refs_1_
  220.1 1.8 collective-permute-done.46.refs_2_
  221.9 1.2 collective-permute-done.47.refs_3_
  223.1 2.8 %unpack.6 = (f32[384,512]{1,0:T(8,128)}, f32[512,384]{1,0:T(8,128)}, f32[512,384]{1,0:T(8,128)}, f32[512,384]{1,0:T(8,128)}, f32[256,128]{1,0:T(8,128)}, /*index...) custom-call(s32[8]{0:T(128)S(1)} %copy-done.1, ...), custom_call_target="tpu_custom_call" | custom-call | tf_op jit(solution)/shard_map/unpack/pallas_call | solution.py:461
  225.9 2.8 %collective-permute-done.48.refs_1_ = f32[8,208,128]{2,1,0:T(8,128)S(1)} collective-permute-done((f32[8,208,128]{2,1,0:T(8,128)S(1)}, f32[8,208,128]{2,1,0:T(8,128)S(1)}, u32[]{:S(2)}, u32[]{:S(2)}) %collective-permute-start.48) | collective-permute-done | bytes 852000 | tf_op jit(solution)/shard_map/ppermute | solution.py:392
  228.7 2.4 %collective-permute-done.50.refs_3_ = f32[8,208,128]{2,1,0:T(8,128)S(1)} collective-permute-done((f32[8,208,128]{2,1,0:T(8,128)S(1)}, f32[8,208,128]{2,1,0:T(8,128)S(1)}, u32[]{:S(2)}, u32[]{:S(2)}) %collective-permute-start.50) | collective-permute-done | bytes 852000 | tf_op jit(solution)/shard_map/ppermute | solution.py:392
  231.1 3.0 %unpack.7 = f32[1664,512]{1,0:T(8,128)} custom-call(s32[8]{0:T(128)S(1)} %copy-done.1, f32[8,208,128]{2,1,0:T(8,128)S(1)} %constant_dynamic-update-slice_fusion.22.refs_0_, f32[8,208,128]{2,1,0:T(8,128)S(1)} %collective-permute-done.48.refs_1_, f32[8,208,128]{2,1,0:T(8,128)S(1)} %collective-permute-done.49.refs_2_, ...), custom_call_target="tpu_custom_call" | custom-call | tf_op jit(solution)/shard_map/unpack/pallas_call | solution.py:461
  (154 shorter events, 10.7 us)
Async XLA Ops:
  1.9 1.5 collective-permute-start
  4.0 44.4 %collective-permute-start.3 = (f32[2]{0:T(128)S(1)}, f32[2]{0:T(128)S(1)}, u32[]{:S(2)}, u32[]{:S(2)}) collective-permute-start(f32[2]{0:T(128)S(1)} %add.120), channel_id=1, source_target_pairs={{0,24},{1,25},{2,26},{3,27},{4,28},{5,29},{6,30},{7,31},{8,16},{9,... | collective-permute-start | bytes 32 | tf_op jit(solution)/shard_map/ppermute | solution.py:392
  8.9 39.5 %collective-permute-start.2 = (f32[2]{0:T(128)S(1)}, f32[2]{0:T(128)S(1)}, u32[]{:S(2)}, u32[]{:S(2)}) collective-permute-start(f32[2]{0:T(128)S(1)} %add.120), channel_id=1, source_target_pairs={{0,16},{1,17},{2,18},{3,19},{4,20},{5,21},{6,22},{7,23},{8,24},{9,... | collective-permute-start | bytes 32 | tf_op jit(solution)/shard_map/ppermute | solution.py:392
  8.9 39.5 %collective-permute-start.1 = (f32[2]{0:T(128)S(1)}, f32[2]{0:T(128)S(1)}, u32[]{:S(2)}, u32[]{:S(2)}) collective-permute-start(f32[2]{0:T(128)S(1)} %add.120), channel_id=1, source_target_pairs={{0,8},{1,9},{2,10},{3,11},{4,12},{5,13},{6,14},{7,15},{8,0},{9,1},... | collective-permute-start | bytes 32 | tf_op jit(solution)/shard_map/ppermute | solution.py:392
  48.4 8.8 %collective-permute-start.7 = (f32[16,384,128]{2,1,0:T(8,128)}, f32[16,384,128]{2,1,0:T(8,128)}, u32[]{:S(2)}, u32[]{:S(2)}) collective-permute-start(f32[16,384,128]{2,1,0:T(8,128)} %get-tuple-element.203), channel_id=1, source_target_pairs={{0,1},{1,0},{2,3},{3,2},{4,5},{5,4},{6,7},{7,6},{8,9},{9,8},{10,11... | collective-permute-start | bytes 9437192 | tf_op jit(solution)/shard_map/ppermute | solution.py:392
  48.5 6.8 %copy-start.23 = (f32[2]{0:T(128)}, f32[2]{0:T(128)S(1)}, u32[]{:S(2)}) copy-start(f32[2]{0:T(128)S(1)} %add_add_fusion.refs_0_) | copy-start | bytes 28
  48.5 4.5 %collective-permute-start.6 = (f32[2]{0:T(128)S(1)}, f32[2]{0:T(128)S(1)}, u32[]{:S(2)}, u32[]{:S(2)}) collective-permute-start(f32[2]{0:T(128)S(1)} %add_add_fusion.refs_0_), channel_id=1, source_target_pairs={{0,6},{1,7},{2,4},{3,5},{4,2},{5,3},{6,0},{7,1},{8,14},{9,15},{10,... | collective-permute-start | bytes 32 | tf_op jit(solution)/shard_map/ppermute | solution.py:392
  51.2 3.5 %collective-permute-start.5 = (f32[2]{0:T(128)S(1)}, f32[2]{0:T(128)S(1)}, u32[]{:S(2)}, u32[]{:S(2)}) collective-permute-start(f32[2]{0:T(128)S(1)} %add_add_fusion.refs_0_), channel_id=1, source_target_pairs={{0,4},{1,5},{2,6},{3,7},{4,0},{5,1},{6,2},{7,3},{8,12},{9,13},{10,... | collective-permute-start | bytes 32 | tf_op jit(solution)/shard_map/ppermute | solution.py:392
  51.7 3.5 %collective-permute-start.4 = (f32[2]{0:T(128)S(1)}, f32[2]{0:T(128)S(1)}, u32[]{:S(2)}, u32[]{:S(2)}) collective-permute-start(f32[2]{0:T(128)S(1)} %add_add_fusion.refs_0_), channel_id=1, source_target_pairs={{0,2},{1,3},{2,0},{3,1},{4,6},{5,7},{6,4},{7,5},{8,10},{9,11},{10,... | collective-permute-start | bytes 32 | tf_op jit(solution)/shard_map/ppermute | solution.py:392
  57.2 2.9 %copy-start.1 = (s32[8]{0:T(128)S(1)}, s32[8]{0:T(128)}, u32[]{:S(2)}) copy-start(s32[8]{0:T(128)} %get-tuple-element.183.code_ref) | copy-start | bytes 100
  57.2 2.9 %copy-start.4 = (bf16[512,384]{1,0:T(8,128)(2,1)S(1)}, bf16[512,384]{1,0:T(8,128)(2,1)}, u32[]{:S(2)}) copy-start(bf16[512,384]{1,0:T(8,128)(2,1)} %wck_ref.3) | copy-start | bytes 1179652
  57.2 2.9 %copy-start.5 = (bf16[512,384]{1,0:T(8,128)(2,1)S(1)}, bf16[512,384]{1,0:T(8,128)(2,1)}, u32[]{:S(2)}) copy-start(bf16[512,384]{1,0:T(8,128)(2,1)} %wcv_ref.3) | copy-start | bytes 1179652
  57.2 2.9 %copy-start.6 = (bf16[512,384]{1,0:T(8,128)(2,1)S(1)}, bf16[512,384]{1,0:T(8,128)(2,1)}, u32[]{:S(2)}) copy-start(bf16[512,384]{1,0:T(8,128)(2,1)} %wcq_ref.3) | copy-start | bytes 1179652
  57.2 2.9 %copy-start.7 = (bf16[384,512]{1,0:T(8,128)(2,1)S(1)}, bf16[384,512]{1,0:T(8,128)(2,1)}, u32[]{:S(2)}) copy-start(bf16[384,512]{1,0:T(8,128)(2,1)} %wco_ref.3) | copy-start | bytes 1179652
  57.2 2.9 %copy-start.12 = (f32[512]{0:T(512)S(1)}, f32[512]{0:T(512)}, u32[]{:S(2)}) copy-start(f32[512]{0:T(512)} %param.33) | copy-start | bytes 6148
  57.3 2.9 %copy-start.17 = (bf16[1024,384]{1,0:T(8,128)(2,1)S(1)}, bf16[1024,384]{1,0:T(8,128)(2,1)}, u32[]{:S(2)}) copy-start(bf16[1024,384]{1,0:T(8,128)(2,1)} %get-tuple-element.209.cq_ref) | copy-start | bytes 2359300
  59.5 20.5 %collective-permute-start.8 = (f32[8,384,128]{2,1,0:T(8,128)S(1)}, f32[8,384,128]{2,1,0:T(8,128)S(1)}, u32[]{:S(2)}, u32[]{:S(2)}) collective-permute-start(f32[8,384,128]{2,1,0:T(8,128)S(1)} %multiply_add_fusion.1), channel_id=1, source_target_pairs={{0,2},{1,5},{2,0},{3,7},{4,6},{5,1},{6,4},{7,3},{8,10},{9,13},{10,... | collective-permute-start | bytes 4718600 | tf_op jit(solution)/shard_map/ppermute | solution.py:392
  60.1 19.8 %copy-start.20 = (f32[16,384,128]{2,1,0:T(8,128)S(1)}, f32[16,384,128]{2,1,0:T(8,128)}, u32[]{:S(2)}) copy-start(f32[16,384,128]{2,1,0:T(8,128)} %get-tuple-element.218) | copy-start | bytes 9437188
  60.1 19.8 %copy-start.21 = (f32[1,1,128]{2,1,0:T(1,128)S(1)}, f32[1,1,128]{2,1,0:T(1,128)}, u32[]{:S(2)}) copy-start(f32[1,1,128]{2,1,0:T(1,128)} %get-tuple-element.205) | copy-start | bytes 1540
  60.2 19.8 %copy-start.22 = (f32[1,1,128]{2,1,0:T(1,128)S(1)}, f32[1,1,128]{2,1,0:T(1,128)}, u32[]{:S(2)}) copy-start(f32[1,1,128]{2,1,0:T(1,128)} %get-tuple-element.207) | copy-start | bytes 1540
  80.0 3.8 %copy-start.15 = (bf16[8,3,256,128]{3,2,1,0:T(8,128)(2,1)S(1)}, bf16[8,3,256,128]{3,2,1,0:T(8,128)(2,1)}, u32[]{:S(2)}) copy-start(bf16[8,3,256,128]{3,2,1,0:T(8,128)(2,1)} %get-tuple-element.224.pt_ref) | copy-start | bytes 4718596
  80.0 3.8 %copy-start.16 = (bf16[1024,384]{1,0:T(8,128)(2,1)S(1)}, bf16[1024,384]{1,0:T(8,128)(2,1)}, u32[]{:S(2)}) copy-start(bf16[1024,384]{1,0:T(8,128)(2,1)} %get-tuple-element.225.o_ref) | copy-start | bytes 2359300
  82.2 15.6 %collective-permute-start.9 = (f32[16,192,128]{2,1,0:T(8,128)S(1)}, f32[16,192,128]{2,1,0:T(8,128)S(1)}, u32[]{:S(2)}, u32[]{:S(2)}) collective-permute-start(f32[16,192,128]{2,1,0:T(8,128)S(1)} %get-tuple-element.233), channel_id=1, source_target_pairs={{0,1},{1,0},{2,3},{3,2},{4,5},{5,4},{6,7},{7,6},{8,9},{9,8},{10,11... | collective-permute-start | bytes 4718600 | tf_op jit(solution)/shard_map/ppermute | solution.py:392
  82.2 16.3 %collective-permute-start.11 = (f32[4,384,128]{2,1,0:T(8,128)S(1)}, f32[4,384,128]{2,1,0:T(8,128)S(1)}, u32[]{:S(2)}, u32[]{:S(2)}) collective-permute-start(f32[4,384,128]{2,1,0:T(8,128)S(1)} %get-tuple-element.348), channel_id=1, source_target_pairs={{0,4},{1,3},{2,6},{3,1},{4,0},{5,7},{6,2},{7,5},{8,12},{9,11},{10,... | collective-permute-start | bytes 2359304 | tf_op jit(solution)/shard_map/ppermute | solution.py:392
  97.8 11.2 %collective-permute-start.10 = (f32[16,200,128]{2,1,0:T(8,128)S(1)}, f32[16,200,128]{2,1,0:T(8,128)S(1)}, u32[]{:S(2)}, u32[]{:S(2)}) collective-permute-start(f32[16,200,128]{2,1,0:T(8,128)S(1)} %get-tuple-element.237), channel_id=1, source_target_pairs={{0,1},{1,0},{2,3},{3,2},{4,5},{5,4},{6,7},{7,6},{8,9},{9,8},{10,11... | collective-permute-start | bytes 4915208 | tf_op jit(solution)/shard_map/ppermute | solution.py:392
  97.9 14.9 %collective-permute-start.13 = (f32[8,192,128]{2,1,0:T(8,128)S(1)}, f32[8,192,128]{2,1,0:T(8,128)S(1)}, u32[]{:S(2)}, u32[]{:S(2)}) collective-permute-start(f32[8,192,128]{2,1,0:T(8,128)S(1)} %multiply_add_fusion.7), channel_id=1, source_target_pairs={{0,2},{1,5},{2,0},{3,7},{4,6},{5,1},{6,4},{7,3},{8,10},{9,13},{10,... | collective-permute-start | bytes 2359304 | tf_op jit(solution)/shard_map/ppermute | solution.py:392
  98.6 11.9 %collective-permute-start.14 = (f32[2,384,128]{2,1,0:T(8,128)S(1)}, f32[2,384,128]{2,1,0:T(8,128)S(1)}, u32[]{:S(2)}, u32[]{:S(2)}) collective-permute-start(f32[2,384,128]{2,1,0:T(8,128)S(1)} %get-tuple-element.356), channel_id=1, source_target_pairs={{0,8},{1,17},{2,10},{3,19},{4,12},{5,21},{6,14},{7,23},{8,0},{9,25... | collective-permute-start | bytes 1179656 | tf_op jit(solution)/shard_map/ppermute | solution.py:392
  110.5 10.5 %collective-permute-start.16 = (f32[16,208,128]{2,1,0:T(8,128)S(1)}, f32[16,208,128]{2,1,0:T(8,128)S(1)}, u32[]{:S(2)}, u32[]{:S(2)}) collective-permute-start(f32[16,208,128]{2,1,0:T(8,128)S(1)} %get-tuple-element.251), channel_id=1, source_target_pairs={{0,1},{1,0},{2,3},{3,2},{4,5},{5,4},{6,7},{7,6},{8,9},{9,8},{10,11... | collective-permute-start | bytes 5111816 | tf_op jit(solution)/shard_map/ppermute | solution.py:392
  111.0 9.6 %collective-permute-start.17 = (f32[1,384,128]{2,1,0:T(8,128)S(1)}, f32[1,384,128]{2,1,0:T(8,128)S(1)}, u32[]{:S(2)}, u32[]{:S(2)}) collective-permute-start(f32[1,384,128]{2,1,0:T(8,128)S(1)} %get-tuple-element.364), channel_id=1, source_target_pairs={{0,16},{1,9},{2,18},{3,11},{4,20},{5,13},{6,22},{7,15},{8,24},{9,1... | collective-permute-start | bytes 589832 | tf_op jit(solution)/shard_map/ppermute | solution.py:392
  113.0 12.0 %collective-permute-start.15 = (f32[4,192,128]{2,1,0:T(8,128)S(1)}, f32[4,192,128]{2,1,0:T(8,128)S(1)}, u32[]{:S(2)}, u32[]{:S(2)}) collective-permute-start(f32[4,192,128]{2,1,0:T(8,128)S(1)} %get-tuple-element.354), channel_id=1, source_target_pairs={{0,4},{1,3},{2,6},{3,1},{4,0},{5,7},{6,2},{7,5},{8,12},{9,11},{10,... | collective-permute-start | bytes 1179656 | tf_op jit(solution)/shard_map/ppermute | solution.py:392
  114.6 20.1 %collective-permute-start.12 = (f32[8,200,128]{2,1,0:T(8,128)S(1)}, f32[8,200,128]{2,1,0:T(8,128)S(1)}, u32[]{:S(2)}, u32[]{:S(2)}) collective-permute-start(f32[8,200,128]{2,1,0:T(8,128)S(1)} %multiply_add_fusion.5), channel_id=1, source_target_pairs={{0,2},{1,5},{2,0},{3,7},{4,6},{5,1},{6,4},{7,3},{8,10},{9,13},{10,... | collective-permute-start | bytes 2457608 | tf_op jit(solution)/shard_map/ppermute | solution.py:392
  120.6 12.1 %collective-permute-start.19 = (f32[1,384,128]{2,1,0:T(8,128)S(1)}, f32[1,384,128]{2,1,0:T(8,128)S(1)}, u32[]{:S(2)}, u32[]{:S(2)}) collective-permute-start(f32[1,384,128]{2,1,0:T(8,128)S(1)} %add.137), channel_id=1, source_target_pairs={{0,16},{1,9},{2,18},{3,11},{4,20},{5,13},{6,22},{7,15},{8,24},{9,1... | collective-permute-start | bytes 589832 | tf_op jit(solution)/shard_map/ppermute | solution.py:392
  121.1 19.2 %collective-permute-start.22 = (f32[8,208,128]{2,1,0:T(8,128)S(1)}, f32[8,208,128]{2,1,0:T(8,128)S(1)}, u32[]{:S(2)}, u32[]{:S(2)}) collective-permute-start(f32[8,208,128]{2,1,0:T(8,128)S(1)} %multiply_add_fusion.3), channel_id=1, source_target_pairs={{0,2},{1,5},{2,0},{3,7},{4,6},{5,1},{6,4},{7,3},{8,10},{9,13},{10,... | collective-permute-start | bytes 2555912 | tf_op jit(solution)/shard_map/ppermute | solution.py:392
  125.0 9.6 %collective-permute-start.18 = (f32[2,192,128]{2,1,0:T(8,128)S(1)}, f32[2,192,128]{2,1,0:T(8,128)S(1)}, u32[]{:S(2)}, u32[]{:S(2)}) collective-permute-start(f32[2,192,128]{2,1,0:T(8,128)S(1)} %get-tuple-element.362), channel_id=1, source_target_pairs={{0,8},{1,17},{2,10},{3,19},{4,12},{5,21},{6,14},{7,23},{8,0},{9,25... | collective-permute-start | bytes 589832 | tf_op jit(solution)/shard_map/ppermute | solution.py:392
  132.7 12.4 %collective-permute-start.21 = (f32[2,384,128]{2,1,0:T(8,128)S(1)}, f32[2,384,128]{2,1,0:T(8,128)S(1)}, u32[]{:S(2)}, u32[]{:S(2)}) collective-permute-start(f32[2,384,128]{2,1,0:T(8,128)S(1)} %constant_dynamic-update-slice_fusion), channel_id=1, source_target_pairs={{0,8},{1,17},{2,10},{3,19},{4,12},{5,21},{6,14},{7,23},{8,0},{9,25... | collective-permute-start | bytes 1179656 | tf_op jit(solution)/shard_map/ppermute | solution.py:392
  134.9 13.3 %collective-permute-start.20 = (f32[4,200,128]{2,1,0:T(8,128)S(1)}, f32[4,200,128]{2,1,0:T(8,128)S(1)}, u32[]{:S(2)}, u32[]{:S(2)}) collective-permute-start(f32[4,200,128]{2,1,0:T(8,128)S(1)} %get-tuple-element.352), channel_id=1, source_target_pairs={{0,4},{1,3},{2,6},{3,1},{4,0},{5,7},{6,2},{7,5},{8,12},{9,11},{10,... | collective-permute-start | bytes 1228808 | tf_op jit(solution)/shard_map/ppermute | solution.py:392
  140.5 10.2 %collective-permute-start.25 = (f32[4,208,128]{2,1,0:T(8,128)S(1)}, f32[4,208,128]{2,1,0:T(8,128)S(1)}, u32[]{:S(2)}, u32[]{:S(2)}) collective-permute-start(f32[4,208,128]{2,1,0:T(8,128)S(1)} %get-tuple-element.350), channel_id=1, source_target_pairs={{0,4},{1,3},{2,6},{3,1},{4,0},{5,7},{6,2},{7,5},{8,12},{9,11},{10,... | collective-permute-start | bytes 1277960 | tf_op jit(solution)/shard_map/ppermute | solution.py:392
  145.2 13.2 %collective-permute-start.29 = (f32[4,384,128]{2,1,0:T(8,128)S(1)}, f32[4,384,128]{2,1,0:T(8,128)S(1)}, u32[]{:S(2)}, u32[]{:S(2)}) collective-permute-start(f32[4,384,128]{2,1,0:T(8,128)S(1)} %constant_dynamic-update-slice_fusion.2), channel_id=1, source_target_pairs={{0,4},{1,3},{2,6},{3,1},{4,0},{5,7},{6,2},{7,5},{8,12},{9,11},{10,... | collective-permute-start | bytes 2359304 | tf_op jit(solution)/shard_map/ppermute | solution.py:392
  147.1 11.1 %collective-permute-start.24 = (f32[1,192,128]{2,1,0:T(8,128)S(1)}, f32[1,192,128]{2,1,0:T(8,128)S(1)}, u32[]{:S(2)}, u32[]{:S(2)}) collective-permute-start(f32[1,192,128]{2,1,0:T(8,128)S(1)} %get-tuple-element.370), channel_id=1, source_target_pairs={{0,16},{1,9},{2,18},{3,11},{4,20},{5,13},{6,22},{7,15},{8,24},{9,1... | collective-permute-start | bytes 294920 | tf_op jit(solution)/shard_map/ppermute | solution.py:392
  148.2 10.1 %collective-permute-start.23 = (f32[2,200,128]{2,1,0:T(8,128)S(1)}, f32[2,200,128]{2,1,0:T(8,128)S(1)}, u32[]{:S(2)}, u32[]{:S(2)}) collective-permute-start(f32[2,200,128]{2,1,0:T(8,128)S(1)} %get-tuple-element.360), channel_id=1, source_target_pairs={{0,8},{1,17},{2,10},{3,19},{4,12},{5,21},{6,14},{7,23},{8,0},{9,25... | collective-permute-start | bytes 614408 | tf_op jit(solution)/shard_map/ppermute | solution.py:392
  150.8 11.3 %collective-permute-start.28 = (f32[2,208,128]{2,1,0:T(8,128)S(1)}, f32[2,208,128]{2,1,0:T(8,128)S(1)}, u32[]{:S(2)}, u32[]{:S(2)}) collective-permute-start(f32[2,208,128]{2,1,0:T(8,128)S(1)} %get-tuple-element.358), channel_id=1, source_target_pairs={{0,8},{1,17},{2,10},{3,19},{4,12},{5,21},{6,14},{7,23},{8,0},{9,25... | collective-permute-start | bytes 638984 | tf_op jit(solution)/shard_map/ppermute | solution.py:392
  158.2 5.6 %collective-permute-start.27 = (f32[1,192,128]{2,1,0:T(8,128)S(1)}, f32[1,192,128]{2,1,0:T(8,128)S(1)}, u32[]{:S(2)}, u32[]{:S(2)}) collective-permute-start(f32[1,192,128]{2,1,0:T(8,128)S(1)} %add.152), channel_id=1, source_target_pairs={{0,16},{1,9},{2,18},{3,11},{4,20},{5,13},{6,22},{7,15},{8,24},{9,1... | collective-permute-start | bytes 294920 | tf_op jit(solution)/shard_map/ppermute | solution.py:392
  158.4 25.3 %collective-permute-start.35 = (f32[8,384,128]{2,1,0:T(8,128)S(1)}, f32[8,384,128]{2,1,0:T(8,128)S(1)}, u32[]{:S(2)}, u32[]{:S(2)}) collective-permute-start(f32[8,384,128]{2,1,0:T(8,128)S(1)} %constant_dynamic-update-slice_fusion.4.refs_0_), channel_id=1, source_target_pairs={{0,1},{1,0},{2,3},{3,2},{4,5},{5,4},{6,7},{7,6},{8,9},{9,8},{10,11... | collective-permute-start | bytes 4718600 | tf_op jit(solution)/shard_map/ppermute | solution.py:392
  160.0 24.6 %collective-permute-start.34 = (f32[8,384,128]{2,1,0:T(8,128)S(1)}, f32[8,384,128]{2,1,0:T(8,128)S(1)}, u32[]{:S(2)}, u32[]{:S(2)}) collective-permute-start(f32[8,384,128]{2,1,0:T(8,128)S(1)} %constant_dynamic-update-slice_fusion.4.refs_0_), channel_id=1, source_target_pairs={{0,2},{1,5},{2,0},{3,7},{4,6},{5,1},{6,4},{7,3},{8,10},{9,13},{10,... | collective-permute-start | bytes 4718600 | tf_op jit(solution)/shard_map/ppermute | solution.py:392
  163.8 11.4 %collective-permute-start.32 = (f32[2,192,128]{2,1,0:T(8,128)S(1)}, f32[2,192,128]{2,1,0:T(8,128)S(1)}, u32[]{:S(2)}, u32[]{:S(2)}) collective-permute-start(f32[2,192,128]{2,1,0:T(8,128)S(1)} %constant_dynamic-update-slice_fusion.6), channel_id=1, source_target_pairs={{0,8},{1,17},{2,10},{3,19},{4,12},{5,21},{6,14},{7,23},{8,0},{9,25... | collective-permute-start | bytes 589832 | tf_op jit(solution)/shard_map/ppermute | solution.py:392
  163.9 7.4 %collective-permute-start.26 = (f32[1,200,128]{2,1,0:T(8,128)S(1)}, f32[1,200,128]{2,1,0:T(8,128)S(1)}, u32[]{:S(2)}, u32[]{:S(2)}) collective-permute-start(f32[1,200,128]{2,1,0:T(8,128)S(1)} %get-tuple-element.368), channel_id=1, source_target_pairs={{0,16},{1,9},{2,18},{3,11},{4,20},{5,13},{6,22},{7,15},{8,24},{9,1... | collective-permute-start | bytes 307208 | tf_op jit(solution)/shard_map/ppermute | solution.py:392
  165.8 9.8 %collective-permute-start.31 = (f32[1,208,128]{2,1,0:T(8,128)S(1)}, f32[1,208,128]{2,1,0:T(8,128)S(1)}, u32[]{:S(2)}, u32[]{:S(2)}) collective-permute-start(f32[1,208,128]{2,1,0:T(8,128)S(1)} %get-tuple-element.366), channel_id=1, source_target_pairs={{0,16},{1,9},{2,18},{3,11},{4,20},{5,13},{6,22},{7,15},{8,24},{9,1... | collective-permute-start | bytes 319496 | tf_op jit(solution)/shard_map/ppermute | solution.py:392
  171.3 6.6 %collective-permute-start.30 = (f32[1,200,128]{2,1,0:T(8,128)S(1)}, f32[1,200,128]{2,1,0:T(8,128)S(1)}, u32[]{:S(2)}, u32[]{:S(2)}) collective-permute-start(f32[1,200,128]{2,1,0:T(8,128)S(1)} %add.157), channel_id=1, source_target_pairs={{0,16},{1,9},{2,18},{3,11},{4,20},{5,13},{6,22},{7,15},{8,24},{9,1... | collective-permute-start | bytes 307208 | tf_op jit(solution)/shard_map/ppermute | solution.py:392
  175.3 8.4 %collective-permute-start.36 = (f32[4,192,128]{2,1,0:T(8,128)S(1)}, f32[4,192,128]{2,1,0:T(8,128)S(1)}, u32[]{:S(2)}, u32[]{:S(2)}) collective-permute-start(f32[4,192,128]{2,1,0:T(8,128)S(1)} %constant_dynamic-update-slice_fusion.8), channel_id=1, source_target_pairs={{0,4},{1,3},{2,6},{3,1},{4,0},{5,7},{6,2},{7,5},{8,12},{9,11},{10,... | collective-permute-start | bytes 1179656 | tf_op jit(solution)/shard_map/ppermute | solution.py:392
  175.7 5.8 %collective-permute-start.37 = (f32[1,208,128]{2,1,0:T(8,128)S(1)}, f32[1,208,128]{2,1,0:T(8,128)S(1)}, u32[]{:S(2)}, u32[]{:S(2)}) collective-permute-start(f32[1,208,128]{2,1,0:T(8,128)S(1)} %add.159), channel_id=1, source_target_pairs={{0,16},{1,9},{2,18},{3,11},{4,20},{5,13},{6,22},{7,15},{8,24},{9,1... | collective-permute-start | bytes 319496 | tf_op jit(solution)/shard_map/ppermute | solution.py:392
  184.6 8.4 %collective-permute-start.41 = (f32[8,384,128]{2,1,0:T(8,128)S(1)}, f32[8,384,128]{2,1,0:T(8,128)S(1)}, u32[]{:S(2)}, u32[]{:S(2)}) collective-permute-start(f32[8,384,128]{2,1,0:T(8,128)S(1)} %collective-permute-done.34.refs_1_), channel_id=1, source_target_pairs={{0,1},{1,0},{2,3},{3,2},{4,5},{5,4},{6,7},{7,6},{8,9},{9,8},{10,11... | collective-permute-start | bytes 4718600 | tf_op jit(solution)/shard_map/ppermute | solution.py:392
  184.6 8.3 %collective-permute-start.33 = (f32[2,200,128]{2,1,0:T(8,128)S(1)}, f32[2,200,128]{2,1,0:T(8,128)S(1)}, u32[]{:S(2)}, u32[]{:S(2)}) collective-permute-start(f32[2,200,128]{2,1,0:T(8,128)S(1)} %constant_dynamic-update-slice_fusion.10), channel_id=1, source_target_pairs={{0,8},{1,17},{2,10},{3,19},{4,12},{5,21},{6,14},{7,23},{8,0},{9,25... | collective-permute-start | bytes 614408 | tf_op jit(solution)/shard_map/ppermute | solution.py:392
  184.6 13.8 %collective-permute-start.39 = (f32[8,192,128]{2,1,0:T(8,128)S(1)}, f32[8,192,128]{2,1,0:T(8,128)S(1)}, u32[]{:S(2)}, u32[]{:S(2)}) collective-permute-start(f32[8,192,128]{2,1,0:T(8,128)S(1)} %constant_dynamic-update-slice_fusion.14.refs_0_), channel_id=1, source_target_pairs={{0,2},{1,5},{2,0},{3,7},{4,6},{5,1},{6,4},{7,3},{8,10},{9,13},{10,... | collective-permute-start | bytes 2359304 | tf_op jit(solution)/shard_map/ppermute | solution.py:392
  185.5 11.7 %collective-permute-start.40 = (f32[2,208,128]{2,1,0:T(8,128)S(1)}, f32[2,208,128]{2,1,0:T(8,128)S(1)}, u32[]{:S(2)}, u32[]{:S(2)}) collective-permute-start(f32[2,208,128]{2,1,0:T(8,128)S(1)} %constant_dynamic-update-slice_fusion.12), channel_id=1, source_target_pairs={{0,8},{1,17},{2,10},{3,19},{4,12},{5,21},{6,14},{7,23},{8,0},{9,25... | collective-permute-start | bytes 638984 | tf_op jit(solution)/shard_map/ppermute | solution.py:392
  192.9 9.7 %collective-permute-start.38 = (f32[4,200,128]{2,1,0:T(8,128)S(1)}, f32[4,200,128]{2,1,0:T(8,128)S(1)}, u32[]{:S(2)}, u32[]{:S(2)}) collective-permute-start(f32[4,200,128]{2,1,0:T(8,128)S(1)} %constant_dynamic-update-slice_fusion.16), channel_id=1, source_target_pairs={{0,4},{1,3},{2,6},{3,1},{4,0},{5,7},{6,2},{7,5},{8,12},{9,11},{10,... | collective-permute-start | bytes 1228808 | tf_op jit(solution)/shard_map/ppermute | solution.py:392
  198.4 6.2 %collective-permute-start.45 = (f32[8,192,128]{2,1,0:T(8,128)S(1)}, f32[8,192,128]{2,1,0:T(8,128)S(1)}, u32[]{:S(2)}, u32[]{:S(2)}) collective-permute-start(f32[8,192,128]{2,1,0:T(8,128)S(1)} %collective-permute-done.39.refs_1_), channel_id=1, source_target_pairs={{0,1},{1,0},{2,3},{3,2},{4,5},{5,4},{6,7},{7,6},{8,9},{9,8},{10,11... | collective-permute-start | bytes 2359304 | tf_op jit(solution)/shard_map/ppermute | solution.py:392
  200.9 3.7 %collective-permute-start.44 = (f32[8,192,128]{2,1,0:T(8,128)S(1)}, f32[8,192,128]{2,1,0:T(8,128)S(1)}, u32[]{:S(2)}, u32[]{:S(2)}) collective-permute-start(f32[8,192,128]{2,1,0:T(8,128)S(1)} %constant_dynamic-update-slice_fusion.14.refs_0_), channel_id=1, source_target_pairs={{0,1},{1,0},{2,3},{3,2},{4,5},{5,4},{6,7},{7,6},{8,9},{9,8},{10,11... | collective-permute-start | bytes 2359304 | tf_op jit(solution)/shard_map/ppermute | solution.py:392
  202.6 17.0 %collective-permute-start.42 = (f32[8,200,128]{2,1,0:T(8,128)S(1)}, f32[8,200,128]{2,1,0:T(8,128)S(1)}, u32[]{:S(2)}, u32[]{:S(2)}) collective-permute-start(f32[8,200,128]{2,1,0:T(8,128)S(1)} %constant_dynamic-update-slice_fusion.20.refs_0_), channel_id=1, source_target_pairs={{0,2},{1,5},{2,0},{3,7},{4,6},{5,1},{6,4},{7,3},{8,10},{9,13},{10,... | collective-permute-start | bytes 2457608 | tf_op jit(solution)/shard_map/ppermute | solution.py:392
  202.7 12.8 %collective-permute-start.43 = (f32[4,208,128]{2,1,0:T(8,128)S(1)}, f32[4,208,128]{2,1,0:T(8,128)S(1)}, u32[]{:S(2)}, u32[]{:S(2)}) collective-permute-start(f32[4,208,128]{2,1,0:T(8,128)S(1)} %constant_dynamic-update-slice_fusion.18), channel_id=1, source_target_pairs={{0,4},{1,3},{2,6},{3,1},{4,0},{5,7},{6,2},{7,5},{8,12},{9,11},{10,... | collective-permute-start | bytes 1277960 | tf_op jit(solution)/shard_map/ppermute | solution.py:392
  215.6 10.3 %collective-permute-start.49 = (f32[8,208,128]{2,1,0:T(8,128)S(1)}, f32[8,208,128]{2,1,0:T(8,128)S(1)}, u32[]{:S(2)}, u32[]{:S(2)}) collective-permute-start(f32[8,208,128]{2,1,0:T(8,128)S(1)} %constant_dynamic-update-slice_fusion.22.refs_0_), channel_id=1, source_target_pairs={{0,1},{1,0},{2,3},{3,2},{4,5},{5,4},{6,7},{7,6},{8,9},{9,8},{10,11... | collective-permute-start | bytes 2555912 | tf_op jit(solution)/shard_map/ppermute | solution.py:392
  215.7 13.1 %collective-permute-start.48 = (f32[8,208,128]{2,1,0:T(8,128)S(1)}, f32[8,208,128]{2,1,0:T(8,128)S(1)}, u32[]{:S(2)}, u32[]{:S(2)}) collective-permute-start(f32[8,208,128]{2,1,0:T(8,128)S(1)} %constant_dynamic-update-slice_fusion.22.refs_0_), channel_id=1, source_target_pairs={{0,2},{1,5},{2,0},{3,7},{4,6},{5,1},{6,4},{7,3},{8,10},{9,13},{10,... | collective-permute-start | bytes 2555912 | tf_op jit(solution)/shard_map/ppermute | solution.py:392
  219.6 2.3 collective-permute-start.46
  219.6 3.5 %collective-permute-start.47 = (f32[8,200,128]{2,1,0:T(8,128)S(1)}, f32[8,200,128]{2,1,0:T(8,128)S(1)}, u32[]{:S(2)}, u32[]{:S(2)}) collective-permute-start(f32[8,200,128]{2,1,0:T(8,128)S(1)} %collective-permute-done.42.refs_1_), channel_id=1, source_target_pairs={{0,1},{1,0},{2,3},{3,2},{4,5},{5,4},{6,7},{7,6},{8,9},{9,8},{10,11... | collective-permute-start | bytes 2457608 | tf_op jit(solution)/shard_map/ppermute | solution.py:392
  228.7 2.4 %collective-permute-start.50 = (f32[8,208,128]{2,1,0:T(8,128)S(1)}, f32[8,208,128]{2,1,0:T(8,128)S(1)}, u32[]{:S(2)}, u32[]{:S(2)}) collective-permute-start(f32[8,208,128]{2,1,0:T(8,128)S(1)} %collective-permute-done.48.refs_1_), channel_id=1, source_target_pairs={{0,1},{1,0},{2,3},{3,2},{4,5},{5,4},{6,7},{7,6},{8,9},{9,8},{10,11... | collective-permute-start | bytes 2555912 | tf_op jit(solution)/shard_map/ppermute | solution.py:392
  (14 other events, 27.0 us)
